TPU v7x, 128 devices: a whole 4x4x4 slice. The times are simulated.
128 devices in a mesh: prow: 8 (over y, core), pcol: 16 (over z, x).
Axes of the slice: x: 4, y: 4, z: 4, core: 2. Of those that a mesh axis runs over, the one named last changes fastest.
Arguments:
- parent: float32 [6, 8, 256, 3, 16, 256], P(None, 'prow', None, None, 'pcol')
- children: float32 [4, 8, 256, 1, 16, 256], P(None, 'prow', None, None, 'pcol')
- index_maps: int32 [2, 16], replicated, may hold values from 0 to 47, as said below
Outputs:
- factored: float32 [6, 8, 256, 3, 16, 256], P(None, 'prow', None, None, 'pcol')
Inputs may be any that keep to these rules, and one draw needn't show every extreme that they name: `index_maps`: entry (k, u) is 3 u, 3 u + 1 or 3 u + 2, so each row rises strictly. Of the blocks u of one child with one remainder modulo 4, at most 1 go to parent blocks of one remainder modulo 2 * 4.
All inputs are finite; a program needn't handle non-finite values.
Results may differ from a plain program's by a relative error of at most 0.00005.
Values sent between devices are 32-bit elements; how exact they have to be, the bound alone decides.
No kernel may reach another device: no remote copies, remote signals or barrier semaphores. Data moves between devices by JAX's collectives and lax.ppermute only.
A program may use at most 128 MiB of HBM per device.

v0:
```python
import jax
import jax.numpy as jnp
from jax import lax
from jax.sharding import PartitionSpec as P

KB = 5


def broadcast(array, axis, root):
    mine = lax.axis_index(axis) == root
    return lax.psum(jnp.where(mine, array, jnp.zeros_like(array)), axis)


def per_device(parent, children, index_maps):
    prow_count = lax.axis_size("prow")
    pcol_count = lax.axis_size("pcol")
    prow_id = lax.axis_index("prow")
    pcol_id = lax.axis_index("pcol")
    half_grid = prow_count // 2
    block_size = parent.shape[2]
    local_rows = parent.shape[0]
    local_cols = parent.shape[3]
    child_rows = children.shape[0]
    child_cols = children.shape[3]
    child_blocks = index_maps.shape[1]
    highest = lax.Precision.HIGHEST
    child_id = prow_id // half_grid
    residue = prow_id % half_grid
    child_map = jnp.where(child_id == 0, index_maps[0], index_maps[1])
    col_ids = jnp.arange(local_cols) * pcol_count + pcol_id
    row_ids = jnp.arange(local_rows) * prow_count + prow_id
    shard_piece = lax.all_gather(children, "pcol", axis=4, tiled=True)
    piece_cols = shard_piece.shape[4]
    col_index = jnp.arange(child_cols)[:, None] * pcol_count + jnp.arange(piece_cols)[None, :]
    mapped = jnp.sum(
        jnp.where(
            col_index[:, :, None] == jnp.arange(child_blocks)[None, None, :],
            child_map[None, None, :],
            0,
        ),
        axis=2,
    )
    select = (mapped[None, :, :] == col_ids[:, None, None]).astype(jnp.float32)
    sectioning = jnp.einsum("luq,rauqb->ralb", select, shard_piece[:, 0], precision=highest)
    row_index = jnp.arange(child_rows) * half_grid + residue
    target = jnp.sum(
        jnp.where(row_index[:, None] == jnp.arange(child_blocks)[None, :], child_map[None, :], 0),
        axis=1,
    )
    target_row = target % prow_count
    slot_row = target // prow_count
    earlier = jnp.arange(child_rows)[:, None] > jnp.arange(child_rows)[None, :]
    position = jnp.sum(earlier & (target_row[:, None] == target_row[None, :]), axis=1)
    most_rows = (child_rows // 2 + 2) // 3 * (2 - min(1, half_grid // 3))
    placed = (target_row[None, None, :] == jnp.arange(prow_count)[:, None, None]) & (
        position[None, None, :] == jnp.arange(most_rows)[None, :, None]
    )
    placement = placed.astype(jnp.float32)
    labels = jnp.sum(jnp.where(placed, slot_row[None, None, :] + 1, 0), axis=2) - 1
    own_front = parent[:, 0, :, :, 0, :]
    received = lax.all_to_all(
        jnp.einsum("dsr,ralb->dsalb", placement, sectioning, precision=highest),
        "prow",
        split_axis=0,
        concat_axis=0,
        tiled=True,
    )
    got_labels = lax.all_to_all(labels, "prow", split_axis=0, concat_axis=0, tiled=True)
    select = (got_labels[None, :, :] == jnp.arange(local_rows)[:, None, None]).astype(jnp.float32)
    front_block = own_front + jnp.einsum("lps,psacb->lacb", select, received, precision=highest)
    for panel_index in range(KB):
        panel_front_block = front_block
        owner_row = panel_index % prow_count
        owner_col = panel_index % pcol_count
        slot_index = panel_index // prow_count
        diagonal = broadcast(panel_front_block[slot_index, :, 0, :], "prow", owner_row)
        owner_here = pcol_id == owner_col
        diagonal = jnp.where(owner_here, diagonal, jnp.eye(block_size, dtype=jnp.float32))
        factor = jnp.tril(jnp.linalg.cholesky(diagonal))
        column = panel_front_block[:, :, 0, :].reshape(local_rows * block_size, block_size)
        solved = lax.linalg.triangular_solve(
            factor, column, left_side=False, lower=True, transpose_a=True
        )
        solved = solved.reshape(local_rows, block_size, block_size)
        below_rows = jnp.where((row_ids > panel_index)[:, None, None], solved, 0.0)
        new_column = jnp.where((row_ids == panel_index)[:, None, None], factor[None], below_rows)
        panel_front_block = panel_front_block.at[:, :, 0, :].set(
            jnp.where(owner_here, new_column, panel_front_block[:, :, 0, :])
        )
        panel_left = broadcast(below_rows, "pcol", owner_col)
        grouped = panel_left.reshape(local_cols, pcol_count // prow_count, block_size, block_size)
        chosen = lax.dynamic_index_in_dim(grouped, pcol_id // prow_count, 1, keepdims=False)
        panel_right = broadcast(chosen, "prow", pcol_id % prow_count)
        front_block, panel_left, panel_right = (panel_front_block, panel_left, panel_right)
        front_block = front_block - jnp.einsum(
            "rab,ceb->race", panel_left, panel_right, precision=highest
        )
    zero_mask = (row_ids < KB)[:, None, None, None] & (col_ids >= KB)[None, None, :, None]
    front_block = jnp.where(zero_mask, 0.0, front_block)
    return front_block.reshape(local_rows, 1, block_size, local_cols, 1, block_size)


def solution(mesh):
    in_specs = (
        P(None, "prow", None, None, "pcol", None),
        P(None, "prow", None, None, "pcol", None),
        P(),
    )
    out_specs = P(None, "prow", None, None, "pcol", None)
    return jax.shard_map(
        per_device, mesh=mesh, in_specs=in_specs, out_specs=out_specs, check_vma=False
    )
```

profile of v0, /device:TPU:102, one launch (start us, length us, event | category | flops | bytes accessed | tf_op | source)
XLA Modules:
  0.0 1704.5 jit_solution(18239185843304473917)
XLA Ops:
  6.5 2.3 copy.219
  10.1 4.5 all-to-all-start
  14.7 105.5 %all-gather.2.cloned.1.call-done = f32[4,1,256,1,16,256]{5,2,3,1,0,4:T(8,128)} async-done(((f32[4,1,256,1,1,256]{5,2,3,1,0,4:T(8,128)}), f32[4,1,256,1,16,256]{5,2,3,1,0,4:T(8,128)}) %all-gather.2.cloned.1.call-update) | async-done | bytes 16777232 | tf_op jit(solution)/shard_map/all_gather | solution.py:32
  120.1 21.0 %fusion.11 = f32[4,256,3,256]{3,2,1,0:T(4,128)S(1)} fusion(f32[4,1,256,1,16,256]{5,2,3,1,0,4:T(8,128)} %all-gather.2.cloned.1.call-done, s32[16]{0:T(128)S(1)} %select_reduce_fusion.10, s32[3]{0:T(128)S(1)} %multiply_add_fusion.1), kind=kOutput, calls=%fused_computation.30 | convolution fusion | flops 150994992 | bytes 19923020 | tf_op jit(solution)/shard_map/luq,rauqb->ralb/dot_general | solution.py:44
  141.1 5.6 fusion.8
  146.7 4.6 copy.222
  151.3 4.7 all-to-all-start.1
  156.1 12.6 copy.217
  168.9 59.2 %all-to-all-done.1 = f32[8,1,256,3,256]{4,2,3,1,0:T(8,128)} async-done(((f32[8,1,256,3,256]{4,2,3,1,0:T(8,128)}), f32[8,1,256,3,256]{4,2,3,1,0:T(8,128)}, u32[]{:S(2)}, u32[]{:S(2)}) %all-to-all-start.1) | async-done | bytes 6291488 | tf_op jit(solution)/shard_map/all_to_all | solution.py:61
  228.2 11.8 fusion.3
  239.9 5.9 copy.224
  245.9 4.4 bitcast_add_fusion
  255.3 57.7 %all-reduce.17.cloned.1.call-done = f32[256,256]{0,1:T(8,128)} async-done(((f32[256,256]{0,1:T(8,128)}), f32[256,256]{0,1:T(8,128)}) %all-reduce.17.cloned.1.call-update) | async-done | bytes 262160 | tf_op jit(solution)/shard_map/psum | solution.py:11
  313.3 11.7 cholesky.256
  325.0 9.8 custom-call.19
  335.3 11.7 cholesky.273
  349.9 4.3 while.15
  354.2 19.7 %custom-call.20 = f32[2,128,128]{1,2,0:T(8,128)S(1)} custom-call(f32[2,128,128]{2,1,0:T(8,128)S(1)} %get-tuple-element.99), custom_call_target="InvertDiagBlocksLowerTriangular" | custom-call | tf_op jit(solution)/shard_map/triangular_solve/custom-call.0 | solution.py:81
  379.1 85.6 %all-reduce.19.cloned.1.call-done = f32[6,256,256]{2,1,0:T(8,128)} async-done(((f32[6,256,256]{2,1,0:T(8,128)}), f32[6,256,256]{2,1,0:T(8,128)}) %all-reduce.19.cloned.1.call-update) | async-done | bytes 1572880 | tf_op jit(solution)/shard_map/psum | solution.py:11
  468.4 3.0 select_dynamic-update-slice_fusion.4
  471.4 58.8 %all-reduce.21.cloned.1.call-done = f32[3,256,256]{2,1,0:T(8,128)} async-done(((f32[3,256,256]{2,1,0:T(8,128)}), f32[3,256,256]{2,1,0:T(8,128)}) %all-reduce.21.cloned.1.call-update) | async-done | bytes 786448 | tf_op jit(solution)/shard_map/psum | solution.py:11
  530.2 6.9 convolution_subtract_fusion.8
  537.1 2.2 copy-done.4
  542.4 56.9 %all-reduce.23.cloned.1.call-done = f32[256,256]{0,1:T(8,128)} async-done(((f32[256,256]{0,1:T(8,128)}), f32[256,256]{0,1:T(8,128)}) %all-reduce.23.cloned.1.call-update) | async-done | bytes 262160 | tf_op jit(solution)/shard_map/psum | solution.py:11
  599.6 11.7 cholesky.290
  611.4 9.8 custom-call.21
  621.6 11.7 cholesky.307
  636.8 4.2 while.16
  641.0 19.7 %custom-call.22 = f32[2,128,128]{1,2,0:T(8,128)S(1)} custom-call(f32[2,128,128]{2,1,0:T(8,128)S(1)} %get-tuple-element.100), custom_call_target="InvertDiagBlocksLowerTriangular" | custom-call | tf_op jit(solution)/shard_map/triangular_solve/custom-call.0 | solution.py:81
  665.9 85.7 %all-reduce.25.cloned.1.call-done = f32[6,256,256]{2,1,0:T(8,128)} async-done(((f32[6,256,256]{2,1,0:T(8,128)}), f32[6,256,256]{2,1,0:T(8,128)}) %all-reduce.25.cloned.1.call-update) | async-done | bytes 1572880 | tf_op jit(solution)/shard_map/psum | solution.py:11
  755.3 3.0 select_dynamic-update-slice_fusion.3
  758.3 59.0 %all-reduce.27.cloned.1.call-done = f32[3,256,256]{2,1,0:T(8,128)} async-done(((f32[3,256,256]{2,1,0:T(8,128)}), f32[3,256,256]{2,1,0:T(8,128)}) %all-reduce.27.cloned.1.call-update) | async-done | bytes 786448 | tf_op jit(solution)/shard_map/psum | solution.py:11
  817.2 6.9 convolution_subtract_fusion.7
  829.2 57.1 %all-reduce.29.cloned.1.call-done = f32[256,256]{0,1:T(8,128)} async-done(((f32[256,256]{0,1:T(8,128)}), f32[256,256]{0,1:T(8,128)}) %all-reduce.29.cloned.1.call-update) | async-done | bytes 262160 | tf_op jit(solution)/shard_map/psum | solution.py:11
  886.6 11.7 cholesky.324
  898.4 9.8 custom-call.23
  908.7 11.7 cholesky.341
  923.8 4.5 while.17
  928.3 19.7 %custom-call.24 = f32[2,128,128]{1,2,0:T(8,128)S(1)} custom-call(f32[2,128,128]{2,1,0:T(8,128)S(1)} %get-tuple-element.101), custom_call_target="InvertDiagBlocksLowerTriangular" | custom-call | tf_op jit(solution)/shard_map/triangular_solve/custom-call.0 | solution.py:81
  953.2 85.6 %all-reduce.31.cloned.1.call-done = f32[6,256,256]{2,1,0:T(8,128)} async-done(((f32[6,256,256]{2,1,0:T(8,128)}), f32[6,256,256]{2,1,0:T(8,128)}) %all-reduce.31.cloned.1.call-update) | async-done | bytes 1572880 | tf_op jit(solution)/shard_map/psum | solution.py:11
  1042.5 3.0 select_dynamic-update-slice_fusion.2
  1045.5 58.8 %all-reduce.33.cloned.1.call-done = f32[3,256,256]{2,1,0:T(8,128)} async-done(((f32[3,256,256]{2,1,0:T(8,128)}), f32[3,256,256]{2,1,0:T(8,128)}) %all-reduce.33.cloned.1.call-update) | async-done | bytes 786448 | tf_op jit(solution)/shard_map/psum | solution.py:11
  1104.3 6.9 convolution_subtract_fusion.6
  1116.3 57.1 %all-reduce.35.cloned.1.call-done = f32[256,256]{0,1:T(8,128)} async-done(((f32[256,256]{0,1:T(8,128)}), f32[256,256]{0,1:T(8,128)}) %all-reduce.35.cloned.1.call-update) | async-done | bytes 262160 | tf_op jit(solution)/shard_map/psum | solution.py:11
  1173.6 11.7 cholesky.358
  1185.4 9.8 custom-call.25
  1195.7 11.7 cholesky.375
  1210.8 4.3 while.18
  1215.1 19.7 %custom-call.26 = f32[2,128,128]{1,2,0:T(8,128)S(1)} custom-call(f32[2,128,128]{2,1,0:T(8,128)S(1)} %get-tuple-element.102), custom_call_target="InvertDiagBlocksLowerTriangular" | custom-call | tf_op jit(solution)/shard_map/triangular_solve/custom-call.0 | solution.py:81
  1240.0 85.6 %all-reduce.37.cloned.1.call-done = f32[6,256,256]{2,1,0:T(8,128)} async-done(((f32[6,256,256]{2,1,0:T(8,128)}), f32[6,256,256]{2,1,0:T(8,128)}) %all-reduce.37.cloned.1.call-update) | async-done | bytes 1572880 | tf_op jit(solution)/shard_map/psum | solution.py:11
  1329.4 3.0 select_dynamic-update-slice_fusion.1
  1332.3 59.0 %all-reduce.39.cloned.1.call-done = f32[3,256,256]{2,1,0:T(8,128)} async-done(((f32[3,256,256]{2,1,0:T(8,128)}), f32[3,256,256]{2,1,0:T(8,128)}) %all-reduce.39.cloned.1.call-update) | async-done | bytes 786448 | tf_op jit(solution)/shard_map/psum | solution.py:11
  1391.3 6.9 convolution_subtract_fusion.5
  1403.5 56.9 %all-reduce.41.cloned.1.call-done = f32[256,256]{0,1:T(8,128)} async-done(((f32[256,256]{0,1:T(8,128)}), f32[256,256]{0,1:T(8,128)}) %all-reduce.41.cloned.1.call-update) | async-done | bytes 262160 | tf_op jit(solution)/shard_map/psum | solution.py:11
  1460.7 11.7 cholesky.392
  1472.4 9.8 custom-call.27
  1482.7 11.7 cholesky.409
  1497.8 4.2 while.19
  1502.1 19.7 %custom-call.28 = f32[2,128,128]{1,2,0:T(8,128)S(1)} custom-call(f32[2,128,128]{2,1,0:T(8,128)S(1)} %get-tuple-element.103), custom_call_target="InvertDiagBlocksLowerTriangular" | custom-call | tf_op jit(solution)/shard_map/triangular_solve/custom-call.0 | solution.py:81
  1527.0 85.6 %all-reduce.43.cloned.1.call-done = f32[6,256,256]{2,1,0:T(8,128)} async-done(((f32[6,256,256]{2,1,0:T(8,128)}), f32[6,256,256]{2,1,0:T(8,128)}) %all-reduce.43.cloned.1.call-update) | async-done | bytes 1572880 | tf_op jit(solution)/shard_map/psum | solution.py:11
  1616.3 3.0 select_dynamic-update-slice_fusion
  1619.3 58.8 %all-reduce.45.cloned.1.call-done = f32[3,256,256]{2,1,0:T(8,128)} async-done(((f32[3,256,256]{2,1,0:T(8,128)}), f32[3,256,256]{2,1,0:T(8,128)}) %all-reduce.45.cloned.1.call-update) | async-done | bytes 786448 | tf_op jit(solution)/shard_map/psum | solution.py:11
  1678.1 7.6 select_bitcast_fusion
  1685.7 12.1 copy.265
  (239 shorter events, 103.2 us)
Async XLA Ops:
  6.5 2.3 copy-start.10
  6.5 113.6 %all-gather.2.cloned.1.call-start = ((), (), s32[]{:S(2)}) async-start(), calls=%async_computation.2 | async-start | bytes 17825792 | tf_op jit(solution)/shard_map/all_gather | solution.py:32
  10.1 141.2 %all-to-all-start = ((s32[8,1,1]{2,1,0:T(1,128)}), s32[8,1,1]{2,1,0:T(1,128)S(1)}, u32[]{:S(2)}, u32[]{:S(2)}) async-start(s32[8,1,1]{2,1,0:T(1,128)} %copy.218), calls=%async_computation | async-start | bytes 8192 | tf_op jit(solution)/shard_map/all_to_all | solution.py:68
  151.3 76.9 %all-to-all-start.1 = ((f32[8,1,256,3,256]{4,2,3,1,0:T(8,128)}), f32[8,1,256,3,256]{4,2,3,1,0:T(8,128)}, u32[]{:S(2)}, u32[]{:S(2)}) async-start(f32[8,1,256,3,256]{4,2,3,1,0:T(8,128)} %copy.222), calls=%async_computation.1 | async-start | bytes 12582912 | tf_op jit(solution)/shard_map/all_to_all | solution.py:61
  156.0 157.0 %all-reduce.17.cloned.1.call-start = ((), (), s32[]{:S(2)}) async-start(), calls=%async_computation.3 | async-start | bytes 524288 | tf_op jit(solution)/shard_map/psum | solution.py:11
  250.2 2.2 copy-start
  253.2 211.5 %all-reduce.19.cloned.1.call-start = ((), (), s32[]{:S(2)}) async-start(), calls=%async_computation.4 | async-start | bytes 3145728 | tf_op jit(solution)/shard_map/psum | solution.py:11
  253.4 1.4 slice-start
  379.0 151.2 %all-reduce.21.cloned.1.call-start = ((), (), s32[]{:S(2)}) async-start(), calls=%async_computation.5 | async-start | bytes 1572864 | tf_op jit(solution)/shard_map/psum | solution.py:11
  466.8 132.5 %all-reduce.23.cloned.1.call-start = ((), (), s32[]{:S(2)}) async-start(), calls=%async_computation.6 | async-start | bytes 524288 | tf_op jit(solution)/shard_map/psum | solution.py:11
  468.4 61.8 %copy-start.6 = (f32[6,256,256]{2,1,0:T(8,128)S(1)}, f32[6,256,256]{2,1,0:T(8,128)}, u32[]{:S(2)}) copy-start(f32[6,256,256]{2,1,0:T(8,128)} %all-reduce.19.cloned.1.call-done) | copy-start | bytes 4718596
  537.1 2.2 copy-start.4
  540.1 211.5 %all-reduce.25.cloned.1.call-start = ((), (), s32[]{:S(2)}) async-start(), calls=%async_computation.7 | async-start | bytes 3145728 | tf_op jit(solution)/shard_map/psum | solution.py:11
  540.5 1.4 slice-start.4
  665.8 151.4 %all-reduce.27.cloned.1.call-start = ((), (), s32[]{:S(2)}) async-start(), calls=%async_computation.8 | async-start | bytes 1572864 | tf_op jit(solution)/shard_map/psum | solution.py:11
  753.7 132.7 %all-reduce.29.cloned.1.call-start = ((), (), s32[]{:S(2)}) async-start(), calls=%async_computation.9 | async-start | bytes 524288 | tf_op jit(solution)/shard_map/psum | solution.py:11
  755.3 61.9 %copy-start.7 = (f32[6,256,256]{2,1,0:T(8,128)S(1)}, f32[6,256,256]{2,1,0:T(8,128)}, u32[]{:S(2)}) copy-start(f32[6,256,256]{2,1,0:T(8,128)} %all-reduce.25.cloned.1.call-done) | copy-start | bytes 4718596
  824.1 2.2 copy-start.2
  827.1 211.7 %all-reduce.31.cloned.1.call-start = ((), (), s32[]{:S(2)}) async-start(), calls=%async_computation.10 | async-start | bytes 3145728 | tf_op jit(solution)/shard_map/psum | solution.py:11
  827.4 1.4 slice-start.2
  953.1 151.2 %all-reduce.33.cloned.1.call-start = ((), (), s32[]{:S(2)}) async-start(), calls=%async_computation.11 | async-start | bytes 1572864 | tf_op jit(solution)/shard_map/psum | solution.py:11
  1040.9 132.5 %all-reduce.35.cloned.1.call-start = ((), (), s32[]{:S(2)}) async-start(), calls=%async_computation.12 | async-start | bytes 524288 | tf_op jit(solution)/shard_map/psum | solution.py:11
  1042.5 61.8 %copy-start.8 = (f32[6,256,256]{2,1,0:T(8,128)S(1)}, f32[6,256,256]{2,1,0:T(8,128)}, u32[]{:S(2)}) copy-start(f32[6,256,256]{2,1,0:T(8,128)} %all-reduce.31.cloned.1.call-done) | copy-start | bytes 4718596
  1111.2 2.2 copy-start.3
  1114.2 211.5 %all-reduce.37.cloned.1.call-start = ((), (), s32[]{:S(2)}) async-start(), calls=%async_computation.13 | async-start | bytes 3145728 | tf_op jit(solution)/shard_map/psum | solution.py:11
  1114.4 1.4 slice-start.3
  1239.9 151.3 %all-reduce.39.cloned.1.call-start = ((), (), s32[]{:S(2)}) async-start(), calls=%async_computation.14 | async-start | bytes 1572864 | tf_op jit(solution)/shard_map/psum | solution.py:11
  1327.7 132.7 %all-reduce.41.cloned.1.call-start = ((), (), s32[]{:S(2)}) async-start(), calls=%async_computation.15 | async-start | bytes 524288 | tf_op jit(solution)/shard_map/psum | solution.py:11
  1329.3 61.9 %copy-start.9 = (f32[6,256,256]{2,1,0:T(8,128)S(1)}, f32[6,256,256]{2,1,0:T(8,128)}, u32[]{:S(2)}) copy-start(f32[6,256,256]{2,1,0:T(8,128)} %all-reduce.37.cloned.1.call-done) | copy-start | bytes 4718596
  1398.2 2.2 copy-start.1
  1401.1 211.4 %all-reduce.43.cloned.1.call-start = ((), (), s32[]{:S(2)}) async-start(), calls=%async_computation.16 | async-start | bytes 3145728 | tf_op jit(solution)/shard_map/psum | solution.py:11
  1401.6 1.4 slice-start.1
  1526.9 151.2 %all-reduce.45.cloned.1.call-start = ((), (), s32[]{:S(2)}) async-start(), calls=%async_computation.17 | async-start | bytes 1572864 | tf_op jit(solution)/shard_map/psum | solution.py:11
  1616.3 61.8 %copy-start.5 = (f32[6,256,256]{2,1,0:T(8,128)S(1)}, f32[6,256,256]{2,1,0:T(8,128)}, u32[]{:S(2)}) copy-start(f32[6,256,256]{2,1,0:T(8,128)} %all-reduce.43.cloned.1.call-done) | copy-start | bytes 4718596
Sparse Core Ops, SparseCore 0:
  9.5 110.5 all-gather.1
  253.3 59.6 all-reduce.16
  379.1 85.4 all-reduce.18
  467.0 63.1 all-reduce.20
  540.2 59.0 all-reduce.22
  666.0 85.5 all-reduce.24
  754.0 63.1 all-reduce.26
  827.2 59.1 all-reduce.28
  953.2 85.5 all-reduce.30
  1041.1 63.1 all-reduce.32
  1114.3 59.0 all-reduce.34
  1240.1 85.4 all-reduce.36
  1328.1 63.1 all-reduce.38
  1401.3 59.1 all-reduce.40
  1527.0 85.4 all-reduce.42
  1614.9 63.1 all-reduce.44
where the time goes:
time: 1710 us; the launch traced here: 1700 us
  waiting for transfers between devices  1170 us (68%)
  other arithmetic  317 us (19%)
  matrix products  91.6 us (5%)
  local copies, waits for them, and re-layouts  89.5 us (5%)
  between operations  20.9 us (1%)
    psum x15, waiting for transfers between devices, broadcast(): return lax.psum(jnp.where(mine, array, jnp.zeros_like(array)), axis)  1010 us
    another operation x34, other arithmetic, per_device(): factor = jnp.tril(jnp.linalg.cholesky(diagonal))  173 us
    all_gather x1, waiting for transfers between devices, per_device(): shard_piece = lax.all_gather(children, 'pcol', axis=4, tiled=True)  105 us
    another operation x16, other arithmetic, per_device(): lax.linalg.triangular_solve(factor, column, left_side=False, lower=True,...  103 us
    all_to_all x1, waiting for transfers between devices, per_device(): lax.all_to_all(jnp.einsum('dsr,ralb->dsalb', placement, sectioning, preci...  59.2 us
    dot_general x5, matrix products, per_device(): jnp.einsum('rab,ceb->race', panel_left, panel_right, precision=highest)  35.2 us
  transfers between devices with their start and end apart: 18, of which 17 were waited for; matrix products, arithmetic and copies ran while one was open for 4% of the time, Pallas kernels for 0%

commit v1 on v0

v1 whole, which is shorter than its diff:
```python
import functools
import jax
import jax.numpy as jnp
from jax import lax
from jax.experimental import pallas as pl
from jax.experimental.pallas import tpu as pltpu
from jax.sharding import PartitionSpec as P

KB = 5
NB = 256
HB = 128
LANES = 128
F32 = jnp.float32
BF16 = jnp.bfloat16
VMEM_LIMIT = 60 * 1024 * 1024
VM = pl.BlockSpec(memory_space=pltpu.VMEM)
SM = pl.BlockSpec(memory_space=pltpu.SMEM)


def route_of(meta, n):
    flip, d = n // 3, n % 3
    row = meta[32]
    residue = (3 * (row + 8 - d)) % 4
    parity = ((row + 16 - 3 * residue - d) // 4) % 2
    child = (parity + flip) % 2
    first = 4 * parity + residue
    second = first + 8
    is_first = meta[child * 16 + first] == 3 * first + d
    is_second = meta[child * 16 + second] == 3 * second + d
    block = jnp.where(is_first, first, second)
    return child, jnp.logical_or(is_first, is_second), (3 * block + d) // 8


def assemble_kernel(meta, parts_ref, out_ref):
    for j in range(KB):
        out_ref[j] = parts_ref[j, 0:6]
    for n in range(6):
        child, there, slot = route_of(meta, n)
        for v in range(2):
            column = meta[child * 16 + v]

            @pl.when(jnp.logical_and(there, column < KB))
            def _():
                out_ref[column, slot] = out_ref[column, slot] + parts_ref[v, 6 + n]


UPPER = [(k, i) for k in range(KB) for i in range(k, KB)]
CHILD_SOURCES = [(c, u, v) for c in range(2) for (u, v) in ((0, 0), (0, 1), (1, 1))]


def exact(a, b, dims):
    return lax.dot_general(a, b, (dims, ((), ())), precision=lax.Precision.HIGHEST, preferred_element_type=F32)


def factor_128(a_ref, x_ref, u_ref):
    shape = (8, LANES)
    lane = lax.broadcasted_iota(jnp.int32, (HB, LANES), 1)
    sub = lax.broadcasted_iota(jnp.int32, (HB, LANES), 0)
    x_ref[...] = jnp.where(lane == sub, 1.0, 0.0).astype(F32)
    for g in range(HB // 8):
        rows = slice(8 * g, 8 * g + 8)
        a_g = a_ref[rows, :]
        x_g = x_ref[rows, :]
        cols = [jnp.broadcast_to(a_g[:, 8 * g + s : 8 * g + s + 1], shape) for s in range(8)]
        d = [[jnp.broadcast_to(cols[s][t : t + 1, :], shape) for s in range(t + 1)] for t in range(8)]
        low = [[None] * 8 for _ in range(8)]
        rinv = []
        for s in range(8):
            r = lax.rsqrt(d[s][s])
            rinv.append(r)
            for t in range(s + 1, 8):
                low[t][s] = d[t][s] * r
            for t in range(s + 1, 8):
                for t2 in range(s + 1, t + 1):
                    d[t][t2] = d[t][t2] - low[t][s] * low[t2][s]
        ub, xb = [], []
        for t in range(8):
            ua = jnp.broadcast_to(a_g[t : t + 1, :], shape)
            xa = jnp.broadcast_to(x_g[t : t + 1, :], shape)
            for s in range(t):
                ua = ua - low[t][s] * ub[s]
                xa = xa - low[t][s] * xb[s]
            ub.append(ua * rinv[t])
            xb.append(xa * rinv[t])
            u_ref[8 * g + t : 8 * g + t + 1, :] = ub[t][0:1, :]
            x_ref[8 * g + t : 8 * g + t + 1, :] = xb[t][0:1, :]
        for i in range(g + 1, HB // 8):
            rows_i = slice(8 * i, 8 * i + 8)
            a_i = a_ref[rows_i, :]
            x_i = x_ref[rows_i, :]
            w = []
            for t in range(8):
                wt = jnp.broadcast_to(a_i[:, 8 * g + t : 8 * g + t + 1], shape)
                for s in range(t):
                    wt = wt - low[t][s] * w[s]
                w.append(wt * rinv[t])
            for t in range(8):
                a_i = a_i - w[t] * ub[t]
                x_i = x_i - w[t] * xb[t]
            a_ref[rows_i, :] = a_i
            x_ref[rows_i, :] = x_i
    u_ref[...] = jnp.where(lane >= sub, u_ref[...], 0.0)


def split(a):
    high = a.astype(BF16)
    return high, (a - high.astype(F32)).astype(BF16)


def chain_kernel(meta, parts_ref, u_ref, th_ref, tl_ref, f_ref, v_ref, a_s, x_s, u_s):
    def take(position, s, h):
        return parts_ref[s, position, pl.ds(h, 16, stride=2), :]

    for at, (k, i) in enumerate(UPPER):
        for s in range(16):
            for h in range(2):
                f_ref[k * KB + i, 16 * s : 16 * s + 16, HB * h : HB * h + HB] = take(at, s, h)
    for at, (c, u, v) in enumerate(CHILD_SOURCES):
        k = meta[c * 16 + u]
        i = meta[c * 16 + v]

        @pl.when(jnp.logical_and(k < KB, i < KB))
        def _():
            for s in range(16):
                for h in range(2):
                    place = (k * KB + i, slice(16 * s, 16 * s + 16), slice(HB * h, HB * h + HB))
                    f_ref[place] = f_ref[place] + take(15 + at, s, h)

    th_ref[...] = jnp.zeros_like(th_ref)
    tl_ref[...] = jnp.zeros_like(tl_ref)
    u_ref[...] = jnp.zeros_like(u_ref)

    @pl.loop(0, 2 * KB)
    def _(step):
        k = step // 2
        half = step % 2
        kk = k * KB + k

        @pl.when(half == 0)
        def _():
            a_s[...] = f_ref[kk, 0:HB, 0:HB]

        @pl.when(half == 1)
        def _():
            u12 = exact(v_ref[0:HB, 0:HB], f_ref[kk, 0:HB, HB:NB], ((1,), (0,)))
            u_ref[kk, 0:HB, HB:NB] = u12
            a_s[...] = f_ref[kk, HB:NB, HB:NB] - exact(u12, u12, ((0,), (0,)))

        factor_128(a_s, x_s, u_s)

        @pl.when(half == 0)
        def _():
            u_ref[kk, 0:HB, 0:HB] = u_s[...]
            v_ref[0:HB, 0:HB] = x_s[...]

        @pl.when(half == 1)
        def _():
            u_ref[kk, HB:NB, HB:NB] = u_s[...]
            v_ref[HB:NB, HB:NB] = x_s[...]
            v_ref[0:HB, HB:NB] = jnp.zeros((HB, HB), F32)
            lx = exact(u_ref[kk, 0:HB, HB:NB], v_ref[0:HB, 0:HB], ((0,), (0,)))
            v_ref[HB:NB, 0:HB] = -exact(x_s[...], lx, ((1,), (0,)))
            high, low = split(v_ref[...].T)
            th_ref[kk] = high
            tl_ref[kk] = low

            @pl.loop(k + 1, KB)
            def _(i):
                u = exact(v_ref[...], f_ref[k * KB + i], ((1,), (0,)))
                u_ref[k * KB + i] = u
                high, low = split(u)
                th_ref[k * KB + i] = high
                tl_ref[k * KB + i] = low

            @pl.loop(k + 1, KB)
            def _(i):
                @pl.loop(i, KB)
                def _(j):
                    f_ref[i * KB + j] = f_ref[i * KB + j] - exact(
                        u_ref[k * KB + i], u_ref[k * KB + j], ((0,), (0,))
                    )


def dot3(ah, al, bh, bl, dims):
    def dot(a, b):
        return lax.dot_general(a, b, (dims, ((), ())), preferred_element_type=F32)

    return dot(ah, bh) + (dot(ah, bl) + dot(al, bh))


NN = ((1,), (0,))
NT = ((1,), (1,))


def solve_rows(raw_ref, yh_ref, yl_ref, th_ref, tl_ref):
    for k in range(KB):
        at = slice(NB * k, NB * k + NB)
        t = raw_ref[:, at]
        for m in range(k):
            am = slice(NB * m, NB * m + NB)
            t = t - dot3(yh_ref[:, am], yl_ref[:, am], th_ref[m * KB + k], tl_ref[m * KB + k], NN)
        high, low = split(t)
        y = dot3(high, low, th_ref[k * KB + k], tl_ref[k * KB + k], NN)
        raw_ref[:, at] = y
        high, low = split(y)
        yh_ref[:, at] = high
        yl_ref[:, at] = low


def right_kernel(parts_ref, th_ref, tl_ref, yh_ref, yl_ref, raw):
    @pl.loop(0, 16)
    def _(s):
        for c in range(3):
            for j in range(KB):
                for h in range(2):
                    raw[pl.ds(pl.multiple_of(NB * c + 16 * s, 16), 16), NB * j + HB * h : NB * j + HB * h + HB] = parts_ref[
                        s, j, c, pl.ds(h, 16, stride=2), :
                    ]
    solve_rows(raw, yh_ref, yl_ref, th_ref, tl_ref)


ROWS_STEP = 2


def schur_kernel(meta, parts_ref, th_ref, tl_ref, rh_ref, rl_ref, u_ref, parent_ref, child_ref, out_ref, raw, yh, yl):
    step = pl.program_id(0)
    row, col = meta[32], meta[33]

    @pl.loop(0, 16)
    def _(s):
        for a in range(ROWS_STEP):
            for j in range(KB):
                for h in range(2):
                    raw[pl.ds(pl.multiple_of(NB * a + 16 * s, 16), 16), NB * j + HB * h : NB * j + HB * h + HB] = parts_ref[
                        s, j, a, pl.ds(h, 16, stride=2), :
                    ]
    solve_rows(raw, yh, yl, th_ref, tl_ref)
    for a in range(ROWS_STEP):
        slot = step * ROWS_STEP + a
        block_row = row + 8 * slot
        rows = slice(NB * a, NB * a + NB)
        for c in range(3):
            block_col = col + 16 * c

            def put(h, value):
                out_ref[pl.ds(1536 * a + 2 * c + h, NB, stride=6), :] = value

            @pl.when(jnp.logical_and(block_row >= KB, block_col >= KB))
            def _():
                cols = slice(NB * c, NB * c + NB)
                product = dot3(yh[rows, :], yl[rows, :], rh_ref[cols, :], rl_ref[cols, :], NT)
                for h in range(2):
                    put(h, parent_ref[pl.ds(1536 * a + 2 * c + h, NB, stride=6), :] - product[:, HB * h : HB * h + HB])
                turn = block_col % 3
                source = block_col // 3
                for n in range(6):
                    child, there, to = route_of(meta, n)
                    here = jnp.logical_and(there, to == slot)

                    @pl.when(jnp.logical_and(here, meta[child * 16 + source] == block_col))
                    def _():
                        for h in range(2):
                            at = pl.ds(1536 * a + 2 * c + h, NB, stride=6)
                            out_ref[at, :] = out_ref[at, :] + child_ref[turn, n, pl.ds(h, NB, stride=2), :]

            @pl.when(jnp.logical_and(block_row < KB, block_col >= KB))
            def _():
                for h in range(2):
                    put(h, jnp.zeros((NB, HB), F32))

            if c == 0:

                @pl.when(jnp.logical_and(block_row >= KB, block_col < KB))
                def _():
                    for j in range(KB):

                        @pl.when(block_col == j)
                        def _():
                            for h in range(2):
                                put(h, raw[rows, NB * j + HB * h : NB * j + HB * h + HB])

                @pl.when(jnp.logical_and(block_row < KB, block_col < KB))
                def _():
                    block = u_ref[jnp.minimum(block_col, KB - 1) * KB + jnp.minimum(block_row, KB - 1)].T
                    for h in range(2):
                        put(h, block[:, HB * h : HB * h + HB])


def call(kernel, out_shape, in_specs, scratch, **extra):
    return pl.pallas_call(
        kernel,
        out_shape=out_shape,
        in_specs=in_specs,
        out_specs=jax.tree.map(lambda _: VM, out_shape),
        scratch_shapes=scratch,
        compiler_params=pltpu.CompilerParams(vmem_limit_bytes=VMEM_LIMIT),
        **extra,
    )


def shaped(shape, dtype=F32):
    return jax.ShapeDtypeStruct(shape, dtype)


def per_device(parent, children, index_maps):
    row = lax.axis_index("prow")
    col = lax.axis_index("pcol")
    meta = jnp.concatenate([index_maps.reshape(-1), jnp.stack([row, col]).astype(jnp.int32)])
    front = parent.reshape(6, NB, 3, 2, LANES)
    lead = front[:, :, 0].reshape(6, 16, 32, LANES)
    child = children.reshape(4, 16, 32, LANES)

    first = jnp.stack([lead[0], child[0]], axis=1)
    first = lax.all_to_all(first, "pcol", 0, 0, tiled=True)
    first = jnp.concatenate([first[0:KB, 0], first[0:2, 1]], axis=0)
    every = lax.all_gather(first, "prow")
    picked = [every[k, i] for k, i in UPPER] + [every[4 * c + u, KB + v] for c, u, v in CHILD_SOURCES]
    lead_parts = lax.all_gather(jnp.stack(picked), "pcol")

    child_id, residue = row // 4, row % 4
    routed = []
    for flip in range(2):
        parity = (child_id + flip) % 2
        for d in range(3):
            block = 4 * parity + residue
            chosen = jnp.where(meta[child_id * 16 + block] == 3 * block + d, parity, parity + 2)
            piece = lax.dynamic_index_in_dim(child, chosen, 0, keepdims=False)
            perm = [(p, (3 * (p % 4) + d + 4 * ((p // 4 + flip) % 2)) % 8) for p in range(8)]
            routed.append(lax.ppermute(piece, "prow", perm))
    routed = jnp.stack(routed)

    panel = jnp.concatenate([lead, routed], axis=0).transpose(1, 0, 2, 3)
    panel = lax.all_to_all(panel, "pcol", 0, 0, tiled=True)
    slices = call(assemble_kernel, shaped((KB, 6, 32, LANES)), [SM, VM], [])(meta, panel[0:KB])

    even, odd = slices[:, 0::2], slices[:, 1::2]
    is_even = col % 2 == 0
    perm_a, perm_b = [], []
    for p in range(8):
        for s in range(16):
            perm_a.append((p * 16 + s, (s // 2) * 16 + p + 8 * (s % 2)))
            perm_b.append((p * 16 + s, (s // 2) * 16 + p + 8 * (1 - s % 2)))
    got_a = lax.ppermute(jnp.where(is_even, even, odd), ("prow", "pcol"), perm_a)
    got_b = lax.ppermute(jnp.where(is_even, odd, even), ("prow", "pcol"), perm_b)
    low_side = col < 8
    pair = jnp.stack([jnp.where(low_side, got_a, got_b), jnp.where(low_side, got_b, got_a)])

    left_parts = lax.all_gather(slices, "pcol")
    right_parts = lax.all_gather(pair, "prow").reshape(16, KB, 3, 32, LANES)

    moved = []
    for d in range(3):
        perm = [(q, (3 * q + d) % 16) for q in range(16) if 3 * q + d >= KB]
        moved.append(lax.ppermute(routed, "pcol", perm))
    moved = jnp.stack(moved).reshape(3, 6, 512, LANES)

    upper, th, tl = call(
        chain_kernel,
        (shaped((25, NB, NB)), shaped((25, NB, NB), BF16), shaped((25, NB, NB), BF16)),
        [SM, VM],
        [
            pltpu.VMEM((25, NB, NB), F32),
            pltpu.VMEM((NB, NB), F32),
            pltpu.VMEM((HB, HB), F32),
            pltpu.VMEM((HB, HB), F32),
            pltpu.VMEM((HB, HB), F32),
        ],
    )(meta, lead_parts)

    rh, rl = call(
        right_kernel,
        (shaped((768, 1280), BF16), shaped((768, 1280), BF16)),
        [VM, VM, VM],
        [pltpu.VMEM((768, 1280), F32)],
    )(right_parts, th, tl)

    rows = NB * ROWS_STEP
    whole3 = pl.BlockSpec((25, NB, NB), lambda g: (0, 0, 0))
    out = pl.pallas_call(
        schur_kernel,
        grid=(6 // ROWS_STEP,),
        out_shape=shaped((9216, LANES)),
        in_specs=[
            SM,
            pl.BlockSpec((16, KB, ROWS_STEP, 32, LANES), lambda g: (0, 0, g, 0, 0)),
            whole3,
            whole3,
            pl.BlockSpec((768, 1280), lambda g: (0, 0)),
            pl.BlockSpec((768, 1280), lambda g: (0, 0)),
            whole3,
            pl.BlockSpec((1536 * ROWS_STEP, LANES), lambda g: (g, 0)),
            pl.BlockSpec((3, 6, 512, LANES), lambda g: (0, 0, 0, 0)),
        ],
        out_specs=pl.BlockSpec((1536 * ROWS_STEP, LANES), lambda g: (g, 0)),
        scratch_shapes=[
            pltpu.VMEM((rows, 1280), F32),
            pltpu.VMEM((rows, 1280), BF16),
            pltpu.VMEM((rows, 1280), BF16),
        ],
        compiler_params=pltpu.CompilerParams(vmem_limit_bytes=VMEM_LIMIT),
    )(meta, left_parts, th, tl, rh, rl, upper, parent.reshape(9216, LANES), moved)
    return out.reshape(6, 1, NB, 3, 1, NB)


def solution(mesh):
    in_specs = (
        P(None, "prow", None, None, "pcol", None),
        P(None, "prow", None, None, "pcol", None),
        P(),
    )
    out_specs = P(None, "prow", None, None, "pcol", None)
    return jax.shard_map(
        per_device, mesh=mesh, in_specs=in_specs, out_specs=out_specs, check_vma=False
    )
```

time: 1710 us -> 408 us (0.24)
  the two profiles are of different devices: /device:TPU:102 before, /device:TPU:104 now
where the time goes in v1:
time: 408 us; the launch traced here: 407 us
  waiting for transfers between devices  190 us (47%)
  Pallas kernels  120 us (29%)
  starting transfers between devices  31 us (8%)
  blocking collectives  29.9 us (7%)
  between operations  17.6 us (4%)
  local copies, waits for them, and re-layouts  13.8 us (3%)
  other arithmetic  4.63 us (1%)
    ppermute x3, waiting for transfers between devices, per_device(): moved.append(lax.ppermute(routed, 'pcol', perm))  99.8 us
    pallas_call x1, Pallas kernels, per_device(): call(chain_kernel, (shaped((25, NB, NB)), shaped((25, NB, NB), BF16), sha...  68.4 us
    all_to_all x1, waiting for transfers between devices, per_device(): panel = lax.all_to_all(panel, 'pcol', 0, 0, tiled=True)  58.1 us
    pallas_call x1, Pallas kernels, per_device(): pl.pallas_call(schur_kernel, grid=(6 // ROWS_STEP,), out_shape=shaped((92...  37.1 us
    all_to_all x1, blocking collectives, per_device(): first = lax.all_to_all(first, 'pcol', 0, 0, tiled=True)  16 us
    all_gather x1, blocking collectives, per_device(): every = lax.all_gather(first, 'prow')  13.8 us
    ppermute x1, waiting for transfers between devices, per_device(): lax.ppermute(jnp.where(is_even, odd, even), ('prow', 'pcol'), perm_b)  13.8 us
    ppermute x6, starting transfers between devices, per_device(): routed.append(lax.ppermute(piece, 'prow', perm))  13.4 us
  transfers between devices with their start and end apart: 15, of which 7 were waited for; matrix products, arithmetic and copies ran while one was open for 3% of the time, Pallas kernels for 20%

profile of v1, /device:TPU:104, one launch (start us, length us, event | category | flops | bytes accessed | tf_op | source)
XLA Modules:
  0.0 407.4 jit_solution(1190774073249855302)
XLA Ops:
  6.5 0.0 all-gather.10.cloned.1.call-start
  6.5 1.1 slice.121
  7.6 1.1 slice.93
  8.8 16.0 %all_to_all.10 = f32[16,2,32,128]{3,2,1,0:T(8,128)S(1)} all-to-all(f32[16,2,32,128]{3,2,1,0:T(8,128)S(1)} %pad_maximum_fusion.1), channel_id=1, replica_groups=mesh['prow'=8,'pcol'=16] {'pcol'}, dimensions={0} | all-to-all | bytes 1048576 | tf_op jit(solution)/shard_map/all_to_all | solution.py:314
  24.9 13.8 %all-gather.1 = f32[56,32,128]{2,1,0:T(8,128)S(1)} all-gather(f32[7,32,128]{2,1,0:T(8,128)S(1)} %pad_maximum_fusion.3), channel_id=3, replica_groups=mesh['prow'=8,'pcol'=16] {'prow'}, dimensions={0}, use_global_device_ids=true | all-gather | bytes 1032192 | tf_op jit(solution)/shard_map/all_gather | solution.py:316
  38.9 0.0 copy-start.1
  38.9 0.8 copy-done.1
  39.7 0.0 all-gather.10.cloned.1.call-update
  39.8 0.0 copy-done.5
  39.8 0.1 reshape.29
  39.9 0.1 pad_add_fusion.meta
  40.0 0.7 fusion
  44.7 0.0 copy-done
  44.7 0.1 dynamic-slice_bitcast_fusion
  44.8 4.0 collective-permute-start
  48.8 0.1 collective-permute-start.1
  48.9 1.9 collective-permute-start.2
  50.8 0.7 collective-permute-start.3
  51.5 2.2 collective-permute-start.4
  53.8 1.5 slice.119
  55.3 0.0 copy-done.4
  55.3 1.3 copy_dynamic-update-slice_fusion
  56.5 0.0 collective-permute-done
  56.6 4.5 %collective-permute-start.5 = (f32[16,32,128]{2,1,0:T(8,128)S(1)}, f32[16,32,128]{2,1,0:T(8,128)S(1)}, u32[]{:S(2)}, u32[]{:S(2)}) collective-permute-start(f32[16,32,128]{2,1,0:T(8,128)S(1)} %get-tuple-element.15), channel_id=1, source_target_pairs={{0,96},{16,16},{32,64},{48,112},{64,32},{80,80},{96,0},{112,48},{1... | collective-permute-start | bytes 786440 | tf_op jit(solution)/shard_map/ppermute | solution.py:329
  61.0 0.7 bitcast_dynamic-update-slice_fusion.10
  61.8 0.0 collective-permute-done.1
  61.8 0.7 bitcast_dynamic-update-slice_fusion.8
  62.5 0.0 collective-permute-done.2
  62.5 0.7 bitcast_dynamic-update-slice_fusion.6
  63.3 0.0 collective-permute-done.3
  63.3 0.7 bitcast_dynamic-update-slice_fusion.4
  64.0 0.0 collective-permute-done.4
  64.0 0.7 bitcast_dynamic-update-slice_fusion.2
  64.8 4.9 %collective-permute-done.5 = f32[16,32,128]{2,1,0:T(8,128)S(1)} collective-permute-done((f32[16,32,128]{2,1,0:T(8,128)S(1)}, f32[16,32,128]{2,1,0:T(8,128)S(1)}, u32[]{:S(2)}, u32[]{:S(2)}) %collective-permute-start.5) | collective-permute-done | bytes 262176 | tf_op jit(solution)/shard_map/ppermute | solution.py:329
  69.7 0.7 bitcast_dynamic-update-slice_fusion
  70.4 1.1 copy-done.2
  71.6 6.0 %all-to-all-start = ((f32[16,12,32,128]{3,2,1,0:T(8,128)}), f32[16,12,32,128]{3,2,1,0:T(8,128)S(1)}, u32[]{:S(2)}, u32[]{:S(2)}) async-start(f32[16,12,32,128]{3,2,1,0:T(8,128)} %bitcast.19), calls=%async_computation | async-start | bytes 6291456 | tf_op jit(solution)/shard_map/all_to_all | solution.py:333
  77.6 0.0 all-gather.12.cloned.1.call-start
  77.6 58.1 %all-to-all-done = f32[16,12,32,128]{3,2,1,0:T(8,128)S(1)} async-done(((f32[16,12,32,128]{3,2,1,0:T(8,128)}), f32[16,12,32,128]{3,2,1,0:T(8,128)S(1)}, u32[]{:S(2)}, u32[]{:S(2)}) %all-to-all-start) | async-done | bytes 3145760 | tf_op jit(solution)/shard_map/all_to_all | solution.py:333
  135.7 1.0 slice.120.parts_ref
  136.7 2.4 shard_map.37
  139.2 1.1 slice_select_fusion.1
  140.3 3.6 collective-permute-start.6
  143.9 0.1 collective-permute-start.7
  144.0 13.2 %collective-permute-done.6 = f32[5,3,32,128]{3,2,1,0:T(8,128)S(1)} collective-permute-done((f32[5,3,32,128]{3,2,1,0:T(8,128)S(1)}, f32[5,3,32,128]{3,2,1,0:T(8,128)S(1)}, u32[]{:S(2)}, u32[]{:S(2)}) %collective-permute-start.6) | collective-permute-done | bytes 245792 | tf_op jit(solution)/shard_map/ppermute | solution.py:343
  157.2 13.8 %collective-permute-done.7 = f32[5,3,32,128]{3,2,1,0:T(8,128)S(1)} collective-permute-done((f32[5,3,32,128]{3,2,1,0:T(8,128)S(1)}, f32[5,3,32,128]{3,2,1,0:T(8,128)S(1)}, u32[]{:S(2)}, u32[]{:S(2)}) %collective-permute-start.7) | collective-permute-done | bytes 245792 | tf_op jit(solution)/shard_map/ppermute | solution.py:344
  171.0 0.8 pad_maximum_fusion.2
  171.8 0.0 all-gather.12.cloned.1.call-update
  171.8 0.0 all-gather.8.cloned.1.call-start
  171.9 0.7 all-gather.8.cloned.1.call-update
  172.6 0.0 copy-done.3
  172.6 1.9 collective-permute-start.8
  174.5 4.0 collective-permute-start.9
  178.6 1.9 collective-permute-start.10
  180.5 25.2 %collective-permute-done.8 = f32[6,16,32,128]{3,2,0,1:T(8,128)S(1)} collective-permute-done((f32[6,16,32,128]{3,2,0,1:T(8,128)S(1)}, f32[6,16,32,128]{3,2,0,1:T(8,128)S(1)}, u32[]{:S(2)}, u32[]{:S(2)}) %collective-permute-start.8) | collective-permute-done | bytes 1572896 | tf_op jit(solution)/shard_map/ppermute | solution.py:354
  205.6 0.2 copy.17
  205.8 62.0 %collective-permute-done.9 = f32[6,16,32,128]{3,2,0,1:T(8,128)S(1)} collective-permute-done((f32[6,16,32,128]{3,2,0,1:T(8,128)S(1)}, f32[6,16,32,128]{3,2,0,1:T(8,128)S(1)}, u32[]{:S(2)}, u32[]{:S(2)}) %collective-permute-start.9) | collective-permute-done | bytes 1572896 | tf_op jit(solution)/shard_map/ppermute | solution.py:354
  267.8 0.2 copy.18
  267.9 12.6 %collective-permute-done.10 = f32[6,16,32,128]{3,2,0,1:T(8,128)S(1)} collective-permute-done((f32[6,16,32,128]{3,2,0,1:T(8,128)S(1)}, f32[6,16,32,128]{3,2,0,1:T(8,128)S(1)}, u32[]{:S(2)}, u32[]{:S(2)}) %collective-permute-start.10) | collective-permute-done | bytes 1572896 | tf_op jit(solution)/shard_map/ppermute | solution.py:354
  280.6 0.2 copy.19
  280.7 2.6 pad_maximum_fusion.child_ref
  283.3 68.4 %shard_map.38 = (f32[25,256,256]{2,1,0:T(8,128)}, bf16[25,256,256]{2,1,0:T(8,128)(2,1)}, bf16[25,256,256]{2,1,0:T(8,128)(2,1)}) custom-call(s32[34]{0:T(128)} %copy-done.4, f32[16,21,32,128]{3,2,1,0:T(8,128)} %bitcast.152), custom_call_target="tpu_custom_call" | custom-call | tf_op jit(solution)/shard_map/pallas_call | solution.py:357
  351.7 12.1 %shard_map.39 = (bf16[768,1280]{1,0:T(8,128)(2,1)}, bf16[768,1280]{1,0:T(8,128)(2,1)}) custom-call(f32[16,5,3,32,128]{4,3,2,1,0:T(8,128)} %all-gather.12.cloned.1.call-done.parts_ref, bf16[25,256,256]{2,1,0:T(8,128)(2,1)} %get-tuple-element.10.th_ref, bf16[25,256,256]{2,1,0:T(8,128)(2,1)} %get-tuple-element.11.tl_ref), custom_call_target="tpu_custom_call" | custom-call | tf_op jit(solution)/shard_map/pallas_call | solution.py:370
  363.8 37.1 %shard_map.40 = f32[9216,128]{1,0:T(8,128)} custom-call(s32[34]{0:T(128)} %copy-done.4, f32[16,5,6,32,128]{4,3,2,1,0:T(8,128)} %bitcast.147, bf16[25,256,256]{2,1,0:T(8,128)(2,1)} %get-tuple-element.10.th_ref, bf16[25,256,256]{2,1,0:T(8,128)(2,1)} %get-tuple-element.11.tl_ref, bf16[768,1280]{1,0:T(8,128)(2,1)} %get-tuple-element.12.rh_ref, ...), custom_call_target="tpu_custom_call" | custom-call | tf_op jit(solution)/shard_map/pallas_call | solution.py:379
  (34 shorter events, 0.2 us)
Async XLA Ops:
  6.5 38.2 %copy-start = (f32[4,1,256,1,1,256]{5,4,3,2,1,0:T(1,128)S(1)}, f32[4,1,256,1,1,256]{5,4,3,2,1,0:T(1,128)}, u32[]{:S(2)}) copy-start(f32[4,1,256,1,1,256]{5,4,3,2,1,0:T(1,128)} %param.4) | copy-start | bytes 3145732
  6.5 33.3 %copy-start.5 = (s32[2,16]{1,0:T(2,128)S(1)}, s32[2,16]{1,0:T(2,128)}, u32[]{:S(2)}) copy-start(s32[2,16]{1,0:T(2,128)} %param.5) | copy-start | bytes 388
  6.5 276.8 %all-gather.10.cloned.1.call-start = ((), (), s32[]{:S(2)}) async-start(), calls=%async_computation.3 | async-start | bytes 5849088 | tf_op jit(solution)/shard_map/all_gather | solution.py:318
  38.9 0.8 copy-start.1
  40.0 15.3 %copy-start.4 = (s32[34]{0:T(128)}, s32[34]{0:T(128)S(1)}, u32[]{:S(2)}) copy-start(s32[34]{0:T(128)S(1)} %pad_add_fusion.meta) | copy-start | bytes 412
  44.8 11.7 %collective-permute-start = (f32[16,32,128]{2,1,0:T(8,128)S(1)}, f32[16,32,128]{2,1,0:T(8,128)S(1)}, u32[]{:S(2)}, u32[]{:S(2)}) collective-permute-start(f32[16,32,128]{2,1,0:T(8,128)S(1)} %get-tuple-element.20), channel_id=1, source_target_pairs={{0,0},{16,48},{32,96},{48,16},{64,64},{80,112},{96,32},{112,80},{1... | collective-permute-start | bytes 786440 | tf_op jit(solution)/shard_map/ppermute | solution.py:329
  48.8 13.0 %collective-permute-start.1 = (f32[16,32,128]{2,1,0:T(8,128)S(1)}, f32[16,32,128]{2,1,0:T(8,128)S(1)}, u32[]{:S(2)}, u32[]{:S(2)}) collective-permute-start(f32[16,32,128]{2,1,0:T(8,128)S(1)} %get-tuple-element.19), channel_id=1, source_target_pairs={{0,16},{16,64},{32,112},{48,32},{64,80},{80,0},{96,48},{112,96},{1... | collective-permute-start | bytes 786440 | tf_op jit(solution)/shard_map/ppermute | solution.py:329
  48.9 13.6 %collective-permute-start.2 = (f32[16,32,128]{2,1,0:T(8,128)S(1)}, f32[16,32,128]{2,1,0:T(8,128)S(1)}, u32[]{:S(2)}, u32[]{:S(2)}) collective-permute-start(f32[16,32,128]{2,1,0:T(8,128)S(1)} %get-tuple-element.18), channel_id=1, source_target_pairs={{0,32},{16,80},{32,0},{48,48},{64,96},{80,16},{96,64},{112,112},{1... | collective-permute-start | bytes 786440 | tf_op jit(solution)/shard_map/ppermute | solution.py:329
  50.8 12.4 %collective-permute-start.3 = (f32[16,32,128]{2,1,0:T(8,128)S(1)}, f32[16,32,128]{2,1,0:T(8,128)S(1)}, u32[]{:S(2)}, u32[]{:S(2)}) collective-permute-start(f32[16,32,128]{2,1,0:T(8,128)S(1)} %get-tuple-element.17), channel_id=1, source_target_pairs={{0,64},{16,112},{32,32},{48,80},{64,0},{80,48},{96,96},{112,16},{1... | collective-permute-start | bytes 786440 | tf_op jit(solution)/shard_map/ppermute | solution.py:329
  51.5 12.5 %collective-permute-start.4 = (f32[16,32,128]{2,1,0:T(8,128)S(1)}, f32[16,32,128]{2,1,0:T(8,128)S(1)}, u32[]{:S(2)}, u32[]{:S(2)}) collective-permute-start(f32[16,32,128]{2,1,0:T(8,128)S(1)} %get-tuple-element.16), channel_id=1, source_target_pairs={{0,80},{16,0},{32,48},{48,96},{64,16},{80,64},{96,112},{112,32},{1... | collective-permute-start | bytes 786440 | tf_op jit(solution)/shard_map/ppermute | solution.py:329
  56.6 13.1 %collective-permute-start.5 = (f32[16,32,128]{2,1,0:T(8,128)S(1)}, f32[16,32,128]{2,1,0:T(8,128)S(1)}, u32[]{:S(2)}, u32[]{:S(2)}) collective-permute-start(f32[16,32,128]{2,1,0:T(8,128)S(1)} %get-tuple-element.15), channel_id=1, source_target_pairs={{0,96},{16,16},{32,64},{48,112},{64,32},{80,80},{96,0},{112,48},{1... | collective-permute-start | bytes 786440 | tf_op jit(solution)/shard_map/ppermute | solution.py:329
  70.4 1.1 copy-start.2
  71.6 64.1 %all-to-all-start = ((f32[16,12,32,128]{3,2,1,0:T(8,128)}), f32[16,12,32,128]{3,2,1,0:T(8,128)S(1)}, u32[]{:S(2)}, u32[]{:S(2)}) async-start(f32[16,12,32,128]{3,2,1,0:T(8,128)} %bitcast.19), calls=%async_computation | async-start | bytes 6291456 | tf_op jit(solution)/shard_map/all_to_all | solution.py:333
  77.6 274.1 %all-gather.12.cloned.1.call-start = ((), (), s32[]{:S(2)}) async-start(), calls=%async_computation.4 | async-start | bytes 4423680 | tf_op jit(solution)/shard_map/all_gather | solution.py:349
  136.7 35.9 %copy-start.3 = (f32[6,16,32,128]{3,2,0,1:T(8,128)S(1)}, f32[6,16,32,128]{3,2,0,1:T(8,128)}, u32[]{:S(2)}) copy-start(f32[6,16,32,128]{3,2,0,1:T(8,128)} %copy-done.2) | copy-start | bytes 4718596
  140.3 16.9 %collective-permute-start.6 = (f32[5,3,32,128]{3,2,1,0:T(8,128)S(1)}, f32[5,3,32,128]{3,2,1,0:T(8,128)S(1)}, u32[]{:S(2)}, u32[]{:S(2)}) collective-permute-start(f32[5,3,32,128]{3,2,1,0:T(8,128)S(1)} %get-tuple-element.23), channel_id=1, source_target_pairs={{0,0},{1,8},{2,16},{3,24},{4,32},{5,40},{6,48},{7,56},{8,64},{9,72... | collective-permute-start | bytes 737288 | tf_op jit(solution)/shard_map/ppermute | solution.py:343
  143.9 27.0 %collective-permute-start.7 = (f32[5,3,32,128]{3,2,1,0:T(8,128)S(1)}, f32[5,3,32,128]{3,2,1,0:T(8,128)S(1)}, u32[]{:S(2)}, u32[]{:S(2)}) collective-permute-start(f32[5,3,32,128]{3,2,1,0:T(8,128)S(1)} %get-tuple-element.24), channel_id=1, source_target_pairs={{0,8},{1,0},{2,24},{3,16},{4,40},{5,32},{6,56},{7,48},{8,72},{9,64... | collective-permute-start | bytes 737288 | tf_op jit(solution)/shard_map/ppermute | solution.py:344
  171.8 191.9 %all-gather.8.cloned.1.call-start = ((), (), s32[]{:S(2)}) async-start(), calls=%async_computation.2 | async-start | bytes 8355840 | tf_op jit(solution)/shard_map/all_gather | solution.py:348
  172.6 33.1 %collective-permute-start.8 = (f32[6,16,32,128]{3,2,0,1:T(8,128)S(1)}, f32[6,16,32,128]{3,2,0,1:T(8,128)S(1)}, u32[]{:S(2)}, u32[]{:S(2)}) collective-permute-start(f32[6,16,32,128]{3,2,0,1:T(8,128)S(1)} %copy-done.3), channel_id=1, source_target_pairs={{2,6},{3,9},{4,12},{5,15},{6,2},{7,5},{8,8},{9,11},{10,14},{11,1},... | collective-permute-start | bytes 4718600 | tf_op jit(solution)/shard_map/ppermute | solution.py:354
  174.5 93.3 %collective-permute-start.9 = (f32[6,16,32,128]{3,2,0,1:T(8,128)S(1)}, f32[6,16,32,128]{3,2,0,1:T(8,128)S(1)}, u32[]{:S(2)}, u32[]{:S(2)}) collective-permute-start(f32[6,16,32,128]{3,2,0,1:T(8,128)S(1)} %copy-done.3), channel_id=1, source_target_pairs={{2,7},{3,10},{4,13},{5,0},{6,3},{7,6},{8,9},{9,12},{10,15},{11,2},... | collective-permute-start | bytes 4718600 | tf_op jit(solution)/shard_map/ppermute | solution.py:354
  178.6 102.0 %collective-permute-start.10 = (f32[6,16,32,128]{3,2,0,1:T(8,128)S(1)}, f32[6,16,32,128]{3,2,0,1:T(8,128)S(1)}, u32[]{:S(2)}, u32[]{:S(2)}) collective-permute-start(f32[6,16,32,128]{3,2,0,1:T(8,128)S(1)} %copy-done.3), channel_id=1, source_target_pairs={{1,5},{2,8},{3,11},{4,14},{5,1},{6,4},{7,7},{8,10},{9,13},{10,0},{... | collective-permute-start | bytes 4718600 | tf_op jit(solution)/shard_map/ppermute | solution.py:354
Sparse Core Ops, SparseCore 0:
  39.8 88.1 all-gather.9
  172.0 27.9 all-gather.11
  202.1 122.8 all-gather.7

commit v2 on v1

--- a/solution.py
+++ b/solution.py
@@ -31,17 +31,24 @@
     return child, jnp.logical_or(is_first, is_second), (3 * block + d) // 8
 
 
-def assemble_kernel(meta, parts_ref, out_ref):
+def assemble_kernel(meta, first_ref, rest_ref, every_ref, more_ref, out_ref):
     for j in range(KB):
-        out_ref[j] = parts_ref[j, 0:6]
-    for n in range(6):
-        child, there, slot = route_of(meta, n)
-        for v in range(2):
-            column = meta[child * 16 + v]
-
-            @pl.when(jnp.logical_and(there, column < KB))
+        out_ref[j, 0] = first_ref[j]
+        out_ref[j, 1:6] = rest_ref[j]
+    for child in range(2):
+        for u in range(16):
+            target = meta[child * 16 + u]
+
+            @pl.when(target % 8 == meta[32])
             def _():
-                out_ref[column, slot] = out_ref[column, slot] + parts_ref[v, 6 + n]
+                for v in range(2):
+                    column = meta[child * 16 + v]
+
+                    @pl.when(column < KB)
+                    def _():
+                        source = 4 * child + u % 4
+                        piece = every_ref[source, KB + v] if u < 4 else more_ref[source, v, u // 4 - 1]
+                        out_ref[column, target // 8] = out_ref[column, target // 8] + piece
 
 
 UPPER = [(k, i) for k in range(KB) for i in range(k, KB)]
@@ -286,7 +293,11 @@
                         put(h, block[:, HB * h : HB * h + HB])
 
 
-def call(kernel, out_shape, in_specs, scratch, **extra):
+def cost(microseconds):
+    return pl.CostEstimate(flops=int(microseconds * 1.1e9), bytes_accessed=1 << 20, transcendentals=0)
+
+
+def call(kernel, out_shape, in_specs, scratch, microseconds=2):
     return pl.pallas_call(
         kernel,
         out_shape=out_shape,
@@ -294,7 +305,7 @@
         out_specs=jax.tree.map(lambda _: VM, out_shape),
         scratch_shapes=scratch,
         compiler_params=pltpu.CompilerParams(vmem_limit_bytes=VMEM_LIMIT),
-        **extra,
+        cost_estimate=cost(microseconds),
     )
 
 
@@ -312,26 +323,31 @@
 
     first = jnp.stack([lead[0], child[0]], axis=1)
     first = lax.all_to_all(first, "pcol", 0, 0, tiled=True)
-    first = jnp.concatenate([first[0:KB, 0], first[0:2, 1]], axis=0)
-    every = lax.all_gather(first, "prow")
+    mine = jnp.concatenate([first[0:KB, 0], first[0:2, 1]], axis=0)
+    every = lax.all_gather(mine, "prow")
     picked = [every[k, i] for k, i in UPPER] + [every[4 * c + u, KB + v] for c, u, v in CHILD_SOURCES]
     lead_parts = lax.all_gather(jnp.stack(picked), "pcol")
 
+    rest = jnp.concatenate([lead[1:], child[1:]], axis=0).transpose(1, 0, 2, 3)
+    rest, every = lax.optimization_barrier((rest, every))
+    rest = lax.all_to_all(rest, "pcol", 0, 0, tiled=True)
+    more = lax.all_gather(rest[0:2, 5:8], "prow")
+    slices = call(assemble_kernel, shaped((KB, 6, 32, LANES)), [SM, VM, VM, VM, VM], [])(
+        meta, mine[0:KB], rest[0:KB, 0:5], every, more
+    )
+
     child_id, residue = row // 4, row % 4
+    free, _ = lax.optimization_barrier((child, every))
     routed = []
     for flip in range(2):
         parity = (child_id + flip) % 2
         for d in range(3):
             block = 4 * parity + residue
             chosen = jnp.where(meta[child_id * 16 + block] == 3 * block + d, parity, parity + 2)
-            piece = lax.dynamic_index_in_dim(child, chosen, 0, keepdims=False)
+            piece = lax.dynamic_index_in_dim(free, chosen, 0, keepdims=False)
             perm = [(p, (3 * (p % 4) + d + 4 * ((p // 4 + flip) % 2)) % 8) for p in range(8)]
             routed.append(lax.ppermute(piece, "prow", perm))
     routed = jnp.stack(routed)
-
-    panel = jnp.concatenate([lead, routed], axis=0).transpose(1, 0, 2, 3)
-    panel = lax.all_to_all(panel, "pcol", 0, 0, tiled=True)
-    slices = call(assemble_kernel, shaped((KB, 6, 32, LANES)), [SM, VM], [])(meta, panel[0:KB])
 
     even, odd = slices[:, 0::2], slices[:, 1::2]
     is_even = col % 2 == 0
@@ -346,7 +362,8 @@
     pair = jnp.stack([jnp.where(low_side, got_a, got_b), jnp.where(low_side, got_b, got_a)])
 
     left_parts = lax.all_gather(slices, "pcol")
-    right_parts = lax.all_gather(pair, "prow").reshape(16, KB, 3, 32, LANES)
+    pairs = jnp.broadcast_to(pair[None], (8,) + pair.shape)
+    right_parts = lax.all_to_all(pairs, "prow", 0, 0, tiled=True).reshape(16, KB, 3, 32, LANES)
 
     moved = []
     for d in range(3):
@@ -365,6 +382,7 @@
             pltpu.VMEM((HB, HB), F32),
             pltpu.VMEM((HB, HB), F32),
         ],
+        70,
     )(meta, lead_parts)
 
     rh, rl = call(
@@ -372,6 +390,7 @@
         (shaped((768, 1280), BF16), shaped((768, 1280), BF16)),
         [VM, VM, VM],
         [pltpu.VMEM((768, 1280), F32)],
+        12,
     )(right_parts, th, tl)
 
     rows = NB * ROWS_STEP
@@ -398,6 +417,7 @@
             pltpu.VMEM((rows, 1280), BF16),
         ],
         compiler_params=pltpu.CompilerParams(vmem_limit_bytes=VMEM_LIMIT),
+        cost_estimate=cost(33),
     )(meta, left_parts, th, tl, rh, rl, upper, parent.reshape(9216, LANES), moved)
     return out.reshape(6, 1, NB, 3, 1, NB)
 

time: 408 us -> 420 us (1.029)
  the two profiles are of different devices: /device:TPU:104 before, /device:TPU:102 now
where the time goes in v2:
time: 420 us; the launch traced here: 415 us
  starting transfers between devices  128 us (30%)
  Pallas kernels  121 us (29%)
  waiting for transfers between devices  86.6 us (21%)
  blocking collectives  42.7 us (10%)
  between operations  17.7 us (4%)
  local copies, waits for them, and re-layouts  13 us (3%)
  other arithmetic  6.66 us (2%)
    all_to_all x1, starting transfers between devices, per_device(): lax.all_to_all(pairs, 'prow', 0, 0, tiled=True)  76.6 us
    pallas_call x1, Pallas kernels, per_device(): call(chain_kernel, (shaped((25, NB, NB)), shaped((25, NB, NB), BF16), sha...  68.4 us
    ppermute x3, waiting for transfers between devices, per_device(): moved.append(lax.ppermute(routed, 'pcol', perm))  46.5 us
    pallas_call x1, Pallas kernels, per_device(): pl.pallas_call(schur_kernel, grid=(6 // ROWS_STEP,), out_shape=shaped((92...  37.1 us
    all_to_all x1, waiting for transfers between devices, per_device(): rest = lax.all_to_all(rest, 'pcol', 0, 0, tiled=True)  32.8 us
    ppermute x3, starting transfers between devices, per_device(): moved.append(lax.ppermute(routed, 'pcol', perm))  20.7 us
    ppermute x6, starting transfers between devices, per_device(): routed.append(lax.ppermute(piece, 'prow', perm))  15.2 us
    all_gather x1, blocking collectives, per_device(): more = lax.all_gather(rest[0:2, 5:8], 'prow')  14.4 us
  transfers between devices with their start and end apart: 15, of which 5 were waited for; matrix products, arithmetic and copies ran while one was open for 4% of the time, Pallas kernels for 20%

profile of v2, /device:TPU:102, one launch (start us, length us, event | category | flops | bytes accessed | tf_op | source)
XLA Modules:
  0.0 415.3 jit_solution(5350978224557220082)
XLA Ops:
  6.5 0.0 all-gather.9.cloned.1.call-start
  6.5 1.0 slice.137
  7.5 1.1 slice.105
  8.7 14.2 %all_to_all.15 = f32[16,2,32,128]{3,2,1,0:T(8,128)S(1)} all-to-all(f32[16,2,32,128]{3,2,1,0:T(8,128)S(1)} %pad_maximum_fusion.2), channel_id=1, replica_groups=mesh['prow'=8,'pcol'=16] {'pcol'}, dimensions={0} | all-to-all | bytes 1048576 | tf_op jit(solution)/shard_map/all_to_all | solution.py:325
  22.9 14.1 %all-gather = f32[56,32,128]{2,1,0:T(8,128)S(1)} all-gather(f32[7,32,128]{2,1,0:T(8,128)S(1)} %pad_maximum_fusion.4), channel_id=2, replica_groups=mesh['prow'=8,'pcol'=16] {'prow'}, dimensions={0}, use_global_device_ids=true | all-gather | bytes 1032192 | tf_op jit(solution)/shard_map/all_gather | solution.py:327
  37.2 0.0 copy-start.3
  37.3 0.9 copy-done.3
  38.1 0.0 all-gather.9.cloned.1.call-update
  38.1 0.0 slice-start
  38.2 1.5 slice.139
  39.6 0.0 copy-done.4
  39.6 0.0 copy-done.2
  39.7 0.0 slice-done
  39.7 1.5 copy_bitcast_fusion
  41.2 7.9 %all-to-all-start.1 = ((f32[16,8,32,128]{3,2,1,0:T(8,128)}), f32[16,8,32,128]{3,2,1,0:T(8,128)S(1)}, u32[]{:S(2)}, u32[]{:S(2)}) async-start(f32[16,8,32,128]{3,2,1,0:T(8,128)} %copy_bitcast_fusion), calls=%async_computation.1 | async-start | bytes 4194304 | tf_op jit(solution)/shard_map/all_to_all | solution.py:333
  49.1 0.0 all-gather.7.cloned.1.call-start
  49.2 0.0 copy-done.6
  49.2 0.1 reshape.32
  49.3 0.6 pad_add_fusion.meta
  49.8 32.8 %all-to-all-done.1 = f32[16,8,32,128]{3,2,1,0:T(8,128)S(1)} async-done(((f32[16,8,32,128]{3,2,1,0:T(8,128)}), f32[16,8,32,128]{3,2,1,0:T(8,128)S(1)}, u32[]{:S(2)}, u32[]{:S(2)}) %all-to-all-start.1) | async-done | bytes 2097184 | tf_op jit(solution)/shard_map/all_to_all | solution.py:333
  82.7 0.8 slice.141.rest_ref
  83.5 14.4 %all-gather.1 = f32[16,3,32,128]{3,2,1,0:T(8,128)} all-gather(f32[2,3,32,128]{3,2,1,0:T(8,128)S(1)} %slice.142), channel_id=3, replica_groups=mesh['prow'=8,'pcol'=16] {'prow'}, dimensions={0}, use_global_device_ids=true | all-gather | bytes 884736 | tf_op jit(solution)/shard_map/all_gather | solution.py:334
  97.9 3.0 shard_map.37
  101.0 0.0 all-gather.7.cloned.1.call-update
  101.1 0.0 copy-done.5
  101.1 0.6 fusion
  105.6 0.0 copy-done
  105.6 0.2 dynamic-slice_bitcast_fusion
  105.8 0.7 collective-permute-start.2
  106.5 1.7 collective-permute-start.3
  108.1 4.1 collective-permute-start.4
  112.2 5.2 %collective-permute-start.5 = (f32[16,32,128]{2,1,0:T(8,128)S(1)}, f32[16,32,128]{2,1,0:T(8,128)S(1)}, u32[]{:S(2)}, u32[]{:S(2)}) collective-permute-start(f32[16,32,128]{2,1,0:T(8,128)S(1)} %get-tuple-element.23), channel_id=1, source_target_pairs={{0,64},{16,112},{32,32},{48,80},{64,0},{80,48},{96,96},{112,16},{1... | collective-permute-start | bytes 786440 | tf_op jit(solution)/shard_map/ppermute | solution.py:349
  117.4 0.1 collective-permute-start.6
  117.5 0.0 collective-permute-done.2
  117.5 3.5 collective-permute-start.7
  121.0 0.7 bitcast_dynamic-update-slice_fusion.5
  121.7 0.0 collective-permute-done.3
  121.7 0.7 bitcast_dynamic-update-slice_fusion.4
  122.5 4.6 %collective-permute-done.4 = f32[16,32,128]{2,1,0:T(8,128)S(1)} collective-permute-done((f32[16,32,128]{2,1,0:T(8,128)S(1)}, f32[16,32,128]{2,1,0:T(8,128)S(1)}, u32[]{:S(2)}, u32[]{:S(2)}) %collective-permute-start.4) | collective-permute-done | bytes 262176 | tf_op jit(solution)/shard_map/ppermute | solution.py:349
  127.1 0.7 bitcast_dynamic-update-slice_fusion.3
  127.8 0.0 collective-permute-done.5
  127.8 0.7 bitcast_dynamic-update-slice_fusion.2
  128.5 0.0 collective-permute-done.6
  128.5 0.7 bitcast_dynamic-update-slice_fusion.1
  129.2 2.5 collective-permute-done.7
  131.8 0.7 bitcast_dynamic-update-slice_fusion
  132.5 4.0 collective-permute-start.8
  136.5 3.4 collective-permute-start.9
  139.9 13.3 %collective-permute-start.10 = (f32[6,16,32,128]{3,2,1,0:T(8,128)}, f32[6,16,32,128]{3,2,1,0:T(8,128)}, u32[]{:S(2)}, u32[]{:S(2)}) collective-permute-start(f32[6,16,32,128]{3,2,1,0:T(8,128)} %bitcast_dynamic-update-slice_fusion), channel_id=1, source_target_pairs={{1,5},{2,8},{3,11},{4,14},{5,1},{6,4},{7,7},{8,10},{9,13},{10,0},{... | collective-permute-start | bytes 4718600 | tf_op jit(solution)/shard_map/ppermute | solution.py:371
  153.2 1.9 collective-permute-start
  155.2 5.7 %collective-permute-start.1 = (f32[5,3,32,128]{3,2,1,0:T(8,128)S(1)}, f32[5,3,32,128]{3,2,1,0:T(8,128)S(1)}, u32[]{:S(2)}, u32[]{:S(2)}) collective-permute-start(f32[5,3,32,128]{3,2,1,0:T(8,128)S(1)} %get-tuple-element.30), channel_id=1, source_target_pairs={{0,8},{1,0},{2,24},{3,16},{4,40},{5,32},{6,56},{7,48},{8,72},{9,64... | collective-permute-start | bytes 737288 | tf_op jit(solution)/shard_map/ppermute | solution.py:360
  160.8 35.4 %collective-permute-done.8 = f32[6,16,32,128]{3,2,1,0:T(8,128)S(1)} collective-permute-done((f32[6,16,32,128]{3,2,1,0:T(8,128)}, f32[6,16,32,128]{3,2,1,0:T(8,128)S(1)}, u32[]{:S(2)}, u32[]{:S(2)}) %collective-permute-start.8) | collective-permute-done | bytes 1572896 | tf_op jit(solution)/shard_map/ppermute | solution.py:371
  196.3 11.1 %collective-permute-done.9 = f32[6,16,32,128]{3,2,1,0:T(8,128)} collective-permute-done((f32[6,16,32,128]{3,2,1,0:T(8,128)}, f32[6,16,32,128]{3,2,1,0:T(8,128)}, u32[]{:S(2)}, u32[]{:S(2)}) %collective-permute-start.9) | collective-permute-done | bytes 1572896 | tf_op jit(solution)/shard_map/ppermute | solution.py:371
  207.3 0.0 collective-permute-done.10
  207.3 4.4 %pad_maximum_fusion.child_ref = f32[3,6,512,128]{3,2,1,0:T(8,128)} fusion(f32[1,6,512,128]{3,2,1,0:T(8,128)} %bitcast.56, f32[1,6,512,128]{3,2,1,0:T(8,128)} %bitcast.55, f32[1,6,512,128]{3,2,1,0:T(8,128)S(1)} %bitcast.171), kind=kLoop, calls=%fused_computation | loop fusion | flops 2359296 | bytes 9437184 | tf_op jit(solution)/shard_map/stack | solution.py:372
  211.7 0.0 collective-permute-done
  211.7 0.0 collective-permute-done.1
  211.8 2.4 broadcast_in_dim.2
  214.2 76.6 %all-to-all-start.2 = ((f32[8,2,5,3,32,128]{5,4,3,2,1,0:T(8,128)}), f32[8,2,5,3,32,128]{5,4,3,2,1,0:T(8,128)}, u32[]{:S(2)}, u32[]{:S(2)}) async-start(f32[8,2,5,3,32,128]{5,4,3,2,1,0:T(8,128)} %broadcast_in_dim.2), calls=%async_computation.2 | async-start | bytes 7864320 | tf_op jit(solution)/shard_map/all_to_all | solution.py:366
  290.8 0.0 all-gather.9.cloned.1.call-done
  290.9 68.4 %shard_map.38 = (f32[25,256,256]{2,1,0:T(8,128)}, bf16[25,256,256]{2,1,0:T(8,128)(2,1)}, bf16[25,256,256]{2,1,0:T(8,128)(2,1)}) custom-call(s32[34]{0:T(128)} %pad_add_fusion.meta, f32[16,21,32,128]{3,2,1,0:T(8,128)} %bitcast.179), custom_call_target="tpu_custom_call" | custom-call | flops 76999999488 | bytes 1048576 | tf_op jit(solution)/shard_map/pallas_call | solution.py:374
  359.3 0.0 all-to-all-done.2
  359.3 12.1 %shard_map.39 = (bf16[768,1280]{1,0:T(8,128)(2,1)}, bf16[768,1280]{1,0:T(8,128)(2,1)}) custom-call(f32[16,5,3,32,128]{4,3,2,1,0:T(8,128)} %bitcast.37.parts_ref, bf16[25,256,256]{2,1,0:T(8,128)(2,1)} %get-tuple-element.15.th_ref, bf16[25,256,256]{2,1,0:T(8,128)(2,1)} %get-tuple-element.16.tl_ref), custom_call_target="tpu_custom_call" | custom-call | flops 13200000000 | bytes 1048576 | tf_op jit(solution)/shard_map/pallas_call | solution.py:388
  371.3 37.1 %shard_map.40 = f32[9216,128]{1,0:T(8,128)} custom-call(s32[34]{0:T(128)} %pad_add_fusion.meta, f32[16,5,6,32,128]{4,3,2,1,0:T(8,128)} %bitcast.178, bf16[25,256,256]{2,1,0:T(8,128)(2,1)} %get-tuple-element.15.th_ref, bf16[25,256,256]{2,1,0:T(8,128)(2,1)} %get-tuple-element.16.tl_ref, bf16[768,1280]{1,0:T(8,128)(2,1)} %get-tuple-element.17.rh_ref, ...), custom_call_target="tpu_custom_call" | custom-call | flops 36300001280 | bytes 1048576 | tf_op jit(solution)/shard_map/pallas_call | solution.py:398
  (37 shorter events, 0.3 us)
Async XLA Ops:
  6.5 284.3 %all-gather.9.cloned.1.call-start = ((), (), s32[]{:S(2)}) async-start(), calls=%async_computation.4 | async-start | bytes 5849088 | tf_op jit(solution)/shard_map/all_gather | solution.py:329
  22.8 16.8 %copy-start.4 = (f32[5,32,128]{2,1,0:T(8,128)}, f32[5,32,128]{2,1,0:T(8,128)S(1)}, u32[]{:S(2)}) copy-start(f32[5,32,128]{2,1,0:T(8,128)S(1)} %slice_bitcast_fusion.first_ref) | copy-start | bytes 245764
  37.0 2.6 copy-start.2
  37.2 0.9 copy-start.3
  38.1 1.5 slice-start
  41.2 8.0 %copy-start.6 = (s32[2,16]{1,0:T(2,128)S(1)}, s32[2,16]{1,0:T(2,128)}, u32[]{:S(2)}) copy-start(s32[2,16]{1,0:T(2,128)} %param.5) | copy-start | bytes 388
  41.2 41.5 %all-to-all-start.1 = ((f32[16,8,32,128]{3,2,1,0:T(8,128)}), f32[16,8,32,128]{3,2,1,0:T(8,128)S(1)}, u32[]{:S(2)}, u32[]{:S(2)}) async-start(f32[16,8,32,128]{3,2,1,0:T(8,128)} %copy_bitcast_fusion), calls=%async_computation.1 | async-start | bytes 4194304 | tf_op jit(solution)/shard_map/all_to_all | solution.py:333
  49.1 322.2 %all-gather.7.cloned.1.call-start = ((), (), s32[]{:S(2)}) async-start(), calls=%async_computation.3 | async-start | bytes 8355840 | tf_op jit(solution)/shard_map/all_gather | solution.py:364
  97.9 3.1 copy-start.5
  97.9 7.6 %copy-start = (f32[4,1,256,1,1,256]{5,4,3,2,1,0:T(1,128)S(1)}, f32[4,1,256,1,1,256]{5,4,3,2,1,0:T(1,128)}, u32[]{:S(2)}) copy-start(f32[4,1,256,1,1,256]{5,4,3,2,1,0:T(1,128)} %param.4) | copy-start | bytes 3145732
  105.8 11.8 %collective-permute-start.2 = (f32[16,32,128]{2,1,0:T(8,128)S(1)}, f32[16,32,128]{2,1,0:T(8,128)S(1)}, u32[]{:S(2)}, u32[]{:S(2)}) collective-permute-start(f32[16,32,128]{2,1,0:T(8,128)S(1)} %get-tuple-element.26), channel_id=1, source_target_pairs={{0,0},{16,48},{32,96},{48,16},{64,64},{80,112},{96,32},{112,80},{1... | collective-permute-start | bytes 786440 | tf_op jit(solution)/shard_map/ppermute | solution.py:349
  106.5 15.3 %collective-permute-start.3 = (f32[16,32,128]{2,1,0:T(8,128)S(1)}, f32[16,32,128]{2,1,0:T(8,128)S(1)}, u32[]{:S(2)}, u32[]{:S(2)}) collective-permute-start(f32[16,32,128]{2,1,0:T(8,128)S(1)} %get-tuple-element.25), channel_id=1, source_target_pairs={{0,16},{16,64},{32,112},{48,32},{64,80},{80,0},{96,48},{112,96},{1... | collective-permute-start | bytes 786440 | tf_op jit(solution)/shard_map/ppermute | solution.py:349
  108.1 18.9 %collective-permute-start.4 = (f32[16,32,128]{2,1,0:T(8,128)S(1)}, f32[16,32,128]{2,1,0:T(8,128)S(1)}, u32[]{:S(2)}, u32[]{:S(2)}) collective-permute-start(f32[16,32,128]{2,1,0:T(8,128)S(1)} %get-tuple-element.24), channel_id=1, source_target_pairs={{0,32},{16,80},{32,0},{48,48},{64,96},{80,16},{96,64},{112,112},{1... | collective-permute-start | bytes 786440 | tf_op jit(solution)/shard_map/ppermute | solution.py:349
  112.2 15.6 %collective-permute-start.5 = (f32[16,32,128]{2,1,0:T(8,128)S(1)}, f32[16,32,128]{2,1,0:T(8,128)S(1)}, u32[]{:S(2)}, u32[]{:S(2)}) collective-permute-start(f32[16,32,128]{2,1,0:T(8,128)S(1)} %get-tuple-element.23), channel_id=1, source_target_pairs={{0,64},{16,112},{32,32},{48,80},{64,0},{80,48},{96,96},{112,16},{1... | collective-permute-start | bytes 786440 | tf_op jit(solution)/shard_map/ppermute | solution.py:349
  117.4 11.1 %collective-permute-start.6 = (f32[16,32,128]{2,1,0:T(8,128)S(1)}, f32[16,32,128]{2,1,0:T(8,128)S(1)}, u32[]{:S(2)}, u32[]{:S(2)}) collective-permute-start(f32[16,32,128]{2,1,0:T(8,128)S(1)} %get-tuple-element.22), channel_id=1, source_target_pairs={{0,80},{16,0},{32,48},{48,96},{64,16},{80,64},{96,112},{112,32},{1... | collective-permute-start | bytes 786440 | tf_op jit(solution)/shard_map/ppermute | solution.py:349
  117.5 35.7 %copy-start.1 = (f32[5,6,32,128]{3,2,1,0:T(8,128)S(1)}, f32[5,6,32,128]{3,2,1,0:T(8,128)}, u32[]{:S(2)}) copy-start(f32[5,6,32,128]{3,2,1,0:T(8,128)} %shard_map.37) | copy-start | bytes 1474564
  117.5 14.2 %collective-permute-start.7 = (f32[16,32,128]{2,1,0:T(8,128)S(1)}, f32[16,32,128]{2,1,0:T(8,128)S(1)}, u32[]{:S(2)}, u32[]{:S(2)}) collective-permute-start(f32[16,32,128]{2,1,0:T(8,128)S(1)} %get-tuple-element.21), channel_id=1, source_target_pairs={{0,96},{16,16},{32,64},{48,112},{64,32},{80,80},{96,0},{112,48},{1... | collective-permute-start | bytes 786440 | tf_op jit(solution)/shard_map/ppermute | solution.py:349
  132.5 63.7 %collective-permute-start.8 = (f32[6,16,32,128]{3,2,1,0:T(8,128)}, f32[6,16,32,128]{3,2,1,0:T(8,128)S(1)}, u32[]{:S(2)}, u32[]{:S(2)}) collective-permute-start(f32[6,16,32,128]{3,2,1,0:T(8,128)} %bitcast_dynamic-update-slice_fusion), channel_id=1, source_target_pairs={{2,6},{3,9},{4,12},{5,15},{6,2},{7,5},{8,8},{9,11},{10,14},{11,1},... | collective-permute-start | bytes 4718600 | tf_op jit(solution)/shard_map/ppermute | solution.py:371
  136.5 70.8 %collective-permute-start.9 = (f32[6,16,32,128]{3,2,1,0:T(8,128)}, f32[6,16,32,128]{3,2,1,0:T(8,128)}, u32[]{:S(2)}, u32[]{:S(2)}) collective-permute-start(f32[6,16,32,128]{3,2,1,0:T(8,128)} %bitcast_dynamic-update-slice_fusion), channel_id=1, source_target_pairs={{2,7},{3,10},{4,13},{5,0},{6,3},{7,6},{8,9},{9,12},{10,15},{11,2},... | collective-permute-start | bytes 4718600 | tf_op jit(solution)/shard_map/ppermute | solution.py:371
  139.9 67.4 %collective-permute-start.10 = (f32[6,16,32,128]{3,2,1,0:T(8,128)}, f32[6,16,32,128]{3,2,1,0:T(8,128)}, u32[]{:S(2)}, u32[]{:S(2)}) collective-permute-start(f32[6,16,32,128]{3,2,1,0:T(8,128)} %bitcast_dynamic-update-slice_fusion), channel_id=1, source_target_pairs={{1,5},{2,8},{3,11},{4,14},{5,1},{6,4},{7,7},{8,10},{9,13},{10,0},{... | collective-permute-start | bytes 4718600 | tf_op jit(solution)/shard_map/ppermute | solution.py:371
  153.2 58.5 %collective-permute-start = (f32[5,3,32,128]{3,2,1,0:T(8,128)S(1)}, f32[5,3,32,128]{3,2,1,0:T(8,128)S(1)}, u32[]{:S(2)}, u32[]{:S(2)}) collective-permute-start(f32[5,3,32,128]{3,2,1,0:T(8,128)S(1)} %get-tuple-element.29), channel_id=1, source_target_pairs={{0,0},{1,8},{2,16},{3,24},{4,32},{5,40},{6,48},{7,56},{8,64},{9,72... | collective-permute-start | bytes 737288 | tf_op jit(solution)/shard_map/ppermute | solution.py:359
  155.2 56.6 %collective-permute-start.1 = (f32[5,3,32,128]{3,2,1,0:T(8,128)S(1)}, f32[5,3,32,128]{3,2,1,0:T(8,128)S(1)}, u32[]{:S(2)}, u32[]{:S(2)}) collective-permute-start(f32[5,3,32,128]{3,2,1,0:T(8,128)S(1)} %get-tuple-element.30), channel_id=1, source_target_pairs={{0,8},{1,0},{2,24},{3,16},{4,40},{5,32},{6,56},{7,48},{8,72},{9,64... | collective-permute-start | bytes 737288 | tf_op jit(solution)/shard_map/ppermute | solution.py:360
  214.2 145.0 %all-to-all-start.2 = ((f32[8,2,5,3,32,128]{5,4,3,2,1,0:T(8,128)}), f32[8,2,5,3,32,128]{5,4,3,2,1,0:T(8,128)}, u32[]{:S(2)}, u32[]{:S(2)}) async-start(f32[8,2,5,3,32,128]{5,4,3,2,1,0:T(8,128)} %broadcast_in_dim.2), calls=%async_computation.2 | async-start | bytes 7864320 | tf_op jit(solution)/shard_map/all_to_all | solution.py:366
Sparse Core Ops, SparseCore 0:
  38.3 76.7 all-gather.8
  117.1 162.8 all-gather.6

commit v3 on v2

v3 whole, which is shorter than its diff:
```python
import jax
import jax.numpy as jnp
from jax import lax
from jax.experimental import pallas as pl
from jax.experimental.pallas import tpu as pltpu
from jax.sharding import PartitionSpec as P

KB = 5
NB = 256
HB = 128
LANES = 128
F32 = jnp.float32
BF16 = jnp.bfloat16
VMEM_LIMIT = 60 * 1024 * 1024
VM = pl.BlockSpec(memory_space=pltpu.VMEM)
SM = pl.BlockSpec(memory_space=pltpu.SMEM)


def route_of(meta, child, residue):
    there, slot = False, 0
    for turn in range(4):
        target = meta[child * 16 + 4 * turn + residue]
        here = target % 8 == meta[32]
        there = jnp.logical_or(there, here)
        slot = jnp.where(here, target // 8, slot)
    return there, slot


def turn_for(meta, target_row):
    child, residue = meta[32] // 4, meta[32] % 4
    chosen = 0
    for turn in range(1, 4):
        chosen = jnp.where(meta[child * 16 + 4 * turn + residue] % 8 == target_row, turn, chosen)
    return chosen


def residue_of(row, e):
    return (3 * row + 4 + e) % 4


def pick_kernel(meta, parts_ref, out_ref):
    for target_row in range(8):
        turn = turn_for(meta, target_row)
        for v in range(2):
            out_ref[target_row, v] = parts_ref[v, turn]


def copy_kernel(meta, block_ref, out_ref):
    out_ref[...] = block_ref[...]


def assemble_kernel(meta, first_ref, rest_ref, got_ref, out_ref):
    for j in range(KB):
        out_ref[j, 0] = first_ref[j]
        out_ref[j, 1:6] = rest_ref[j]
    for child in range(2):
        for residue in range(4):
            there, slot = route_of(meta, child, residue)
            for v in range(2):
                column = meta[child * 16 + v]

                @pl.when(jnp.logical_and(there, column < KB))
                def _():
                    out_ref[column, slot] = out_ref[column, slot] + got_ref[4 * child + residue, v]


def chunk_kernel(meta, mine_ref, got_a_ref, got_b_ref, out_ref):
    for row, picks in enumerate(CHUNKS):

        @pl.when(meta[32] == row)
        def _():
            for at in range(3):
                kind, index = picks[at] if at < len(picks) else (0, 0)
                source = (mine_ref, got_a_ref, got_b_ref)[kind]
                out_ref[at] = source[index]


CHUNKS = [
    [(0, 0), (0, 5), (0, 6)],
    [(0, 1), (0, 2), (0, 6)],
    [(0, 2), (0, 3), (0, 4)],
    [(0, 3), (0, 4)],
    [(0, 4), (0, 5), (0, 6)],
    [(1, 0), (1, 1), (0, 6)],
    [(1, 0), (1, 1), (1, 2)],
    [(2, 0)],
]
UPPER_AT = {
    (0, 0): (0, 0),
    (0, 1): (7, 0),
    (0, 2): (6, 0),
    (0, 3): (6, 1),
    (0, 4): (6, 2),
    (1, 1): (1, 0),
    (1, 2): (1, 1),
    (1, 3): (5, 0),
    (1, 4): (5, 1),
    (2, 2): (2, 0),
    (2, 3): (2, 1),
    (2, 4): (2, 2),
    (3, 3): (3, 0),
    (3, 4): (3, 1),
    (4, 4): (4, 0),
}
CHILD_AT = {
    (0, 0, 0): (0, 1),
    (0, 0, 1): (0, 2),
    (0, 1, 1): (1, 2),
    (1, 0, 0): (4, 1),
    (1, 0, 1): (4, 2),
    (1, 1, 1): (5, 2),
}


def exact(a, b, dims):
    return lax.dot_general(a, b, (dims, ((), ())), precision=lax.Precision.HIGHEST, preferred_element_type=F32)


def factor_128(a_ref, x_ref, u_ref):
    shape = (8, LANES)
    lane = lax.broadcasted_iota(jnp.int32, (HB, LANES), 1)
    sub = lax.broadcasted_iota(jnp.int32, (HB, LANES), 0)
    x_ref[...] = jnp.where(lane == sub, 1.0, 0.0).astype(F32)
    for g in range(HB // 8):
        rows = slice(8 * g, 8 * g + 8)
        a_g = a_ref[rows, :]
        x_g = x_ref[rows, :]
        cols = [jnp.broadcast_to(a_g[:, 8 * g + s : 8 * g + s + 1], shape) for s in range(8)]
        d = [[jnp.broadcast_to(cols[s][t : t + 1, :], shape) for s in range(t + 1)] for t in range(8)]
        low = [[None] * 8 for _ in range(8)]
        rinv = []
        for s in range(8):
            r = lax.rsqrt(d[s][s])
            rinv.append(r)
            for t in range(s + 1, 8):
                low[t][s] = d[t][s] * r
            for t in range(s + 1, 8):
                for t2 in range(s + 1, t + 1):
                    d[t][t2] = d[t][t2] - low[t][s] * low[t2][s]
        ub, xb = [], []
        for t in range(8):
            ua = jnp.broadcast_to(a_g[t : t + 1, :], shape)
            xa = jnp.broadcast_to(x_g[t : t + 1, :], shape)
            for s in range(t):
                ua = ua - low[t][s] * ub[s]
                xa = xa - low[t][s] * xb[s]
            ub.append(ua * rinv[t])
            xb.append(xa * rinv[t])
            u_ref[8 * g + t : 8 * g + t + 1, :] = ub[t][0:1, :]
            x_ref[8 * g + t : 8 * g + t + 1, :] = xb[t][0:1, :]
        for i in range(g + 1, HB // 8):
            rows_i = slice(8 * i, 8 * i + 8)
            a_i = a_ref[rows_i, :]
            x_i = x_ref[rows_i, :]
            w = []
            for t in range(8):
                wt = jnp.broadcast_to(a_i[:, 8 * g + t : 8 * g + t + 1], shape)
                for s in range(t):
                    wt = wt - low[t][s] * w[s]
                w.append(wt * rinv[t])
            for t in range(8):
                a_i = a_i - w[t] * ub[t]
                x_i = x_i - w[t] * xb[t]
            a_ref[rows_i, :] = a_i
            x_ref[rows_i, :] = x_i
    u_ref[...] = jnp.where(lane >= sub, u_ref[...], 0.0)


def split(a):
    high = a.astype(BF16)
    return high, (a - high.astype(F32)).astype(BF16)


CUT = 2
REST = KB - CUT


def eliminate(n, steps, f_ref, u_ref, th_ref, tl_ref, v_ref, a_s, x_s, u_s):
    @pl.loop(0, 2 * steps)
    def _(step):
        k = step // 2
        half = step % 2
        kk = k * n + k

        @pl.when(half == 0)
        def _():
            a_s[...] = f_ref[kk, 0:HB, 0:HB]

        @pl.when(half == 1)
        def _():
            u12 = exact(v_ref[0:HB, 0:HB], f_ref[kk, 0:HB, HB:NB], ((1,), (0,)))
            u_ref[kk, 0:HB, HB:NB] = u12
            a_s[...] = f_ref[kk, HB:NB, HB:NB] - exact(u12, u12, ((0,), (0,)))

        factor_128(a_s, x_s, u_s)

        @pl.when(half == 0)
        def _():
            u_ref[kk, 0:HB, 0:HB] = u_s[...]
            v_ref[0:HB, 0:HB] = x_s[...]

        @pl.when(half == 1)
        def _():
            u_ref[kk, HB:NB, HB:NB] = u_s[...]
            u_ref[kk, HB:NB, 0:HB] = jnp.zeros((HB, HB), F32)
            v_ref[HB:NB, HB:NB] = x_s[...]
            v_ref[0:HB, HB:NB] = jnp.zeros((HB, HB), F32)
            lx = exact(u_ref[kk, 0:HB, HB:NB], v_ref[0:HB, 0:HB], ((0,), (0,)))
            v_ref[HB:NB, 0:HB] = -exact(x_s[...], lx, ((1,), (0,)))
            high, low = split(v_ref[...].T)
            th_ref[kk] = high
            tl_ref[kk] = low

            @pl.loop(k + 1, n)
            def _(i):
                u = exact(v_ref[...], f_ref[k * n + i], ((1,), (0,)))
                u_ref[k * n + i] = u
                high, low = split(u)
                th_ref[k * n + i] = high
                tl_ref[k * n + i] = low

            @pl.loop(k + 1, n)
            def _(i):
                @pl.loop(i, n)
                def _(j):
                    f_ref[i * n + j] = f_ref[i * n + j] - exact(u_ref[k * n + i], u_ref[k * n + j], ((0,), (0,)))


def chain_head_kernel(meta, parts_ref, u_ref, th_ref, tl_ref, rest_ref, f_ref, *scratch):
    def take(at, s, h):
        return parts_ref[at[0], s, at[1], pl.ds(h, 16, stride=2), :]

    for (k, i), at in UPPER_AT.items():
        for s in range(16):
            for h in range(2):
                f_ref[k * KB + i, 16 * s : 16 * s + 16, HB * h : HB * h + HB] = take(at, s, h)
    for (c, u, v), at in CHILD_AT.items():
        k = meta[c * 16 + u]
        i = meta[c * 16 + v]

        @pl.when(jnp.logical_and(k < KB, i < KB))
        def _():
            for s in range(16):
                for h in range(2):
                    place = (k * KB + i, slice(16 * s, 16 * s + 16), slice(HB * h, HB * h + HB))
                    f_ref[place] = f_ref[place] + take(at, s, h)

    for ref in (th_ref, tl_ref, u_ref):
        ref[KB] = jnp.zeros((NB, NB), ref.dtype)
    eliminate(KB, CUT, f_ref, u_ref, th_ref, tl_ref, *scratch)
    for i in range(REST):
        for j in range(REST):
            if j >= i:
                rest_ref[i * REST + j] = f_ref[(CUT + i) * KB + CUT + j]
            else:
                rest_ref[i * REST + j] = jnp.zeros((NB, NB), F32)


def chain_tail_kernel(rest_ref, u_ref, th_ref, tl_ref, f_ref, *scratch):
    f_ref[...] = rest_ref[...]
    for i in range(REST):
        for j in range(i):
            for ref in (th_ref, tl_ref, u_ref):
                ref[i * REST + j] = jnp.zeros((NB, NB), ref.dtype)
    eliminate(REST, REST, f_ref, u_ref, th_ref, tl_ref, *scratch)


def dot3(ah, al, bh, bl, dims):
    def dot(a, b):
        return lax.dot_general(a, b, (dims, ((), ())), preferred_element_type=F32)

    return dot(ah, bh) + (dot(ah, bl) + dot(al, bh))


NN = ((1,), (0,))
NT = ((1,), (1,))


def solve_rows(raw_ref, yh_ref, yl_ref, factors):
    head_h, head_l, tail_h, tail_l = factors

    def factor(m, k):
        if m < CUT:
            return head_h[m * KB + k], head_l[m * KB + k]
        at = (m - CUT) * REST + k - CUT
        return tail_h[at], tail_l[at]

    for k in range(KB):
        at = slice(NB * k, NB * k + NB)
        t = raw_ref[:, at]
        for m in range(k):
            am = slice(NB * m, NB * m + NB)
            t = t - dot3(yh_ref[:, am], yl_ref[:, am], *factor(m, k), NN)
        high, low = split(t)
        y = dot3(high, low, *factor(k, k), NN)
        raw_ref[:, at] = y
        high, low = split(y)
        yh_ref[:, at] = high
        yl_ref[:, at] = low


def right_kernel(parts_ref, hh_ref, hl_ref, th_ref, tl_ref, yh_ref, yl_ref, raw):
    @pl.loop(0, 16)
    def _(s):
        for c in range(3):
            for j in range(KB):
                for h in range(2):
                    raw[pl.ds(pl.multiple_of(NB * c + 16 * s, 16), 16), NB * j + HB * h : NB * j + HB * h + HB] = parts_ref[
                        s, j, c, pl.ds(h, 16, stride=2), :
                    ]
    solve_rows(raw, yh_ref, yl_ref, (hh_ref, hl_ref, th_ref, tl_ref))


ROWS_STEP = 2


def left_kernel(meta, parts_ref, hh_ref, hl_ref, th_ref, tl_ref, yh_ref, yl_ref, own_ref, raw):
    @pl.loop(0, 16)
    def _(s):
        for a in range(ROWS_STEP):
            for j in range(KB):
                for h in range(2):
                    raw[pl.ds(pl.multiple_of(NB * a + 16 * s, 16), 16), NB * j + HB * h : NB * j + HB * h + HB] = parts_ref[
                        s, j, a, pl.ds(h, 16, stride=2), :
                    ]
    solve_rows(raw, yh_ref, yl_ref, (hh_ref, hl_ref, th_ref, tl_ref))
    for j in range(KB):

        @pl.when(meta[33] == j)
        def _():
            own_ref[...] = raw[:, NB * j : NB * j + NB]


def schur_kernel(meta, yh, yl, own_ref, rh_ref, rl_ref, head_ref, tail_ref, parent_ref, child_0, child_1, child_2, out_ref):
    step = pl.program_id(0)
    row, col = meta[32], meta[33]
    routes = []
    for child in range(2):
        for e in range(3):
            routes.append((child, *route_of(meta, child, residue_of(row, e))))

    for a in range(ROWS_STEP):
        slot = step * ROWS_STEP + a
        block_row = row + 8 * slot
        rows = slice(NB * a, NB * a + NB)
        for c in range(3):
            block_col = col + 16 * c

            def put(h, value):
                out_ref[pl.ds(1536 * a + 2 * c + h, NB, stride=6), :] = value

            @pl.when(jnp.logical_and(block_row >= KB, block_col >= KB))
            def _():
                cols = slice(NB * c, NB * c + NB)
                product = dot3(yh[rows, :], yl[rows, :], rh_ref[cols, :], rl_ref[cols, :], NT)
                for h in range(2):
                    put(h, parent_ref[pl.ds(1536 * a + 2 * c + h, NB, stride=6), :] - product[:, HB * h : HB * h + HB])
                turn = block_col % 3
                source = block_col // 3
                for n, (child, there, to) in enumerate(routes):
                    here = jnp.logical_and(there, to == slot)
                    here = jnp.logical_and(here, meta[child * 16 + source] == block_col)
                    for d, child_ref in enumerate((child_0, child_1, child_2)):

                        @pl.when(jnp.logical_and(here, turn == d))
                        def _():
                            for h in range(2):
                                at = pl.ds(1536 * a + 2 * c + h, NB, stride=6)
                                out_ref[at, :] = out_ref[at, :] + child_ref[n, pl.ds(h, NB, stride=2), :]

            @pl.when(jnp.logical_and(block_row < KB, block_col >= KB))
            def _():
                for h in range(2):
                    put(h, jnp.zeros((NB, HB), F32))

            if c == 0:

                @pl.when(jnp.logical_and(block_row >= KB, block_col < KB))
                def _():
                    for h in range(2):
                        put(h, own_ref[rows, HB * h : HB * h + HB])

                in_lead = jnp.logical_and(block_row < KB, block_col < KB)
                upper = block_row < block_col

                @pl.when(jnp.logical_and(in_lead, upper))
                def _():
                    for h in range(2):
                        put(h, jnp.zeros((NB, HB), F32))

                lower = jnp.logical_and(in_lead, jnp.logical_not(upper))

                @pl.when(jnp.logical_and(lower, block_col < CUT))
                def _():
                    block = head_ref[jnp.minimum(block_col, CUT - 1) * KB + jnp.minimum(block_row, KB - 1)].T
                    for h in range(2):
                        put(h, block[:, HB * h : HB * h + HB])

                @pl.when(jnp.logical_and(lower, block_col >= CUT))
                def _():
                    at_col = jnp.clip(block_col - CUT, 0, REST - 1)
                    block = tail_ref[at_col * REST + jnp.clip(block_row - CUT, 0, REST - 1)].T
                    for h in range(2):
                        put(h, block[:, HB * h : HB * h + HB])


def cost(microseconds):
    return pl.CostEstimate(flops=int(microseconds * 1.1e9), bytes_accessed=1 << 20, transcendentals=0)


def call(kernel, out_shape, in_specs, scratch, microseconds=2):
    return pl.pallas_call(
        kernel,
        out_shape=out_shape,
        in_specs=in_specs,
        out_specs=jax.tree.map(lambda _: VM, out_shape),
        scratch_shapes=scratch,
        compiler_params=pltpu.CompilerParams(vmem_limit_bytes=VMEM_LIMIT),
        cost_estimate=cost(microseconds),
    )


def shaped(shape, dtype=F32):
    return jax.ShapeDtypeStruct(shape, dtype)


def per_device(parent, children, index_maps):
    row = lax.axis_index("prow")
    col = lax.axis_index("pcol")
    meta = jnp.concatenate([index_maps.reshape(-1), jnp.stack([row, col]).astype(jnp.int32)])
    front = parent.reshape(6, NB, 3, 2, LANES)
    lead = front[:, :, 0].reshape(6, 16, 32, LANES)
    child = children.reshape(4, 16, 32, LANES)

    picked = pl.pallas_call(
        copy_kernel,
        grid_spec=pltpu.PrefetchScalarGridSpec(
            num_scalar_prefetch=1,
            grid=(8,),
            in_specs=[pl.BlockSpec((1, 512, LANES), lambda t, meta: (turn_for(meta, t), 0, 0))],
            out_specs=pl.BlockSpec((1, 512, LANES), lambda t, meta: (t, 0, 0)),
        ),
        out_shape=shaped((8, 512, LANES)),
        cost_estimate=cost(3),
    )(meta, child.reshape(4, 512, LANES))

    first = jnp.stack([lead[0], child[0]], axis=1)
    first = lax.all_to_all(first, "pcol", 0, 0, tiled=True)
    mine = jnp.concatenate([first[0:KB, 0], first[0:2, 1]], axis=0)
    shed = jnp.where(row == 0, mine[2:5], mine[3:6])
    got_a = lax.ppermute(shed, "prow", [(0, 6), (1, 5)])
    got_b = lax.ppermute(mine[1:2], "prow", [(0, 7)])
    chunk = call(chunk_kernel, shaped((3, 32, LANES)), [SM, VM, VM, VM], [])(meta, mine, got_a, got_b)
    chunk = lax.all_gather(chunk, "pcol")
    lead_parts = lax.all_gather(chunk, "prow")

    rest = jnp.concatenate([lead[1:], child], axis=0).transpose(1, 0, 2, 3)
    rest, chunk = lax.optimization_barrier((rest, chunk))
    rest = lax.all_to_all(rest, "pcol", 0, 0, tiled=True)
    pieces = call(pick_kernel, shaped((8, 2, 32, LANES)), [SM, VM], [])(meta, rest[0:2, 5:9])
    pieces = lax.all_to_all(pieces, "prow", 0, 0, tiled=True)
    slices = call(assemble_kernel, shaped((KB, 6, 32, LANES)), [SM, VM, VM, VM], [])(
        meta, mine[0:KB], rest[0:KB, 0:5], pieces
    )

    left_parts = lax.all_gather(slices, "pcol")

    lead_parts, slices, picked = lax.optimization_barrier((lead_parts, slices, picked))
    got = lax.all_to_all(picked, "prow", 0, 0, tiled=True)
    routed = jnp.stack(
        [
            lax.dynamic_index_in_dim(got, 4 * c + residue_of(row, e), 0, keepdims=False)
            for c in range(2)
            for e in range(3)
        ]
    )
    even, odd = slices[:, 0::2], slices[:, 1::2]
    is_even = col % 2 == 0
    perm_a, perm_b = [], []
    for p in range(8):
        for s in range(16):
            perm_a.append((p * 16 + s, (s // 2) * 16 + p + 8 * (s % 2)))
            perm_b.append((p * 16 + s, (s // 2) * 16 + p + 8 * (1 - s % 2)))
    pair_a = lax.ppermute(jnp.where(is_even, even, odd), ("prow", "pcol"), perm_a)
    pair_b = lax.ppermute(jnp.where(is_even, odd, even), ("prow", "pcol"), perm_b)
    low_side = col < 8
    pair = jnp.stack([jnp.where(low_side, pair_a, pair_b), jnp.where(low_side, pair_b, pair_a)])
    pairs = jnp.broadcast_to(pair[None], (8,) + pair.shape)

    scratch = [
        pltpu.VMEM((NB, NB), F32),
        pltpu.VMEM((HB, HB), F32),
        pltpu.VMEM((HB, HB), F32),
        pltpu.VMEM((HB, HB), F32),
    ]
    heads = CUT * KB
    head_u, head_h, head_l, left_over = call(
        chain_head_kernel,
        (
            shaped((heads, NB, NB)),
            shaped((heads, NB, NB), BF16),
            shaped((heads, NB, NB), BF16),
            shaped((REST * REST, NB, NB)),
        ),
        [SM, VM],
        [pltpu.VMEM((KB * KB, NB, NB), F32)] + scratch,
        32,
    )(meta, lead_parts)

    left_over, pairs, routed = lax.optimization_barrier((left_over, pairs, routed))
    right_parts = lax.all_to_all(pairs, "prow", 0, 0, tiled=True).reshape(16, KB, 3, 32, LANES)
    middle = lax.ppermute(routed, "pcol", [(q, (3 * q + 1) % 16) for q in range(1, 16)])
    tails = REST * REST
    tail_u, tail_h, tail_l = call(
        chain_tail_kernel,
        (shaped((tails, NB, NB)), shaped((tails, NB, NB), BF16), shaped((tails, NB, NB), BF16)),
        [VM],
        [pltpu.VMEM((tails, NB, NB), F32)] + scratch,
        40,
    )(left_over)

    middle, tail_h = lax.optimization_barrier((middle, tail_h))
    below = lax.ppermute(middle, "pcol", [(q, (q + 1) % 16) for q in range(16)])
    above = lax.ppermute(middle, "pcol", [(q, (q + 15) % 16) for q in range(16)])

    rh, rl = call(
        right_kernel,
        (shaped((768, 1280), BF16), shaped((768, 1280), BF16)),
        [VM] * 5,
        [pltpu.VMEM((768, 1280), F32)],
        12,
    )(right_parts, head_h, head_l, tail_h, tail_l)

    rows = NB * ROWS_STEP
    steps = 6 // ROWS_STEP
    whole_head = pl.BlockSpec((heads, NB, NB), lambda g: (0, 0, 0))
    whole_tail = pl.BlockSpec((tails, NB, NB), lambda g: (0, 0, 0))
    by_rows = pl.BlockSpec((rows, 1280), lambda g: (g, 0))
    own_rows = pl.BlockSpec((rows, NB), lambda g: (g, 0))
    yh, yl, own = pl.pallas_call(
        left_kernel,
        grid=(steps,),
        out_shape=(shaped((1536, 1280), BF16), shaped((1536, 1280), BF16), shaped((1536, NB))),
        in_specs=[
            SM,
            pl.BlockSpec((16, KB, ROWS_STEP, 32, LANES), lambda g: (0, 0, g, 0, 0)),
            whole_head,
            whole_head,
            whole_tail,
            whole_tail,
        ],
        out_specs=(by_rows, by_rows, own_rows),
        scratch_shapes=[pltpu.VMEM((rows, 1280), F32)],
        compiler_params=pltpu.CompilerParams(vmem_limit_bytes=VMEM_LIMIT),
        cost_estimate=cost(20),
    )(meta, left_parts, head_h, head_l, tail_h, tail_l)

    whole_right = pl.BlockSpec((768, 1280), lambda g: (0, 0))
    whole_child = pl.BlockSpec((6, 512, LANES), lambda g: (0, 0, 0))
    front_rows = pl.BlockSpec((1536 * ROWS_STEP, LANES), lambda g: (g, 0))
    out = pl.pallas_call(
        schur_kernel,
        grid=(steps,),
        out_shape=shaped((9216, LANES)),
        in_specs=[SM, by_rows, by_rows, own_rows, whole_right, whole_right, whole_head, whole_tail, front_rows]
        + [whole_child] * 3,
        out_specs=front_rows,
        compiler_params=pltpu.CompilerParams(vmem_limit_bytes=VMEM_LIMIT),
        cost_estimate=cost(18),
    )(
        meta,
        yh,
        yl,
        own,
        rh,
        rl,
        head_u,
        tail_u,
        parent.reshape(9216, LANES),
        *(x.reshape(6, 512, LANES) for x in (above, middle, below)),
    )
    return out.reshape(6, 1, NB, 3, 1, NB)


def solution(mesh):
    in_specs = (
        P(None, "prow", None, None, "pcol", None),
        P(None, "prow", None, None, "pcol", None),
        P(),
    )
    out_specs = P(None, "prow", None, None, "pcol", None)
    return jax.shard_map(
        per_device, mesh=mesh, in_specs=in_specs, out_specs=out_specs, check_vma=False
    )
```

time: 420 us -> 295 us (0.70)
  starting transfers between devices: 128 us -> 43 us
  waiting for transfers between devices: 86.6 us -> 35.6 us
  Pallas kernels: 121 us -> 133 us
  blocking collectives: 42.7 us -> 53.6 us
  other arithmetic: 6.66 us -> 2.43 us
    all_to_all x1, starting transfers between devices: 76.6 us -> 5.97 us  [per_device(): lax.all_to_all(pairs, 'prow', 0, 0, tiled=True)]
    ppermute x9 -> x5, waiting for transfers between devices: 53.7 us -> 22.1 us  [the longest x1 11.1 us: per_device(): lax.ppermute(routed, 'pcol', [(q, (3 * q + 1) % 16) for q in range(1, 16)])]
    ppermute x9 -> x5, starting transfers between devices: 35.8 us -> 12.8 us  [the longest x1 4.82 us: per_device(): lax.ppermute(routed, 'pcol', [(q, (3 * q + 1) % 16) for q in range(1, 16)])]
    all_to_all x1 -> x3, waiting for transfers between devices: 32.8 us -> 13.5 us  [the longest x1 6.77 us: per_device(): pieces = lax.all_to_all(pieces, 'prow', 0, 0, tiled=True)]
    all_to_all x1, blocking collectives: 14.2 us -> 27.2 us  [per_device(): rest = lax.all_to_all(rest, 'pcol', 0, 0, tiled=True)]
    pallas_call x3 -> x8, Pallas kernels: 109 us -> 122 us  [the longest x1 35.4 us: per_device(): call(chain_tail_kernel, (shaped((tails, NB, NB)), shaped((tails, NB, NB),...]
    all_to_all x1 -> x3, starting transfers between devices: 7.91 us -> 15.6 us  [the longest x1 6.91 us: per_device(): first = lax.all_to_all(first, 'pcol', 0, 0, tiled=True)]
    ppermute x1, starting transfers between devices: 1.92 us -> 6.55 us  [per_device(): lax.ppermute(jnp.where(is_even, even, odd), ('prow', 'pcol'), perm_a)]
  transfers between devices with their start and end apart: 15 -> 13, of which waited for: 5 -> 6; matrix products, arithmetic and copies ran while one was open for 4% -> 2% of each run, Pallas kernels for 20% -> 38%
where the time goes in v3:
time: 295 us; the launch traced here: 292 us
  Pallas kernels  133 us (45%)
  blocking collectives  53.6 us (18%)
  starting transfers between devices  43 us (15%)
  waiting for transfers between devices  35.6 us (12%)
  between operations  13.7 us (5%)
  local copies, waits for them, and re-layouts  10.3 us (3%)
    pallas_call x1, Pallas kernels, per_device(): call(chain_tail_kernel, (shaped((tails, NB, NB)), shaped((tails, NB, NB),...  35.4 us
    pallas_call x1, Pallas kernels, per_device(): call(chain_head_kernel, (shaped((heads, NB, NB)), shaped((heads, NB, NB),...  34.9 us
    all_to_all x1, blocking collectives, per_device(): rest = lax.all_to_all(rest, 'pcol', 0, 0, tiled=True)  27.2 us
    all_gather x1, blocking collectives, per_device(): chunk = lax.all_gather(chunk, 'pcol')  26.4 us
    pallas_call x1, Pallas kernels, per_device(): pl.pallas_call(schur_kernel, grid=(steps,), out_shape=shaped((9216, LANES...  21.4 us
    pallas_call x1, Pallas kernels, per_device(): pl.pallas_call(left_kernel, grid=(steps,), out_shape=(shaped((1536, 1280)...  17.9 us
    pallas_call x1, Pallas kernels, per_device(): call(right_kernel, (shaped((768, 1280), BF16), shaped((768, 1280), BF16))...  11.6 us
    ppermute x1, waiting for transfers between devices, per_device(): lax.ppermute(routed, 'pcol', [(q, (3 * q + 1) % 16) for q in range(1, 16)])  11.1 us
  transfers between devices with their start and end apart: 13, of which 6 were waited for; matrix products, arithmetic and copies ran while one was open for 2% of the time, Pallas kernels for 38%

profile of v3, /device:TPU:102, one launch (start us, length us, event | category | flops | bytes accessed | tf_op | source)
XLA Modules:
  0.0 291.8 jit_solution(11068914996359045850)
XLA Ops:
  6.5 0.0 copy-start.10
  6.5 1.0 slice.67
  7.5 1.1 slice.53
  8.7 0.8 pad_maximum_fusion.1
  9.5 6.9 %all-to-all-start = ((f32[16,2,32,128]{3,2,1,0:T(8,128)}), f32[16,2,32,128]{3,2,1,0:T(8,128)S(1)}, u32[]{:S(2)}, u32[]{:S(2)}) async-start(f32[16,2,32,128]{3,2,1,0:T(8,128)} %pad_maximum_fusion.1), calls=%async_computation | async-start | bytes 1048576 | tf_op jit(solution)/shard_map/all_to_all | solution.py:448
  16.4 0.0 all-gather.8.cloned.1.call-start
  16.4 0.0 copy-done.10
  16.5 0.1 reshape.26
  16.5 0.6 pad_add_fusion.meta
  17.2 6.7 %all-to-all-done = f32[16,2,32,128]{3,2,1,0:T(8,128)S(1)} async-done(((f32[16,2,32,128]{3,2,1,0:T(8,128)}), f32[16,2,32,128]{3,2,1,0:T(8,128)S(1)}, u32[]{:S(2)}, u32[]{:S(2)}) %all-to-all-start) | async-done | bytes 524320 | tf_op jit(solution)/shard_map/all_to_all | solution.py:448
  23.9 3.2 %collective-permute-start.1 = (f32[1,32,128]{2,1,0:T(8,128)S(1)}, f32[1,32,128]{2,1,0:T(8,128)S(1)}, u32[]{:S(2)}, u32[]{:S(2)}) collective-permute-start(f32[1,32,128]{2,1,0:T(8,128)S(1)} %slice_bitcast_fusion.3), channel_id=1, source_target_pairs={{0,112},{1,113},{2,114},{3,115},{4,116},{5,117},{6,118},{7,119},{8... | collective-permute-start | bytes 49160 | tf_op jit(solution)/shard_map/ppermute | solution.py:452
  27.1 0.0 copy-start.2
  27.1 2.4 collective-permute-start
  29.5 0.7 pad_maximum_fusion.3.mine_ref
  30.1 0.0 collective-permute-done.1.got_b_ref
  30.2 0.0 copy-start.9
  30.2 1.1 collective-permute-done.got_a_ref
  31.2 0.0 copy-done.9
  31.2 0.0 copy-start.8
  31.2 0.6 copy-done.8
  31.8 1.6 shard_map.37
  33.5 0.0 copy-done.2
  33.5 26.4 %all-gather = f32[48,32,128]{2,1,0:T(8,128)} all-gather(f32[3,32,128]{2,1,0:T(8,128)} %shard_map.37), channel_id=2, replica_groups=mesh['prow'=8,'pcol'=16] {'pcol'}, dimensions={0}, use_global_device_ids=true | all-gather | bytes 835584 | tf_op jit(solution)/shard_map/all_gather | solution.py:454
  59.9 0.0 all-gather.8.cloned.1.call-update
  59.9 1.5 slice.69
  61.4 0.1 copy-done.1
  61.5 0.2 copy_bitcast_fusion
  61.7 27.2 %all_to_all.25 = f32[16,9,32,128]{3,2,1,0:T(8,128)S(1)} all-to-all(f32[16,9,32,128]{3,2,1,0:T(8,128)S(1)} %copy_bitcast_fusion), channel_id=1, replica_groups=mesh['prow'=8,'pcol'=16] {'pcol'}, dimensions={0} | all-to-all | bytes 4718592 | tf_op jit(solution)/shard_map/all_to_all | solution.py:459
  88.9 0.7 slice.76.parts_ref
  89.6 1.7 shard_map.38
  91.3 5.0 %all-to-all-start.2 = ((f32[8,2,32,128]{3,2,1,0:T(8,128)}), f32[8,2,32,128]{3,2,1,0:T(8,128)S(1)}, u32[]{:S(2)}, u32[]{:S(2)}) async-start(f32[8,2,32,128]{3,2,1,0:T(8,128)} %shard_map.38), calls=%async_computation.2 | async-start | bytes 524288 | tf_op jit(solution)/shard_map/all_to_all | solution.py:461
  96.2 0.0 all-gather.6.cloned.1.call-start
  96.3 0.8 slice.75.rest_ref
  97.0 6.8 %all-to-all-done.2.got_ref = f32[8,2,32,128]{3,2,1,0:T(8,128)S(1)} async-done(((f32[8,2,32,128]{3,2,1,0:T(8,128)}), f32[8,2,32,128]{3,2,1,0:T(8,128)S(1)}, u32[]{:S(2)}, u32[]{:S(2)}) %all-to-all-start.2) | async-done | bytes 262176 | tf_op jit(solution)/shard_map/all_to_all | solution.py:461
  103.8 0.7 copy-done.3
  104.5 2.3 shard_map.39
  106.8 0.0 all-gather.6.cloned.1.call-update
  106.9 6.4 %shard_map.40 = f32[8,512,128]{2,1,0:T(8,128)} custom-call(s32[34]{0:T(128)} %pad_add_fusion.meta, f32[4,512,128]{2,1,0:T(8,128)} %bitcast.42), custom_call_target="tpu_custom_call" | custom-call | flops 3300000000 | bytes 1048576 | tf_op jit(solution)/shard_map/pallas_call | solution.py:435
  113.3 3.8 %all-to-all-start.3 = ((f32[8,512,128]{2,1,0:T(8,128)}), f32[8,512,128]{2,1,0:T(8,128)S(1)}, u32[]{:S(2)}, u32[]{:S(2)}) async-start(f32[8,512,128]{2,1,0:T(8,128)} %shard_map.40), calls=%async_computation.3 | async-start | bytes 4194304 | tf_op jit(solution)/shard_map/all_to_all | solution.py:469
  117.0 0.0 copy-done
  117.1 6.6 %collective-permute-start.2 = (f32[5,3,32,128]{3,2,1,0:T(8,128)S(1)}, f32[5,3,32,128]{3,2,1,0:T(8,128)S(1)}, u32[]{:S(2)}, u32[]{:S(2)}) collective-permute-start(f32[5,3,32,128]{3,2,1,0:T(8,128)S(1)} %get-tuple-element.49), channel_id=1, source_target_pairs={{0,0},{1,8},{2,16},{3,24},{4,32},{5,40},{6,48},{7,56},{8,64},{9,72... | collective-permute-start | bytes 737288 | tf_op jit(solution)/shard_map/ppermute | solution.py:484
  123.7 2.0 collective-permute-start.3
  125.6 34.9 %shard_map.41 = (f32[10,256,256]{2,1,0:T(8,128)}, bf16[10,256,256]{2,1,0:T(8,128)(2,1)}, bf16[10,256,256]{2,1,0:T(8,128)(2,1)}, f32[9,256,256]{2,1,0:T(8,128)}) custom-call(s32[34]{0:T(128)} %pad_add_fusion.meta, f32[8,16,3,32,128]{4,3,2,1,0:T(8,128)} %bitcast.50), custom_call_target="tpu_custom_call" | custom-call | flops 35200000000 | bytes 1048576 | tf_op jit(solution)/shard_map/pallas_call | solution.py:497
  160.5 0.0 collective-permute-done.2
  160.5 0.0 collective-permute-done.3
  160.6 0.0 all-to-all-done.3
  160.8 0.0 copy-start.4
  160.8 1.2 copy-done.4
  162.0 2.4 broadcast_in_dim.2
  164.4 6.0 %all-to-all-start.4 = ((f32[8,2,5,3,32,128]{5,4,3,2,1,0:T(8,128)}), f32[8,2,5,3,32,128]{5,4,3,2,1,0:T(8,128)}, u32[]{:S(2)}, u32[]{:S(2)}) async-start(f32[8,2,5,3,32,128]{5,4,3,2,1,0:T(8,128)} %broadcast_in_dim.2), calls=%async_computation.4 | async-start | bytes 7864320 | tf_op jit(solution)/shard_map/all_to_all | solution.py:511
  170.4 0.0 copy-done.5
  170.4 4.8 %collective-permute-start.4 = (f32[6,512,128]{2,1,0:T(8,128)S(1)}, f32[6,512,128]{2,1,0:T(8,128)S(1)}, u32[]{:S(2)}, u32[]{:S(2)}) collective-permute-start(f32[6,512,128]{2,1,0:T(8,128)S(1)} %copy-done.5), channel_id=1, source_target_pairs={{1,4},{2,7},{3,10},{4,13},{5,0},{6,3},{7,6},{8,9},{9,12},{10,15},{... | collective-permute-start | bytes 4718600 | tf_op jit(solution)/shard_map/ppermute | solution.py:512
  175.2 35.4 %shard_map.42 = (f32[9,256,256]{2,1,0:T(8,128)}, bf16[9,256,256]{2,1,0:T(8,128)(2,1)}, bf16[9,256,256]{2,1,0:T(8,128)(2,1)}) custom-call(f32[9,256,256]{2,1,0:T(8,128)} %get-tuple-element.34.rest_ref), custom_call_target="tpu_custom_call" | custom-call | flops 44000002048 | bytes 1048576 | tf_op jit(solution)/shard_map/pallas_call | solution.py:514
  210.6 11.1 %collective-permute-done.4.child_1 = f32[6,512,128]{2,1,0:T(8,128)S(1)} collective-permute-done((f32[6,512,128]{2,1,0:T(8,128)S(1)}, f32[6,512,128]{2,1,0:T(8,128)S(1)}, u32[]{:S(2)}, u32[]{:S(2)}) %collective-permute-start.4) | collective-permute-done | bytes 1572896 | tf_op jit(solution)/shard_map/ppermute | solution.py:512
  221.7 2.4 collective-permute-start.6
  224.1 0.0 collective-permute-start.5
  224.1 0.0 all-to-all-done.4
  224.1 11.6 %shard_map.44 = (bf16[768,1280]{1,0:T(8,128)(2,1)}, bf16[768,1280]{1,0:T(8,128)(2,1)}) custom-call(f32[16,5,3,32,128]{4,3,2,1,0:T(8,128)} %bitcast.18.parts_ref, bf16[10,256,256]{2,1,0:T(8,128)(2,1)} %get-tuple-element.28.hh_ref, bf16[10,256,256]{2,1,0:T(8,128)(2,1)} %get-tuple-element.29.hl_ref, bf16[9,256,256]{2,1,0:T(8,128)(2,1)} %get-tuple-element.36.th_ref, ...), custom_call_target="tpu_custom_call" | custom-call | flops 13200000000 | bytes 1048576 | tf_op jit(solution)/shard_map/pallas_call | solution.py:526
  235.7 0.0 copy-done.6
  235.7 17.9 %shard_map.43 = (bf16[1536,1280]{1,0:T(8,128)(2,1)}, bf16[1536,1280]{1,0:T(8,128)(2,1)}, f32[1536,256]{1,0:T(8,128)}) custom-call(s32[34]{0:T(128)} %pad_add_fusion.meta, f32[16,5,6,32,128]{4,3,2,1,0:T(8,128)} %bitcast.49, bf16[10,256,256]{2,1,0:T(8,128)(2,1)} %get-tuple-element.28.hh_ref, bf16[10,256,256]{2,1,0:T(8,128)(2,1)} %get-tuple-element.29.hl_ref, ...), custom_call_target="tpu_custom_call" | custom-call | flops 22000001024 | bytes 1048576 | tf_op jit(solution)/shard_map/pallas_call | solution.py:540
  253.6 4.9 %collective-permute-done.6.child_2 = f32[6,512,128]{2,1,0:T(8,128)S(1)} collective-permute-done((f32[6,512,128]{2,1,0:T(8,128)S(1)}, f32[6,512,128]{2,1,0:T(8,128)S(1)}, u32[]{:S(2)}, u32[]{:S(2)}) %collective-permute-start.6) | collective-permute-done | bytes 1572896 | tf_op jit(solution)/shard_map/ppermute | solution.py:523
  258.5 5.0 %collective-permute-done.5.child_0 = f32[6,512,128]{2,1,0:T(8,128)} collective-permute-done((f32[6,512,128]{2,1,0:T(8,128)S(1)}, f32[6,512,128]{2,1,0:T(8,128)}, u32[]{:S(2)}, u32[]{:S(2)}) %collective-permute-start.5) | collective-permute-done | bytes 1572896 | tf_op jit(solution)/shard_map/ppermute | solution.py:524
  263.5 0.0 copy-done.7
  263.5 21.4 %shard_map.45 = f32[9216,128]{1,0:T(8,128)} custom-call(s32[34]{0:T(128)} %pad_add_fusion.meta, bf16[1536,1280]{1,0:T(8,128)(2,1)} %get-tuple-element.38.yh, bf16[1536,1280]{1,0:T(8,128)(2,1)} %get-tuple-element.39.yl, f32[1536,256]{1,0:T(8,128)} %get-tuple-element.40.own_ref, bf16[768,1280]{1,0:T(8,128)(2,1)} %get-tuple-element.42.rh_ref, ...), custom_call_target="tpu_custom_call" | custom-call | flops 19800000512 | bytes 1048576 | tf_op jit(solution)/shard_map/pallas_call | solution.py:561
  (21 shorter events, 0.3 us)
Async XLA Ops:
  6.5 9.9 %copy-start.10 = (s32[2,16]{1,0:T(2,128)S(1)}, s32[2,16]{1,0:T(2,128)}, u32[]{:S(2)}) copy-start(s32[2,16]{1,0:T(2,128)} %param.5) | copy-start | bytes 388
  9.5 14.4 %all-to-all-start = ((f32[16,2,32,128]{3,2,1,0:T(8,128)}), f32[16,2,32,128]{3,2,1,0:T(8,128)S(1)}, u32[]{:S(2)}, u32[]{:S(2)}) async-start(f32[16,2,32,128]{3,2,1,0:T(8,128)} %pad_maximum_fusion.1), calls=%async_computation | async-start | bytes 1048576 | tf_op jit(solution)/shard_map/all_to_all | solution.py:448
  16.4 96.9 %all-gather.8.cloned.1.call-start = ((), (), s32[]{:S(2)}) async-start(), calls=%async_computation.6 | async-start | bytes 7077888 | tf_op jit(solution)/shard_map/all_gather | solution.py:455
  23.9 6.3 %collective-permute-start.1 = (f32[1,32,128]{2,1,0:T(8,128)S(1)}, f32[1,32,128]{2,1,0:T(8,128)S(1)}, u32[]{:S(2)}, u32[]{:S(2)}) collective-permute-start(f32[1,32,128]{2,1,0:T(8,128)S(1)} %slice_bitcast_fusion.3), channel_id=1, source_target_pairs={{0,112},{1,113},{2,114},{3,115},{4,116},{5,117},{6,118},{7,119},{8... | collective-permute-start | bytes 49160 | tf_op jit(solution)/shard_map/ppermute | solution.py:452
  27.1 6.4 %copy-start.2 = (f32[5,32,128]{2,1,0:T(8,128)}, f32[5,32,128]{2,1,0:T(8,128)S(1)}, u32[]{:S(2)}) copy-start(f32[5,32,128]{2,1,0:T(8,128)S(1)} %slice_bitcast_fusion.first_ref) | copy-start | bytes 245764
  27.1 4.1 %collective-permute-start = (f32[3,32,128]{2,1,0:T(8,128)S(1)}, f32[3,32,128]{2,1,0:T(8,128)S(1)}, u32[]{:S(2)}, u32[]{:S(2)}) collective-permute-start(f32[3,32,128]{2,1,0:T(8,128)S(1)} %fusion.1), channel_id=1, source_target_pairs={{0,96},{16,80},{1,97},{17,81},{2,98},{18,82},{3,99},{19,83},{4,100... | collective-permute-start | bytes 147464 | tf_op jit(solution)/shard_map/ppermute | solution.py:451
  30.2 1.1 copy-start.9
  31.2 0.6 copy-start.8
  59.9 1.6 copy-start.1
  91.3 12.5 %all-to-all-start.2 = ((f32[8,2,32,128]{3,2,1,0:T(8,128)}), f32[8,2,32,128]{3,2,1,0:T(8,128)S(1)}, u32[]{:S(2)}, u32[]{:S(2)}) async-start(f32[8,2,32,128]{3,2,1,0:T(8,128)} %shard_map.38), calls=%async_computation.2 | async-start | bytes 524288 | tf_op jit(solution)/shard_map/all_to_all | solution.py:461
  96.2 139.4 %all-gather.6.cloned.1.call-start = ((), (), s32[]{:S(2)}) async-start(), calls=%async_computation.5 | async-start | bytes 8355840 | tf_op jit(solution)/shard_map/all_gather | solution.py:466
  103.8 0.7 copy-start.3
  113.3 3.8 %copy-start = (f32[5,6,32,128]{3,2,1,0:T(8,128)S(1)}, f32[5,6,32,128]{3,2,1,0:T(8,128)}, u32[]{:S(2)}) copy-start(f32[5,6,32,128]{3,2,1,0:T(8,128)} %shard_map.39) | copy-start | bytes 1474564
  113.3 47.3 %all-to-all-start.3 = ((f32[8,512,128]{2,1,0:T(8,128)}), f32[8,512,128]{2,1,0:T(8,128)S(1)}, u32[]{:S(2)}, u32[]{:S(2)}) async-start(f32[8,512,128]{2,1,0:T(8,128)} %shard_map.40), calls=%async_computation.3 | async-start | bytes 4194304 | tf_op jit(solution)/shard_map/all_to_all | solution.py:469
  117.1 43.4 %collective-permute-start.2 = (f32[5,3,32,128]{3,2,1,0:T(8,128)S(1)}, f32[5,3,32,128]{3,2,1,0:T(8,128)S(1)}, u32[]{:S(2)}, u32[]{:S(2)}) collective-permute-start(f32[5,3,32,128]{3,2,1,0:T(8,128)S(1)} %get-tuple-element.49), channel_id=1, source_target_pairs={{0,0},{1,8},{2,16},{3,24},{4,32},{5,40},{6,48},{7,56},{8,64},{9,72... | collective-permute-start | bytes 737288 | tf_op jit(solution)/shard_map/ppermute | solution.py:484
  123.7 36.8 %collective-permute-start.3 = (f32[5,3,32,128]{3,2,1,0:T(8,128)S(1)}, f32[5,3,32,128]{3,2,1,0:T(8,128)S(1)}, u32[]{:S(2)}, u32[]{:S(2)}) collective-permute-start(f32[5,3,32,128]{3,2,1,0:T(8,128)S(1)} %get-tuple-element.50), channel_id=1, source_target_pairs={{0,8},{1,0},{2,24},{3,16},{4,40},{5,32},{6,56},{7,48},{8,72},{9,64... | collective-permute-start | bytes 737288 | tf_op jit(solution)/shard_map/ppermute | solution.py:485
  160.8 1.2 copy-start.4
  164.4 6.0 %copy-start.5 = (f32[6,512,128]{2,1,0:T(8,128)S(1)}, f32[6,512,128]{2,1,0:T(8,128)}, u32[]{:S(2)}) copy-start(f32[6,512,128]{2,1,0:T(8,128)} %copy-done.4) | copy-start | bytes 4718596
  164.4 59.7 %all-to-all-start.4 = ((f32[8,2,5,3,32,128]{5,4,3,2,1,0:T(8,128)}), f32[8,2,5,3,32,128]{5,4,3,2,1,0:T(8,128)}, u32[]{:S(2)}, u32[]{:S(2)}) async-start(f32[8,2,5,3,32,128]{5,4,3,2,1,0:T(8,128)} %broadcast_in_dim.2), calls=%async_computation.4 | async-start | bytes 7864320 | tf_op jit(solution)/shard_map/all_to_all | solution.py:511
  170.4 51.3 %collective-permute-start.4 = (f32[6,512,128]{2,1,0:T(8,128)S(1)}, f32[6,512,128]{2,1,0:T(8,128)S(1)}, u32[]{:S(2)}, u32[]{:S(2)}) collective-permute-start(f32[6,512,128]{2,1,0:T(8,128)S(1)} %copy-done.5), channel_id=1, source_target_pairs={{1,4},{2,7},{3,10},{4,13},{5,0},{6,3},{7,6},{8,9},{9,12},{10,15},{... | collective-permute-start | bytes 4718600 | tf_op jit(solution)/shard_map/ppermute | solution.py:512
  221.7 14.0 %copy-start.6 = (f32[6,512,128]{2,1,0:T(8,128)}, f32[6,512,128]{2,1,0:T(8,128)S(1)}, u32[]{:S(2)}) copy-start(f32[6,512,128]{2,1,0:T(8,128)S(1)} %collective-permute-done.4.child_1) | copy-start | bytes 4718596
  221.7 36.8 %collective-permute-start.6 = (f32[6,512,128]{2,1,0:T(8,128)S(1)}, f32[6,512,128]{2,1,0:T(8,128)S(1)}, u32[]{:S(2)}, u32[]{:S(2)}) collective-permute-start(f32[6,512,128]{2,1,0:T(8,128)S(1)} %collective-permute-done.4.child_1), channel_id=1, source_target_pairs={{0,1},{1,2},{2,3},{3,4},{4,5},{5,6},{6,7},{7,8},{8,9},{9,10},{10,1... | collective-permute-start | bytes 4718600 | tf_op jit(solution)/shard_map/ppermute | solution.py:523
  224.1 39.5 %collective-permute-start.5 = (f32[6,512,128]{2,1,0:T(8,128)S(1)}, f32[6,512,128]{2,1,0:T(8,128)}, u32[]{:S(2)}, u32[]{:S(2)}) collective-permute-start(f32[6,512,128]{2,1,0:T(8,128)S(1)} %collective-permute-done.4.child_1), channel_id=1, source_target_pairs={{0,15},{1,0},{2,1},{3,2},{4,3},{5,4},{6,5},{7,6},{8,7},{9,8},{10,9... | collective-permute-start | bytes 4718600 | tf_op jit(solution)/shard_map/ppermute | solution.py:524
  258.5 5.0 %copy-start.7 = (f32[6,512,128]{2,1,0:T(8,128)}, f32[6,512,128]{2,1,0:T(8,128)S(1)}, u32[]{:S(2)}) copy-start(f32[6,512,128]{2,1,0:T(8,128)S(1)} %collective-permute-done.6.child_2) | copy-start | bytes 4718596
Sparse Core Ops, SparseCore 0:
  60.0 42.4 all-gather.7
  106.9 93.5 all-gather.5

commit v4 on v3

--- a/solution.py
+++ b/solution.py
@@ -64,56 +64,29 @@
                     out_ref[column, slot] = out_ref[column, slot] + got_ref[4 * child + residue, v]
 
 
-def chunk_kernel(meta, mine_ref, got_a_ref, got_b_ref, out_ref):
-    for row, picks in enumerate(CHUNKS):
-
-        @pl.when(meta[32] == row)
-        def _():
-            for at in range(3):
-                kind, index = picks[at] if at < len(picks) else (0, 0)
-                source = (mine_ref, got_a_ref, got_b_ref)[kind]
-                out_ref[at] = source[index]
-
-
-CHUNKS = [
-    [(0, 0), (0, 5), (0, 6)],
-    [(0, 1), (0, 2), (0, 6)],
-    [(0, 2), (0, 3), (0, 4)],
-    [(0, 3), (0, 4)],
-    [(0, 4), (0, 5), (0, 6)],
-    [(1, 0), (1, 1), (0, 6)],
-    [(1, 0), (1, 1), (1, 2)],
-    [(2, 0)],
-]
-UPPER_AT = {
-    (0, 0): (0, 0),
-    (0, 1): (7, 0),
-    (0, 2): (6, 0),
-    (0, 3): (6, 1),
-    (0, 4): (6, 2),
-    (1, 1): (1, 0),
-    (1, 2): (1, 1),
-    (1, 3): (5, 0),
-    (1, 4): (5, 1),
-    (2, 2): (2, 0),
-    (2, 3): (2, 1),
-    (2, 4): (2, 2),
-    (3, 3): (3, 0),
-    (3, 4): (3, 1),
-    (4, 4): (4, 0),
-}
-CHILD_AT = {
-    (0, 0, 0): (0, 1),
-    (0, 0, 1): (0, 2),
-    (0, 1, 1): (1, 2),
-    (1, 0, 0): (4, 1),
-    (1, 0, 1): (4, 2),
-    (1, 1, 1): (5, 2),
-}
+UPPER = [(k, i) for k in range(KB) for i in range(k, KB)]
+CHILD_SOURCES = [(c, u, v) for c in range(2) for (u, v) in ((0, 0), (0, 1), (1, 1))]
+TRI = len(UPPER)
+
+
+def packed(k, i):
+    return k * (2 * KB + 1 - k) // 2 + i - k
 
 
 def exact(a, b, dims):
     return lax.dot_general(a, b, (dims, ((), ())), precision=lax.Precision.HIGHEST, preferred_element_type=F32)
+
+
+def dot3(ah, al, bh, bl, dims):
+    def dot(a, b):
+        return lax.dot_general(a, b, (dims, ((), ())), preferred_element_type=F32)
+
+    return dot(ah, bh) + (dot(ah, bl) + dot(al, bh))
+
+
+NN = ((1,), (0,))
+NT = ((1,), (1,))
+TN = ((0,), (0,))
 
 
 def factor_128(a_ref, x_ref, u_ref):
@@ -171,70 +144,24 @@
     return high, (a - high.astype(F32)).astype(BF16)
 
 
-CUT = 2
-REST = KB - CUT
-
-
-def eliminate(n, steps, f_ref, u_ref, th_ref, tl_ref, v_ref, a_s, x_s, u_s):
-    @pl.loop(0, 2 * steps)
-    def _(step):
-        k = step // 2
-        half = step % 2
-        kk = k * n + k
-
-        @pl.when(half == 0)
-        def _():
-            a_s[...] = f_ref[kk, 0:HB, 0:HB]
-
-        @pl.when(half == 1)
-        def _():
-            u12 = exact(v_ref[0:HB, 0:HB], f_ref[kk, 0:HB, HB:NB], ((1,), (0,)))
-            u_ref[kk, 0:HB, HB:NB] = u12
-            a_s[...] = f_ref[kk, HB:NB, HB:NB] - exact(u12, u12, ((0,), (0,)))
-
-        factor_128(a_s, x_s, u_s)
-
-        @pl.when(half == 0)
-        def _():
-            u_ref[kk, 0:HB, 0:HB] = u_s[...]
-            v_ref[0:HB, 0:HB] = x_s[...]
-
-        @pl.when(half == 1)
-        def _():
-            u_ref[kk, HB:NB, HB:NB] = u_s[...]
-            u_ref[kk, HB:NB, 0:HB] = jnp.zeros((HB, HB), F32)
-            v_ref[HB:NB, HB:NB] = x_s[...]
-            v_ref[0:HB, HB:NB] = jnp.zeros((HB, HB), F32)
-            lx = exact(u_ref[kk, 0:HB, HB:NB], v_ref[0:HB, 0:HB], ((0,), (0,)))
-            v_ref[HB:NB, 0:HB] = -exact(x_s[...], lx, ((1,), (0,)))
-            high, low = split(v_ref[...].T)
-            th_ref[kk] = high
-            tl_ref[kk] = low
-
-            @pl.loop(k + 1, n)
-            def _(i):
-                u = exact(v_ref[...], f_ref[k * n + i], ((1,), (0,)))
-                u_ref[k * n + i] = u
-                high, low = split(u)
-                th_ref[k * n + i] = high
-                tl_ref[k * n + i] = low
-
-            @pl.loop(k + 1, n)
-            def _(i):
-                @pl.loop(i, n)
-                def _(j):
-                    f_ref[i * n + j] = f_ref[i * n + j] - exact(u_ref[k * n + i], u_ref[k * n + j], ((0,), (0,)))
-
-
-def chain_head_kernel(meta, parts_ref, u_ref, th_ref, tl_ref, rest_ref, f_ref, *scratch):
+def chain_kernel(meta, parts_ref, u_ref, th_ref, tl_ref, f_ref, v_ref, a_s, x_s, u_s, stage, sems):
+    sources = UPPER + [(4 * c + u, KB + v) for c, u, v in CHILD_SOURCES]
+    copies = [
+        pltpu.make_async_copy(parts_ref.at[p, :, j], stage.at[at], sems.at[at]) for at, (p, j) in enumerate(sources)
+    ]
+    for copy in copies:
+        copy.start()
+
     def take(at, s, h):
-        return parts_ref[at[0], s, at[1], pl.ds(h, 16, stride=2), :]
-
-    for (k, i), at in UPPER_AT.items():
+        return stage[at, s, pl.ds(h, 16, stride=2), :]
+
+    for at, (k, i) in enumerate(UPPER):
+        copies[at].wait()
         for s in range(16):
             for h in range(2):
                 f_ref[k * KB + i, 16 * s : 16 * s + 16, HB * h : HB * h + HB] = take(at, s, h)
-    for (c, u, v), at in CHILD_AT.items():
+    for at, (c, u, v) in enumerate(CHILD_SOURCES):
+        copies[TRI + at].wait()
         k = meta[c * 16 + u]
         i = meta[c * 16 + v]
 
@@ -243,47 +170,69 @@
             for s in range(16):
                 for h in range(2):
                     place = (k * KB + i, slice(16 * s, 16 * s + 16), slice(HB * h, HB * h + HB))
-                    f_ref[place] = f_ref[place] + take(at, s, h)
-
-    for ref in (th_ref, tl_ref, u_ref):
-        ref[KB] = jnp.zeros((NB, NB), ref.dtype)
-    eliminate(KB, CUT, f_ref, u_ref, th_ref, tl_ref, *scratch)
-    for i in range(REST):
-        for j in range(REST):
-            if j >= i:
-                rest_ref[i * REST + j] = f_ref[(CUT + i) * KB + CUT + j]
-            else:
-                rest_ref[i * REST + j] = jnp.zeros((NB, NB), F32)
-
-
-def chain_tail_kernel(rest_ref, u_ref, th_ref, tl_ref, f_ref, *scratch):
-    f_ref[...] = rest_ref[...]
-    for i in range(REST):
-        for j in range(i):
-            for ref in (th_ref, tl_ref, u_ref):
-                ref[i * REST + j] = jnp.zeros((NB, NB), ref.dtype)
-    eliminate(REST, REST, f_ref, u_ref, th_ref, tl_ref, *scratch)
-
-
-def dot3(ah, al, bh, bl, dims):
-    def dot(a, b):
-        return lax.dot_general(a, b, (dims, ((), ())), preferred_element_type=F32)
-
-    return dot(ah, bh) + (dot(ah, bl) + dot(al, bh))
-
-
-NN = ((1,), (0,))
-NT = ((1,), (1,))
-
-
-def solve_rows(raw_ref, yh_ref, yl_ref, factors):
-    head_h, head_l, tail_h, tail_l = factors
-
+                    f_ref[place] = f_ref[place] + take(TRI + at, s, h)
+
+    @pl.loop(0, 2 * KB)
+    def _(step):
+        k = step // 2
+        half = step % 2
+        kk = k * KB + k
+        pk = packed(k, k)
+
+        @pl.when(half == 0)
+        def _():
+            a_s[...] = f_ref[kk, 0:HB, 0:HB]
+
+        @pl.when(half == 1)
+        def _():
+            u12 = exact(v_ref[0:HB, 0:HB], f_ref[kk, 0:HB, HB:NB], NN)
+            u_ref[pk, 0:HB, HB:NB] = u12
+            a_s[...] = f_ref[kk, HB:NB, HB:NB] - exact(u12, u12, TN)
+
+        factor_128(a_s, x_s, u_s)
+
+        @pl.when(half == 0)
+        def _():
+            u_ref[pk, 0:HB, 0:HB] = u_s[...]
+            v_ref[0:HB, 0:HB] = x_s[...]
+
+        @pl.when(half == 1)
+        def _():
+            u_ref[pk, HB:NB, HB:NB] = u_s[...]
+            u_ref[pk, HB:NB, 0:HB] = jnp.zeros((HB, HB), F32)
+            v_ref[HB:NB, HB:NB] = x_s[...]
+            v_ref[0:HB, HB:NB] = jnp.zeros((HB, HB), F32)
+            lx = exact(u_ref[pk, 0:HB, HB:NB], v_ref[0:HB, 0:HB], TN)
+            v_ref[HB:NB, 0:HB] = -exact(x_s[...], lx, NN)
+            high, low = split(v_ref[...].T)
+            th_ref[pk] = high
+            tl_ref[pk] = low
+            vh, vl = split(v_ref[...])
+
+            @pl.loop(k + 1, KB)
+            def _(i):
+                u = dot3(vh, vl, *split(f_ref[k * KB + i]), NN)
+                at = packed(k, i)
+                u_ref[at] = u
+                high, low = split(u)
+                th_ref[at] = high
+                tl_ref[at] = low
+
+            @pl.loop(k + 1, KB)
+            def _(i):
+                at_i = packed(k, i)
+
+                @pl.loop(i, KB)
+                def _(j):
+                    at_j = packed(k, j)
+                    f_ref[i * KB + j] = f_ref[i * KB + j] - dot3(
+                        th_ref[at_i], tl_ref[at_i], th_ref[at_j], tl_ref[at_j], TN
+                    )
+
+
+def solve_rows(raw_ref, yh_ref, yl_ref, th_ref, tl_ref):
     def factor(m, k):
-        if m < CUT:
-            return head_h[m * KB + k], head_l[m * KB + k]
-        at = (m - CUT) * REST + k - CUT
-        return tail_h[at], tail_l[at]
+        return th_ref[packed(m, k)], tl_ref[packed(m, k)]
 
     for k in range(KB):
         at = slice(NB * k, NB * k + NB)
@@ -299,7 +248,7 @@
         yl_ref[:, at] = low
 
 
-def right_kernel(parts_ref, hh_ref, hl_ref, th_ref, tl_ref, yh_ref, yl_ref, raw):
+def right_kernel(parts_ref, th_ref, tl_ref, yh_ref, yl_ref, raw):
     @pl.loop(0, 16)
     def _(s):
         for c in range(3):
@@ -308,13 +257,13 @@
                     raw[pl.ds(pl.multiple_of(NB * c + 16 * s, 16), 16), NB * j + HB * h : NB * j + HB * h + HB] = parts_ref[
                         s, j, c, pl.ds(h, 16, stride=2), :
                     ]
-    solve_rows(raw, yh_ref, yl_ref, (hh_ref, hl_ref, th_ref, tl_ref))
+    solve_rows(raw, yh_ref, yl_ref, th_ref, tl_ref)
 
 
 ROWS_STEP = 2
 
 
-def left_kernel(meta, parts_ref, hh_ref, hl_ref, th_ref, tl_ref, yh_ref, yl_ref, own_ref, raw):
+def left_kernel(meta, parts_ref, th_ref, tl_ref, yh_ref, yl_ref, own_ref, raw):
     @pl.loop(0, 16)
     def _(s):
         for a in range(ROWS_STEP):
@@ -323,7 +272,7 @@
                     raw[pl.ds(pl.multiple_of(NB * a + 16 * s, 16), 16), NB * j + HB * h : NB * j + HB * h + HB] = parts_ref[
                         s, j, a, pl.ds(h, 16, stride=2), :
                     ]
-    solve_rows(raw, yh_ref, yl_ref, (hh_ref, hl_ref, th_ref, tl_ref))
+    solve_rows(raw, yh_ref, yl_ref, th_ref, tl_ref)
     for j in range(KB):
 
         @pl.when(meta[33] == j)
@@ -331,7 +280,7 @@
             own_ref[...] = raw[:, NB * j : NB * j + NB]
 
 
-def schur_kernel(meta, yh, yl, own_ref, rh_ref, rl_ref, head_ref, tail_ref, parent_ref, child_0, child_1, child_2, out_ref):
+def schur_kernel(meta, yh, yl, own_ref, rh_ref, rl_ref, u_ref, parent_ref, child_0, child_1, child_2, out_ref):
     step = pl.program_id(0)
     row, col = meta[32], meta[33]
     routes = []
@@ -388,18 +337,9 @@
                     for h in range(2):
                         put(h, jnp.zeros((NB, HB), F32))
 
-                lower = jnp.logical_and(in_lead, jnp.logical_not(upper))
-
-                @pl.when(jnp.logical_and(lower, block_col < CUT))
+                @pl.when(jnp.logical_and(in_lead, jnp.logical_not(upper)))
                 def _():
-                    block = head_ref[jnp.minimum(block_col, CUT - 1) * KB + jnp.minimum(block_row, KB - 1)].T
-                    for h in range(2):
-                        put(h, block[:, HB * h : HB * h + HB])
-
-                @pl.when(jnp.logical_and(lower, block_col >= CUT))
-                def _():
-                    at_col = jnp.clip(block_col - CUT, 0, REST - 1)
-                    block = tail_ref[at_col * REST + jnp.clip(block_row - CUT, 0, REST - 1)].T
+                    block = u_ref[jnp.clip(packed(block_col, block_row), 0, TRI - 1)].T
                     for h in range(2):
                         put(h, block[:, HB * h : HB * h + HB])
 
@@ -447,15 +387,11 @@
     first = jnp.stack([lead[0], child[0]], axis=1)
     first = lax.all_to_all(first, "pcol", 0, 0, tiled=True)
     mine = jnp.concatenate([first[0:KB, 0], first[0:2, 1]], axis=0)
-    shed = jnp.where(row == 0, mine[2:5], mine[3:6])
-    got_a = lax.ppermute(shed, "prow", [(0, 6), (1, 5)])
-    got_b = lax.ppermute(mine[1:2], "prow", [(0, 7)])
-    chunk = call(chunk_kernel, shaped((3, 32, LANES)), [SM, VM, VM, VM], [])(meta, mine, got_a, got_b)
-    chunk = lax.all_gather(chunk, "pcol")
-    lead_parts = lax.all_gather(chunk, "prow")
+    mine, picked = lax.optimization_barrier((mine, picked))
+    lead_parts = lax.all_gather(mine, ("prow", "pcol")).reshape(8, 16, KB + 2, 32, LANES)
 
     rest = jnp.concatenate([lead[1:], child], axis=0).transpose(1, 0, 2, 3)
-    rest, chunk = lax.optimization_barrier((rest, chunk))
+    rest, mine = lax.optimization_barrier((rest, mine))
     rest = lax.all_to_all(rest, "pcol", 0, 0, tiled=True)
     pieces = call(pick_kernel, shaped((8, 2, 32, LANES)), [SM, VM], [])(meta, rest[0:2, 5:9])
     pieces = lax.all_to_all(pieces, "prow", 0, 0, tiled=True)
@@ -465,7 +401,7 @@
 
     left_parts = lax.all_gather(slices, "pcol")
 
-    lead_parts, slices, picked = lax.optimization_barrier((lead_parts, slices, picked))
+    slices, picked = lax.optimization_barrier((slices, picked))
     got = lax.all_to_all(picked, "prow", 0, 0, tiled=True)
     routed = jnp.stack(
         [
@@ -487,54 +423,43 @@
     pair = jnp.stack([jnp.where(low_side, pair_a, pair_b), jnp.where(low_side, pair_b, pair_a)])
     pairs = jnp.broadcast_to(pair[None], (8,) + pair.shape)
 
-    scratch = [
-        pltpu.VMEM((NB, NB), F32),
-        pltpu.VMEM((HB, HB), F32),
-        pltpu.VMEM((HB, HB), F32),
-        pltpu.VMEM((HB, HB), F32),
-    ]
-    heads = CUT * KB
-    head_u, head_h, head_l, left_over = call(
-        chain_head_kernel,
-        (
-            shaped((heads, NB, NB)),
-            shaped((heads, NB, NB), BF16),
-            shaped((heads, NB, NB), BF16),
-            shaped((REST * REST, NB, NB)),
-        ),
-        [SM, VM],
-        [pltpu.VMEM((KB * KB, NB, NB), F32)] + scratch,
-        32,
-    )(meta, lead_parts)
-
-    left_over, pairs, routed = lax.optimization_barrier((left_over, pairs, routed))
     right_parts = lax.all_to_all(pairs, "prow", 0, 0, tiled=True).reshape(16, KB, 3, 32, LANES)
     middle = lax.ppermute(routed, "pcol", [(q, (3 * q + 1) % 16) for q in range(1, 16)])
-    tails = REST * REST
-    tail_u, tail_h, tail_l = call(
-        chain_tail_kernel,
-        (shaped((tails, NB, NB)), shaped((tails, NB, NB), BF16), shaped((tails, NB, NB), BF16)),
-        [VM],
-        [pltpu.VMEM((tails, NB, NB), F32)] + scratch,
-        40,
-    )(left_over)
-
-    middle, tail_h = lax.optimization_barrier((middle, tail_h))
+
+    lead_parts, _, _ = lax.optimization_barrier((lead_parts, pairs, routed))
+    upper, th, tl = pl.pallas_call(
+        chain_kernel,
+        out_shape=(shaped((TRI, NB, NB)), shaped((TRI, NB, NB), BF16), shaped((TRI, NB, NB), BF16)),
+        in_specs=[SM, pl.BlockSpec(memory_space=pl.ANY)],
+        out_specs=(VM, VM, VM),
+        scratch_shapes=[
+            pltpu.VMEM((KB * KB, NB, NB), F32),
+            pltpu.VMEM((NB, NB), F32),
+            pltpu.VMEM((HB, HB), F32),
+            pltpu.VMEM((HB, HB), F32),
+            pltpu.VMEM((HB, HB), F32),
+            pltpu.VMEM((TRI + 6, 16, 32, LANES), F32),
+            pltpu.SemaphoreType.DMA((TRI + 6,)),
+        ],
+        compiler_params=pltpu.CompilerParams(vmem_limit_bytes=VMEM_LIMIT),
+        cost_estimate=cost(66),
+    )(meta, lead_parts)
+
+    middle, th = lax.optimization_barrier((middle, th))
     below = lax.ppermute(middle, "pcol", [(q, (q + 1) % 16) for q in range(16)])
     above = lax.ppermute(middle, "pcol", [(q, (q + 15) % 16) for q in range(16)])
 
     rh, rl = call(
         right_kernel,
         (shaped((768, 1280), BF16), shaped((768, 1280), BF16)),
-        [VM] * 5,
+        [VM] * 3,
         [pltpu.VMEM((768, 1280), F32)],
         12,
-    )(right_parts, head_h, head_l, tail_h, tail_l)
+    )(right_parts, th, tl)
 
     rows = NB * ROWS_STEP
     steps = 6 // ROWS_STEP
-    whole_head = pl.BlockSpec((heads, NB, NB), lambda g: (0, 0, 0))
-    whole_tail = pl.BlockSpec((tails, NB, NB), lambda g: (0, 0, 0))
+    whole_tri = pl.BlockSpec((TRI, NB, NB), lambda g: (0, 0, 0))
     by_rows = pl.BlockSpec((rows, 1280), lambda g: (g, 0))
     own_rows = pl.BlockSpec((rows, NB), lambda g: (g, 0))
     yh, yl, own = pl.pallas_call(
@@ -544,16 +469,14 @@
         in_specs=[
             SM,
             pl.BlockSpec((16, KB, ROWS_STEP, 32, LANES), lambda g: (0, 0, g, 0, 0)),
-            whole_head,
-            whole_head,
-            whole_tail,
-            whole_tail,
+            whole_tri,
+            whole_tri,
         ],
         out_specs=(by_rows, by_rows, own_rows),
         scratch_shapes=[pltpu.VMEM((rows, 1280), F32)],
         compiler_params=pltpu.CompilerParams(vmem_limit_bytes=VMEM_LIMIT),
         cost_estimate=cost(20),
-    )(meta, left_parts, head_h, head_l, tail_h, tail_l)
+    )(meta, left_parts, th, tl)
 
     whole_right = pl.BlockSpec((768, 1280), lambda g: (0, 0))
     whole_child = pl.BlockSpec((6, 512, LANES), lambda g: (0, 0, 0))
@@ -562,7 +485,7 @@
         schur_kernel,
         grid=(steps,),
         out_shape=shaped((9216, LANES)),
-        in_specs=[SM, by_rows, by_rows, own_rows, whole_right, whole_right, whole_head, whole_tail, front_rows]
+        in_specs=[SM, by_rows, by_rows, own_rows, whole_right, whole_right, whole_tri, front_rows]
         + [whole_child] * 3,
         out_specs=front_rows,
         compiler_params=pltpu.CompilerParams(vmem_limit_bytes=VMEM_LIMIT),
@@ -574,8 +497,7 @@
         own,
         rh,
         rl,
-        head_u,
-        tail_u,
+        upper,
         parent.reshape(9216, LANES),
         *(x.reshape(6, 512, LANES) for x in (above, middle, below)),
     )

time: 295 us -> 343 us (1.16)
  waiting for transfers between devices: 35.6 us -> 101 us
  blocking collectives: 53.6 us -> 34.9 us
  Pallas kernels: 133 us -> 123 us
  starting transfers between devices: 43 us -> 52.6 us
  local copies, waits for them, and re-layouts: 10.3 us -> 14.3 us
    all_gather x1, waiting for transfers between devices: 0.01 us -> 51.3 us  [per_device(): left_parts = lax.all_gather(slices, 'pcol')]
    all_gather x1 -> x0, blocking collectives: 26.4 us -> none  [per_device(): chunk = lax.all_gather(chunk, 'pcol')]
    all_to_all x1, waiting for transfers between devices: 0.01 us -> 20.8 us  [per_device(): got = lax.all_to_all(picked, 'prow', 0, 0, tiled=True)]
    all_to_all x1, starting transfers between devices: 5.97 us -> 18.9 us  [per_device(): lax.all_to_all(pairs, 'prow', 0, 0, tiled=True)]
    ppermute x1, waiting for transfers between devices: 0.01 us -> 12.7 us  [per_device(): lax.ppermute(jnp.where(is_even, even, odd), ('prow', 'pcol'), perm_a)]
    ppermute x1, waiting for transfers between devices: 11.1 us -> 0.01 us  [per_device(): lax.ppermute(routed, 'pcol', [(q, (3 * q + 1) % 16) for q in range(1, 16)])]
    pallas_call x3 -> x1, Pallas kernels: 71.9 us -> 63.1 us  [per_device(): pl.pallas_call(chain_kernel, out_shape=(shaped((TRI, NB, NB)), shaped((TR...]
    all_to_all x1, blocking collectives: 27.2 us -> 34.9 us  [per_device(): rest = lax.all_to_all(rest, 'pcol', 0, 0, tiled=True)]
  transfers between devices with their start and end apart: 13 -> 11, of which waited for: 6 -> 6; matrix products, arithmetic and copies ran while one was open for 2% -> 3% of each run, Pallas kernels for 38% -> 30%
where the time goes in v4:
time: 343 us; the launch traced here: 342 us
  Pallas kernels  123 us (36%)
  waiting for transfers between devices  101 us (29%)
  starting transfers between devices  52.6 us (15%)
  blocking collectives  34.9 us (10%)
  local copies, waits for them, and re-layouts  14.3 us (4%)
  between operations  13.6 us (4%)
    pallas_call x1, Pallas kernels, per_device(): pl.pallas_call(chain_kernel, out_shape=(shaped((TRI, NB, NB)), shaped((TR...  63.1 us
    all_gather x1, waiting for transfers between devices, per_device(): left_parts = lax.all_gather(slices, 'pcol')  51.3 us
    all_to_all x1, blocking collectives, per_device(): rest = lax.all_to_all(rest, 'pcol', 0, 0, tiled=True)  34.9 us
    all_to_all x1, waiting for transfers between devices, per_device(): got = lax.all_to_all(picked, 'prow', 0, 0, tiled=True)  20.8 us
    pallas_call x1, Pallas kernels, per_device(): pl.pallas_call(schur_kernel, grid=(steps,), out_shape=shaped((9216, LANES...  20.7 us
    all_to_all x1, starting transfers between devices, per_device(): lax.all_to_all(pairs, 'prow', 0, 0, tiled=True)  18.9 us
    pallas_call x1, Pallas kernels, per_device(): pl.pallas_call(left_kernel, grid=(steps,), out_shape=(shaped((1536, 1280)...  17.8 us
    ppermute x1, waiting for transfers between devices, per_device(): lax.ppermute(jnp.where(is_even, even, odd), ('prow', 'pcol'), perm_a)  12.7 us
  transfers between devices with their start and end apart: 11, of which 6 were waited for; matrix products, arithmetic and copies ran while one was open for 3% of the time, Pallas kernels for 30%

profile of v4, /device:TPU:102, one launch (start us, length us, event | category | flops | bytes accessed | tf_op | source)
XLA Modules:
  0.0 342.2 jit_solution(17887394214332775667)
XLA Ops:
  6.5 0.0 copy-start.6
  6.5 1.0 slice.50
  7.5 1.1 slice.41
  8.7 0.9 pad_maximum_fusion.1
  9.5 6.9 %all-to-all-start = ((f32[16,2,32,128]{3,2,1,0:T(8,128)}), f32[16,2,32,128]{3,2,1,0:T(8,128)S(1)}, u32[]{:S(2)}, u32[]{:S(2)}) async-start(f32[16,2,32,128]{3,2,1,0:T(8,128)} %pad_maximum_fusion.1), calls=%async_computation | async-start | bytes 1048576 | tf_op jit(solution)/shard_map/all_to_all | solution.py:388
  16.4 0.0 all-gather.7.cloned.1.call-start
  16.5 0.0 copy-done.6
  16.5 0.1 reshape.27
  16.6 0.6 pad_add_fusion.meta
  17.2 6.0 %shard_map.37 = f32[8,512,128]{2,1,0:T(8,128)} custom-call(s32[34]{0:T(128)} %pad_add_fusion.meta, f32[4,512,128]{2,1,0:T(8,128)} %bitcast.32), custom_call_target="tpu_custom_call" | custom-call | flops 3300000000 | bytes 1048576 | tf_op jit(solution)/shard_map/pallas_call | solution.py:375
  23.1 0.0 copy-start.1
  23.1 0.7 all-to-all-done
  23.9 0.7 pad_maximum_fusion.3
  24.5 0.0 all-gather.7.cloned.1.call-update
  24.6 1.4 slice.49
  26.0 0.0 copy-done.1
  26.0 0.2 copy_bitcast_fusion
  26.2 34.9 %all_to_all.25 = f32[16,9,32,128]{3,2,1,0:T(8,128)S(1)} all-to-all(f32[16,9,32,128]{3,2,1,0:T(8,128)S(1)} %copy_bitcast_fusion), channel_id=1, replica_groups=mesh['prow'=8,'pcol'=16] {'pcol'}, dimensions={0} | all-to-all | bytes 4718592 | tf_op jit(solution)/shard_map/all_to_all | solution.py:395
  61.1 0.7 slice.54.parts_ref
  61.8 0.0 copy-start.2
  61.8 1.8 shard_map.38
  63.5 4.5 %all-to-all-start.2 = ((f32[8,2,32,128]{3,2,1,0:T(8,128)}), f32[8,2,32,128]{3,2,1,0:T(8,128)S(1)}, u32[]{:S(2)}, u32[]{:S(2)}) async-start(f32[8,2,32,128]{3,2,1,0:T(8,128)} %shard_map.38), calls=%async_computation.2 | async-start | bytes 524288 | tf_op jit(solution)/shard_map/all_to_all | solution.py:397
  68.0 0.0 all-gather.5.cloned.1.call-start
  68.0 0.0 copy-done.2
  68.0 0.6 slice.44.first_ref
  68.7 0.8 slice.53.rest_ref
  69.5 8.4 %all-to-all-done.2.got_ref = f32[8,2,32,128]{3,2,1,0:T(8,128)S(1)} async-done(((f32[8,2,32,128]{3,2,1,0:T(8,128)}), f32[8,2,32,128]{3,2,1,0:T(8,128)S(1)}, u32[]{:S(2)}, u32[]{:S(2)}) %all-to-all-start.2) | async-done | bytes 262176 | tf_op jit(solution)/shard_map/all_to_all | solution.py:397
  77.9 0.0 copy-start.3
  77.9 0.7 copy-done.3
  78.5 2.3 shard_map.39
  80.8 0.0 all-gather.5.cloned.1.call-update
  80.8 0.0 copy-start
  80.8 3.7 %all-to-all-start.3 = ((f32[8,512,128]{2,1,0:T(8,128)}), f32[8,512,128]{2,1,0:T(8,128)S(1)}, u32[]{:S(2)}, u32[]{:S(2)}) async-start(f32[8,512,128]{2,1,0:T(8,128)} %shard_map.37), calls=%async_computation.3 | async-start | bytes 4194304 | tf_op jit(solution)/shard_map/all_to_all | solution.py:405
  84.6 0.0 copy-done
  84.7 6.5 %collective-permute-start.1 = (f32[5,3,32,128]{3,2,1,0:T(8,128)S(1)}, f32[5,3,32,128]{3,2,1,0:T(8,128)S(1)}, u32[]{:S(2)}, u32[]{:S(2)}) collective-permute-start(f32[5,3,32,128]{3,2,1,0:T(8,128)S(1)} %get-tuple-element.41), channel_id=1, source_target_pairs={{0,0},{1,8},{2,16},{3,24},{4,32},{5,40},{6,48},{7,56},{8,64},{9,72... | collective-permute-start | bytes 737288 | tf_op jit(solution)/shard_map/ppermute | solution.py:420
  91.2 1.7 collective-permute-start.2
  92.9 12.7 %collective-permute-done.1 = f32[5,3,32,128]{3,2,1,0:T(8,128)S(1)} collective-permute-done((f32[5,3,32,128]{3,2,1,0:T(8,128)S(1)}, f32[5,3,32,128]{3,2,1,0:T(8,128)S(1)}, u32[]{:S(2)}, u32[]{:S(2)}) %collective-permute-start.1) | collective-permute-done | bytes 245792 | tf_op jit(solution)/shard_map/ppermute | solution.py:420
  105.6 7.4 %collective-permute-done.2 = f32[5,3,32,128]{3,2,1,0:T(8,128)S(1)} collective-permute-done((f32[5,3,32,128]{3,2,1,0:T(8,128)S(1)}, f32[5,3,32,128]{3,2,1,0:T(8,128)S(1)}, u32[]{:S(2)}, u32[]{:S(2)}) %collective-permute-start.2) | collective-permute-done | bytes 245792 | tf_op jit(solution)/shard_map/ppermute | solution.py:421
  113.1 20.8 %all-to-all-done.3 = f32[8,512,128]{2,1,0:T(8,128)S(1)} async-done(((f32[8,512,128]{2,1,0:T(8,128)}), f32[8,512,128]{2,1,0:T(8,128)S(1)}, u32[]{:S(2)}, u32[]{:S(2)}) %all-to-all-start.3) | async-done | bytes 2097184 | tf_op jit(solution)/shard_map/all_to_all | solution.py:405
  133.9 2.4 broadcast_in_dim.2
  136.3 18.9 %all-to-all-start.4 = ((f32[8,2,5,3,32,128]{5,4,3,2,1,0:T(8,128)}), f32[8,2,5,3,32,128]{5,4,3,2,1,0:T(8,128)}, u32[]{:S(2)}, u32[]{:S(2)}) async-start(f32[8,2,5,3,32,128]{5,4,3,2,1,0:T(8,128)} %broadcast_in_dim.2), calls=%async_computation.4 | async-start | bytes 7864320 | tf_op jit(solution)/shard_map/all_to_all | solution.py:426
  155.2 0.7 dynamic-slice_dynamic-update-slice_fusion.5
  155.9 0.7 dynamic-slice_dynamic-update-slice_fusion.4
  156.6 0.7 dynamic-slice_dynamic-update-slice_fusion.3
  157.4 0.7 dynamic-slice_dynamic-update-slice_fusion.2
  158.1 0.7 dynamic-slice_dynamic-update-slice_fusion.1
  158.8 0.7 dynamic-slice_dynamic-update-slice_fusion
  159.5 4.9 %collective-permute-start = (f32[6,512,128]{2,1,0:T(8,128)}, f32[6,512,128]{2,1,0:T(8,128)S(1)}, u32[]{:S(2)}, u32[]{:S(2)}) collective-permute-start(f32[6,512,128]{2,1,0:T(8,128)} %dynamic-slice_dynamic-update-slice_fusion), channel_id=1, source_target_pairs={{1,4},{2,7},{3,10},{4,13},{5,0},{6,3},{7,6},{8,9},{9,12},{10,15},{... | collective-permute-start | bytes 4718600 | tf_op jit(solution)/shard_map/ppermute | solution.py:427
  164.4 0.0 all-gather.7.cloned.1.call-done
  164.5 63.1 %shard_map.40 = (f32[15,256,256]{2,1,0:T(8,128)}, bf16[15,256,256]{2,1,0:T(8,128)(2,1)}, bf16[15,256,256]{2,1,0:T(8,128)(2,1)}) custom-call(s32[34]{0:T(128)} %pad_add_fusion.meta, f32[8,16,7,32,128]{4,3,2,1,0:T(8,128)} %bitcast.39), custom_call_target="tpu_custom_call" | custom-call | flops 72600002560 | bytes 1048576 | tf_op jit(solution)/shard_map/pallas_call | solution.py:430
  227.6 0.0 collective-permute-done.child_1
  227.6 0.0 copy-start.4
  227.6 0.2 collective-permute-start.3
  227.9 5.2 %collective-permute-start.4 = (f32[6,512,128]{2,1,0:T(8,128)S(1)}, f32[6,512,128]{2,1,0:T(8,128)}, u32[]{:S(2)}, u32[]{:S(2)}) collective-permute-start(f32[6,512,128]{2,1,0:T(8,128)S(1)} %collective-permute-done.child_1), channel_id=1, source_target_pairs={{0,1},{1,2},{2,3},{3,4},{4,5},{5,6},{6,7},{7,8},{8,9},{9,10},{10,1... | collective-permute-start | bytes 4718600 | tf_op jit(solution)/shard_map/ppermute | solution.py:449
  233.1 51.3 %all-gather.5.cloned.1.call-done = f32[80,6,32,128]{3,2,1,0:T(8,128)} async-done(((f32[5,6,32,128]{3,2,1,0:T(8,128)}), f32[80,6,32,128]{3,2,1,0:T(8,128)}) %all-gather.5.cloned.1.call-update) | async-done | bytes 7864336 | tf_op jit(solution)/shard_map/all_gather | solution.py:402
  284.4 17.8 %shard_map.41 = (bf16[1536,1280]{1,0:T(8,128)(2,1)}, bf16[1536,1280]{1,0:T(8,128)(2,1)}, f32[1536,256]{1,0:T(8,128)}) custom-call(s32[34]{0:T(128)} %pad_add_fusion.meta, f32[16,5,6,32,128]{4,3,2,1,0:T(8,128)} %bitcast.40, bf16[15,256,256]{2,1,0:T(8,128)(2,1)} %get-tuple-element.30.th_ref, bf16[15,256,256]{2,1,0:T(8,128)(2,1)} %get-tuple-element.31.tl_ref), custom_call_target="tpu_custom_call" | custom-call | flops 22000001024 | bytes 1048576 | tf_op jit(solution)/shard_map/pallas_call | solution.py:465
  302.1 0.0 copy-done.4
  302.1 0.0 all-to-all-done.4
  302.1 11.4 %shard_map.42 = (bf16[768,1280]{1,0:T(8,128)(2,1)}, bf16[768,1280]{1,0:T(8,128)(2,1)}) custom-call(f32[16,5,3,32,128]{4,3,2,1,0:T(8,128)} %bitcast.15.parts_ref, bf16[15,256,256]{2,1,0:T(8,128)(2,1)} %get-tuple-element.30.th_ref, bf16[15,256,256]{2,1,0:T(8,128)(2,1)} %get-tuple-element.31.tl_ref), custom_call_target="tpu_custom_call" | custom-call | flops 13200000000 | bytes 1048576 | tf_op jit(solution)/shard_map/pallas_call | solution.py:452
  313.5 0.0 collective-permute-done.3.child_0
  313.5 0.0 copy-start.5
  313.5 0.0 collective-permute-done.4.child_2
  313.5 1.1 copy-done.5
  314.7 20.7 %shard_map.43 = f32[9216,128]{1,0:T(8,128)} custom-call(s32[34]{0:T(128)} %pad_add_fusion.meta, bf16[1536,1280]{1,0:T(8,128)(2,1)} %get-tuple-element.32.yh, bf16[1536,1280]{1,0:T(8,128)(2,1)} %get-tuple-element.33.yl, f32[1536,256]{1,0:T(8,128)} %get-tuple-element.34.own_ref, bf16[768,1280]{1,0:T(8,128)(2,1)} %get-tuple-element.35.rh_ref, ...), custom_call_target="tpu_custom_call" | custom-call | flops 19800000512 | bytes 1048576 | tf_op jit(solution)/shard_map/pallas_call | solution.py:484
  (5 shorter events, 0.1 us)
Async XLA Ops:
  6.5 9.9 %copy-start.6 = (s32[2,16]{1,0:T(2,128)S(1)}, s32[2,16]{1,0:T(2,128)}, u32[]{:S(2)}) copy-start(s32[2,16]{1,0:T(2,128)} %param.5) | copy-start | bytes 388
  9.5 14.4 %all-to-all-start = ((f32[16,2,32,128]{3,2,1,0:T(8,128)}), f32[16,2,32,128]{3,2,1,0:T(8,128)S(1)}, u32[]{:S(2)}, u32[]{:S(2)}) async-start(f32[16,2,32,128]{3,2,1,0:T(8,128)} %pad_maximum_fusion.1), calls=%async_computation | async-start | bytes 1048576 | tf_op jit(solution)/shard_map/all_to_all | solution.py:388
  16.4 148.0 %all-gather.7.cloned.1.call-start = ((), (), s32[]{:S(2)}) async-start(), calls=%async_computation.6 | async-start | bytes 14794752 | tf_op jit(solution)/shard_map/all_gather | solution.py:391
  23.1 2.8 copy-start.1
  61.8 6.3 %copy-start.2 = (f32[7,32,128]{2,1,0:T(8,128)S(1)}, f32[7,32,128]{2,1,0:T(8,128)}, u32[]{:S(2)}) copy-start(f32[7,32,128]{2,1,0:T(8,128)} %pad_maximum_fusion.3) | copy-start | bytes 344068
  63.5 14.3 %all-to-all-start.2 = ((f32[8,2,32,128]{3,2,1,0:T(8,128)}), f32[8,2,32,128]{3,2,1,0:T(8,128)S(1)}, u32[]{:S(2)}, u32[]{:S(2)}) async-start(f32[8,2,32,128]{3,2,1,0:T(8,128)} %shard_map.38), calls=%async_computation.2 | async-start | bytes 524288 | tf_op jit(solution)/shard_map/all_to_all | solution.py:397
  68.0 216.4 %all-gather.5.cloned.1.call-start = ((), (), s32[]{:S(2)}) async-start(), calls=%async_computation.5 | async-start | bytes 8355840 | tf_op jit(solution)/shard_map/all_gather | solution.py:402
  77.9 0.7 copy-start.3
  80.8 3.8 %copy-start = (f32[5,6,32,128]{3,2,1,0:T(8,128)S(1)}, f32[5,6,32,128]{3,2,1,0:T(8,128)}, u32[]{:S(2)}) copy-start(f32[5,6,32,128]{3,2,1,0:T(8,128)} %shard_map.39) | copy-start | bytes 1474564
  80.8 53.1 %all-to-all-start.3 = ((f32[8,512,128]{2,1,0:T(8,128)}), f32[8,512,128]{2,1,0:T(8,128)S(1)}, u32[]{:S(2)}, u32[]{:S(2)}) async-start(f32[8,512,128]{2,1,0:T(8,128)} %shard_map.37), calls=%async_computation.3 | async-start | bytes 4194304 | tf_op jit(solution)/shard_map/all_to_all | solution.py:405
  84.7 21.0 %collective-permute-start.1 = (f32[5,3,32,128]{3,2,1,0:T(8,128)S(1)}, f32[5,3,32,128]{3,2,1,0:T(8,128)S(1)}, u32[]{:S(2)}, u32[]{:S(2)}) collective-permute-start(f32[5,3,32,128]{3,2,1,0:T(8,128)S(1)} %get-tuple-element.41), channel_id=1, source_target_pairs={{0,0},{1,8},{2,16},{3,24},{4,32},{5,40},{6,48},{7,56},{8,64},{9,72... | collective-permute-start | bytes 737288 | tf_op jit(solution)/shard_map/ppermute | solution.py:420
  91.2 21.9 %collective-permute-start.2 = (f32[5,3,32,128]{3,2,1,0:T(8,128)S(1)}, f32[5,3,32,128]{3,2,1,0:T(8,128)S(1)}, u32[]{:S(2)}, u32[]{:S(2)}) collective-permute-start(f32[5,3,32,128]{3,2,1,0:T(8,128)S(1)} %get-tuple-element.42), channel_id=1, source_target_pairs={{0,8},{1,0},{2,24},{3,16},{4,40},{5,32},{6,56},{7,48},{8,72},{9,64... | collective-permute-start | bytes 737288 | tf_op jit(solution)/shard_map/ppermute | solution.py:421
  136.3 165.8 %all-to-all-start.4 = ((f32[8,2,5,3,32,128]{5,4,3,2,1,0:T(8,128)}), f32[8,2,5,3,32,128]{5,4,3,2,1,0:T(8,128)}, u32[]{:S(2)}, u32[]{:S(2)}) async-start(f32[8,2,5,3,32,128]{5,4,3,2,1,0:T(8,128)} %broadcast_in_dim.2), calls=%async_computation.4 | async-start | bytes 7864320 | tf_op jit(solution)/shard_map/all_to_all | solution.py:426
  159.5 68.1 %collective-permute-start = (f32[6,512,128]{2,1,0:T(8,128)}, f32[6,512,128]{2,1,0:T(8,128)S(1)}, u32[]{:S(2)}, u32[]{:S(2)}) collective-permute-start(f32[6,512,128]{2,1,0:T(8,128)} %dynamic-slice_dynamic-update-slice_fusion), channel_id=1, source_target_pairs={{1,4},{2,7},{3,10},{4,13},{5,0},{6,3},{7,6},{8,9},{9,12},{10,15},{... | collective-permute-start | bytes 4718600 | tf_op jit(solution)/shard_map/ppermute | solution.py:427
  227.6 74.5 %copy-start.4 = (f32[6,512,128]{2,1,0:T(8,128)}, f32[6,512,128]{2,1,0:T(8,128)S(1)}, u32[]{:S(2)}) copy-start(f32[6,512,128]{2,1,0:T(8,128)S(1)} %collective-permute-done.child_1) | copy-start | bytes 4718596
  227.6 85.9 %collective-permute-start.3 = (f32[6,512,128]{2,1,0:T(8,128)S(1)}, f32[6,512,128]{2,1,0:T(8,128)S(1)}, u32[]{:S(2)}, u32[]{:S(2)}) collective-permute-start(f32[6,512,128]{2,1,0:T(8,128)S(1)} %collective-permute-done.child_1), channel_id=1, source_target_pairs={{0,15},{1,0},{2,1},{3,2},{4,3},{5,4},{6,5},{7,6},{8,7},{9,8},{10,9... | collective-permute-start | bytes 4718600 | tf_op jit(solution)/shard_map/ppermute | solution.py:450
  227.9 85.7 %collective-permute-start.4 = (f32[6,512,128]{2,1,0:T(8,128)S(1)}, f32[6,512,128]{2,1,0:T(8,128)}, u32[]{:S(2)}, u32[]{:S(2)}) collective-permute-start(f32[6,512,128]{2,1,0:T(8,128)S(1)} %collective-permute-done.child_1), channel_id=1, source_target_pairs={{0,1},{1,2},{2,3},{3,4},{4,5},{5,6},{6,7},{7,8},{8,9},{9,10},{10,1... | collective-permute-start | bytes 4718600 | tf_op jit(solution)/shard_map/ppermute | solution.py:449
  313.5 1.1 copy-start.5
Sparse Core Ops, SparseCore 0:
  24.7 122.3 all-gather.6
  149.2 135.1 all-gather.4

commit v5 on v3

--- a/solution.py
+++ b/solution.py
@@ -114,6 +114,18 @@
 
 def exact(a, b, dims):
     return lax.dot_general(a, b, (dims, ((), ())), precision=lax.Precision.HIGHEST, preferred_element_type=F32)
+
+
+def dot3(ah, al, bh, bl, dims):
+    def dot(a, b):
+        return lax.dot_general(a, b, (dims, ((), ())), preferred_element_type=F32)
+
+    return dot(ah, bh) + (dot(ah, bl) + dot(al, bh))
+
+
+NN = ((1,), (0,))
+NT = ((1,), (1,))
+TN = ((0,), (0,))
 
 
 def factor_128(a_ref, x_ref, u_ref):
@@ -175,12 +187,21 @@
 REST = KB - CUT
 
 
+def packed(n, k, i):
+    return k * (2 * n + 1 - k) // 2 + i - k
+
+
+HEADS = packed(KB, CUT, CUT)
+TAILS = packed(REST, REST, REST)
+
+
 def eliminate(n, steps, f_ref, u_ref, th_ref, tl_ref, v_ref, a_s, x_s, u_s):
     @pl.loop(0, 2 * steps)
     def _(step):
         k = step // 2
         half = step % 2
         kk = k * n + k
+        pk = packed(n, k, k)
 
         @pl.when(half == 0)
         def _():
@@ -188,42 +209,49 @@
 
         @pl.when(half == 1)
         def _():
-            u12 = exact(v_ref[0:HB, 0:HB], f_ref[kk, 0:HB, HB:NB], ((1,), (0,)))
-            u_ref[kk, 0:HB, HB:NB] = u12
-            a_s[...] = f_ref[kk, HB:NB, HB:NB] - exact(u12, u12, ((0,), (0,)))
+            u12 = exact(v_ref[0:HB, 0:HB], f_ref[kk, 0:HB, HB:NB], NN)
+            u_ref[pk, 0:HB, HB:NB] = u12
+            a_s[...] = f_ref[kk, HB:NB, HB:NB] - exact(u12, u12, TN)
 
         factor_128(a_s, x_s, u_s)
 
         @pl.when(half == 0)
         def _():
-            u_ref[kk, 0:HB, 0:HB] = u_s[...]
+            u_ref[pk, 0:HB, 0:HB] = u_s[...]
             v_ref[0:HB, 0:HB] = x_s[...]
 
         @pl.when(half == 1)
         def _():
-            u_ref[kk, HB:NB, HB:NB] = u_s[...]
-            u_ref[kk, HB:NB, 0:HB] = jnp.zeros((HB, HB), F32)
+            u_ref[pk, HB:NB, HB:NB] = u_s[...]
+            u_ref[pk, HB:NB, 0:HB] = jnp.zeros((HB, HB), F32)
             v_ref[HB:NB, HB:NB] = x_s[...]
             v_ref[0:HB, HB:NB] = jnp.zeros((HB, HB), F32)
-            lx = exact(u_ref[kk, 0:HB, HB:NB], v_ref[0:HB, 0:HB], ((0,), (0,)))
-            v_ref[HB:NB, 0:HB] = -exact(x_s[...], lx, ((1,), (0,)))
+            lx = exact(u_ref[pk, 0:HB, HB:NB], v_ref[0:HB, 0:HB], TN)
+            v_ref[HB:NB, 0:HB] = -exact(x_s[...], lx, NN)
             high, low = split(v_ref[...].T)
-            th_ref[kk] = high
-            tl_ref[kk] = low
+            th_ref[pk] = high
+            tl_ref[pk] = low
+            vh, vl = split(v_ref[...])
 
             @pl.loop(k + 1, n)
             def _(i):
-                u = exact(v_ref[...], f_ref[k * n + i], ((1,), (0,)))
-                u_ref[k * n + i] = u
+                u = dot3(vh, vl, *split(f_ref[k * n + i]), NN)
+                at = packed(n, k, i)
+                u_ref[at] = u
                 high, low = split(u)
-                th_ref[k * n + i] = high
-                tl_ref[k * n + i] = low
+                th_ref[at] = high
+                tl_ref[at] = low
 
             @pl.loop(k + 1, n)
             def _(i):
+                at_i = packed(n, k, i)
+
                 @pl.loop(i, n)
                 def _(j):
-                    f_ref[i * n + j] = f_ref[i * n + j] - exact(u_ref[k * n + i], u_ref[k * n + j], ((0,), (0,)))
+                    at_j = packed(n, k, j)
+                    f_ref[i * n + j] = f_ref[i * n + j] - dot3(
+                        th_ref[at_i], tl_ref[at_i], th_ref[at_j], tl_ref[at_j], TN
+                    )
 
 
 def chain_head_kernel(meta, parts_ref, u_ref, th_ref, tl_ref, rest_ref, f_ref, *scratch):
@@ -245,35 +273,17 @@
                     place = (k * KB + i, slice(16 * s, 16 * s + 16), slice(HB * h, HB * h + HB))
                     f_ref[place] = f_ref[place] + take(at, s, h)
 
-    for ref in (th_ref, tl_ref, u_ref):
-        ref[KB] = jnp.zeros((NB, NB), ref.dtype)
     eliminate(KB, CUT, f_ref, u_ref, th_ref, tl_ref, *scratch)
     for i in range(REST):
-        for j in range(REST):
-            if j >= i:
-                rest_ref[i * REST + j] = f_ref[(CUT + i) * KB + CUT + j]
-            else:
-                rest_ref[i * REST + j] = jnp.zeros((NB, NB), F32)
+        for j in range(i, REST):
+            rest_ref[packed(REST, i, j)] = f_ref[(CUT + i) * KB + CUT + j]
 
 
 def chain_tail_kernel(rest_ref, u_ref, th_ref, tl_ref, f_ref, *scratch):
-    f_ref[...] = rest_ref[...]
     for i in range(REST):
-        for j in range(i):
-            for ref in (th_ref, tl_ref, u_ref):
-                ref[i * REST + j] = jnp.zeros((NB, NB), ref.dtype)
+        for j in range(i, REST):
+            f_ref[i * REST + j] = rest_ref[packed(REST, i, j)]
     eliminate(REST, REST, f_ref, u_ref, th_ref, tl_ref, *scratch)
-
-
-def dot3(ah, al, bh, bl, dims):
-    def dot(a, b):
-        return lax.dot_general(a, b, (dims, ((), ())), preferred_element_type=F32)
-
-    return dot(ah, bh) + (dot(ah, bl) + dot(al, bh))
-
-
-NN = ((1,), (0,))
-NT = ((1,), (1,))
 
 
 def solve_rows(raw_ref, yh_ref, yl_ref, factors):
@@ -281,8 +291,8 @@
 
     def factor(m, k):
         if m < CUT:
-            return head_h[m * KB + k], head_l[m * KB + k]
-        at = (m - CUT) * REST + k - CUT
+            return head_h[packed(KB, m, k)], head_l[packed(KB, m, k)]
+        at = packed(REST, m - CUT, k - CUT)
         return tail_h[at], tail_l[at]
 
     for k in range(KB):
@@ -392,14 +402,14 @@
 
                 @pl.when(jnp.logical_and(lower, block_col < CUT))
                 def _():
-                    block = head_ref[jnp.minimum(block_col, CUT - 1) * KB + jnp.minimum(block_row, KB - 1)].T
+                    block = head_ref[jnp.clip(packed(KB, block_col, block_row), 0, HEADS - 1)].T
                     for h in range(2):
                         put(h, block[:, HB * h : HB * h + HB])
 
                 @pl.when(jnp.logical_and(lower, block_col >= CUT))
                 def _():
-                    at_col = jnp.clip(block_col - CUT, 0, REST - 1)
-                    block = tail_ref[at_col * REST + jnp.clip(block_row - CUT, 0, REST - 1)].T
+                    at = jnp.clip(packed(REST, block_col - CUT, block_row - CUT), 0, TAILS - 1)
+                    block = tail_ref[at].T
                     for h in range(2):
                         put(h, block[:, HB * h : HB * h + HB])
 
@@ -447,6 +457,7 @@
     first = jnp.stack([lead[0], child[0]], axis=1)
     first = lax.all_to_all(first, "pcol", 0, 0, tiled=True)
     mine = jnp.concatenate([first[0:KB, 0], first[0:2, 1]], axis=0)
+    mine, picked = lax.optimization_barrier((mine, picked))
     shed = jnp.where(row == 0, mine[2:5], mine[3:6])
     got_a = lax.ppermute(shed, "prow", [(0, 6), (1, 5)])
     got_b = lax.ppermute(mine[1:2], "prow", [(0, 7)])
@@ -493,14 +504,13 @@
         pltpu.VMEM((HB, HB), F32),
         pltpu.VMEM((HB, HB), F32),
     ]
-    heads = CUT * KB
     head_u, head_h, head_l, left_over = call(
         chain_head_kernel,
         (
-            shaped((heads, NB, NB)),
-            shaped((heads, NB, NB), BF16),
-            shaped((heads, NB, NB), BF16),
-            shaped((REST * REST, NB, NB)),
+            shaped((HEADS, NB, NB)),
+            shaped((HEADS, NB, NB), BF16),
+            shaped((HEADS, NB, NB), BF16),
+            shaped((TAILS, NB, NB)),
         ),
         [SM, VM],
         [pltpu.VMEM((KB * KB, NB, NB), F32)] + scratch,
@@ -508,14 +518,13 @@
     )(meta, lead_parts)
 
     left_over, pairs, routed = lax.optimization_barrier((left_over, pairs, routed))
+    middle = lax.ppermute(routed, "pcol", [(q, (3 * q + 1) % 16) for q in range(1, 16)])
     right_parts = lax.all_to_all(pairs, "prow", 0, 0, tiled=True).reshape(16, KB, 3, 32, LANES)
-    middle = lax.ppermute(routed, "pcol", [(q, (3 * q + 1) % 16) for q in range(1, 16)])
-    tails = REST * REST
     tail_u, tail_h, tail_l = call(
         chain_tail_kernel,
-        (shaped((tails, NB, NB)), shaped((tails, NB, NB), BF16), shaped((tails, NB, NB), BF16)),
+        (shaped((TAILS, NB, NB)), shaped((TAILS, NB, NB), BF16), shaped((TAILS, NB, NB), BF16)),
         [VM],
-        [pltpu.VMEM((tails, NB, NB), F32)] + scratch,
+        [pltpu.VMEM((REST * REST, NB, NB), F32)] + scratch,
         40,
     )(left_over)
 
@@ -533,8 +542,8 @@
 
     rows = NB * ROWS_STEP
     steps = 6 // ROWS_STEP
-    whole_head = pl.BlockSpec((heads, NB, NB), lambda g: (0, 0, 0))
-    whole_tail = pl.BlockSpec((tails, NB, NB), lambda g: (0, 0, 0))
+    whole_head = pl.BlockSpec((HEADS, NB, NB), lambda g: (0, 0, 0))
+    whole_tail = pl.BlockSpec((TAILS, NB, NB), lambda g: (0, 0, 0))
     by_rows = pl.BlockSpec((rows, 1280), lambda g: (g, 0))
     own_rows = pl.BlockSpec((rows, NB), lambda g: (g, 0))
     yh, yl, own = pl.pallas_call(

time: 295 us -> 296 us (level)
  starting transfers between devices: 43 us -> 49.8 us
  Pallas kernels: 133 us -> 128 us
    ppermute x1, waiting for transfers between devices: 11.1 us -> 17.8 us  [per_device(): lax.ppermute(routed, 'pcol', [(q, (3 * q + 1) % 16) for q in range(1, 16)])]
    all_to_all x1, waiting for transfers between devices: 6.69 us -> 0.29 us  [per_device(): first = lax.all_to_all(first, 'pcol', 0, 0, tiled=True)]
    pallas_call x2, Pallas kernels: 70.2 us -> 65.7 us  [the longest x1 33.8 us: per_device(): call(chain_tail_kernel, (shaped((TAILS, NB, NB)), shaped((TAILS, NB, NB),...]
    all_to_all x1, starting transfers between devices: 4.95 us -> 8.21 us  [per_device(): pieces = lax.all_to_all(pieces, 'prow', 0, 0, tiled=True)]
  transfers between devices with their start and end apart: 13 -> 13, of which waited for: 6 -> 6; matrix products, arithmetic and copies ran while one was open for 2% -> 2% of each run, Pallas kernels for 38% -> 36%
where the time goes in v5:
time: 296 us; the launch traced here: 293 us
  Pallas kernels  128 us (43%)
  blocking collectives  51.9 us (18%)
  starting transfers between devices  49.8 us (17%)
  waiting for transfers between devices  36.2 us (12%)
  between operations  13.7 us (5%)
  local copies, waits for them, and re-layouts  11.7 us (4%)
    pallas_call x1, Pallas kernels, per_device(): call(chain_tail_kernel, (shaped((TAILS, NB, NB)), shaped((TAILS, NB, NB),...  33.8 us
    pallas_call x1, Pallas kernels, per_device(): call(chain_head_kernel, (shaped((HEADS, NB, NB)), shaped((HEADS, NB, NB),...  31.9 us
    all_gather x1, blocking collectives, per_device(): chunk = lax.all_gather(chunk, 'pcol')  26.1 us
    all_to_all x1, blocking collectives, per_device(): rest = lax.all_to_all(rest, 'pcol', 0, 0, tiled=True)  25.9 us
    pallas_call x1, Pallas kernels, per_device(): pl.pallas_call(schur_kernel, grid=(steps,), out_shape=shaped((9216, LANES...  21.2 us
    ppermute x1, waiting for transfers between devices, per_device(): lax.ppermute(routed, 'pcol', [(q, (3 * q + 1) % 16) for q in range(1, 16)])  17.8 us
    pallas_call x1, Pallas kernels, per_device(): pl.pallas_call(left_kernel, grid=(steps,), out_shape=(shaped((1536, 1280)...  17.6 us
    pallas_call x1, Pallas kernels, per_device(): call(right_kernel, (shaped((768, 1280), BF16), shaped((768, 1280), BF16))...  11.3 us
  transfers between devices with their start and end apart: 13, of which 6 were waited for; matrix products, arithmetic and copies ran while one was open for 2% of the time, Pallas kernels for 36%

profile of v5, /device:TPU:102, one launch (start us, length us, event | category | flops | bytes accessed | tf_op | source)
XLA Modules:
  0.0 292.9 jit_solution(11571178480953577831)
XLA Ops:
  6.5 1.0 slice.61
  7.5 1.1 slice.48
  8.7 0.8 pad_maximum_fusion.1
  9.5 6.9 %all-to-all-start = ((f32[16,2,32,128]{3,2,1,0:T(8,128)}), f32[16,2,32,128]{3,2,1,0:T(8,128)S(1)}, u32[]{:S(2)}, u32[]{:S(2)}) async-start(f32[16,2,32,128]{3,2,1,0:T(8,128)} %pad_maximum_fusion.1), calls=%async_computation | async-start | bytes 1048576 | tf_op jit(solution)/shard_map/all_to_all | solution.py:458
  16.4 0.0 all-gather.8.cloned.1.call-start
  16.4 0.0 copy-done.11
  16.5 0.1 reshape.24
  16.5 0.7 pad_add_fusion.meta
  17.2 6.3 %shard_map.37 = f32[8,512,128]{2,1,0:T(8,128)} custom-call(s32[34]{0:T(128)} %pad_add_fusion.meta, f32[4,512,128]{2,1,0:T(8,128)} %bitcast.34), custom_call_target="tpu_custom_call" | custom-call | flops 3300000000 | bytes 1048576 | tf_op jit(solution)/shard_map/pallas_call | solution.py:445
  23.6 0.3 all-to-all-done
  23.9 0.0 copy-start.2
  23.9 4.9 %collective-permute-start = (f32[3,32,128]{2,1,0:T(8,128)S(1)}, f32[3,32,128]{2,1,0:T(8,128)S(1)}, u32[]{:S(2)}, u32[]{:S(2)}) collective-permute-start(f32[3,32,128]{2,1,0:T(8,128)S(1)} %slice_select_fusion.2), channel_id=1, source_target_pairs={{0,96},{16,80},{1,97},{17,81},{2,98},{18,82},{3,99},{19,83},{4,100... | collective-permute-start | bytes 147464 | tf_op jit(solution)/shard_map/ppermute | solution.py:462
  28.8 1.3 collective-permute-start.1
  30.1 1.4 collective-permute-done.1.got_b_ref
  31.6 0.0 collective-permute-done.got_a_ref
  31.6 0.0 copy-done.2
  31.6 0.6 copy-done.10
  32.2 0.6 copy-done.9
  32.8 1.6 shard_map.38
  34.4 26.1 %all-gather = f32[48,32,128]{2,1,0:T(8,128)} all-gather(f32[3,32,128]{2,1,0:T(8,128)} %shard_map.38), channel_id=2, replica_groups=mesh['prow'=8,'pcol'=16] {'pcol'}, dimensions={0}, use_global_device_ids=true | all-gather | bytes 835584 | tf_op jit(solution)/shard_map/all_gather | solution.py:465
  60.5 0.0 all-gather.8.cloned.1.call-update
  60.5 1.5 slice.64
  62.0 0.1 copy-done.1
  62.1 0.2 copy_bitcast_fusion
  62.3 25.9 %all_to_all.25 = f32[16,9,32,128]{3,2,1,0:T(8,128)S(1)} all-to-all(f32[16,9,32,128]{3,2,1,0:T(8,128)S(1)} %copy_bitcast_fusion), channel_id=1, replica_groups=mesh['prow'=8,'pcol'=16] {'pcol'}, dimensions={0} | all-to-all | bytes 4718592 | tf_op jit(solution)/shard_map/all_to_all | solution.py:470
  88.2 0.7 slice.66.parts_ref
  88.8 1.8 shard_map.39
  90.6 8.2 %all-to-all-start.2 = ((f32[8,2,32,128]{3,2,1,0:T(8,128)}), f32[8,2,32,128]{3,2,1,0:T(8,128)S(1)}, u32[]{:S(2)}, u32[]{:S(2)}) async-start(f32[8,2,32,128]{3,2,1,0:T(8,128)} %shard_map.39), calls=%async_computation.2 | async-start | bytes 524288 | tf_op jit(solution)/shard_map/all_to_all | solution.py:472
  98.8 0.0 all-gather.6.cloned.1.call-start
  98.9 0.0 copy-done.3
  98.9 0.6 slice.51.first_ref
  99.5 0.8 slice.65.rest_ref
  100.3 6.1 %all-to-all-done.2.got_ref = f32[8,2,32,128]{3,2,1,0:T(8,128)S(1)} async-done(((f32[8,2,32,128]{3,2,1,0:T(8,128)}), f32[8,2,32,128]{3,2,1,0:T(8,128)S(1)}, u32[]{:S(2)}, u32[]{:S(2)}) %all-to-all-start.2) | async-done | bytes 262176 | tf_op jit(solution)/shard_map/all_to_all | solution.py:472
  106.4 0.7 copy-done.4
  107.1 2.3 shard_map.40
  109.3 0.0 all-gather.6.cloned.1.call-update
  109.4 0.0 all-gather.8.cloned.1.call-done
  109.4 0.0 copy-start
  109.5 3.7 %all-to-all-start.3 = ((f32[8,512,128]{2,1,0:T(8,128)}), f32[8,512,128]{2,1,0:T(8,128)S(1)}, u32[]{:S(2)}, u32[]{:S(2)}) async-start(f32[8,512,128]{2,1,0:T(8,128)} %shard_map.37), calls=%async_computation.3 | async-start | bytes 4194304 | tf_op jit(solution)/shard_map/all_to_all | solution.py:480
  113.2 0.0 copy-done
  113.3 6.5 %collective-permute-start.2 = (f32[5,3,32,128]{3,2,1,0:T(8,128)S(1)}, f32[5,3,32,128]{3,2,1,0:T(8,128)S(1)}, u32[]{:S(2)}, u32[]{:S(2)}) collective-permute-start(f32[5,3,32,128]{3,2,1,0:T(8,128)S(1)} %get-tuple-element.53), channel_id=1, source_target_pairs={{0,0},{1,8},{2,16},{3,24},{4,32},{5,40},{6,48},{7,56},{8,64},{9,72... | collective-permute-start | bytes 737288 | tf_op jit(solution)/shard_map/ppermute | solution.py:495
  119.8 2.0 collective-permute-start.3
  121.8 31.9 %shard_map.41 = (f32[9,256,256]{2,1,0:T(8,128)}, bf16[9,256,256]{2,1,0:T(8,128)(2,1)}, bf16[9,256,256]{2,1,0:T(8,128)(2,1)}, f32[6,256,256]{2,1,0:T(8,128)}) custom-call(s32[34]{0:T(128)} %pad_add_fusion.meta, f32[8,16,3,32,128]{4,3,2,1,0:T(8,128)} %bitcast.42), custom_call_target="tpu_custom_call" | custom-call | flops 35200000000 | bytes 1048576 | tf_op jit(solution)/shard_map/pallas_call | solution.py:507
  153.8 0.0 collective-permute-done.2
  153.8 0.0 collective-permute-done.3
  153.8 0.0 all-to-all-done.3
  154.1 0.0 copy-start.5
  154.1 1.2 copy-done.5
  155.3 2.5 broadcast_in_dim.2
  157.8 8.7 %all-to-all-start.4 = ((f32[8,2,5,3,32,128]{5,4,3,2,1,0:T(8,128)}), f32[8,2,5,3,32,128]{5,4,3,2,1,0:T(8,128)}, u32[]{:S(2)}, u32[]{:S(2)}) async-start(f32[8,2,5,3,32,128]{5,4,3,2,1,0:T(8,128)} %broadcast_in_dim.2), calls=%async_computation.4 | async-start | bytes 7864320 | tf_op jit(solution)/shard_map/all_to_all | solution.py:522
  166.5 0.0 copy-done.6
  166.5 4.9 %collective-permute-start.4 = (f32[6,512,128]{2,1,0:T(8,128)S(1)}, f32[6,512,128]{2,1,0:T(8,128)S(1)}, u32[]{:S(2)}, u32[]{:S(2)}) collective-permute-start(f32[6,512,128]{2,1,0:T(8,128)S(1)} %copy-done.6), channel_id=1, source_target_pairs={{1,4},{2,7},{3,10},{4,13},{5,0},{6,3},{7,6},{8,9},{9,12},{10,15},{... | collective-permute-start | bytes 4718600 | tf_op jit(solution)/shard_map/ppermute | solution.py:521
  171.4 33.8 %shard_map.42 = (f32[6,256,256]{2,1,0:T(8,128)}, bf16[6,256,256]{2,1,0:T(8,128)(2,1)}, bf16[6,256,256]{2,1,0:T(8,128)(2,1)}) custom-call(f32[6,256,256]{2,1,0:T(8,128)} %get-tuple-element.38.rest_ref), custom_call_target="tpu_custom_call" | custom-call | flops 44000002048 | bytes 1048576 | tf_op jit(solution)/shard_map/pallas_call | solution.py:523
  205.2 17.8 %collective-permute-done.4.child_1 = f32[6,512,128]{2,1,0:T(8,128)S(1)} collective-permute-done((f32[6,512,128]{2,1,0:T(8,128)S(1)}, f32[6,512,128]{2,1,0:T(8,128)S(1)}, u32[]{:S(2)}, u32[]{:S(2)}) %collective-permute-start.4) | collective-permute-done | bytes 1572896 | tf_op jit(solution)/shard_map/ppermute | solution.py:521
  223.0 2.5 collective-permute-start.6
  225.4 0.0 collective-permute-start.5
  225.4 0.0 all-to-all-done.4
  225.4 11.3 %shard_map.44 = (bf16[768,1280]{1,0:T(8,128)(2,1)}, bf16[768,1280]{1,0:T(8,128)(2,1)}) custom-call(f32[16,5,3,32,128]{4,3,2,1,0:T(8,128)} %bitcast.16.parts_ref, bf16[9,256,256]{2,1,0:T(8,128)(2,1)} %get-tuple-element.32.hh_ref, bf16[9,256,256]{2,1,0:T(8,128)(2,1)} %get-tuple-element.33.hl_ref, bf16[6,256,256]{2,1,0:T(8,128)(2,1)} %get-tuple-element.40.th_ref, ...), custom_call_target="tpu_custom_call" | custom-call | flops 13200000000 | bytes 1048576 | tf_op jit(solution)/shard_map/pallas_call | solution.py:535
  236.7 0.0 copy-done.7
  236.7 17.6 %shard_map.43 = (bf16[1536,1280]{1,0:T(8,128)(2,1)}, bf16[1536,1280]{1,0:T(8,128)(2,1)}, f32[1536,256]{1,0:T(8,128)}) custom-call(s32[34]{0:T(128)} %pad_add_fusion.meta, f32[16,5,6,32,128]{4,3,2,1,0:T(8,128)} %bitcast.41, bf16[9,256,256]{2,1,0:T(8,128)(2,1)} %get-tuple-element.32.hh_ref, bf16[9,256,256]{2,1,0:T(8,128)(2,1)} %get-tuple-element.33.hl_ref, ...), custom_call_target="tpu_custom_call" | custom-call | flops 22000001024 | bytes 1048576 | tf_op jit(solution)/shard_map/pallas_call | solution.py:549
  254.3 5.6 %collective-permute-done.6.child_2 = f32[6,512,128]{2,1,0:T(8,128)S(1)} collective-permute-done((f32[6,512,128]{2,1,0:T(8,128)S(1)}, f32[6,512,128]{2,1,0:T(8,128)S(1)}, u32[]{:S(2)}, u32[]{:S(2)}) %collective-permute-start.6) | collective-permute-done | bytes 1572896 | tf_op jit(solution)/shard_map/ppermute | solution.py:532
  259.9 5.0 %collective-permute-done.5.child_0 = f32[6,512,128]{2,1,0:T(8,128)} collective-permute-done((f32[6,512,128]{2,1,0:T(8,128)S(1)}, f32[6,512,128]{2,1,0:T(8,128)}, u32[]{:S(2)}, u32[]{:S(2)}) %collective-permute-start.5) | collective-permute-done | bytes 1572896 | tf_op jit(solution)/shard_map/ppermute | solution.py:533
  264.9 0.0 copy-done.8
  264.9 21.2 %shard_map.45 = f32[9216,128]{1,0:T(8,128)} custom-call(s32[34]{0:T(128)} %pad_add_fusion.meta, bf16[1536,1280]{1,0:T(8,128)(2,1)} %get-tuple-element.42.yh, bf16[1536,1280]{1,0:T(8,128)(2,1)} %get-tuple-element.43.yl, f32[1536,256]{1,0:T(8,128)} %get-tuple-element.44.own_ref, bf16[768,1280]{1,0:T(8,128)(2,1)} %get-tuple-element.46.rh_ref, ...), custom_call_target="tpu_custom_call" | custom-call | flops 19800000512 | bytes 1048576 | tf_op jit(solution)/shard_map/pallas_call | solution.py:570
  (24 shorter events, 0.3 us)
Async XLA Ops:
  6.5 9.9 %copy-start.11 = (s32[2,16]{1,0:T(2,128)S(1)}, s32[2,16]{1,0:T(2,128)}, u32[]{:S(2)}) copy-start(s32[2,16]{1,0:T(2,128)} %param.5) | copy-start | bytes 388
  9.5 14.4 %all-to-all-start = ((f32[16,2,32,128]{3,2,1,0:T(8,128)}), f32[16,2,32,128]{3,2,1,0:T(8,128)S(1)}, u32[]{:S(2)}, u32[]{:S(2)}) async-start(f32[16,2,32,128]{3,2,1,0:T(8,128)} %pad_maximum_fusion.1), calls=%async_computation | async-start | bytes 1048576 | tf_op jit(solution)/shard_map/all_to_all | solution.py:458
  16.4 93.0 %all-gather.8.cloned.1.call-start = ((), (), s32[]{:S(2)}) async-start(), calls=%async_computation.6 | async-start | bytes 7077888 | tf_op jit(solution)/shard_map/all_gather | solution.py:466
  23.9 7.7 %copy-start.2 = (f32[7,32,128]{2,1,0:T(8,128)}, f32[7,32,128]{2,1,0:T(8,128)S(1)}, u32[]{:S(2)}) copy-start(f32[7,32,128]{2,1,0:T(8,128)S(1)} %pad_maximum_fusion.3.mine_ref) | copy-start | bytes 344068
  23.9 7.7 %collective-permute-start = (f32[3,32,128]{2,1,0:T(8,128)S(1)}, f32[3,32,128]{2,1,0:T(8,128)S(1)}, u32[]{:S(2)}, u32[]{:S(2)}) collective-permute-start(f32[3,32,128]{2,1,0:T(8,128)S(1)} %slice_select_fusion.2), channel_id=1, source_target_pairs={{0,96},{16,80},{1,97},{17,81},{2,98},{18,82},{3,99},{19,83},{4,100... | collective-permute-start | bytes 147464 | tf_op jit(solution)/shard_map/ppermute | solution.py:462
  28.8 2.7 collective-permute-start.1
  31.6 0.6 copy-start.10
  32.2 0.6 copy-start.9
  60.5 1.6 copy-start.1
  88.8 10.0 %copy-start.3 = (f32[7,32,128]{2,1,0:T(8,128)S(1)}, f32[7,32,128]{2,1,0:T(8,128)}, u32[]{:S(2)}) copy-start(f32[7,32,128]{2,1,0:T(8,128)} %copy-done.2) | copy-start | bytes 344068
  90.6 15.7 %all-to-all-start.2 = ((f32[8,2,32,128]{3,2,1,0:T(8,128)}), f32[8,2,32,128]{3,2,1,0:T(8,128)S(1)}, u32[]{:S(2)}, u32[]{:S(2)}) async-start(f32[8,2,32,128]{3,2,1,0:T(8,128)} %shard_map.39), calls=%async_computation.2 | async-start | bytes 524288 | tf_op jit(solution)/shard_map/all_to_all | solution.py:472
  98.8 137.9 %all-gather.6.cloned.1.call-start = ((), (), s32[]{:S(2)}) async-start(), calls=%async_computation.5 | async-start | bytes 8355840 | tf_op jit(solution)/shard_map/all_gather | solution.py:477
  106.4 0.7 copy-start.4
  109.4 3.8 %copy-start = (f32[5,6,32,128]{3,2,1,0:T(8,128)S(1)}, f32[5,6,32,128]{3,2,1,0:T(8,128)}, u32[]{:S(2)}) copy-start(f32[5,6,32,128]{3,2,1,0:T(8,128)} %shard_map.40) | copy-start | bytes 1474564
  109.5 44.4 %all-to-all-start.3 = ((f32[8,512,128]{2,1,0:T(8,128)}), f32[8,512,128]{2,1,0:T(8,128)S(1)}, u32[]{:S(2)}, u32[]{:S(2)}) async-start(f32[8,512,128]{2,1,0:T(8,128)} %shard_map.37), calls=%async_computation.3 | async-start | bytes 4194304 | tf_op jit(solution)/shard_map/all_to_all | solution.py:480
  113.3 40.5 %collective-permute-start.2 = (f32[5,3,32,128]{3,2,1,0:T(8,128)S(1)}, f32[5,3,32,128]{3,2,1,0:T(8,128)S(1)}, u32[]{:S(2)}, u32[]{:S(2)}) collective-permute-start(f32[5,3,32,128]{3,2,1,0:T(8,128)S(1)} %get-tuple-element.53), channel_id=1, source_target_pairs={{0,0},{1,8},{2,16},{3,24},{4,32},{5,40},{6,48},{7,56},{8,64},{9,72... | collective-permute-start | bytes 737288 | tf_op jit(solution)/shard_map/ppermute | solution.py:495
  119.8 34.0 %collective-permute-start.3 = (f32[5,3,32,128]{3,2,1,0:T(8,128)S(1)}, f32[5,3,32,128]{3,2,1,0:T(8,128)S(1)}, u32[]{:S(2)}, u32[]{:S(2)}) collective-permute-start(f32[5,3,32,128]{3,2,1,0:T(8,128)S(1)} %get-tuple-element.54), channel_id=1, source_target_pairs={{0,8},{1,0},{2,24},{3,16},{4,40},{5,32},{6,56},{7,48},{8,72},{9,64... | collective-permute-start | bytes 737288 | tf_op jit(solution)/shard_map/ppermute | solution.py:496
  154.1 1.2 copy-start.5
  157.8 8.7 %copy-start.6 = (f32[6,512,128]{2,1,0:T(8,128)S(1)}, f32[6,512,128]{2,1,0:T(8,128)}, u32[]{:S(2)}) copy-start(f32[6,512,128]{2,1,0:T(8,128)} %copy-done.5) | copy-start | bytes 4718596
  157.8 67.6 %all-to-all-start.4 = ((f32[8,2,5,3,32,128]{5,4,3,2,1,0:T(8,128)}), f32[8,2,5,3,32,128]{5,4,3,2,1,0:T(8,128)}, u32[]{:S(2)}, u32[]{:S(2)}) async-start(f32[8,2,5,3,32,128]{5,4,3,2,1,0:T(8,128)} %broadcast_in_dim.2), calls=%async_computation.4 | async-start | bytes 7864320 | tf_op jit(solution)/shard_map/all_to_all | solution.py:522
  166.5 56.4 %collective-permute-start.4 = (f32[6,512,128]{2,1,0:T(8,128)S(1)}, f32[6,512,128]{2,1,0:T(8,128)S(1)}, u32[]{:S(2)}, u32[]{:S(2)}) collective-permute-start(f32[6,512,128]{2,1,0:T(8,128)S(1)} %copy-done.6), channel_id=1, source_target_pairs={{1,4},{2,7},{3,10},{4,13},{5,0},{6,3},{7,6},{8,9},{9,12},{10,15},{... | collective-permute-start | bytes 4718600 | tf_op jit(solution)/shard_map/ppermute | solution.py:521
  222.9 13.8 %copy-start.7 = (f32[6,512,128]{2,1,0:T(8,128)}, f32[6,512,128]{2,1,0:T(8,128)S(1)}, u32[]{:S(2)}) copy-start(f32[6,512,128]{2,1,0:T(8,128)S(1)} %collective-permute-done.4.child_1) | copy-start | bytes 4718596
  223.0 36.9 %collective-permute-start.6 = (f32[6,512,128]{2,1,0:T(8,128)S(1)}, f32[6,512,128]{2,1,0:T(8,128)S(1)}, u32[]{:S(2)}, u32[]{:S(2)}) collective-permute-start(f32[6,512,128]{2,1,0:T(8,128)S(1)} %collective-permute-done.4.child_1), channel_id=1, source_target_pairs={{0,1},{1,2},{2,3},{3,4},{4,5},{5,6},{6,7},{7,8},{8,9},{9,10},{10,1... | collective-permute-start | bytes 4718600 | tf_op jit(solution)/shard_map/ppermute | solution.py:532
  225.4 39.5 %collective-permute-start.5 = (f32[6,512,128]{2,1,0:T(8,128)S(1)}, f32[6,512,128]{2,1,0:T(8,128)}, u32[]{:S(2)}, u32[]{:S(2)}) collective-permute-start(f32[6,512,128]{2,1,0:T(8,128)S(1)} %collective-permute-done.4.child_1), channel_id=1, source_target_pairs={{0,15},{1,0},{2,1},{3,2},{4,3},{5,4},{6,5},{7,6},{8,7},{9,8},{10,9... | collective-permute-start | bytes 4718600 | tf_op jit(solution)/shard_map/ppermute | solution.py:533
  259.9 5.0 %copy-start.8 = (f32[6,512,128]{2,1,0:T(8,128)}, f32[6,512,128]{2,1,0:T(8,128)S(1)}, u32[]{:S(2)}) copy-start(f32[6,512,128]{2,1,0:T(8,128)S(1)} %collective-permute-done.6.child_2) | copy-start | bytes 4718596
Sparse Core Ops, SparseCore 0:
  60.6 41.1 all-gather.7
  109.5 97.4 all-gather.5

commit v6 on v4

--- a/solution.py
+++ b/solution.py
@@ -49,10 +49,8 @@
     out_ref[...] = block_ref[...]
 
 
-def assemble_kernel(meta, first_ref, rest_ref, got_ref, out_ref):
-    for j in range(KB):
-        out_ref[j, 0] = first_ref[j]
-        out_ref[j, 1:6] = rest_ref[j]
+def assemble_kernel(meta, rest_ref, got_ref, out_ref):
+    out_ref[...] = rest_ref[...]
     for child in range(2):
         for residue in range(4):
             there, slot = route_of(meta, child, residue)
@@ -64,8 +62,55 @@
                     out_ref[column, slot] = out_ref[column, slot] + got_ref[4 * child + residue, v]
 
 
-UPPER = [(k, i) for k in range(KB) for i in range(k, KB)]
-CHILD_SOURCES = [(c, u, v) for c in range(2) for (u, v) in ((0, 0), (0, 1), (1, 1))]
+def chunk_kernel(meta, mine_ref, got_a_ref, got_b_ref, out_ref):
+    for row, picks in enumerate(CHUNKS):
+
+        @pl.when(meta[32] == row)
+        def _():
+            for at in range(3):
+                kind, index = picks[at] if at < len(picks) else (0, 0)
+                source = (mine_ref, got_a_ref, got_b_ref)[kind]
+                out_ref[at] = source[index]
+
+
+CHUNKS = [
+    [(0, 0), (0, 5), (0, 6)],
+    [(0, 1), (0, 2), (0, 6)],
+    [(0, 2), (0, 3), (0, 4)],
+    [(0, 3), (0, 4)],
+    [(0, 4), (0, 5), (0, 6)],
+    [(1, 0), (1, 1), (0, 6)],
+    [(1, 0), (1, 1), (1, 2)],
+    [(2, 0)],
+]
+UPPER_AT = {
+    (0, 0): (0, 0),
+    (0, 1): (7, 0),
+    (0, 2): (6, 0),
+    (0, 3): (6, 1),
+    (0, 4): (6, 2),
+    (1, 1): (1, 0),
+    (1, 2): (1, 1),
+    (1, 3): (5, 0),
+    (1, 4): (5, 1),
+    (2, 2): (2, 0),
+    (2, 3): (2, 1),
+    (2, 4): (2, 2),
+    (3, 3): (3, 0),
+    (3, 4): (3, 1),
+    (4, 4): (4, 0),
+}
+CHILD_AT = {
+    (0, 0, 0): (0, 1),
+    (0, 0, 1): (0, 2),
+    (0, 1, 1): (1, 2),
+    (1, 0, 0): (4, 1),
+    (1, 0, 1): (4, 2),
+    (1, 1, 1): (5, 2),
+}
+
+
+UPPER = list(UPPER_AT)
 TRI = len(UPPER)
 
 
@@ -145,7 +190,7 @@
 
 
 def chain_kernel(meta, parts_ref, u_ref, th_ref, tl_ref, f_ref, v_ref, a_s, x_s, u_s, stage, sems):
-    sources = UPPER + [(4 * c + u, KB + v) for c, u, v in CHILD_SOURCES]
+    sources = list(UPPER_AT.values()) + list(CHILD_AT.values())
     copies = [
         pltpu.make_async_copy(parts_ref.at[p, :, j], stage.at[at], sems.at[at]) for at, (p, j) in enumerate(sources)
     ]
@@ -160,7 +205,7 @@
         for s in range(16):
             for h in range(2):
                 f_ref[k * KB + i, 16 * s : 16 * s + 16, HB * h : HB * h + HB] = take(at, s, h)
-    for at, (c, u, v) in enumerate(CHILD_SOURCES):
+    for at, (c, u, v) in enumerate(CHILD_AT):
         copies[TRI + at].wait()
         k = meta[c * 16 + u]
         i = meta[c * 16 + v]
@@ -384,20 +429,22 @@
         cost_estimate=cost(3),
     )(meta, child.reshape(4, 512, LANES))
 
-    first = jnp.stack([lead[0], child[0]], axis=1)
-    first = lax.all_to_all(first, "pcol", 0, 0, tiled=True)
-    mine = jnp.concatenate([first[0:KB, 0], first[0:2, 1]], axis=0)
+    rest = jnp.concatenate([lead, child], axis=0).transpose(1, 0, 2, 3)
+    rest = lax.all_to_all(rest, "pcol", 0, 0, tiled=True)
+
+    mine = jnp.concatenate([rest[0:KB, 0], rest[0:2, 6]], axis=0)
     mine, picked = lax.optimization_barrier((mine, picked))
-    lead_parts = lax.all_gather(mine, ("prow", "pcol")).reshape(8, 16, KB + 2, 32, LANES)
-
-    rest = jnp.concatenate([lead[1:], child], axis=0).transpose(1, 0, 2, 3)
-    rest, mine = lax.optimization_barrier((rest, mine))
-    rest = lax.all_to_all(rest, "pcol", 0, 0, tiled=True)
-    pieces = call(pick_kernel, shaped((8, 2, 32, LANES)), [SM, VM], [])(meta, rest[0:2, 5:9])
+    shed = jnp.where(row == 0, mine[2:5], mine[3:6])
+    got_a = lax.ppermute(shed, "prow", [(0, 6), (1, 5)])
+    got_b = lax.ppermute(mine[1:2], "prow", [(0, 7)])
+    chunk = call(chunk_kernel, shaped((3, 32, LANES)), [SM, VM, VM, VM], [])(meta, mine, got_a, got_b)
+    chunk = lax.all_gather(chunk, "pcol")
+    lead_parts = lax.all_gather(chunk, "prow")
+
+    rest, chunk = lax.optimization_barrier((rest, chunk))
+    pieces = call(pick_kernel, shaped((8, 2, 32, LANES)), [SM, VM], [])(meta, rest[0:2, 6:10])
     pieces = lax.all_to_all(pieces, "prow", 0, 0, tiled=True)
-    slices = call(assemble_kernel, shaped((KB, 6, 32, LANES)), [SM, VM, VM, VM], [])(
-        meta, mine[0:KB], rest[0:KB, 0:5], pieces
-    )
+    slices = call(assemble_kernel, shaped((KB, 6, 32, LANES)), [SM, VM, VM], [])(meta, rest[0:KB, 0:6], pieces)
 
     left_parts = lax.all_gather(slices, "pcol")
 

time: 343 us -> 352 us (1.026)
  waiting for transfers between devices: 101 us -> 117 us
  blocking collectives: 34.9 us -> 26.9 us
    all_to_all x1 -> x0, blocking collectives: 34.9 us -> none  [per_device(): rest = lax.all_to_all(rest, 'pcol', 0, 0, tiled=True)]
    all_to_all x1, waiting for transfers between devices: 0.72 us -> 27.8 us  [per_device(): rest = lax.all_to_all(rest, 'pcol', 0, 0, tiled=True)]
    all_gather x0 -> x1, blocking collectives: none -> 26.9 us  [per_device(): chunk = lax.all_gather(chunk, 'pcol')]
    all_gather x1, waiting for transfers between devices: 51.3 us -> 39.4 us  [per_device(): left_parts = lax.all_gather(slices, 'pcol')]
    ppermute x0 -> x2, starting transfers between devices: none -> 6.21 us  [the longest x1 4.92 us: per_device(): got_a = lax.ppermute(shed, 'prow', [(0, 6), (1, 5)])]
    ppermute x1, waiting for transfers between devices: 12.7 us -> 7.4 us  [per_device(): lax.ppermute(jnp.where(is_even, even, odd), ('prow', 'pcol'), perm_a)]
    ppermute x1, starting transfers between devices: 5.2 us -> 0.07 us  [per_device(): below = lax.ppermute(middle, 'pcol', [(q, (q + 1) % 16) for q in range(16)])]
    all_to_all x1, starting transfers between devices: 18.9 us -> 14.4 us  [per_device(): lax.all_to_all(pairs, 'prow', 0, 0, tiled=True)]
  transfers between devices with their start and end apart: 11 -> 13, of which waited for: 6 -> 7; matrix products, arithmetic and copies ran while one was open for 3% -> 3% of each run, Pallas kernels for 30% -> 29%
where the time goes in v6:
time: 352 us; the launch traced here: 349 us
  Pallas kernels  125 us (36%)
  waiting for transfers between devices  117 us (33%)
  starting transfers between devices  51.1 us (15%)
  blocking collectives  26.9 us (8%)
  between operations  13.6 us (4%)
  local copies, waits for them, and re-layouts  13.2 us (4%)
    pallas_call x1, Pallas kernels, per_device(): pl.pallas_call(chain_kernel, out_shape=(shaped((TRI, NB, NB)), shaped((TR...  63.1 us
    all_gather x1, waiting for transfers between devices, per_device(): left_parts = lax.all_gather(slices, 'pcol')  39.4 us
    all_to_all x1, waiting for transfers between devices, per_device(): rest = lax.all_to_all(rest, 'pcol', 0, 0, tiled=True)  27.8 us
    all_gather x1, blocking collectives, per_device(): chunk = lax.all_gather(chunk, 'pcol')  26.9 us
    all_to_all x1, waiting for transfers between devices, per_device(): got = lax.all_to_all(picked, 'prow', 0, 0, tiled=True)  24.6 us
    pallas_call x1, Pallas kernels, per_device(): pl.pallas_call(schur_kernel, grid=(steps,), out_shape=shaped((9216, LANES...  20.7 us
    pallas_call x1, Pallas kernels, per_device(): pl.pallas_call(left_kernel, grid=(steps,), out_shape=(shaped((1536, 1280)...  17.7 us
    all_to_all x1, starting transfers between devices, per_device(): lax.all_to_all(pairs, 'prow', 0, 0, tiled=True)  14.4 us
  transfers between devices with their start and end apart: 13, of which 7 were waited for; matrix products, arithmetic and copies ran while one was open for 3% of the time, Pallas kernels for 29%

profile of v6, /device:TPU:102, one launch (start us, length us, event | category | flops | bytes accessed | tf_op | source)
XLA Modules:
  0.0 349.3 jit_solution(8446838856889091230)
XLA Ops:
  6.5 0.0 copy-start.1
  6.5 1.6 slice.40
  8.1 0.1 copy-done.1
  8.2 1.8 copy_bitcast_fusion
  10.0 0.0 copy-start.8
  10.0 7.0 %all-to-all-start = ((f32[16,10,32,128]{3,2,1,0:T(8,128)}), f32[16,10,32,128]{3,2,1,0:T(8,128)S(1)}, u32[]{:S(2)}, u32[]{:S(2)}) async-start(f32[16,10,32,128]{3,2,1,0:T(8,128)} %copy_bitcast_fusion), calls=%async_computation | async-start | bytes 5242880 | tf_op jit(solution)/shard_map/all_to_all | solution.py:433
  17.0 0.0 all-gather.8.cloned.1.call-start
  17.1 0.0 copy-done.8
  17.1 0.1 reshape.19
  17.2 0.6 pad_add_fusion.meta
  17.8 6.5 %shard_map.37 = f32[8,512,128]{2,1,0:T(8,128)} custom-call(s32[34]{0:T(128)} %pad_add_fusion.meta, f32[4,512,128]{2,1,0:T(8,128)} %bitcast.26), custom_call_target="tpu_custom_call" | custom-call | flops 3300000000 | bytes 1048576 | tf_op jit(solution)/shard_map/pallas_call | solution.py:420
  24.2 27.8 %all-to-all-done = f32[16,10,32,128]{3,2,1,0:T(8,128)S(1)} async-done(((f32[16,10,32,128]{3,2,1,0:T(8,128)}), f32[16,10,32,128]{3,2,1,0:T(8,128)S(1)}, u32[]{:S(2)}, u32[]{:S(2)}) %all-to-all-start) | async-done | bytes 2621472 | tf_op jit(solution)/shard_map/all_to_all | solution.py:433
  52.1 0.0 copy-start.2
  52.1 4.9 %collective-permute-start = (f32[3,32,128]{2,1,0:T(8,128)S(1)}, f32[3,32,128]{2,1,0:T(8,128)S(1)}, u32[]{:S(2)}, u32[]{:S(2)}) collective-permute-start(f32[3,32,128]{2,1,0:T(8,128)S(1)} %slice_select_fusion.2), channel_id=1, source_target_pairs={{0,96},{16,80},{1,97},{17,81},{2,98},{18,82},{3,99},{19,83},{4,100... | collective-permute-start | bytes 147464 | tf_op jit(solution)/shard_map/ppermute | solution.py:438
  57.0 1.3 collective-permute-start.1
  58.3 1.4 collective-permute-done.1.got_b_ref
  59.7 0.0 collective-permute-done.got_a_ref
  59.8 0.0 copy-done.2
  59.8 0.6 copy-done.7
  60.3 0.6 copy-done.6
  61.0 1.6 shard_map.38
  62.6 26.9 %all-gather = f32[48,32,128]{2,1,0:T(8,128)} all-gather(f32[3,32,128]{2,1,0:T(8,128)} %shard_map.38), channel_id=2, replica_groups=mesh['prow'=8,'pcol'=16] {'pcol'}, dimensions={0}, use_global_device_ids=true | all-gather | bytes 835584 | tf_op jit(solution)/shard_map/all_gather | solution.py:441
  89.4 0.0 all-gather.8.cloned.1.call-update
  89.5 0.7 slice.37.parts_ref
  90.1 1.7 shard_map.39
  91.8 3.5 %all-to-all-start.1 = ((f32[8,2,32,128]{3,2,1,0:T(8,128)}), f32[8,2,32,128]{3,2,1,0:T(8,128)S(1)}, u32[]{:S(2)}, u32[]{:S(2)}) async-start(f32[8,2,32,128]{3,2,1,0:T(8,128)} %shard_map.39), calls=%async_computation.1 | async-start | bytes 524288 | tf_op jit(solution)/shard_map/all_to_all | solution.py:446
  95.4 0.0 all-gather.6.cloned.1.call-start
  95.4 0.8 slice.36.rest_ref
  96.2 6.7 %all-to-all-done.1.got_ref = f32[8,2,32,128]{3,2,1,0:T(8,128)S(1)} async-done(((f32[8,2,32,128]{3,2,1,0:T(8,128)}), f32[8,2,32,128]{3,2,1,0:T(8,128)S(1)}, u32[]{:S(2)}, u32[]{:S(2)}) %all-to-all-start.1) | async-done | bytes 262176 | tf_op jit(solution)/shard_map/all_to_all | solution.py:446
  102.9 0.7 copy-done.3
  103.6 2.3 shard_map.40
  105.9 0.0 all-gather.6.cloned.1.call-update
  105.9 0.0 copy-start
  105.9 3.7 %all-to-all-start.2 = ((f32[8,512,128]{2,1,0:T(8,128)}), f32[8,512,128]{2,1,0:T(8,128)S(1)}, u32[]{:S(2)}, u32[]{:S(2)}) async-start(f32[8,512,128]{2,1,0:T(8,128)} %shard_map.37), calls=%async_computation.2 | async-start | bytes 4194304 | tf_op jit(solution)/shard_map/all_to_all | solution.py:452
  109.7 0.0 copy-done
  109.7 5.8 %collective-permute-start.3 = (f32[5,3,32,128]{3,2,1,0:T(8,128)S(1)}, f32[5,3,32,128]{3,2,1,0:T(8,128)S(1)}, u32[]{:S(2)}, u32[]{:S(2)}) collective-permute-start(f32[5,3,32,128]{3,2,1,0:T(8,128)S(1)} %get-tuple-element.39), channel_id=1, source_target_pairs={{0,0},{1,8},{2,16},{3,24},{4,32},{5,40},{6,48},{7,56},{8,64},{9,72... | collective-permute-start | bytes 737288 | tf_op jit(solution)/shard_map/ppermute | solution.py:467
  115.5 3.1 collective-permute-start.4
  118.7 7.4 %collective-permute-done.3 = f32[5,3,32,128]{3,2,1,0:T(8,128)S(1)} collective-permute-done((f32[5,3,32,128]{3,2,1,0:T(8,128)S(1)}, f32[5,3,32,128]{3,2,1,0:T(8,128)S(1)}, u32[]{:S(2)}, u32[]{:S(2)}) %collective-permute-start.3) | collective-permute-done | bytes 245792 | tf_op jit(solution)/shard_map/ppermute | solution.py:467
  126.1 9.8 %collective-permute-done.4 = f32[5,3,32,128]{3,2,1,0:T(8,128)S(1)} collective-permute-done((f32[5,3,32,128]{3,2,1,0:T(8,128)S(1)}, f32[5,3,32,128]{3,2,1,0:T(8,128)S(1)}, u32[]{:S(2)}, u32[]{:S(2)}) %collective-permute-start.4) | collective-permute-done | bytes 245792 | tf_op jit(solution)/shard_map/ppermute | solution.py:468
  136.0 24.6 %all-to-all-done.2 = f32[8,512,128]{2,1,0:T(8,128)S(1)} async-done(((f32[8,512,128]{2,1,0:T(8,128)}), f32[8,512,128]{2,1,0:T(8,128)S(1)}, u32[]{:S(2)}, u32[]{:S(2)}) %all-to-all-start.2) | async-done | bytes 2097184 | tf_op jit(solution)/shard_map/all_to_all | solution.py:452
  160.6 2.4 broadcast_in_dim.2
  163.0 14.4 %all-to-all-start.3 = ((f32[8,2,5,3,32,128]{5,4,3,2,1,0:T(8,128)}), f32[8,2,5,3,32,128]{5,4,3,2,1,0:T(8,128)}, u32[]{:S(2)}, u32[]{:S(2)}) async-start(f32[8,2,5,3,32,128]{5,4,3,2,1,0:T(8,128)} %broadcast_in_dim.2), calls=%async_computation.3 | async-start | bytes 7864320 | tf_op jit(solution)/shard_map/all_to_all | solution.py:473
  177.4 0.7 dynamic-slice_dynamic-update-slice_fusion.5
  178.2 0.7 dynamic-slice_dynamic-update-slice_fusion.4
  178.9 0.7 dynamic-slice_dynamic-update-slice_fusion.3
  179.6 0.7 dynamic-slice_dynamic-update-slice_fusion.2
  180.3 0.7 dynamic-slice_dynamic-update-slice_fusion.1
  181.1 0.7 dynamic-slice_dynamic-update-slice_fusion
  181.8 5.0 %collective-permute-start.2 = (f32[6,512,128]{2,1,0:T(8,128)}, f32[6,512,128]{2,1,0:T(8,128)S(1)}, u32[]{:S(2)}, u32[]{:S(2)}) collective-permute-start(f32[6,512,128]{2,1,0:T(8,128)} %dynamic-slice_dynamic-update-slice_fusion), channel_id=1, source_target_pairs={{1,4},{2,7},{3,10},{4,13},{5,0},{6,3},{7,6},{8,9},{9,12},{10,15},{... | collective-permute-start | bytes 4718600 | tf_op jit(solution)/shard_map/ppermute | solution.py:474
  186.8 0.0 all-gather.8.cloned.1.call-done
  186.9 63.1 %shard_map.41 = (f32[15,256,256]{2,1,0:T(8,128)}, bf16[15,256,256]{2,1,0:T(8,128)(2,1)}, bf16[15,256,256]{2,1,0:T(8,128)(2,1)}) custom-call(s32[34]{0:T(128)} %pad_add_fusion.meta, f32[8,16,3,32,128]{4,3,2,1,0:T(8,128)} %bitcast.31), custom_call_target="tpu_custom_call" | custom-call | flops 72600002560 | bytes 1048576 | tf_op jit(solution)/shard_map/pallas_call | solution.py:477
  250.0 0.0 collective-permute-done.2.child_1
  250.0 0.0 copy-start.4
  250.0 0.1 collective-permute-start.6
  250.1 2.0 collective-permute-start.5
  252.1 0.0 all-to-all-done.3
  252.1 11.4 %shard_map.43 = (bf16[768,1280]{1,0:T(8,128)(2,1)}, bf16[768,1280]{1,0:T(8,128)(2,1)}) custom-call(f32[16,5,3,32,128]{4,3,2,1,0:T(8,128)} %bitcast.14.parts_ref, bf16[15,256,256]{2,1,0:T(8,128)(2,1)} %get-tuple-element.28.th_ref, bf16[15,256,256]{2,1,0:T(8,128)(2,1)} %get-tuple-element.29.tl_ref), custom_call_target="tpu_custom_call" | custom-call | flops 13200000000 | bytes 1048576 | tf_op jit(solution)/shard_map/pallas_call | solution.py:499
  263.5 0.0 copy-done.4
  263.5 39.4 %all-gather.6.cloned.1.call-done = f32[80,6,32,128]{3,2,1,0:T(8,128)} async-done(((f32[5,6,32,128]{3,2,1,0:T(8,128)}), f32[80,6,32,128]{3,2,1,0:T(8,128)}) %all-gather.6.cloned.1.call-update) | async-done | bytes 7864336 | tf_op jit(solution)/shard_map/all_gather | solution.py:449
  302.9 17.7 %shard_map.42 = (bf16[1536,1280]{1,0:T(8,128)(2,1)}, bf16[1536,1280]{1,0:T(8,128)(2,1)}, f32[1536,256]{1,0:T(8,128)}) custom-call(s32[34]{0:T(128)} %pad_add_fusion.meta, f32[16,5,6,32,128]{4,3,2,1,0:T(8,128)} %bitcast.30, bf16[15,256,256]{2,1,0:T(8,128)(2,1)} %get-tuple-element.28.th_ref, bf16[15,256,256]{2,1,0:T(8,128)(2,1)} %get-tuple-element.29.tl_ref), custom_call_target="tpu_custom_call" | custom-call | flops 22000001024 | bytes 1048576 | tf_op jit(solution)/shard_map/pallas_call | solution.py:512
  320.6 0.0 collective-permute-done.6.child_2
  320.6 0.0 collective-permute-done.5.child_0
  320.6 1.2 copy-done.5
  321.8 20.7 %shard_map.44 = f32[9216,128]{1,0:T(8,128)} custom-call(s32[34]{0:T(128)} %pad_add_fusion.meta, bf16[1536,1280]{1,0:T(8,128)(2,1)} %get-tuple-element.30.yh, bf16[1536,1280]{1,0:T(8,128)(2,1)} %get-tuple-element.31.yl, f32[1536,256]{1,0:T(8,128)} %get-tuple-element.32.own_ref, bf16[768,1280]{1,0:T(8,128)(2,1)} %get-tuple-element.33.rh_ref, ...), custom_call_target="tpu_custom_call" | custom-call | flops 19800000512 | bytes 1048576 | tf_op jit(solution)/shard_map/pallas_call | solution.py:531
  (12 shorter events, 0.1 us)
Async XLA Ops:
  6.5 1.7 copy-start.1
  10.0 7.1 %copy-start.8 = (s32[2,16]{1,0:T(2,128)S(1)}, s32[2,16]{1,0:T(2,128)}, u32[]{:S(2)}) copy-start(s32[2,16]{1,0:T(2,128)} %param.5) | copy-start | bytes 388
  10.0 42.0 %all-to-all-start = ((f32[16,10,32,128]{3,2,1,0:T(8,128)}), f32[16,10,32,128]{3,2,1,0:T(8,128)S(1)}, u32[]{:S(2)}, u32[]{:S(2)}) async-start(f32[16,10,32,128]{3,2,1,0:T(8,128)} %copy_bitcast_fusion), calls=%async_computation | async-start | bytes 5242880 | tf_op jit(solution)/shard_map/all_to_all | solution.py:433
  17.0 169.8 %all-gather.8.cloned.1.call-start = ((), (), s32[]{:S(2)}) async-start(), calls=%async_computation.5 | async-start | bytes 7077888 | tf_op jit(solution)/shard_map/all_gather | solution.py:442
  52.1 7.7 %copy-start.2 = (f32[7,32,128]{2,1,0:T(8,128)}, f32[7,32,128]{2,1,0:T(8,128)S(1)}, u32[]{:S(2)}) copy-start(f32[7,32,128]{2,1,0:T(8,128)S(1)} %pad_maximum_fusion.2.mine_ref) | copy-start | bytes 344068
  52.1 7.7 %collective-permute-start = (f32[3,32,128]{2,1,0:T(8,128)S(1)}, f32[3,32,128]{2,1,0:T(8,128)S(1)}, u32[]{:S(2)}, u32[]{:S(2)}) collective-permute-start(f32[3,32,128]{2,1,0:T(8,128)S(1)} %slice_select_fusion.2), channel_id=1, source_target_pairs={{0,96},{16,80},{1,97},{17,81},{2,98},{18,82},{3,99},{19,83},{4,100... | collective-permute-start | bytes 147464 | tf_op jit(solution)/shard_map/ppermute | solution.py:438
  57.0 2.7 collective-permute-start.1
  59.7 0.6 copy-start.7
  60.3 0.6 copy-start.6
  91.8 11.1 %all-to-all-start.1 = ((f32[8,2,32,128]{3,2,1,0:T(8,128)}), f32[8,2,32,128]{3,2,1,0:T(8,128)S(1)}, u32[]{:S(2)}, u32[]{:S(2)}) async-start(f32[8,2,32,128]{3,2,1,0:T(8,128)} %shard_map.39), calls=%async_computation.1 | async-start | bytes 524288 | tf_op jit(solution)/shard_map/all_to_all | solution.py:446
  95.4 207.6 %all-gather.6.cloned.1.call-start = ((), (), s32[]{:S(2)}) async-start(), calls=%async_computation.4 | async-start | bytes 8355840 | tf_op jit(solution)/shard_map/all_gather | solution.py:449
  102.9 0.7 copy-start.3
  105.9 3.8 %copy-start = (f32[5,6,32,128]{3,2,1,0:T(8,128)S(1)}, f32[5,6,32,128]{3,2,1,0:T(8,128)}, u32[]{:S(2)}) copy-start(f32[5,6,32,128]{3,2,1,0:T(8,128)} %shard_map.40) | copy-start | bytes 1474564
  105.9 54.7 %all-to-all-start.2 = ((f32[8,512,128]{2,1,0:T(8,128)}), f32[8,512,128]{2,1,0:T(8,128)S(1)}, u32[]{:S(2)}, u32[]{:S(2)}) async-start(f32[8,512,128]{2,1,0:T(8,128)} %shard_map.37), calls=%async_computation.2 | async-start | bytes 4194304 | tf_op jit(solution)/shard_map/all_to_all | solution.py:452
  109.7 16.4 %collective-permute-start.3 = (f32[5,3,32,128]{3,2,1,0:T(8,128)S(1)}, f32[5,3,32,128]{3,2,1,0:T(8,128)S(1)}, u32[]{:S(2)}, u32[]{:S(2)}) collective-permute-start(f32[5,3,32,128]{3,2,1,0:T(8,128)S(1)} %get-tuple-element.39), channel_id=1, source_target_pairs={{0,0},{1,8},{2,16},{3,24},{4,32},{5,40},{6,48},{7,56},{8,64},{9,72... | collective-permute-start | bytes 737288 | tf_op jit(solution)/shard_map/ppermute | solution.py:467
  115.5 20.4 %collective-permute-start.4 = (f32[5,3,32,128]{3,2,1,0:T(8,128)S(1)}, f32[5,3,32,128]{3,2,1,0:T(8,128)S(1)}, u32[]{:S(2)}, u32[]{:S(2)}) collective-permute-start(f32[5,3,32,128]{3,2,1,0:T(8,128)S(1)} %get-tuple-element.40), channel_id=1, source_target_pairs={{0,8},{1,0},{2,24},{3,16},{4,40},{5,32},{6,56},{7,48},{8,72},{9,64... | collective-permute-start | bytes 737288 | tf_op jit(solution)/shard_map/ppermute | solution.py:468
  163.0 89.1 %all-to-all-start.3 = ((f32[8,2,5,3,32,128]{5,4,3,2,1,0:T(8,128)}), f32[8,2,5,3,32,128]{5,4,3,2,1,0:T(8,128)}, u32[]{:S(2)}, u32[]{:S(2)}) async-start(f32[8,2,5,3,32,128]{5,4,3,2,1,0:T(8,128)} %broadcast_in_dim.2), calls=%async_computation.3 | async-start | bytes 7864320 | tf_op jit(solution)/shard_map/all_to_all | solution.py:473
  181.8 68.2 %collective-permute-start.2 = (f32[6,512,128]{2,1,0:T(8,128)}, f32[6,512,128]{2,1,0:T(8,128)S(1)}, u32[]{:S(2)}, u32[]{:S(2)}) collective-permute-start(f32[6,512,128]{2,1,0:T(8,128)} %dynamic-slice_dynamic-update-slice_fusion), channel_id=1, source_target_pairs={{1,4},{2,7},{3,10},{4,13},{5,0},{6,3},{7,6},{8,9},{9,12},{10,15},{... | collective-permute-start | bytes 4718600 | tf_op jit(solution)/shard_map/ppermute | solution.py:474
  250.0 13.5 %copy-start.4 = (f32[6,512,128]{2,1,0:T(8,128)}, f32[6,512,128]{2,1,0:T(8,128)S(1)}, u32[]{:S(2)}) copy-start(f32[6,512,128]{2,1,0:T(8,128)S(1)} %collective-permute-done.2.child_1) | copy-start | bytes 4718596
  250.0 70.6 %collective-permute-start.6 = (f32[6,512,128]{2,1,0:T(8,128)S(1)}, f32[6,512,128]{2,1,0:T(8,128)S(1)}, u32[]{:S(2)}, u32[]{:S(2)}) collective-permute-start(f32[6,512,128]{2,1,0:T(8,128)S(1)} %collective-permute-done.2.child_1), channel_id=1, source_target_pairs={{0,1},{1,2},{2,3},{3,4},{4,5},{5,6},{6,7},{7,8},{8,9},{9,10},{10,1... | collective-permute-start | bytes 4718600 | tf_op jit(solution)/shard_map/ppermute | solution.py:496
  250.1 70.5 %collective-permute-start.5 = (f32[6,512,128]{2,1,0:T(8,128)S(1)}, f32[6,512,128]{2,1,0:T(8,128)}, u32[]{:S(2)}, u32[]{:S(2)}) collective-permute-start(f32[6,512,128]{2,1,0:T(8,128)S(1)} %collective-permute-done.2.child_1), channel_id=1, source_target_pairs={{0,15},{1,0},{2,1},{3,2},{4,3},{5,4},{6,5},{7,6},{8,7},{9,8},{10,9... | collective-permute-start | bytes 4718600 | tf_op jit(solution)/shard_map/ppermute | solution.py:497
  320.6 1.2 copy-start.5
Sparse Core Ops, SparseCore 0:
  89.6 71.2 all-gather.7
  163.1 139.8 all-gather.5

commit v7 on v5

--- a/solution.py
+++ b/solution.py
@@ -34,8 +34,21 @@
     return chosen
 
 
-def residue_of(row, e):
-    return (3 * row + 4 + e) % 4
+def routed_from(meta, n):
+    flip, d = n // 3, n % 3
+    row = meta[32]
+    residue = (3 * (row + 8 - d)) % 4
+    parity = ((row + 16 - 3 * residue - d) // 4) % 2
+    child = (parity + flip) % 2
+    first = 4 * parity + residue
+    second = first + 8
+    is_first = meta[child * 16 + first] == 3 * first + d
+    is_second = meta[child * 16 + second] == 3 * second + d
+    block = jnp.where(is_first, first, second)
+    return child, jnp.logical_or(is_first, is_second), (3 * block + d) // 8
+
+
+ROUTED = (1, 4, 0, 3, 2, 5)
 
 
 def pick_kernel(meta, parts_ref, out_ref):
@@ -43,10 +56,6 @@
         turn = turn_for(meta, target_row)
         for v in range(2):
             out_ref[target_row, v] = parts_ref[v, turn]
-
-
-def copy_kernel(meta, block_ref, out_ref):
-    out_ref[...] = block_ref[...]
 
 
 def assemble_kernel(meta, first_ref, rest_ref, got_ref, out_ref):
@@ -345,9 +354,8 @@
     step = pl.program_id(0)
     row, col = meta[32], meta[33]
     routes = []
-    for child in range(2):
-        for e in range(3):
-            routes.append((child, *route_of(meta, child, residue_of(row, e))))
+    for n in ROUTED:
+        routes.append(routed_from(meta, n))
 
     for a in range(ROWS_STEP):
         slot = step * ROWS_STEP + a
@@ -442,22 +450,14 @@
     lead = front[:, :, 0].reshape(6, 16, 32, LANES)
     child = children.reshape(4, 16, 32, LANES)
 
-    picked = pl.pallas_call(
-        copy_kernel,
-        grid_spec=pltpu.PrefetchScalarGridSpec(
-            num_scalar_prefetch=1,
-            grid=(8,),
-            in_specs=[pl.BlockSpec((1, 512, LANES), lambda t, meta: (turn_for(meta, t), 0, 0))],
-            out_specs=pl.BlockSpec((1, 512, LANES), lambda t, meta: (t, 0, 0)),
-        ),
-        out_shape=shaped((8, 512, LANES)),
-        cost_estimate=cost(3),
-    )(meta, child.reshape(4, 512, LANES))
+    child_id = row // 4
+    twos = child.reshape(2, 2, 512, LANES)
+    picked = [lax.dynamic_index_in_dim(twos, (child_id + flip) % 2, 1, keepdims=False) for flip in range(2)]
 
     first = jnp.stack([lead[0], child[0]], axis=1)
     first = lax.all_to_all(first, "pcol", 0, 0, tiled=True)
     mine = jnp.concatenate([first[0:KB, 0], first[0:2, 1]], axis=0)
-    mine, picked = lax.optimization_barrier((mine, picked))
+    mine, *picked = lax.optimization_barrier((mine, *picked))
     shed = jnp.where(row == 0, mine[2:5], mine[3:6])
     got_a = lax.ppermute(shed, "prow", [(0, 6), (1, 5)])
     got_b = lax.ppermute(mine[1:2], "prow", [(0, 7)])
@@ -476,15 +476,14 @@
 
     left_parts = lax.all_gather(slices, "pcol")
 
-    lead_parts, slices, picked = lax.optimization_barrier((lead_parts, slices, picked))
-    got = lax.all_to_all(picked, "prow", 0, 0, tiled=True)
-    routed = jnp.stack(
-        [
-            lax.dynamic_index_in_dim(got, 4 * c + residue_of(row, e), 0, keepdims=False)
-            for c in range(2)
-            for e in range(3)
-        ]
-    )
+    lead_parts, slices, *picked = lax.optimization_barrier((lead_parts, slices, *picked))
+    got = []
+    for flip in range(2):
+        perm = []
+        for p in range(8):
+            target = (3 * (p % 4) + 1 + 4 * ((p // 4 + flip) % 2)) % 8
+            perm += [(p * 16 + q, target * 16 + (3 * q + 1) % 16) for q in range(1, 16)]
+        got.append(lax.ppermute(picked[flip], ("prow", "pcol"), perm))
     even, odd = slices[:, 0::2], slices[:, 1::2]
     is_even = col % 2 == 0
     perm_a, perm_b = [], []
@@ -517,8 +516,21 @@
         32,
     )(meta, lead_parts)
 
-    left_over, pairs, routed = lax.optimization_barrier((left_over, pairs, routed))
-    middle = lax.ppermute(routed, "pcol", [(q, (3 * q + 1) % 16) for q in range(1, 16)])
+    left_over, pairs, *got = lax.optimization_barrier((left_over, pairs, *got))
+
+    residue = (3 * (row + 7)) % 4
+    parity = ((row + 15 - 3 * residue) // 4) % 2
+    chosen = {}
+    for flip in range(2):
+        block = 4 * parity + residue
+        origin = meta[(parity + flip) % 2 * 16 + block] - 3 * block
+        for d in range(3):
+            which = jnp.where(origin == d, 0, 1)
+            chosen[flip, d] = lax.dynamic_index_in_dim(got[flip], which, 0, keepdims=False)
+    down = jnp.stack([chosen[0, 0], chosen[1, 0]])
+    up = jnp.stack([chosen[0, 2], chosen[1, 2]])
+    down = lax.ppermute(down, "prow", [(p, (p + 7) % 8) for p in range(8)])
+    up = lax.ppermute(up, "prow", [(p, (p + 1) % 8) for p in range(8)])
     right_parts = lax.all_to_all(pairs, "prow", 0, 0, tiled=True).reshape(16, KB, 3, 32, LANES)
     tail_u, tail_h, tail_l = call(
         chain_tail_kernel,
@@ -528,6 +540,7 @@
         40,
     )(left_over)
 
+    middle = jnp.concatenate([jnp.stack([chosen[0, 1], chosen[1, 1]]), down, up])
     middle, tail_h = lax.optimization_barrier((middle, tail_h))
     below = lax.ppermute(middle, "pcol", [(q, (q + 1) % 16) for q in range(16)])
     above = lax.ppermute(middle, "pcol", [(q, (q + 15) % 16) for q in range(16)])

time: 296 us -> 296 us (level)
  Pallas kernels: 128 us -> 121 us
  waiting for transfers between devices: 36.2 us -> 39.3 us
    all_to_all x1, waiting for transfers between devices: 0.29 us -> 7.18 us  [per_device(): first = lax.all_to_all(first, 'pcol', 0, 0, tiled=True)]
    pallas_call x1 -> x0, Pallas kernels: 6.34 us -> none  [per_device(): pl.pallas_call(copy_kernel, grid_spec=pltpu.PrefetchScalarGridSpec(num_sc...]
    ppermute x1 -> x4, starting transfers between devices: 4.89 us -> 11 us  [the longest x2 7.57 us: per_device(): got.append(lax.ppermute(picked[flip], ('prow', 'pcol'), perm))]
    ppermute x1, starting transfers between devices: 2.47 us -> 6.94 us  [per_device(): below = lax.ppermute(middle, 'pcol', [(q, (q + 1) % 16) for q in range(16)])]
    all_to_all x1 -> x0, starting transfers between devices: 3.75 us -> none  [per_device(): got = lax.all_to_all(picked, 'prow', 0, 0, tiled=True)]
    all_to_all x1, starting transfers between devices: 8.21 us -> 4.9 us  [per_device(): pieces = lax.all_to_all(pieces, 'prow', 0, 0, tiled=True)]
    ppermute x1 -> x4, waiting for transfers between devices: 17.8 us -> 15.1 us  [the longest x1 11.6 us: per_device(): down = lax.ppermute(down, 'prow', [(p, (p + 7) % 8) for p in range(8)])]
  transfers between devices with their start and end apart: 13 -> 15, of which waited for: 6 -> 7; matrix products, arithmetic and copies ran while one was open for 2% -> 3% of each run, Pallas kernels for 36% -> 34%
where the time goes in v7:
time: 296 us; the launch traced here: 293 us
  Pallas kernels  121 us (41%)
  blocking collectives  53.6 us (18%)
  starting transfers between devices  50.8 us (17%)
  waiting for transfers between devices  39.3 us (13%)
  between operations  15.1 us (5%)
  local copies, waits for them, and re-layouts  9.69 us (3%)
  other arithmetic  3.03 us (1%)
    pallas_call x1, Pallas kernels, per_device(): call(chain_tail_kernel, (shaped((TAILS, NB, NB)), shaped((TAILS, NB, NB),...  33.8 us
    pallas_call x1, Pallas kernels, per_device(): call(chain_head_kernel, (shaped((HEADS, NB, NB)), shaped((HEADS, NB, NB),...  31.9 us
    all_to_all x1, blocking collectives, per_device(): rest = lax.all_to_all(rest, 'pcol', 0, 0, tiled=True)  27.1 us
    all_gather x1, blocking collectives, per_device(): chunk = lax.all_gather(chunk, 'pcol')  26.5 us
    pallas_call x1, Pallas kernels, per_device(): pl.pallas_call(schur_kernel, grid=(steps,), out_shape=shaped((9216, LANES...  20.9 us
    pallas_call x1, Pallas kernels, per_device(): pl.pallas_call(left_kernel, grid=(steps,), out_shape=(shaped((1536, 1280)...  17.6 us
    ppermute x1, waiting for transfers between devices, per_device(): down = lax.ppermute(down, 'prow', [(p, (p + 7) % 8) for p in range(8)])  11.6 us
    pallas_call x1, Pallas kernels, per_device(): call(right_kernel, (shaped((768, 1280), BF16), shaped((768, 1280), BF16))...  11.3 us
  transfers between devices with their start and end apart: 15, of which 7 were waited for; matrix products, arithmetic and copies ran while one was open for 3% of the time, Pallas kernels for 34%

profile of v7, /device:TPU:102, one launch (start us, length us, event | category | flops | bytes accessed | tf_op | source)
XLA Modules:
  0.0 292.6 jit_solution(10296990043879522994)
XLA Ops:
  6.5 1.1 slice.61
  7.6 1.1 slice.48
  8.7 0.8 pad_maximum_fusion.2
  9.6 6.9 %all-to-all-start = ((f32[16,2,32,128]{3,2,1,0:T(8,128)}), f32[16,2,32,128]{3,2,1,0:T(8,128)S(1)}, u32[]{:S(2)}, u32[]{:S(2)}) async-start(f32[16,2,32,128]{3,2,1,0:T(8,128)} %pad_maximum_fusion.2), calls=%async_computation | async-start | bytes 1048576 | tf_op jit(solution)/shard_map/all_to_all | solution.py:458
  16.5 0.0 all-gather.8.cloned.1.call-start
  16.6 0.0 copy-done.7
  16.6 0.1 reshape.24
  16.7 0.0 copy-done
  16.7 0.1 dynamic-slice_bitcast_fusion
  16.8 7.2 %all-to-all-done = f32[16,2,32,128]{3,2,1,0:T(8,128)S(1)} async-done(((f32[16,2,32,128]{3,2,1,0:T(8,128)}), f32[16,2,32,128]{3,2,1,0:T(8,128)S(1)}, u32[]{:S(2)}, u32[]{:S(2)}) %all-to-all-start) | async-done | bytes 524320 | tf_op jit(solution)/shard_map/all_to_all | solution.py:458
  24.0 0.0 copy-start.2
  24.0 3.2 %collective-permute-start.1 = (f32[1,32,128]{2,1,0:T(8,128)S(1)}, f32[1,32,128]{2,1,0:T(8,128)S(1)}, u32[]{:S(2)}, u32[]{:S(2)}) collective-permute-start(f32[1,32,128]{2,1,0:T(8,128)S(1)} %slice.56), channel_id=1, source_target_pairs={{0,112},{1,113},{2,114},{3,115},{4,116},{5,117},{6,118},{7,119},{8... | collective-permute-start | bytes 49160 | tf_op jit(solution)/shard_map/ppermute | solution.py:463
  27.2 2.4 collective-permute-start
  29.6 0.6 pad_add_fusion.meta
  30.2 0.0 collective-permute-done.1.got_b_ref
  30.2 1.1 collective-permute-done.got_a_ref
  31.3 0.0 copy-done.2
  31.3 0.0 copy-done.6
  31.3 0.6 copy-done.5
  32.0 1.6 shard_map.37
  33.6 26.5 %all-gather = f32[48,32,128]{2,1,0:T(8,128)} all-gather(f32[3,32,128]{2,1,0:T(8,128)} %shard_map.37), channel_id=2, replica_groups=mesh['prow'=8,'pcol'=16] {'pcol'}, dimensions={0}, use_global_device_ids=true | all-gather | bytes 835584 | tf_op jit(solution)/shard_map/all_gather | solution.py:465
  60.1 0.0 all-gather.8.cloned.1.call-update
  60.1 1.4 slice.64
  61.5 0.2 copy_bitcast_fusion
  61.7 27.1 %all_to_all.20 = f32[16,9,32,128]{3,2,1,0:T(8,128)S(1)} all-to-all(f32[16,9,32,128]{3,2,1,0:T(8,128)S(1)} %copy_bitcast_fusion), channel_id=1, replica_groups=mesh['prow'=8,'pcol'=16] {'pcol'}, dimensions={0} | all-to-all | bytes 4718592 | tf_op jit(solution)/shard_map/all_to_all | solution.py:470
  88.8 0.7 slice.66.parts_ref
  89.5 1.8 shard_map.38
  91.3 4.9 %all-to-all-start.2 = ((f32[8,2,32,128]{3,2,1,0:T(8,128)}), f32[8,2,32,128]{3,2,1,0:T(8,128)}, u32[]{:S(2)}, u32[]{:S(2)}) async-start(f32[8,2,32,128]{3,2,1,0:T(8,128)} %shard_map.38), calls=%async_computation.2 | async-start | bytes 524288 | tf_op jit(solution)/shard_map/all_to_all | solution.py:472
  96.2 0.0 all-gather.6.cloned.1.call-start
  96.2 0.0 copy-done.3
  96.2 0.6 slice.51.first_ref
  96.9 0.8 slice.65.rest_ref
  97.6 6.4 %all-to-all-done.2.got_ref = f32[8,2,32,128]{3,2,1,0:T(8,128)} async-done(((f32[8,2,32,128]{3,2,1,0:T(8,128)}), f32[8,2,32,128]{3,2,1,0:T(8,128)}, u32[]{:S(2)}, u32[]{:S(2)}) %all-to-all-start.2) | async-done | bytes 262176 | tf_op jit(solution)/shard_map/all_to_all | solution.py:472
  104.0 2.2 shard_map.39
  106.2 0.0 all-gather.6.cloned.1.call-update
  106.4 0.7 fusion
  108.4 0.0 all-gather.8.cloned.1.call-done
  108.4 1.1 slice_select_fusion.1
  109.5 3.8 %collective-permute-start.2 = (f32[5,3,32,128]{3,2,1,0:T(8,128)S(1)}, f32[5,3,32,128]{3,2,1,0:T(8,128)S(1)}, u32[]{:S(2)}, u32[]{:S(2)}) collective-permute-start(f32[5,3,32,128]{3,2,1,0:T(8,128)S(1)} %get-tuple-element.67), channel_id=1, source_target_pairs={{0,0},{1,8},{2,16},{3,24},{4,32},{5,40},{6,48},{7,56},{8,64},{9,72... | collective-permute-start | bytes 737288 | tf_op jit(solution)/shard_map/ppermute | solution.py:494
  113.3 4.6 %collective-permute-start.3 = (f32[5,3,32,128]{3,2,1,0:T(8,128)S(1)}, f32[5,3,32,128]{3,2,1,0:T(8,128)S(1)}, u32[]{:S(2)}, u32[]{:S(2)}) collective-permute-start(f32[5,3,32,128]{3,2,1,0:T(8,128)S(1)} %get-tuple-element.68), channel_id=1, source_target_pairs={{0,8},{1,0},{2,24},{3,16},{4,40},{5,32},{6,56},{7,48},{8,72},{9,64... | collective-permute-start | bytes 737288 | tf_op jit(solution)/shard_map/ppermute | solution.py:495
  117.9 1.9 collective-permute-start.4
  119.8 5.7 %collective-permute-start.5 = (f32[2,512,128]{2,1,0:T(8,128)S(1)}, f32[2,512,128]{2,1,0:T(8,128)S(1)}, u32[]{:S(2)}, u32[]{:S(2)}) collective-permute-start(f32[2,512,128]{2,1,0:T(8,128)S(1)} %get-tuple-element.41), channel_id=1, source_target_pairs={{1,84},{2,87},{3,90},{4,93},{5,80},{6,83},{7,86},{8,89},{9,92},{10... | collective-permute-start | bytes 1572872 | tf_op jit(solution)/shard_map/ppermute | solution.py:486
  125.5 31.9 %shard_map.40 = (f32[9,256,256]{2,1,0:T(8,128)}, bf16[9,256,256]{2,1,0:T(8,128)(2,1)}, bf16[9,256,256]{2,1,0:T(8,128)(2,1)}, f32[6,256,256]{2,1,0:T(8,128)}) custom-call(s32[34]{0:T(128)} %pad_add_fusion.meta, f32[8,16,3,32,128]{4,3,2,1,0:T(8,128)} %bitcast.52), custom_call_target="tpu_custom_call" | custom-call | flops 35200000000 | bytes 1048576 | tf_op jit(solution)/shard_map/pallas_call | solution.py:506
  157.4 0.0 collective-permute-done.2
  157.4 0.0 collective-permute-done.3
  157.5 0.0 collective-permute-done.4
  157.5 0.0 collective-permute-done.5
  157.5 2.4 broadcast_in_dim.2
  159.9 7.0 %all-to-all-start.3 = ((f32[8,2,5,3,32,128]{5,4,3,2,1,0:T(8,128)}), f32[8,2,5,3,32,128]{5,4,3,2,1,0:T(8,128)}, u32[]{:S(2)}, u32[]{:S(2)}) async-start(f32[8,2,5,3,32,128]{5,4,3,2,1,0:T(8,128)} %broadcast_in_dim.2), calls=%async_computation.3 | async-start | bytes 7864320 | tf_op jit(solution)/shard_map/all_to_all | solution.py:534
  167.0 0.1 constant_dynamic-slice_fusion.4
  167.1 3.4 %collective-permute-start.6 = (f32[2,512,128]{2,1,0:T(8,128)S(1)}, f32[2,512,128]{2,1,0:T(8,128)S(1)}, u32[]{:S(2)}, u32[]{:S(2)}) collective-permute-start(f32[2,512,128]{2,1,0:T(8,128)S(1)} %pad_maximum_fusion.3), channel_id=1, source_target_pairs={{0,112},{16,0},{32,16},{48,32},{64,48},{80,64},{96,80},{112,96},{1... | collective-permute-start | bytes 1572872 | tf_op jit(solution)/shard_map/ppermute | solution.py:532
  170.6 0.0 collective-permute-start.7
  170.6 33.8 %shard_map.41 = (f32[6,256,256]{2,1,0:T(8,128)}, bf16[6,256,256]{2,1,0:T(8,128)(2,1)}, bf16[6,256,256]{2,1,0:T(8,128)(2,1)}) custom-call(f32[6,256,256]{2,1,0:T(8,128)} %get-tuple-element.44.rest_ref), custom_call_target="tpu_custom_call" | custom-call | flops 44000002048 | bytes 1048576 | tf_op jit(solution)/shard_map/pallas_call | solution.py:535
  204.4 11.6 %collective-permute-done.6 = f32[2,512,128]{2,1,0:T(8,128)S(1)} collective-permute-done((f32[2,512,128]{2,1,0:T(8,128)S(1)}, f32[2,512,128]{2,1,0:T(8,128)S(1)}, u32[]{:S(2)}, u32[]{:S(2)}) %collective-permute-start.6) | collective-permute-done | bytes 524320 | tf_op jit(solution)/shard_map/ppermute | solution.py:532
  216.0 3.4 %collective-permute-done.7 = f32[2,512,128]{2,1,0:T(8,128)S(1)} collective-permute-done((f32[2,512,128]{2,1,0:T(8,128)S(1)}, f32[2,512,128]{2,1,0:T(8,128)S(1)}, u32[]{:S(2)}, u32[]{:S(2)}) %collective-permute-start.7) | collective-permute-done | bytes 524320 | tf_op jit(solution)/shard_map/ppermute | solution.py:533
  219.4 0.1 pad_maximum_fusion.1.child_1
  219.6 6.9 %collective-permute-start.9 = (f32[6,512,128]{2,1,0:T(8,128)S(1)}, f32[6,512,128]{2,1,0:T(8,128)}, u32[]{:S(2)}, u32[]{:S(2)}) collective-permute-start(f32[6,512,128]{2,1,0:T(8,128)S(1)} %pad_maximum_fusion.1.child_1), channel_id=1, source_target_pairs={{0,1},{1,2},{2,3},{3,4},{4,5},{5,6},{6,7},{7,8},{8,9},{9,10},{10,1... | collective-permute-start | bytes 4718600 | tf_op jit(solution)/shard_map/ppermute | solution.py:545
  226.5 0.0 collective-permute-start.8
  226.5 0.0 all-to-all-done.3
  226.5 11.3 %shard_map.43 = (bf16[768,1280]{1,0:T(8,128)(2,1)}, bf16[768,1280]{1,0:T(8,128)(2,1)}) custom-call(f32[16,5,3,32,128]{4,3,2,1,0:T(8,128)} %bitcast.20.parts_ref, bf16[9,256,256]{2,1,0:T(8,128)(2,1)} %get-tuple-element.36.hh_ref, bf16[9,256,256]{2,1,0:T(8,128)(2,1)} %get-tuple-element.37.hl_ref, bf16[6,256,256]{2,1,0:T(8,128)(2,1)} %get-tuple-element.46.th_ref, ...), custom_call_target="tpu_custom_call" | custom-call | flops 13200000000 | bytes 1048576 | tf_op jit(solution)/shard_map/pallas_call | solution.py:548
  237.8 17.6 %shard_map.42 = (bf16[1536,1280]{1,0:T(8,128)(2,1)}, bf16[1536,1280]{1,0:T(8,128)(2,1)}, f32[1536,256]{1,0:T(8,128)}) custom-call(s32[34]{0:T(128)} %pad_add_fusion.meta, f32[16,5,6,32,128]{4,3,2,1,0:T(8,128)} %bitcast.51, bf16[9,256,256]{2,1,0:T(8,128)(2,1)} %get-tuple-element.36.hh_ref, bf16[9,256,256]{2,1,0:T(8,128)(2,1)} %get-tuple-element.37.hl_ref, ...), custom_call_target="tpu_custom_call" | custom-call | flops 22000001024 | bytes 1048576 | tf_op jit(solution)/shard_map/pallas_call | solution.py:562
  255.4 3.9 %collective-permute-done.9.child_2 = f32[6,512,128]{2,1,0:T(8,128)} collective-permute-done((f32[6,512,128]{2,1,0:T(8,128)S(1)}, f32[6,512,128]{2,1,0:T(8,128)}, u32[]{:S(2)}, u32[]{:S(2)}) %collective-permute-start.9) | collective-permute-done | bytes 1572896 | tf_op jit(solution)/shard_map/ppermute | solution.py:545
  259.2 5.6 %collective-permute-done.8.child_0 = f32[6,512,128]{2,1,0:T(8,128)} collective-permute-done((f32[6,512,128]{2,1,0:T(8,128)S(1)}, f32[6,512,128]{2,1,0:T(8,128)}, u32[]{:S(2)}, u32[]{:S(2)}) %collective-permute-start.8) | collective-permute-done | bytes 1572896 | tf_op jit(solution)/shard_map/ppermute | solution.py:546
  264.9 20.9 %shard_map.44 = f32[9216,128]{1,0:T(8,128)} custom-call(s32[34]{0:T(128)} %pad_add_fusion.meta, bf16[1536,1280]{1,0:T(8,128)(2,1)} %get-tuple-element.48.yh, bf16[1536,1280]{1,0:T(8,128)(2,1)} %get-tuple-element.49.yl, f32[1536,256]{1,0:T(8,128)} %get-tuple-element.50.own_ref, bf16[768,1280]{1,0:T(8,128)(2,1)} %get-tuple-element.52.rh_ref, ...), custom_call_target="tpu_custom_call" | custom-call | flops 19800000512 | bytes 1048576 | tf_op jit(solution)/shard_map/pallas_call | solution.py:583
  (19 shorter events, 0.2 us)
Async XLA Ops:
  6.5 10.1 %copy-start = (f32[4,1,256,1,1,256]{5,4,3,2,1,0:T(1,128)S(1)}, f32[4,1,256,1,1,256]{5,4,3,2,1,0:T(1,128)}, u32[]{:S(2)}) copy-start(f32[4,1,256,1,1,256]{5,4,3,2,1,0:T(1,128)} %param.4) | copy-start | bytes 3145732
  6.5 10.1 %copy-start.7 = (s32[2,16]{1,0:T(2,128)S(1)}, s32[2,16]{1,0:T(2,128)}, u32[]{:S(2)}) copy-start(s32[2,16]{1,0:T(2,128)} %param.5) | copy-start | bytes 388
  9.6 14.4 %all-to-all-start = ((f32[16,2,32,128]{3,2,1,0:T(8,128)}), f32[16,2,32,128]{3,2,1,0:T(8,128)S(1)}, u32[]{:S(2)}, u32[]{:S(2)}) async-start(f32[16,2,32,128]{3,2,1,0:T(8,128)} %pad_maximum_fusion.2), calls=%async_computation | async-start | bytes 1048576 | tf_op jit(solution)/shard_map/all_to_all | solution.py:458
  16.5 91.9 %all-gather.8.cloned.1.call-start = ((), (), s32[]{:S(2)}) async-start(), calls=%async_computation.5 | async-start | bytes 7077888 | tf_op jit(solution)/shard_map/all_gather | solution.py:466
  24.0 7.4 %copy-start.2 = (f32[7,32,128]{2,1,0:T(8,128)}, f32[7,32,128]{2,1,0:T(8,128)S(1)}, u32[]{:S(2)}) copy-start(f32[7,32,128]{2,1,0:T(8,128)S(1)} %pad_maximum_fusion.6.mine_ref) | copy-start | bytes 344068
  24.0 6.2 %collective-permute-start.1 = (f32[1,32,128]{2,1,0:T(8,128)S(1)}, f32[1,32,128]{2,1,0:T(8,128)S(1)}, u32[]{:S(2)}, u32[]{:S(2)}) collective-permute-start(f32[1,32,128]{2,1,0:T(8,128)S(1)} %slice.56), channel_id=1, source_target_pairs={{0,112},{1,113},{2,114},{3,115},{4,116},{5,117},{6,118},{7,119},{8... | collective-permute-start | bytes 49160 | tf_op jit(solution)/shard_map/ppermute | solution.py:463
  27.2 4.1 %collective-permute-start = (f32[3,32,128]{2,1,0:T(8,128)S(1)}, f32[3,32,128]{2,1,0:T(8,128)S(1)}, u32[]{:S(2)}, u32[]{:S(2)}) collective-permute-start(f32[3,32,128]{2,1,0:T(8,128)S(1)} %slice_select_fusion.2), channel_id=1, source_target_pairs={{0,96},{16,80},{1,97},{17,81},{2,98},{18,82},{3,99},{19,83},{4,100... | collective-permute-start | bytes 147464 | tf_op jit(solution)/shard_map/ppermute | solution.py:462
  30.2 1.1 copy-start.6
  31.3 0.6 copy-start.5
  89.5 6.7 %copy-start.3 = (f32[7,32,128]{2,1,0:T(8,128)S(1)}, f32[7,32,128]{2,1,0:T(8,128)}, u32[]{:S(2)}) copy-start(f32[7,32,128]{2,1,0:T(8,128)} %copy-done.2) | copy-start | bytes 344068
  91.3 12.7 %all-to-all-start.2 = ((f32[8,2,32,128]{3,2,1,0:T(8,128)}), f32[8,2,32,128]{3,2,1,0:T(8,128)}, u32[]{:S(2)}, u32[]{:S(2)}) async-start(f32[8,2,32,128]{3,2,1,0:T(8,128)} %shard_map.38), calls=%async_computation.2 | async-start | bytes 524288 | tf_op jit(solution)/shard_map/all_to_all | solution.py:472
  96.2 141.6 %all-gather.6.cloned.1.call-start = ((), (), s32[]{:S(2)}) async-start(), calls=%async_computation.4 | async-start | bytes 8355840 | tf_op jit(solution)/shard_map/all_gather | solution.py:477
  97.6 8.7 %copy-start.4 = (s32[34]{0:T(128)S(1)}, s32[34]{0:T(128)}, u32[]{:S(2)}) copy-start(s32[34]{0:T(128)} %pad_add_fusion.meta) | copy-start | bytes 412
  109.5 47.9 %collective-permute-start.2 = (f32[5,3,32,128]{3,2,1,0:T(8,128)S(1)}, f32[5,3,32,128]{3,2,1,0:T(8,128)S(1)}, u32[]{:S(2)}, u32[]{:S(2)}) collective-permute-start(f32[5,3,32,128]{3,2,1,0:T(8,128)S(1)} %get-tuple-element.67), channel_id=1, source_target_pairs={{0,0},{1,8},{2,16},{3,24},{4,32},{5,40},{6,48},{7,56},{8,64},{9,72... | collective-permute-start | bytes 737288 | tf_op jit(solution)/shard_map/ppermute | solution.py:494
  113.3 44.1 %collective-permute-start.3 = (f32[5,3,32,128]{3,2,1,0:T(8,128)S(1)}, f32[5,3,32,128]{3,2,1,0:T(8,128)S(1)}, u32[]{:S(2)}, u32[]{:S(2)}) collective-permute-start(f32[5,3,32,128]{3,2,1,0:T(8,128)S(1)} %get-tuple-element.68), channel_id=1, source_target_pairs={{0,8},{1,0},{2,24},{3,16},{4,40},{5,32},{6,56},{7,48},{8,72},{9,64... | collective-permute-start | bytes 737288 | tf_op jit(solution)/shard_map/ppermute | solution.py:495
  117.9 39.5 %collective-permute-start.4 = (f32[2,512,128]{2,1,0:T(8,128)S(1)}, f32[2,512,128]{2,1,0:T(8,128)S(1)}, u32[]{:S(2)}, u32[]{:S(2)}) collective-permute-start(f32[2,512,128]{2,1,0:T(8,128)S(1)} %get-tuple-element.40), channel_id=1, source_target_pairs={{1,20},{2,23},{3,26},{4,29},{5,16},{6,19},{7,22},{8,25},{9,28},{10... | collective-permute-start | bytes 1572872 | tf_op jit(solution)/shard_map/ppermute | solution.py:486
  119.8 37.6 %collective-permute-start.5 = (f32[2,512,128]{2,1,0:T(8,128)S(1)}, f32[2,512,128]{2,1,0:T(8,128)S(1)}, u32[]{:S(2)}, u32[]{:S(2)}) collective-permute-start(f32[2,512,128]{2,1,0:T(8,128)S(1)} %get-tuple-element.41), channel_id=1, source_target_pairs={{1,84},{2,87},{3,90},{4,93},{5,80},{6,83},{7,86},{8,89},{9,92},{10... | collective-permute-start | bytes 1572872 | tf_op jit(solution)/shard_map/ppermute | solution.py:486
  159.9 66.6 %all-to-all-start.3 = ((f32[8,2,5,3,32,128]{5,4,3,2,1,0:T(8,128)}), f32[8,2,5,3,32,128]{5,4,3,2,1,0:T(8,128)}, u32[]{:S(2)}, u32[]{:S(2)}) async-start(f32[8,2,5,3,32,128]{5,4,3,2,1,0:T(8,128)} %broadcast_in_dim.2), calls=%async_computation.3 | async-start | bytes 7864320 | tf_op jit(solution)/shard_map/all_to_all | solution.py:534
  167.1 48.9 %collective-permute-start.6 = (f32[2,512,128]{2,1,0:T(8,128)S(1)}, f32[2,512,128]{2,1,0:T(8,128)S(1)}, u32[]{:S(2)}, u32[]{:S(2)}) collective-permute-start(f32[2,512,128]{2,1,0:T(8,128)S(1)} %pad_maximum_fusion.3), channel_id=1, source_target_pairs={{0,112},{16,0},{32,16},{48,32},{64,48},{80,64},{96,80},{112,96},{1... | collective-permute-start | bytes 1572872 | tf_op jit(solution)/shard_map/ppermute | solution.py:532
  170.6 48.9 %collective-permute-start.7 = (f32[2,512,128]{2,1,0:T(8,128)S(1)}, f32[2,512,128]{2,1,0:T(8,128)S(1)}, u32[]{:S(2)}, u32[]{:S(2)}) collective-permute-start(f32[2,512,128]{2,1,0:T(8,128)S(1)} %pad_maximum_fusion.4), channel_id=1, source_target_pairs={{0,16},{16,32},{32,48},{48,64},{64,80},{80,96},{96,112},{112,0},{1... | collective-permute-start | bytes 1572872 | tf_op jit(solution)/shard_map/ppermute | solution.py:533
  219.5 18.2 %copy-start.1 = (f32[6,512,128]{2,1,0:T(8,128)}, f32[6,512,128]{2,1,0:T(8,128)S(1)}, u32[]{:S(2)}) copy-start(f32[6,512,128]{2,1,0:T(8,128)S(1)} %pad_maximum_fusion.1.child_1) | copy-start | bytes 4718596
  219.6 39.7 %collective-permute-start.9 = (f32[6,512,128]{2,1,0:T(8,128)S(1)}, f32[6,512,128]{2,1,0:T(8,128)}, u32[]{:S(2)}, u32[]{:S(2)}) collective-permute-start(f32[6,512,128]{2,1,0:T(8,128)S(1)} %pad_maximum_fusion.1.child_1), channel_id=1, source_target_pairs={{0,1},{1,2},{2,3},{3,4},{4,5},{5,6},{6,7},{7,8},{8,9},{9,10},{10,1... | collective-permute-start | bytes 4718600 | tf_op jit(solution)/shard_map/ppermute | solution.py:545
  226.5 38.4 %collective-permute-start.8 = (f32[6,512,128]{2,1,0:T(8,128)S(1)}, f32[6,512,128]{2,1,0:T(8,128)}, u32[]{:S(2)}, u32[]{:S(2)}) collective-permute-start(f32[6,512,128]{2,1,0:T(8,128)S(1)} %pad_maximum_fusion.1.child_1), channel_id=1, source_target_pairs={{0,15},{1,0},{2,1},{3,2},{4,3},{5,4},{6,5},{7,6},{8,7},{9,8},{10,9... | collective-permute-start | bytes 4718600 | tf_op jit(solution)/shard_map/ppermute | solution.py:546
Sparse Core Ops, SparseCore 0:
  60.2 42.7 all-gather.7
  106.4 104.7 all-gather.5

commit v8 on v7

--- a/solution.py
+++ b/solution.py
@@ -495,7 +495,6 @@
     pair_b = lax.ppermute(jnp.where(is_even, odd, even), ("prow", "pcol"), perm_b)
     low_side = col < 8
     pair = jnp.stack([jnp.where(low_side, pair_a, pair_b), jnp.where(low_side, pair_b, pair_a)])
-    pairs = jnp.broadcast_to(pair[None], (8,) + pair.shape)
 
     scratch = [
         pltpu.VMEM((NB, NB), F32),
@@ -516,7 +515,7 @@
         32,
     )(meta, lead_parts)
 
-    left_over, pairs, *got = lax.optimization_barrier((left_over, pairs, *got))
+    left_over, pair, *got = lax.optimization_barrier((left_over, pair, *got))
 
     residue = (3 * (row + 7)) % 4
     parity = ((row + 15 - 3 * residue) // 4) % 2
@@ -531,7 +530,7 @@
     up = jnp.stack([chosen[0, 2], chosen[1, 2]])
     down = lax.ppermute(down, "prow", [(p, (p + 7) % 8) for p in range(8)])
     up = lax.ppermute(up, "prow", [(p, (p + 1) % 8) for p in range(8)])
-    right_parts = lax.all_to_all(pairs, "prow", 0, 0, tiled=True).reshape(16, KB, 3, 32, LANES)
+    right_parts = lax.all_gather(pair, "prow").reshape(16, KB, 3, 32, LANES)
     tail_u, tail_h, tail_l = call(
         chain_tail_kernel,
         (shaped((TAILS, NB, NB)), shaped((TAILS, NB, NB), BF16), shaped((TAILS, NB, NB), BF16)),

time: 296 us -> 320 us (1.081)
  waiting for transfers between devices: 39.3 us -> 66.2 us
    all_gather x1, waiting for transfers between devices: 0.01 us -> 38.4 us  [per_device(): left_parts = lax.all_gather(slices, 'pcol')]
    all_gather x0 -> x1, waiting for transfers between devices: none -> 13.5 us  [per_device(): right_parts = lax.all_gather(pair, 'prow').reshape(16, KB, 3, 32, LANES)]
    ppermute x1, waiting for transfers between devices: 11.6 us -> 0.01 us  [per_device(): down = lax.ppermute(down, 'prow', [(p, (p + 7) % 8) for p in range(8)])]
    all_to_all x1 -> x0, starting transfers between devices: 7.05 us -> none  [per_device(): lax.all_to_all(pairs, 'prow', 0, 0, tiled=True)]
    ppermute x1, waiting for transfers between devices: 5.63 us -> 0.01 us  [per_device(): lax.ppermute(middle, 'pcol', [(q, (q + 15) % 16) for q in range(16)])]
    ppermute x1, waiting for transfers between devices: 3.86 us -> 0.01 us  [per_device(): below = lax.ppermute(middle, 'pcol', [(q, (q + 1) % 16) for q in range(16)])]
    ppermute x1, waiting for transfers between devices: 3.44 us -> 0.01 us  [per_device(): up = lax.ppermute(up, 'prow', [(p, (p + 1) % 8) for p in range(8)])]
  transfers between devices with their start and end apart: 15 -> 15, of which waited for: 7 -> 5; matrix products, arithmetic and copies ran while one was open for 3% -> 2% of each run, Pallas kernels for 34% -> 31%
where the time goes in v8:
time: 320 us; the launch traced here: 317 us
  Pallas kernels  121 us (38%)
  waiting for transfers between devices  66.2 us (21%)
  blocking collectives  52.3 us (16%)
  starting transfers between devices  49.9 us (16%)
  between operations  14.8 us (5%)
  local copies, waits for them, and re-layouts  9.04 us (3%)
  other arithmetic  3.84 us (1%)
    all_gather x1, waiting for transfers between devices, per_device(): left_parts = lax.all_gather(slices, 'pcol')  38.4 us
    pallas_call x1, Pallas kernels, per_device(): call(chain_tail_kernel, (shaped((TAILS, NB, NB)), shaped((TAILS, NB, NB),...  33.7 us
    pallas_call x1, Pallas kernels, per_device(): call(chain_head_kernel, (shaped((HEADS, NB, NB)), shaped((HEADS, NB, NB),...  32.1 us
    all_to_all x1, blocking collectives, per_device(): rest = lax.all_to_all(rest, 'pcol', 0, 0, tiled=True)  26.2 us
    all_gather x1, blocking collectives, per_device(): chunk = lax.all_gather(chunk, 'pcol')  26.1 us
    pallas_call x1, Pallas kernels, per_device(): pl.pallas_call(schur_kernel, grid=(steps,), out_shape=shaped((9216, LANES...  20.8 us
    pallas_call x1, Pallas kernels, per_device(): pl.pallas_call(left_kernel, grid=(steps,), out_shape=(shaped((1536, 1280)...  17.6 us
    all_gather x1, waiting for transfers between devices, per_device(): right_parts = lax.all_gather(pair, 'prow').reshape(16, KB, 3, 32, LANES)  13.5 us
  transfers between devices with their start and end apart: 15, of which 5 were waited for; matrix products, arithmetic and copies ran while one was open for 2% of the time, Pallas kernels for 31%

profile of v8, /device:TPU:102, one launch (start us, length us, event | category | flops | bytes accessed | tf_op | source)
XLA Modules:
  0.0 317.1 jit_solution(1310873929288590175)
XLA Ops:
  6.5 1.2 slice.48
  7.8 1.0 slice.61
  8.7 0.8 pad_maximum_fusion.2
  9.6 6.9 %all-to-all-start = ((f32[16,2,32,128]{3,2,1,0:T(8,128)}), f32[16,2,32,128]{3,2,1,0:T(8,128)S(1)}, u32[]{:S(2)}, u32[]{:S(2)}) async-start(f32[16,2,32,128]{3,2,1,0:T(8,128)} %pad_maximum_fusion.2), calls=%async_computation | async-start | bytes 1048576 | tf_op jit(solution)/shard_map/all_to_all | solution.py:458
  16.5 0.0 all-gather.10.cloned.1.call-start
  16.6 0.1 reshape.23
  16.7 0.0 copy-done
  16.7 0.1 dynamic-slice_bitcast_fusion
  16.8 7.2 %all-to-all-done = f32[16,2,32,128]{3,2,1,0:T(8,128)S(1)} async-done(((f32[16,2,32,128]{3,2,1,0:T(8,128)}), f32[16,2,32,128]{3,2,1,0:T(8,128)S(1)}, u32[]{:S(2)}, u32[]{:S(2)}) %all-to-all-start) | async-done | bytes 524320 | tf_op jit(solution)/shard_map/all_to_all | solution.py:458
  24.0 4.9 %collective-permute-start = (f32[3,32,128]{2,1,0:T(8,128)S(1)}, f32[3,32,128]{2,1,0:T(8,128)S(1)}, u32[]{:S(2)}, u32[]{:S(2)}) collective-permute-start(f32[3,32,128]{2,1,0:T(8,128)S(1)} %slice_select_fusion.2), channel_id=1, source_target_pairs={{0,96},{16,80},{1,97},{17,81},{2,98},{18,82},{3,99},{19,83},{4,100... | collective-permute-start | bytes 147464 | tf_op jit(solution)/shard_map/ppermute | solution.py:462
  28.9 1.3 collective-permute-start.1
  30.2 0.7 pad_add_fusion.meta
  30.9 0.8 collective-permute-done.1.got_b_ref
  31.7 0.0 collective-permute-done.got_a_ref
  31.7 0.0 copy-done.2
  31.7 0.6 copy-done.7
  32.3 0.6 copy-done.6
  32.9 1.6 shard_map.37
  34.5 26.1 %all-gather = f32[48,32,128]{2,1,0:T(8,128)} all-gather(f32[3,32,128]{2,1,0:T(8,128)} %shard_map.37), channel_id=2, replica_groups=mesh['prow'=8,'pcol'=16] {'pcol'}, dimensions={0}, use_global_device_ids=true | all-gather | bytes 835584 | tf_op jit(solution)/shard_map/all_gather | solution.py:465
  60.6 0.0 all-gather.10.cloned.1.call-update
  60.6 1.4 slice.64
  62.0 0.2 copy_bitcast_fusion
  62.2 26.2 %all_to_all.15 = f32[16,9,32,128]{3,2,1,0:T(8,128)S(1)} all-to-all(f32[16,9,32,128]{3,2,1,0:T(8,128)S(1)} %copy_bitcast_fusion), channel_id=1, replica_groups=mesh['prow'=8,'pcol'=16] {'pcol'}, dimensions={0} | all-to-all | bytes 4718592 | tf_op jit(solution)/shard_map/all_to_all | solution.py:470
  88.5 0.7 slice.66.parts_ref
  89.1 1.8 shard_map.38
  90.9 7.9 %all-to-all-start.2 = ((f32[8,2,32,128]{3,2,1,0:T(8,128)}), f32[8,2,32,128]{3,2,1,0:T(8,128)}, u32[]{:S(2)}, u32[]{:S(2)}) async-start(f32[8,2,32,128]{3,2,1,0:T(8,128)} %shard_map.38), calls=%async_computation.2 | async-start | bytes 524288 | tf_op jit(solution)/shard_map/all_to_all | solution.py:472
  98.7 0.0 all-gather.8.cloned.1.call-start
  98.8 0.6 slice.51.first_ref
  99.4 0.8 slice.65.rest_ref
  100.2 6.2 %all-to-all-done.2.got_ref = f32[8,2,32,128]{3,2,1,0:T(8,128)} async-done(((f32[8,2,32,128]{3,2,1,0:T(8,128)}), f32[8,2,32,128]{3,2,1,0:T(8,128)}, u32[]{:S(2)}, u32[]{:S(2)}) %all-to-all-start.2) | async-done | bytes 262176 | tf_op jit(solution)/shard_map/all_to_all | solution.py:472
  106.4 2.3 shard_map.39
  108.7 0.0 all-gather.8.cloned.1.call-update
  108.7 0.0 all-gather.12.cloned.1.call-start
  108.8 0.0 all-gather.10.cloned.1.call-done
  108.8 1.1 slice_select_fusion.1
  109.9 3.8 %collective-permute-start.2 = (f32[5,3,32,128]{3,2,1,0:T(8,128)S(1)}, f32[5,3,32,128]{3,2,1,0:T(8,128)S(1)}, u32[]{:S(2)}, u32[]{:S(2)}) collective-permute-start(f32[5,3,32,128]{3,2,1,0:T(8,128)S(1)} %get-tuple-element.67), channel_id=1, source_target_pairs={{0,0},{1,8},{2,16},{3,24},{4,32},{5,40},{6,48},{7,56},{8,64},{9,72... | collective-permute-start | bytes 737288 | tf_op jit(solution)/shard_map/ppermute | solution.py:494
  113.7 4.7 %collective-permute-start.3 = (f32[5,3,32,128]{3,2,1,0:T(8,128)S(1)}, f32[5,3,32,128]{3,2,1,0:T(8,128)S(1)}, u32[]{:S(2)}, u32[]{:S(2)}) collective-permute-start(f32[5,3,32,128]{3,2,1,0:T(8,128)S(1)} %get-tuple-element.68), channel_id=1, source_target_pairs={{0,8},{1,0},{2,24},{3,16},{4,40},{5,32},{6,56},{7,48},{8,72},{9,64... | collective-permute-start | bytes 737288 | tf_op jit(solution)/shard_map/ppermute | solution.py:495
  118.5 1.9 collective-permute-start.4
  120.4 5.6 %collective-permute-start.5 = (f32[2,512,128]{2,1,0:T(8,128)S(1)}, f32[2,512,128]{2,1,0:T(8,128)S(1)}, u32[]{:S(2)}, u32[]{:S(2)}) collective-permute-start(f32[2,512,128]{2,1,0:T(8,128)S(1)} %get-tuple-element.41), channel_id=1, source_target_pairs={{1,84},{2,87},{3,90},{4,93},{5,80},{6,83},{7,86},{8,89},{9,92},{10... | collective-permute-start | bytes 1572872 | tf_op jit(solution)/shard_map/ppermute | solution.py:486
  126.0 32.1 %shard_map.40 = (f32[9,256,256]{2,1,0:T(8,128)}, bf16[9,256,256]{2,1,0:T(8,128)(2,1)}, bf16[9,256,256]{2,1,0:T(8,128)(2,1)}, f32[6,256,256]{2,1,0:T(8,128)}) custom-call(s32[34]{0:T(128)} %pad_add_fusion.meta, f32[8,16,3,32,128]{4,3,2,1,0:T(8,128)} %bitcast.51), custom_call_target="tpu_custom_call" | custom-call | flops 35200000000 | bytes 1048576 | tf_op jit(solution)/shard_map/pallas_call | solution.py:505
  158.2 0.0 collective-permute-done.2
  158.2 0.0 collective-permute-done.3
  158.2 0.8 pad_maximum_fusion.5
  159.0 0.0 collective-permute-done.4
  159.0 0.0 collective-permute-done.5
  159.0 0.0 all-gather.12.cloned.1.call-update
  159.1 0.7 fusion
  161.1 0.1 constant_dynamic-slice_fusion.4
  161.3 1.1 collective-permute-start.7
  162.5 4.6 %collective-permute-start.6 = (f32[2,512,128]{2,1,0:T(8,128)S(1)}, f32[2,512,128]{2,1,0:T(8,128)S(1)}, u32[]{:S(2)}, u32[]{:S(2)}) collective-permute-start(f32[2,512,128]{2,1,0:T(8,128)S(1)} %pad_maximum_fusion.3), channel_id=1, source_target_pairs={{0,112},{16,0},{32,16},{48,32},{64,48},{80,64},{96,80},{112,96},{1... | collective-permute-start | bytes 1572872 | tf_op jit(solution)/shard_map/ppermute | solution.py:531
  167.0 33.7 %shard_map.41 = (f32[6,256,256]{2,1,0:T(8,128)}, bf16[6,256,256]{2,1,0:T(8,128)(2,1)}, bf16[6,256,256]{2,1,0:T(8,128)(2,1)}) custom-call(f32[6,256,256]{2,1,0:T(8,128)} %get-tuple-element.44.rest_ref), custom_call_target="tpu_custom_call" | custom-call | flops 44000002048 | bytes 1048576 | tf_op jit(solution)/shard_map/pallas_call | solution.py:534
  200.7 0.0 collective-permute-done.7
  200.7 0.0 collective-permute-done.6
  200.7 0.1 pad_maximum_fusion.1.child_1
  200.8 0.1 collective-permute-start.8
  200.9 6.9 %collective-permute-start.9 = (f32[6,512,128]{2,1,0:T(8,128)S(1)}, f32[6,512,128]{2,1,0:T(8,128)}, u32[]{:S(2)}, u32[]{:S(2)}) collective-permute-start(f32[6,512,128]{2,1,0:T(8,128)S(1)} %pad_maximum_fusion.1.child_1), channel_id=1, source_target_pairs={{0,1},{1,2},{2,3},{3,4},{4,5},{5,6},{6,7},{7,8},{8,9},{9,10},{10,1... | collective-permute-start | bytes 4718600 | tf_op jit(solution)/shard_map/ppermute | solution.py:544
  207.8 38.4 %all-gather.8.cloned.1.call-done = f32[80,6,32,128]{3,2,1,0:T(8,128)} async-done(((f32[5,6,32,128]{3,2,1,0:T(8,128)}), f32[80,6,32,128]{3,2,1,0:T(8,128)}) %all-gather.8.cloned.1.call-update) | async-done | bytes 7864336 | tf_op jit(solution)/shard_map/all_gather | solution.py:477
  246.3 17.6 %shard_map.42 = (bf16[1536,1280]{1,0:T(8,128)(2,1)}, bf16[1536,1280]{1,0:T(8,128)(2,1)}, f32[1536,256]{1,0:T(8,128)}) custom-call(s32[34]{0:T(128)} %pad_add_fusion.meta, f32[16,5,6,32,128]{4,3,2,1,0:T(8,128)} %bitcast.50, bf16[9,256,256]{2,1,0:T(8,128)(2,1)} %get-tuple-element.36.hh_ref, bf16[9,256,256]{2,1,0:T(8,128)(2,1)} %get-tuple-element.37.hl_ref, ...), custom_call_target="tpu_custom_call" | custom-call | flops 22000001024 | bytes 1048576 | tf_op jit(solution)/shard_map/pallas_call | solution.py:561
  263.9 13.5 %all-gather.12.cloned.1.call-done.parts_ref = f32[16,5,3,32,128]{4,3,2,1,0:T(8,128)} async-done(((f32[2,5,3,32,128]{4,3,2,1,0:T(8,128)}), f32[16,5,3,32,128]{4,3,2,1,0:T(8,128)}) %all-gather.12.cloned.1.call-update) | async-done | bytes 3932176 | tf_op jit(solution)/shard_map/all_gather | solution.py:533
  277.4 11.2 %shard_map.43 = (bf16[768,1280]{1,0:T(8,128)(2,1)}, bf16[768,1280]{1,0:T(8,128)(2,1)}) custom-call(f32[16,5,3,32,128]{4,3,2,1,0:T(8,128)} %all-gather.12.cloned.1.call-done.parts_ref, bf16[9,256,256]{2,1,0:T(8,128)(2,1)} %get-tuple-element.36.hh_ref, bf16[9,256,256]{2,1,0:T(8,128)(2,1)} %get-tuple-element.37.hl_ref, ...), custom_call_target="tpu_custom_call" | custom-call | flops 13200000000 | bytes 1048576 | tf_op jit(solution)/shard_map/pallas_call | solution.py:547
  288.6 0.0 collective-permute-done.8.child_0
  288.6 0.0 collective-permute-done.9.child_2
  288.6 1.2 copy-done.5
  289.8 20.8 %shard_map.44 = f32[9216,128]{1,0:T(8,128)} custom-call(s32[34]{0:T(128)} %pad_add_fusion.meta, bf16[1536,1280]{1,0:T(8,128)(2,1)} %get-tuple-element.48.yh, bf16[1536,1280]{1,0:T(8,128)(2,1)} %get-tuple-element.49.yl, f32[1536,256]{1,0:T(8,128)} %get-tuple-element.50.own_ref, bf16[768,1280]{1,0:T(8,128)(2,1)} %get-tuple-element.52.rh_ref, ...), custom_call_target="tpu_custom_call" | custom-call | flops 19800000512 | bytes 1048576 | tf_op jit(solution)/shard_map/pallas_call | solution.py:582
  (21 shorter events, 0.2 us)
Async XLA Ops:
  6.5 10.1 %copy-start = (f32[4,1,256,1,1,256]{5,4,3,2,1,0:T(1,128)S(1)}, f32[4,1,256,1,1,256]{5,4,3,2,1,0:T(1,128)}, u32[]{:S(2)}) copy-start(f32[4,1,256,1,1,256]{5,4,3,2,1,0:T(1,128)} %param.4) | copy-start | bytes 3145732
  6.5 10.1 %copy-start.8 = (s32[2,16]{1,0:T(2,128)S(1)}, s32[2,16]{1,0:T(2,128)}, u32[]{:S(2)}) copy-start(s32[2,16]{1,0:T(2,128)} %param.5) | copy-start | bytes 388
  9.6 14.4 %all-to-all-start = ((f32[16,2,32,128]{3,2,1,0:T(8,128)}), f32[16,2,32,128]{3,2,1,0:T(8,128)S(1)}, u32[]{:S(2)}, u32[]{:S(2)}) async-start(f32[16,2,32,128]{3,2,1,0:T(8,128)} %pad_maximum_fusion.2), calls=%async_computation | async-start | bytes 1048576 | tf_op jit(solution)/shard_map/all_to_all | solution.py:458
  16.5 92.3 %all-gather.10.cloned.1.call-start = ((), (), s32[]{:S(2)}) async-start(), calls=%async_computation.4 | async-start | bytes 7077888 | tf_op jit(solution)/shard_map/all_gather | solution.py:466
  24.0 7.7 %copy-start.2 = (f32[7,32,128]{2,1,0:T(8,128)}, f32[7,32,128]{2,1,0:T(8,128)S(1)}, u32[]{:S(2)}) copy-start(f32[7,32,128]{2,1,0:T(8,128)S(1)} %pad_maximum_fusion.6.mine_ref) | copy-start | bytes 344068
  24.0 7.7 %collective-permute-start = (f32[3,32,128]{2,1,0:T(8,128)S(1)}, f32[3,32,128]{2,1,0:T(8,128)S(1)}, u32[]{:S(2)}, u32[]{:S(2)}) collective-permute-start(f32[3,32,128]{2,1,0:T(8,128)S(1)} %slice_select_fusion.2), channel_id=1, source_target_pairs={{0,96},{16,80},{1,97},{17,81},{2,98},{18,82},{3,99},{19,83},{4,100... | collective-permute-start | bytes 147464 | tf_op jit(solution)/shard_map/ppermute | solution.py:462
  28.9 2.7 collective-permute-start.1
  31.7 0.6 copy-start.7
  32.3 0.6 copy-start.6
  89.1 9.7 %copy-start.3 = (f32[7,32,128]{2,1,0:T(8,128)S(1)}, f32[7,32,128]{2,1,0:T(8,128)}, u32[]{:S(2)}) copy-start(f32[7,32,128]{2,1,0:T(8,128)} %copy-done.2) | copy-start | bytes 344068
  90.9 15.5 %all-to-all-start.2 = ((f32[8,2,32,128]{3,2,1,0:T(8,128)}), f32[8,2,32,128]{3,2,1,0:T(8,128)}, u32[]{:S(2)}, u32[]{:S(2)}) async-start(f32[8,2,32,128]{3,2,1,0:T(8,128)} %shard_map.38), calls=%async_computation.2 | async-start | bytes 524288 | tf_op jit(solution)/shard_map/all_to_all | solution.py:472
  98.7 147.5 %all-gather.8.cloned.1.call-start = ((), (), s32[]{:S(2)}) async-start(), calls=%async_computation.3 | async-start | bytes 8355840 | tf_op jit(solution)/shard_map/all_gather | solution.py:477
  108.7 168.7 %all-gather.12.cloned.1.call-start = ((), (), s32[]{:S(2)}) async-start(), calls=%async_computation.5 | async-start | bytes 4423680 | tf_op jit(solution)/shard_map/all_gather | solution.py:533
  109.9 48.3 %collective-permute-start.2 = (f32[5,3,32,128]{3,2,1,0:T(8,128)S(1)}, f32[5,3,32,128]{3,2,1,0:T(8,128)S(1)}, u32[]{:S(2)}, u32[]{:S(2)}) collective-permute-start(f32[5,3,32,128]{3,2,1,0:T(8,128)S(1)} %get-tuple-element.67), channel_id=1, source_target_pairs={{0,0},{1,8},{2,16},{3,24},{4,32},{5,40},{6,48},{7,56},{8,64},{9,72... | collective-permute-start | bytes 737288 | tf_op jit(solution)/shard_map/ppermute | solution.py:494
  113.7 44.4 %collective-permute-start.3 = (f32[5,3,32,128]{3,2,1,0:T(8,128)S(1)}, f32[5,3,32,128]{3,2,1,0:T(8,128)S(1)}, u32[]{:S(2)}, u32[]{:S(2)}) collective-permute-start(f32[5,3,32,128]{3,2,1,0:T(8,128)S(1)} %get-tuple-element.68), channel_id=1, source_target_pairs={{0,8},{1,0},{2,24},{3,16},{4,40},{5,32},{6,56},{7,48},{8,72},{9,64... | collective-permute-start | bytes 737288 | tf_op jit(solution)/shard_map/ppermute | solution.py:495
  118.5 40.6 %collective-permute-start.4 = (f32[2,512,128]{2,1,0:T(8,128)S(1)}, f32[2,512,128]{2,1,0:T(8,128)S(1)}, u32[]{:S(2)}, u32[]{:S(2)}) collective-permute-start(f32[2,512,128]{2,1,0:T(8,128)S(1)} %get-tuple-element.40), channel_id=1, source_target_pairs={{1,20},{2,23},{3,26},{4,29},{5,16},{6,19},{7,22},{8,25},{9,28},{10... | collective-permute-start | bytes 1572872 | tf_op jit(solution)/shard_map/ppermute | solution.py:486
  120.4 38.6 %collective-permute-start.5 = (f32[2,512,128]{2,1,0:T(8,128)S(1)}, f32[2,512,128]{2,1,0:T(8,128)S(1)}, u32[]{:S(2)}, u32[]{:S(2)}) collective-permute-start(f32[2,512,128]{2,1,0:T(8,128)S(1)} %get-tuple-element.41), channel_id=1, source_target_pairs={{1,84},{2,87},{3,90},{4,93},{5,80},{6,83},{7,86},{8,89},{9,92},{10... | collective-permute-start | bytes 1572872 | tf_op jit(solution)/shard_map/ppermute | solution.py:486
  158.2 1.0 copy-start.4
  161.3 39.4 %collective-permute-start.7 = (f32[2,512,128]{2,1,0:T(8,128)S(1)}, f32[2,512,128]{2,1,0:T(8,128)S(1)}, u32[]{:S(2)}, u32[]{:S(2)}) collective-permute-start(f32[2,512,128]{2,1,0:T(8,128)S(1)} %pad_maximum_fusion.4), channel_id=1, source_target_pairs={{0,16},{16,32},{32,48},{48,64},{64,80},{80,96},{96,112},{112,0},{1... | collective-permute-start | bytes 1572872 | tf_op jit(solution)/shard_map/ppermute | solution.py:532
  162.5 38.3 %collective-permute-start.6 = (f32[2,512,128]{2,1,0:T(8,128)S(1)}, f32[2,512,128]{2,1,0:T(8,128)S(1)}, u32[]{:S(2)}, u32[]{:S(2)}) collective-permute-start(f32[2,512,128]{2,1,0:T(8,128)S(1)} %pad_maximum_fusion.3), channel_id=1, source_target_pairs={{0,112},{16,0},{32,16},{48,32},{64,48},{80,64},{96,80},{112,96},{1... | collective-permute-start | bytes 1572872 | tf_op jit(solution)/shard_map/ppermute | solution.py:531
  200.8 63.0 %copy-start.1 = (f32[6,512,128]{2,1,0:T(8,128)}, f32[6,512,128]{2,1,0:T(8,128)S(1)}, u32[]{:S(2)}) copy-start(f32[6,512,128]{2,1,0:T(8,128)S(1)} %pad_maximum_fusion.1.child_1) | copy-start | bytes 4718596
  200.8 87.7 %collective-permute-start.8 = (f32[6,512,128]{2,1,0:T(8,128)S(1)}, f32[6,512,128]{2,1,0:T(8,128)S(1)}, u32[]{:S(2)}, u32[]{:S(2)}) collective-permute-start(f32[6,512,128]{2,1,0:T(8,128)S(1)} %pad_maximum_fusion.1.child_1), channel_id=1, source_target_pairs={{0,15},{1,0},{2,1},{3,2},{4,3},{5,4},{6,5},{7,6},{8,7},{9,8},{10,9... | collective-permute-start | bytes 4718600 | tf_op jit(solution)/shard_map/ppermute | solution.py:545
  200.9 87.7 %collective-permute-start.9 = (f32[6,512,128]{2,1,0:T(8,128)S(1)}, f32[6,512,128]{2,1,0:T(8,128)}, u32[]{:S(2)}, u32[]{:S(2)}) collective-permute-start(f32[6,512,128]{2,1,0:T(8,128)S(1)} %pad_maximum_fusion.1.child_1), channel_id=1, source_target_pairs={{0,1},{1,2},{2,3},{3,4},{4,5},{5,6},{6,7},{7,8},{8,9},{9,10},{10,1... | collective-permute-start | bytes 4718600 | tf_op jit(solution)/shard_map/ppermute | solution.py:544
  288.6 1.2 copy-start.5
Sparse Core Ops, SparseCore 0:
  60.7 41.1 all-gather.9
  108.8 137.4 all-gather.7
  248.0 29.3 all-gather.11

commit v9 on v7

--- a/solution.py
+++ b/solution.py
@@ -196,21 +196,27 @@
 REST = KB - CUT
 
 
-def packed(n, k, i):
-    return k * (2 * n + 1 - k) // 2 + i - k
-
-
-HEADS = packed(KB, CUT, CUT)
-TAILS = packed(REST, REST, REST)
-
-
-def eliminate(n, steps, f_ref, u_ref, th_ref, tl_ref, v_ref, a_s, x_s, u_s):
+def place_head(k, i):
+    if isinstance(i, int):
+        return k + (i if i < CUT else 2 * i - 1)
+    return k + jnp.where(i < CUT, i, 2 * i - 1)
+
+
+def place_tail(k, i):
+    return i * (i + 1) // 2 + k
+
+
+HEADS = CUT * KB - 1
+TAILS = REST * (REST + 1) // 2
+
+
+def eliminate(n, steps, place, f_ref, u_ref, th_ref, tl_ref, v_ref, a_s, x_s, u_s):
     @pl.loop(0, 2 * steps)
     def _(step):
         k = step // 2
         half = step % 2
         kk = k * n + k
-        pk = packed(n, k, k)
+        pk = place(k, k)
 
         @pl.when(half == 0)
         def _():
@@ -245,7 +251,7 @@
             @pl.loop(k + 1, n)
             def _(i):
                 u = dot3(vh, vl, *split(f_ref[k * n + i]), NN)
-                at = packed(n, k, i)
+                at = place(k, i)
                 u_ref[at] = u
                 high, low = split(u)
                 th_ref[at] = high
@@ -253,11 +259,11 @@
 
             @pl.loop(k + 1, n)
             def _(i):
-                at_i = packed(n, k, i)
+                at_i = place(k, i)
 
                 @pl.loop(i, n)
                 def _(j):
-                    at_j = packed(n, k, j)
+                    at_j = place(k, j)
                     f_ref[i * n + j] = f_ref[i * n + j] - dot3(
                         th_ref[at_i], tl_ref[at_i], th_ref[at_j], tl_ref[at_j], TN
                     )
@@ -282,36 +288,43 @@
                     place = (k * KB + i, slice(16 * s, 16 * s + 16), slice(HB * h, HB * h + HB))
                     f_ref[place] = f_ref[place] + take(at, s, h)
 
-    eliminate(KB, CUT, f_ref, u_ref, th_ref, tl_ref, *scratch)
+    eliminate(KB, CUT, place_head, f_ref, u_ref, th_ref, tl_ref, *scratch)
     for i in range(REST):
         for j in range(i, REST):
-            rest_ref[packed(REST, i, j)] = f_ref[(CUT + i) * KB + CUT + j]
+            rest_ref[place_tail(i, j)] = f_ref[(CUT + i) * KB + CUT + j]
 
 
 def chain_tail_kernel(rest_ref, u_ref, th_ref, tl_ref, f_ref, *scratch):
     for i in range(REST):
         for j in range(i, REST):
-            f_ref[i * REST + j] = rest_ref[packed(REST, i, j)]
-    eliminate(REST, REST, f_ref, u_ref, th_ref, tl_ref, *scratch)
+            f_ref[i * REST + j] = rest_ref[place_tail(i, j)]
+    eliminate(REST, REST, place_tail, f_ref, u_ref, th_ref, tl_ref, *scratch)
 
 
 def solve_rows(raw_ref, yh_ref, yl_ref, factors):
     head_h, head_l, tail_h, tail_l = factors
 
-    def factor(m, k):
-        if m < CUT:
-            return head_h[packed(KB, m, k)], head_l[packed(KB, m, k)]
-        at = packed(REST, m - CUT, k - CUT)
-        return tail_h[at], tail_l[at]
+    def column(high, low, start, count):
+        return [ref[start : start + count].reshape(count * NB, NB) for ref in (high, low)]
 
     for k in range(KB):
         at = slice(NB * k, NB * k + NB)
         t = raw_ref[:, at]
-        for m in range(k):
-            am = slice(NB * m, NB * m + NB)
-            t = t - dot3(yh_ref[:, am], yl_ref[:, am], *factor(m, k), NN)
+        if k > 0:
+            count = min(k, CUT)
+            before = slice(0, NB * count)
+            part = column(head_h, head_l, place_head(0, k), count)
+            t = t - dot3(yh_ref[:, before], yl_ref[:, before], *part, NN)
+        if k > CUT:
+            before = slice(NB * CUT, NB * k)
+            part = column(tail_h, tail_l, place_tail(0, k - CUT), k - CUT)
+            t = t - dot3(yh_ref[:, before], yl_ref[:, before], *part, NN)
         high, low = split(t)
-        y = dot3(high, low, *factor(k, k), NN)
+        if k < CUT:
+            own = column(head_h, head_l, place_head(k, k), 1)
+        else:
+            own = column(tail_h, tail_l, place_tail(k - CUT, k - CUT), 1)
+        y = dot3(high, low, *own, NN)
         raw_ref[:, at] = y
         high, low = split(y)
         yh_ref[:, at] = high
@@ -410,13 +423,13 @@
 
                 @pl.when(jnp.logical_and(lower, block_col < CUT))
                 def _():
-                    block = head_ref[jnp.clip(packed(KB, block_col, block_row), 0, HEADS - 1)].T
+                    block = head_ref[jnp.clip(place_head(block_col, block_row), 0, HEADS - 1)].T
                     for h in range(2):
                         put(h, block[:, HB * h : HB * h + HB])
 
                 @pl.when(jnp.logical_and(lower, block_col >= CUT))
                 def _():
-                    at = jnp.clip(packed(REST, block_col - CUT, block_row - CUT), 0, TAILS - 1)
+                    at = jnp.clip(place_tail(block_col - CUT, block_row - CUT), 0, TAILS - 1)
                     block = tail_ref[at].T
                     for h in range(2):
                         put(h, block[:, HB * h : HB * h + HB])
@@ -469,14 +482,9 @@
     rest, chunk = lax.optimization_barrier((rest, chunk))
     rest = lax.all_to_all(rest, "pcol", 0, 0, tiled=True)
     pieces = call(pick_kernel, shaped((8, 2, 32, LANES)), [SM, VM], [])(meta, rest[0:2, 5:9])
+    pieces, *picked = lax.optimization_barrier((pieces, *picked))
     pieces = lax.all_to_all(pieces, "prow", 0, 0, tiled=True)
-    slices = call(assemble_kernel, shaped((KB, 6, 32, LANES)), [SM, VM, VM, VM], [])(
-        meta, mine[0:KB], rest[0:KB, 0:5], pieces
-    )
-
-    left_parts = lax.all_gather(slices, "pcol")
-
-    lead_parts, slices, *picked = lax.optimization_barrier((lead_parts, slices, *picked))
+
     got = []
     for flip in range(2):
         perm = []
@@ -484,6 +492,28 @@
             target = (3 * (p % 4) + 1 + 4 * ((p // 4 + flip) % 2)) % 8
             perm += [(p * 16 + q, target * 16 + (3 * q + 1) % 16) for q in range(1, 16)]
         got.append(lax.ppermute(picked[flip], ("prow", "pcol"), perm))
+    pieces, *got = lax.optimization_barrier((pieces, *got))
+    slices = call(assemble_kernel, shaped((KB, 6, 32, LANES)), [SM, VM, VM, VM], [])(
+        meta, mine[0:KB], rest[0:KB, 0:5], pieces
+    )
+
+    left_parts = lax.all_gather(slices, "pcol")
+
+    lead_parts, slices, *got = lax.optimization_barrier((lead_parts, slices, *got))
+
+    residue = (3 * (row + 7)) % 4
+    parity = ((row + 15 - 3 * residue) // 4) % 2
+    chosen = {}
+    for flip in range(2):
+        block = 4 * parity + residue
+        origin = meta[(parity + flip) % 2 * 16 + block] - 3 * block
+        for d in range(3):
+            which = jnp.where(origin == d, 0, 1)
+            chosen[flip, d] = lax.dynamic_index_in_dim(got[flip], which, 0, keepdims=False)
+    down = jnp.stack([chosen[0, 0], chosen[1, 0]])
+    up = jnp.stack([chosen[0, 2], chosen[1, 2]])
+    down = lax.ppermute(down, "prow", [(p, (p + 7) % 8) for p in range(8)])
+    up = lax.ppermute(up, "prow", [(p, (p + 1) % 8) for p in range(8)])
     even, odd = slices[:, 0::2], slices[:, 1::2]
     is_even = col % 2 == 0
     perm_a, perm_b = [], []
@@ -516,21 +546,7 @@
         32,
     )(meta, lead_parts)
 
-    left_over, pairs, *got = lax.optimization_barrier((left_over, pairs, *got))
-
-    residue = (3 * (row + 7)) % 4
-    parity = ((row + 15 - 3 * residue) // 4) % 2
-    chosen = {}
-    for flip in range(2):
-        block = 4 * parity + residue
-        origin = meta[(parity + flip) % 2 * 16 + block] - 3 * block
-        for d in range(3):
-            which = jnp.where(origin == d, 0, 1)
-            chosen[flip, d] = lax.dynamic_index_in_dim(got[flip], which, 0, keepdims=False)
-    down = jnp.stack([chosen[0, 0], chosen[1, 0]])
-    up = jnp.stack([chosen[0, 2], chosen[1, 2]])
-    down = lax.ppermute(down, "prow", [(p, (p + 7) % 8) for p in range(8)])
-    up = lax.ppermute(up, "prow", [(p, (p + 1) % 8) for p in range(8)])
+    left_over, pairs, down, up = lax.optimization_barrier((left_over, pairs, down, up))
     right_parts = lax.all_to_all(pairs, "prow", 0, 0, tiled=True).reshape(16, KB, 3, 32, LANES)
     tail_u, tail_h, tail_l = call(
         chain_tail_kernel,
@@ -544,14 +560,6 @@
     middle, tail_h = lax.optimization_barrier((middle, tail_h))
     below = lax.ppermute(middle, "pcol", [(q, (q + 1) % 16) for q in range(16)])
     above = lax.ppermute(middle, "pcol", [(q, (q + 15) % 16) for q in range(16)])
-
-    rh, rl = call(
-        right_kernel,
-        (shaped((768, 1280), BF16), shaped((768, 1280), BF16)),
-        [VM] * 5,
-        [pltpu.VMEM((768, 1280), F32)],
-        12,
-    )(right_parts, head_h, head_l, tail_h, tail_l)
 
     rows = NB * ROWS_STEP
     steps = 6 // ROWS_STEP
@@ -576,6 +584,15 @@
         compiler_params=pltpu.CompilerParams(vmem_limit_bytes=VMEM_LIMIT),
         cost_estimate=cost(20),
     )(meta, left_parts, head_h, head_l, tail_h, tail_l)
+
+    right_parts, own = lax.optimization_barrier((right_parts, own))
+    rh, rl = call(
+        right_kernel,
+        (shaped((768, 1280), BF16), shaped((768, 1280), BF16)),
+        [VM] * 5,
+        [pltpu.VMEM((768, 1280), F32)],
+        12,
+    )(right_parts, head_h, head_l, tail_h, tail_l)
 
     whole_right = pl.BlockSpec((768, 1280), lambda g: (0, 0))
     whole_child = pl.BlockSpec((6, 512, LANES), lambda g: (0, 0, 0))

time: 296 us -> 283 us (0.956)
  starting transfers between devices: 50.8 us -> 42.1 us
  waiting for transfers between devices: 39.3 us -> 31.9 us
  Pallas kernels: 121 us -> 124 us
    ppermute x1, waiting for transfers between devices: 11.6 us -> 0.01 us  [per_device(): down = lax.ppermute(down, 'prow', [(p, (p + 7) % 8) for p in range(8)])]
    all_to_all x1, waiting for transfers between devices: 6.36 us -> 13.2 us  [per_device(): pieces = lax.all_to_all(pieces, 'prow', 0, 0, tiled=True)]
    ppermute x1, starting transfers between devices: 6.94 us -> 0.97 us  [per_device(): below = lax.ppermute(middle, 'pcol', [(q, (q + 1) % 16) for q in range(16)])]
    ppermute x2, waiting for transfers between devices: 0.01 us -> 3.55 us  [per_device(): got.append(lax.ppermute(picked[flip], ('prow', 'pcol'), perm))]
    ppermute x1, waiting for transfers between devices: 3.44 us -> 0.01 us  [per_device(): up = lax.ppermute(up, 'prow', [(p, (p + 1) % 8) for p in range(8)])]
    ppermute x1, starting transfers between devices: 3.41 us -> 0.02 us  [per_device(): down = lax.ppermute(down, 'prow', [(p, (p + 7) % 8) for p in range(8)])]
  transfers between devices with their start and end apart: 15 -> 15, of which waited for: 7 -> 6; matrix products, arithmetic and copies ran while one was open for 3% -> 4% of each run, Pallas kernels for 34% -> 36%
where the time goes in v9:
time: 283 us; the launch traced here: 281 us
  Pallas kernels  124 us (44%)
  blocking collectives  53.6 us (19%)
  starting transfers between devices  42.1 us (15%)
  waiting for transfers between devices  31.9 us (11%)
  between operations  15.1 us (5%)
  local copies, waits for them, and re-layouts  10.7 us (4%)
  other arithmetic  3 us (1%)
    pallas_call x1, Pallas kernels, per_device(): call(chain_tail_kernel, (shaped((TAILS, NB, NB)), shaped((TAILS, NB, NB),...  33.8 us
    pallas_call x1, Pallas kernels, per_device(): call(chain_head_kernel, (shaped((HEADS, NB, NB)), shaped((HEADS, NB, NB),...  31.8 us
    all_to_all x1, blocking collectives, per_device(): rest = lax.all_to_all(rest, 'pcol', 0, 0, tiled=True)  27.1 us
    all_gather x1, blocking collectives, per_device(): chunk = lax.all_gather(chunk, 'pcol')  26.5 us
    pallas_call x1, Pallas kernels, per_device(): pl.pallas_call(schur_kernel, grid=(steps,), out_shape=shaped((9216, LANES...  21.3 us
    pallas_call x1, Pallas kernels, per_device(): pl.pallas_call(left_kernel, grid=(steps,), out_shape=(shaped((1536, 1280)...  19.5 us
    all_to_all x1, waiting for transfers between devices, per_device(): pieces = lax.all_to_all(pieces, 'prow', 0, 0, tiled=True)  13.2 us
    pallas_call x1, Pallas kernels, per_device(): call(right_kernel, (shaped((768, 1280), BF16), shaped((768, 1280), BF16))...  12.1 us
  transfers between devices with their start and end apart: 15, of which 6 were waited for; matrix products, arithmetic and copies ran while one was open for 4% of the time, Pallas kernels for 36%

profile of v9, /device:TPU:102, one launch (start us, length us, event | category | flops | bytes accessed | tf_op | source)
XLA Modules:
  0.0 280.5 jit_solution(10868956594903011296)
XLA Ops:
  6.5 1.1 slice.61
  7.6 1.1 slice.48
  8.7 0.8 pad_maximum_fusion.2
  9.6 6.9 %all-to-all-start = ((f32[16,2,32,128]{3,2,1,0:T(8,128)}), f32[16,2,32,128]{3,2,1,0:T(8,128)S(1)}, u32[]{:S(2)}, u32[]{:S(2)}) async-start(f32[16,2,32,128]{3,2,1,0:T(8,128)} %pad_maximum_fusion.2), calls=%async_computation | async-start | bytes 1048576 | tf_op jit(solution)/shard_map/all_to_all | solution.py:471
  16.5 0.0 all-gather.8.cloned.1.call-start
  16.6 0.0 copy-done.10
  16.6 0.1 reshape.24
  16.7 0.0 copy-done
  16.7 1.1 dynamic-slice_bitcast_fusion
  17.7 6.2 %all-to-all-done = f32[16,2,32,128]{3,2,1,0:T(8,128)S(1)} async-done(((f32[16,2,32,128]{3,2,1,0:T(8,128)}), f32[16,2,32,128]{3,2,1,0:T(8,128)S(1)}, u32[]{:S(2)}, u32[]{:S(2)}) %all-to-all-start) | async-done | bytes 524320 | tf_op jit(solution)/shard_map/all_to_all | solution.py:471
  24.0 0.0 copy-start.2
  24.0 3.2 %collective-permute-start.1 = (f32[1,32,128]{2,1,0:T(8,128)S(1)}, f32[1,32,128]{2,1,0:T(8,128)S(1)}, u32[]{:S(2)}, u32[]{:S(2)}) collective-permute-start(f32[1,32,128]{2,1,0:T(8,128)S(1)} %slice.56), channel_id=1, source_target_pairs={{0,112},{1,113},{2,114},{3,115},{4,116},{5,117},{6,118},{7,119},{8... | collective-permute-start | bytes 49160 | tf_op jit(solution)/shard_map/ppermute | solution.py:476
  27.2 2.4 collective-permute-start
  29.6 0.6 pad_add_fusion.meta
  30.2 0.0 collective-permute-done.1.got_b_ref
  30.2 1.1 collective-permute-done.got_a_ref
  31.3 0.0 copy-done.2
  31.3 0.0 copy-done.9
  31.3 0.6 copy-done.8
  32.0 1.6 shard_map.37
  33.6 26.5 %all-gather = f32[48,32,128]{2,1,0:T(8,128)} all-gather(f32[3,32,128]{2,1,0:T(8,128)} %shard_map.37), channel_id=2, replica_groups=mesh['prow'=8,'pcol'=16] {'pcol'}, dimensions={0}, use_global_device_ids=true | all-gather | bytes 835584 | tf_op jit(solution)/shard_map/all_gather | solution.py:478
  60.1 0.0 all-gather.8.cloned.1.call-update
  60.1 1.4 slice.64
  61.5 0.2 copy_bitcast_fusion
  61.7 27.1 %all_to_all.20 = f32[16,9,32,128]{3,2,1,0:T(8,128)S(1)} all-to-all(f32[16,9,32,128]{3,2,1,0:T(8,128)S(1)} %copy_bitcast_fusion), channel_id=1, replica_groups=mesh['prow'=8,'pcol'=16] {'pcol'}, dimensions={0} | all-to-all | bytes 4718592 | tf_op jit(solution)/shard_map/all_to_all | solution.py:483
  88.9 0.7 slice.66.parts_ref
  89.5 1.8 shard_map.38
  91.3 1.9 collective-permute-start.2
  93.2 6.2 %collective-permute-start.3 = (f32[2,512,128]{2,1,0:T(8,128)}, f32[2,512,128]{2,1,0:T(8,128)S(1)}, u32[]{:S(2)}, u32[]{:S(2)}) collective-permute-start(f32[2,512,128]{2,1,0:T(8,128)} %get-tuple-element.45), channel_id=1, source_target_pairs={{1,84},{2,87},{3,90},{4,93},{5,80},{6,83},{7,86},{8,89},{9,92},{10... | collective-permute-start | bytes 1572872 | tf_op jit(solution)/shard_map/ppermute | solution.py:494
  99.5 4.5 %all-to-all-start.2 = ((f32[8,2,32,128]{3,2,1,0:T(8,128)}), f32[8,2,32,128]{3,2,1,0:T(8,128)}, u32[]{:S(2)}, u32[]{:S(2)}) async-start(f32[8,2,32,128]{3,2,1,0:T(8,128)} %shard_map.38), calls=%async_computation.2 | async-start | bytes 524288 | tf_op jit(solution)/shard_map/all_to_all | solution.py:486
  104.0 0.0 all-gather.6.cloned.1.call-start
  104.1 0.6 slice.51.first_ref
  104.7 0.8 slice.65.rest_ref
  105.5 13.2 %all-to-all-done.2.got_ref = f32[8,2,32,128]{3,2,1,0:T(8,128)} async-done(((f32[8,2,32,128]{3,2,1,0:T(8,128)}), f32[8,2,32,128]{3,2,1,0:T(8,128)}, u32[]{:S(2)}, u32[]{:S(2)}) %all-to-all-start.2) | async-done | bytes 262176 | tf_op jit(solution)/shard_map/all_to_all | solution.py:486
  118.7 0.0 collective-permute-done.2
  118.7 3.5 %collective-permute-done.3 = f32[2,512,128]{2,1,0:T(8,128)S(1)} collective-permute-done((f32[2,512,128]{2,1,0:T(8,128)}, f32[2,512,128]{2,1,0:T(8,128)S(1)}, u32[]{:S(2)}, u32[]{:S(2)}) %collective-permute-start.3) | collective-permute-done | bytes 524320 | tf_op jit(solution)/shard_map/ppermute | solution.py:494
  122.2 2.3 shard_map.39
  124.5 0.0 all-gather.6.cloned.1.call-update
  124.6 0.6 fusion
  126.5 0.0 all-gather.8.cloned.1.call-done
  126.6 1.1 slice_select_fusion.1
  127.7 3.0 %collective-permute-start.4 = (f32[5,3,32,128]{3,2,1,0:T(8,128)S(1)}, f32[5,3,32,128]{3,2,1,0:T(8,128)S(1)}, u32[]{:S(2)}, u32[]{:S(2)}) collective-permute-start(f32[5,3,32,128]{3,2,1,0:T(8,128)S(1)} %get-tuple-element.83), channel_id=1, source_target_pairs={{0,0},{1,8},{2,16},{3,24},{4,32},{5,40},{6,48},{7,56},{8,64},{9,72... | collective-permute-start | bytes 737288 | tf_op jit(solution)/shard_map/ppermute | solution.py:524
  130.7 6.2 %collective-permute-start.5 = (f32[5,3,32,128]{3,2,1,0:T(8,128)S(1)}, f32[5,3,32,128]{3,2,1,0:T(8,128)S(1)}, u32[]{:S(2)}, u32[]{:S(2)}) collective-permute-start(f32[5,3,32,128]{3,2,1,0:T(8,128)S(1)} %get-tuple-element.84), channel_id=1, source_target_pairs={{0,8},{1,0},{2,24},{3,16},{4,40},{5,32},{6,56},{7,48},{8,72},{9,64... | collective-permute-start | bytes 737288 | tf_op jit(solution)/shard_map/ppermute | solution.py:525
  136.9 0.1 constant_dynamic-slice_fusion.4
  137.0 0.0 collective-permute-start.6
  137.1 0.5 collective-permute-start.7
  137.6 31.8 %shard_map.40 = (f32[9,256,256]{2,1,0:T(8,128)}, bf16[9,256,256]{2,1,0:T(8,128)(2,1)}, bf16[9,256,256]{2,1,0:T(8,128)(2,1)}, f32[6,256,256]{2,1,0:T(8,128)}) custom-call(s32[34]{0:T(128)} %pad_add_fusion.meta, f32[8,16,3,32,128]{4,3,2,1,0:T(8,128)} %bitcast.52), custom_call_target="tpu_custom_call" | custom-call | flops 35200000000 | bytes 1048576 | tf_op jit(solution)/shard_map/pallas_call | solution.py:536
  169.4 0.0 collective-permute-done.4
  169.4 0.0 collective-permute-done.5
  169.5 0.0 collective-permute-done.6
  169.5 0.0 collective-permute-done.7
  169.5 0.0 copy-start.4
  169.5 2.4 broadcast_in_dim.2
  171.9 5.0 %all-to-all-start.3 = ((f32[8,2,5,3,32,128]{5,4,3,2,1,0:T(8,128)}), f32[8,2,5,3,32,128]{5,4,3,2,1,0:T(8,128)}, u32[]{:S(2)}, u32[]{:S(2)}) async-start(f32[8,2,5,3,32,128]{5,4,3,2,1,0:T(8,128)} %broadcast_in_dim.2), calls=%async_computation.3 | async-start | bytes 7864320 | tf_op jit(solution)/shard_map/all_to_all | solution.py:550
  177.0 33.8 %shard_map.41 = (f32[6,256,256]{2,1,0:T(8,128)}, bf16[6,256,256]{2,1,0:T(8,128)(2,1)}, bf16[6,256,256]{2,1,0:T(8,128)(2,1)}) custom-call(f32[6,256,256]{2,1,0:T(8,128)} %get-tuple-element.58.rest_ref), custom_call_target="tpu_custom_call" | custom-call | flops 44000002048 | bytes 1048576 | tf_op jit(solution)/shard_map/pallas_call | solution.py:551
  210.7 0.1 pad_maximum_fusion.1.child_1
  210.8 1.0 collective-permute-start.9
  211.8 1.1 collective-permute-start.8
  212.9 19.5 %shard_map.42 = (bf16[1536,1280]{1,0:T(8,128)(2,1)}, bf16[1536,1280]{1,0:T(8,128)(2,1)}, f32[1536,256]{1,0:T(8,128)}) custom-call(s32[34]{0:T(128)} %pad_add_fusion.meta, f32[16,5,6,32,128]{4,3,2,1,0:T(8,128)} %bitcast.51, bf16[9,256,256]{2,1,0:T(8,128)(2,1)} %get-tuple-element.50.hh_ref, bf16[9,256,256]{2,1,0:T(8,128)(2,1)} %get-tuple-element.51.hl_ref, ...), custom_call_target="tpu_custom_call" | custom-call | flops 22000001024 | bytes 1048576 | tf_op jit(solution)/shard_map/pallas_call | solution.py:570
  232.4 0.0 all-to-all-done.3
  232.4 12.1 %shard_map.43 = (bf16[768,1280]{1,0:T(8,128)(2,1)}, bf16[768,1280]{1,0:T(8,128)(2,1)}) custom-call(f32[16,5,3,32,128]{4,3,2,1,0:T(8,128)} %bitcast.20.parts_ref, bf16[9,256,256]{2,1,0:T(8,128)(2,1)} %get-tuple-element.50.hh_ref, bf16[9,256,256]{2,1,0:T(8,128)(2,1)} %get-tuple-element.51.hl_ref, bf16[6,256,256]{2,1,0:T(8,128)(2,1)} %get-tuple-element.60.th_ref, ...), custom_call_target="tpu_custom_call" | custom-call | flops 13200000000 | bytes 1048576 | tf_op jit(solution)/shard_map/pallas_call | solution.py:589
  244.5 3.3 %collective-permute-done.9.child_2 = f32[6,512,128]{2,1,0:T(8,128)S(1)} collective-permute-done((f32[6,512,128]{2,1,0:T(8,128)S(1)}, f32[6,512,128]{2,1,0:T(8,128)S(1)}, u32[]{:S(2)}, u32[]{:S(2)}) %collective-permute-start.9) | collective-permute-done | bytes 1572896 | tf_op jit(solution)/shard_map/ppermute | solution.py:561
  247.8 4.5 %collective-permute-done.8.child_0 = f32[6,512,128]{2,1,0:T(8,128)} collective-permute-done((f32[6,512,128]{2,1,0:T(8,128)S(1)}, f32[6,512,128]{2,1,0:T(8,128)}, u32[]{:S(2)}, u32[]{:S(2)}) %collective-permute-start.8) | collective-permute-done | bytes 1572896 | tf_op jit(solution)/shard_map/ppermute | solution.py:562
  252.3 21.3 %shard_map.44 = f32[9216,128]{1,0:T(8,128)} custom-call(s32[34]{0:T(128)} %pad_add_fusion.meta, bf16[1536,1280]{1,0:T(8,128)(2,1)} %get-tuple-element.62.yh, bf16[1536,1280]{1,0:T(8,128)(2,1)} %get-tuple-element.63.yl, f32[1536,256]{1,0:T(8,128)} %get-tuple-element.66.own_ref, bf16[768,1280]{1,0:T(8,128)(2,1)} %get-tuple-element.68.rh_ref, ...), custom_call_target="tpu_custom_call" | custom-call | flops 19800000512 | bytes 1048576 | tf_op jit(solution)/shard_map/pallas_call | solution.py:600
  (25 shorter events, 0.2 us)
Async XLA Ops:
  6.5 10.1 %copy-start = (f32[4,1,256,1,1,256]{5,4,3,2,1,0:T(1,128)S(1)}, f32[4,1,256,1,1,256]{5,4,3,2,1,0:T(1,128)}, u32[]{:S(2)}) copy-start(f32[4,1,256,1,1,256]{5,4,3,2,1,0:T(1,128)} %param.4) | copy-start | bytes 3145732
  6.5 10.1 %copy-start.10 = (s32[2,16]{1,0:T(2,128)S(1)}, s32[2,16]{1,0:T(2,128)}, u32[]{:S(2)}) copy-start(s32[2,16]{1,0:T(2,128)} %param.5) | copy-start | bytes 388
  9.6 14.4 %all-to-all-start = ((f32[16,2,32,128]{3,2,1,0:T(8,128)}), f32[16,2,32,128]{3,2,1,0:T(8,128)S(1)}, u32[]{:S(2)}, u32[]{:S(2)}) async-start(f32[16,2,32,128]{3,2,1,0:T(8,128)} %pad_maximum_fusion.2), calls=%async_computation | async-start | bytes 1048576 | tf_op jit(solution)/shard_map/all_to_all | solution.py:471
  16.5 110.1 %all-gather.8.cloned.1.call-start = ((), (), s32[]{:S(2)}) async-start(), calls=%async_computation.5 | async-start | bytes 7077888 | tf_op jit(solution)/shard_map/all_gather | solution.py:479
  24.0 7.4 %copy-start.2 = (f32[7,32,128]{2,1,0:T(8,128)}, f32[7,32,128]{2,1,0:T(8,128)S(1)}, u32[]{:S(2)}) copy-start(f32[7,32,128]{2,1,0:T(8,128)S(1)} %pad_maximum_fusion.6.mine_ref) | copy-start | bytes 344068
  24.0 6.2 %collective-permute-start.1 = (f32[1,32,128]{2,1,0:T(8,128)S(1)}, f32[1,32,128]{2,1,0:T(8,128)S(1)}, u32[]{:S(2)}, u32[]{:S(2)}) collective-permute-start(f32[1,32,128]{2,1,0:T(8,128)S(1)} %slice.56), channel_id=1, source_target_pairs={{0,112},{1,113},{2,114},{3,115},{4,116},{5,117},{6,118},{7,119},{8... | collective-permute-start | bytes 49160 | tf_op jit(solution)/shard_map/ppermute | solution.py:476
  27.2 4.1 %collective-permute-start = (f32[3,32,128]{2,1,0:T(8,128)S(1)}, f32[3,32,128]{2,1,0:T(8,128)S(1)}, u32[]{:S(2)}, u32[]{:S(2)}) collective-permute-start(f32[3,32,128]{2,1,0:T(8,128)S(1)} %slice_select_fusion.2), channel_id=1, source_target_pairs={{0,96},{16,80},{1,97},{17,81},{2,98},{18,82},{3,99},{19,83},{4,100... | collective-permute-start | bytes 147464 | tf_op jit(solution)/shard_map/ppermute | solution.py:475
  30.2 1.1 copy-start.9
  31.3 0.6 copy-start.8
  89.5 14.5 %copy-start.3 = (f32[7,32,128]{2,1,0:T(8,128)S(1)}, f32[7,32,128]{2,1,0:T(8,128)}, u32[]{:S(2)}) copy-start(f32[7,32,128]{2,1,0:T(8,128)} %copy-done.2) | copy-start | bytes 344068
  91.3 27.4 %collective-permute-start.2 = (f32[2,512,128]{2,1,0:T(8,128)}, f32[2,512,128]{2,1,0:T(8,128)S(1)}, u32[]{:S(2)}, u32[]{:S(2)}) collective-permute-start(f32[2,512,128]{2,1,0:T(8,128)} %get-tuple-element.44), channel_id=1, source_target_pairs={{1,20},{2,23},{3,26},{4,29},{5,16},{6,19},{7,22},{8,25},{9,28},{10... | collective-permute-start | bytes 1572872 | tf_op jit(solution)/shard_map/ppermute | solution.py:494
  93.2 29.0 %collective-permute-start.3 = (f32[2,512,128]{2,1,0:T(8,128)}, f32[2,512,128]{2,1,0:T(8,128)S(1)}, u32[]{:S(2)}, u32[]{:S(2)}) collective-permute-start(f32[2,512,128]{2,1,0:T(8,128)} %get-tuple-element.45), channel_id=1, source_target_pairs={{1,84},{2,87},{3,90},{4,93},{5,80},{6,83},{7,86},{8,89},{9,92},{10... | collective-permute-start | bytes 1572872 | tf_op jit(solution)/shard_map/ppermute | solution.py:494
  99.5 19.2 %all-to-all-start.2 = ((f32[8,2,32,128]{3,2,1,0:T(8,128)}), f32[8,2,32,128]{3,2,1,0:T(8,128)}, u32[]{:S(2)}, u32[]{:S(2)}) async-start(f32[8,2,32,128]{3,2,1,0:T(8,128)} %shard_map.38), calls=%async_computation.2 | async-start | bytes 524288 | tf_op jit(solution)/shard_map/all_to_all | solution.py:486
  104.0 108.9 %all-gather.6.cloned.1.call-start = ((), (), s32[]{:S(2)}) async-start(), calls=%async_computation.4 | async-start | bytes 8355840 | tf_op jit(solution)/shard_map/all_gather | solution.py:500
  105.5 19.1 %copy-start.6 = (s32[34]{0:T(128)S(1)}, s32[34]{0:T(128)}, u32[]{:S(2)}) copy-start(s32[34]{0:T(128)} %pad_add_fusion.meta) | copy-start | bytes 412
  127.7 41.7 %collective-permute-start.4 = (f32[5,3,32,128]{3,2,1,0:T(8,128)S(1)}, f32[5,3,32,128]{3,2,1,0:T(8,128)S(1)}, u32[]{:S(2)}, u32[]{:S(2)}) collective-permute-start(f32[5,3,32,128]{3,2,1,0:T(8,128)S(1)} %get-tuple-element.83), channel_id=1, source_target_pairs={{0,0},{1,8},{2,16},{3,24},{4,32},{5,40},{6,48},{7,56},{8,64},{9,72... | collective-permute-start | bytes 737288 | tf_op jit(solution)/shard_map/ppermute | solution.py:524
  130.7 38.7 %collective-permute-start.5 = (f32[5,3,32,128]{3,2,1,0:T(8,128)S(1)}, f32[5,3,32,128]{3,2,1,0:T(8,128)S(1)}, u32[]{:S(2)}, u32[]{:S(2)}) collective-permute-start(f32[5,3,32,128]{3,2,1,0:T(8,128)S(1)} %get-tuple-element.84), channel_id=1, source_target_pairs={{0,8},{1,0},{2,24},{3,16},{4,40},{5,32},{6,56},{7,48},{8,72},{9,64... | collective-permute-start | bytes 737288 | tf_op jit(solution)/shard_map/ppermute | solution.py:525
  137.0 32.5 %collective-permute-start.6 = (f32[2,512,128]{2,1,0:T(8,128)S(1)}, f32[2,512,128]{2,1,0:T(8,128)S(1)}, u32[]{:S(2)}, u32[]{:S(2)}) collective-permute-start(f32[2,512,128]{2,1,0:T(8,128)S(1)} %pad_maximum_fusion.3), channel_id=1, source_target_pairs={{0,112},{16,0},{32,16},{48,32},{64,48},{80,64},{96,80},{112,96},{1... | collective-permute-start | bytes 1572872 | tf_op jit(solution)/shard_map/ppermute | solution.py:515
  137.1 32.4 %collective-permute-start.7 = (f32[2,512,128]{2,1,0:T(8,128)S(1)}, f32[2,512,128]{2,1,0:T(8,128)S(1)}, u32[]{:S(2)}, u32[]{:S(2)}) collective-permute-start(f32[2,512,128]{2,1,0:T(8,128)S(1)} %pad_maximum_fusion.4), channel_id=1, source_target_pairs={{0,16},{16,32},{32,48},{48,64},{64,80},{80,96},{96,112},{112,0},{1... | collective-permute-start | bytes 1572872 | tf_op jit(solution)/shard_map/ppermute | solution.py:516
  169.5 2.4 copy-start.4
  171.9 60.5 %all-to-all-start.3 = ((f32[8,2,5,3,32,128]{5,4,3,2,1,0:T(8,128)}), f32[8,2,5,3,32,128]{5,4,3,2,1,0:T(8,128)}, u32[]{:S(2)}, u32[]{:S(2)}) async-start(f32[8,2,5,3,32,128]{5,4,3,2,1,0:T(8,128)} %broadcast_in_dim.2), calls=%async_computation.3 | async-start | bytes 7864320 | tf_op jit(solution)/shard_map/all_to_all | solution.py:550
  177.0 33.8 %copy-start.5 = (f32[2,512,128]{2,1,0:T(8,128)S(1)}, f32[2,512,128]{2,1,0:T(8,128)}, u32[]{:S(2)}) copy-start(f32[2,512,128]{2,1,0:T(8,128)} %copy-done.4) | copy-start | bytes 1572868
  210.8 21.6 %copy-start.1 = (f32[6,512,128]{2,1,0:T(8,128)}, f32[6,512,128]{2,1,0:T(8,128)S(1)}, u32[]{:S(2)}) copy-start(f32[6,512,128]{2,1,0:T(8,128)S(1)} %pad_maximum_fusion.1.child_1) | copy-start | bytes 4718596
  210.8 37.0 %collective-permute-start.9 = (f32[6,512,128]{2,1,0:T(8,128)S(1)}, f32[6,512,128]{2,1,0:T(8,128)S(1)}, u32[]{:S(2)}, u32[]{:S(2)}) collective-permute-start(f32[6,512,128]{2,1,0:T(8,128)S(1)} %pad_maximum_fusion.1.child_1), channel_id=1, source_target_pairs={{0,1},{1,2},{2,3},{3,4},{4,5},{5,6},{6,7},{7,8},{8,9},{9,10},{10,1... | collective-permute-start | bytes 4718600 | tf_op jit(solution)/shard_map/ppermute | solution.py:561
  211.8 40.5 %collective-permute-start.8 = (f32[6,512,128]{2,1,0:T(8,128)S(1)}, f32[6,512,128]{2,1,0:T(8,128)}, u32[]{:S(2)}, u32[]{:S(2)}) collective-permute-start(f32[6,512,128]{2,1,0:T(8,128)S(1)} %pad_maximum_fusion.1.child_1), channel_id=1, source_target_pairs={{0,15},{1,0},{2,1},{3,2},{4,3},{5,4},{6,5},{7,6},{8,7},{9,8},{10,9... | collective-permute-start | bytes 4718600 | tf_op jit(solution)/shard_map/ppermute | solution.py:562
  247.8 4.5 %copy-start.7 = (f32[6,512,128]{2,1,0:T(8,128)}, f32[6,512,128]{2,1,0:T(8,128)S(1)}, u32[]{:S(2)}) copy-start(f32[6,512,128]{2,1,0:T(8,128)S(1)} %collective-permute-done.9.child_2) | copy-start | bytes 4718596
Sparse Core Ops, SparseCore 0:
  60.2 47.9 all-gather.7
  124.6 82.8 all-gather.5

commit v10 on v9

--- a/solution.py
+++ b/solution.py
@@ -192,31 +192,27 @@
     return high, (a - high.astype(F32)).astype(BF16)
 
 
-CUT = 2
-REST = KB - CUT
-
-
-def place_head(k, i):
-    if isinstance(i, int):
-        return k + (i if i < CUT else 2 * i - 1)
-    return k + jnp.where(i < CUT, i, 2 * i - 1)
-
-
-def place_tail(k, i):
-    return i * (i + 1) // 2 + k
-
-
-HEADS = CUT * KB - 1
-TAILS = REST * (REST + 1) // 2
-
-
-def eliminate(n, steps, place, f_ref, u_ref, th_ref, tl_ref, v_ref, a_s, x_s, u_s):
+STAGES = ((0, 1), (1, 2), (3, 2))
+
+
+def place(n, k, i):
+    return k * (2 * n + 1 - k) // 2 + i - k
+
+
+def sizes(stage):
+    start, steps = STAGES[stage]
+    n = KB - start
+    rest = n - steps
+    return n, place(n, steps, steps), rest * (rest + 1) // 2
+
+
+def eliminate(n, steps, f_ref, u_ref, th_ref, tl_ref, v_ref, a_s, x_s, u_s):
     @pl.loop(0, 2 * steps)
     def _(step):
         k = step // 2
         half = step % 2
         kk = k * n + k
-        pk = place(k, k)
+        pk = place(n, k, k)
 
         @pl.when(half == 0)
         def _():
@@ -251,7 +247,7 @@
             @pl.loop(k + 1, n)
             def _(i):
                 u = dot3(vh, vl, *split(f_ref[k * n + i]), NN)
-                at = place(k, i)
+                at = place(n, k, i)
                 u_ref[at] = u
                 high, low = split(u)
                 th_ref[at] = high
@@ -259,17 +255,23 @@
 
             @pl.loop(k + 1, n)
             def _(i):
-                at_i = place(k, i)
+                at_i = place(n, k, i)
 
                 @pl.loop(i, n)
                 def _(j):
-                    at_j = place(k, j)
+                    at_j = place(n, k, j)
                     f_ref[i * n + j] = f_ref[i * n + j] - dot3(
                         th_ref[at_i], tl_ref[at_i], th_ref[at_j], tl_ref[at_j], TN
                     )
 
 
-def chain_head_kernel(meta, parts_ref, u_ref, th_ref, tl_ref, rest_ref, f_ref, *scratch):
+def hand_on(n, steps, f_ref, rest_ref):
+    for i in range(n - steps):
+        for j in range(i, n - steps):
+            rest_ref[place(n - steps, i, j)] = f_ref[(steps + i) * n + steps + j]
+
+
+def chain_first_kernel(meta, parts_ref, u_ref, th_ref, tl_ref, rest_ref, f_ref, *scratch):
     def take(at, s, h):
         return parts_ref[at[0], s, at[1], pl.ds(h, 16, stride=2), :]
 
@@ -285,53 +287,54 @@
         def _():
             for s in range(16):
                 for h in range(2):
-                    place = (k * KB + i, slice(16 * s, 16 * s + 16), slice(HB * h, HB * h + HB))
-                    f_ref[place] = f_ref[place] + take(at, s, h)
-
-    eliminate(KB, CUT, place_head, f_ref, u_ref, th_ref, tl_ref, *scratch)
-    for i in range(REST):
-        for j in range(i, REST):
-            rest_ref[place_tail(i, j)] = f_ref[(CUT + i) * KB + CUT + j]
-
-
-def chain_tail_kernel(rest_ref, u_ref, th_ref, tl_ref, f_ref, *scratch):
-    for i in range(REST):
-        for j in range(i, REST):
-            f_ref[i * REST + j] = rest_ref[place_tail(i, j)]
-    eliminate(REST, REST, place_tail, f_ref, u_ref, th_ref, tl_ref, *scratch)
+                    place_of = (k * KB + i, slice(16 * s, 16 * s + 16), slice(HB * h, HB * h + HB))
+                    f_ref[place_of] = f_ref[place_of] + take(at, s, h)
+
+    steps = STAGES[0][1]
+    eliminate(KB, steps, f_ref, u_ref, th_ref, tl_ref, *scratch)
+    hand_on(KB, steps, f_ref, rest_ref)
+
+
+def chain_next_kernel(stage, left_ref, u_ref, th_ref, tl_ref, *refs):
+    n, _, rest = sizes(stage)
+    steps = STAGES[stage][1]
+    rest_ref, (f_ref, *scratch) = (refs[0], refs[1:]) if rest else (None, refs)
+    for i in range(n):
+        for j in range(i, n):
+            f_ref[i * n + j] = left_ref[place(n, i, j)]
+    eliminate(n, steps, f_ref, u_ref, th_ref, tl_ref, *scratch)
+    if rest:
+        hand_on(n, steps, f_ref, rest_ref)
+
+
+def stage_of(k):
+    return sum(1 for start, _ in STAGES if start <= k) - 1
 
 
 def solve_rows(raw_ref, yh_ref, yl_ref, factors):
-    head_h, head_l, tail_h, tail_l = factors
-
-    def column(high, low, start, count):
-        return [ref[start : start + count].reshape(count * NB, NB) for ref in (high, low)]
+    def factor(m, k):
+        stage = stage_of(m)
+        start = STAGES[stage][0]
+        at = place(KB - start, m - start, k - start)
+        return factors[2 * stage][at], factors[2 * stage + 1][at]
 
     for k in range(KB):
         at = slice(NB * k, NB * k + NB)
         t = raw_ref[:, at]
-        if k > 0:
-            count = min(k, CUT)
-            before = slice(0, NB * count)
-            part = column(head_h, head_l, place_head(0, k), count)
-            t = t - dot3(yh_ref[:, before], yl_ref[:, before], *part, NN)
-        if k > CUT:
-            before = slice(NB * CUT, NB * k)
-            part = column(tail_h, tail_l, place_tail(0, k - CUT), k - CUT)
-            t = t - dot3(yh_ref[:, before], yl_ref[:, before], *part, NN)
+        for m in range(k):
+            am = slice(NB * m, NB * m + NB)
+            t = t - dot3(yh_ref[:, am], yl_ref[:, am], *factor(m, k), NN)
         high, low = split(t)
-        if k < CUT:
-            own = column(head_h, head_l, place_head(k, k), 1)
-        else:
-            own = column(tail_h, tail_l, place_tail(k - CUT, k - CUT), 1)
-        y = dot3(high, low, *own, NN)
+        y = dot3(high, low, *factor(k, k), NN)
         raw_ref[:, at] = y
         high, low = split(y)
         yh_ref[:, at] = high
         yl_ref[:, at] = low
 
 
-def right_kernel(parts_ref, hh_ref, hl_ref, th_ref, tl_ref, yh_ref, yl_ref, raw):
+def right_kernel(parts_ref, *refs):
+    *factors, yh_ref, yl_ref, raw = refs
+
     @pl.loop(0, 16)
     def _(s):
         for c in range(3):
@@ -340,13 +343,15 @@
                     raw[pl.ds(pl.multiple_of(NB * c + 16 * s, 16), 16), NB * j + HB * h : NB * j + HB * h + HB] = parts_ref[
                         s, j, c, pl.ds(h, 16, stride=2), :
                     ]
-    solve_rows(raw, yh_ref, yl_ref, (hh_ref, hl_ref, th_ref, tl_ref))
+    solve_rows(raw, yh_ref, yl_ref, factors)
 
 
 ROWS_STEP = 2
 
 
-def left_kernel(meta, parts_ref, hh_ref, hl_ref, th_ref, tl_ref, yh_ref, yl_ref, own_ref, raw):
+def left_kernel(meta, parts_ref, *refs):
+    *factors, yh_ref, yl_ref, own_ref, raw = refs
+
     @pl.loop(0, 16)
     def _(s):
         for a in range(ROWS_STEP):
@@ -355,7 +360,7 @@
                     raw[pl.ds(pl.multiple_of(NB * a + 16 * s, 16), 16), NB * j + HB * h : NB * j + HB * h + HB] = parts_ref[
                         s, j, a, pl.ds(h, 16, stride=2), :
                     ]
-    solve_rows(raw, yh_ref, yl_ref, (hh_ref, hl_ref, th_ref, tl_ref))
+    solve_rows(raw, yh_ref, yl_ref, factors)
     for j in range(KB):
 
         @pl.when(meta[33] == j)
@@ -363,15 +368,18 @@
             own_ref[...] = raw[:, NB * j : NB * j + NB]
 
 
-def schur_kernel(meta, yh, yl, own_ref, rh_ref, rl_ref, head_ref, tail_ref, parent_ref, child_0, child_1, child_2, out_ref):
+SCHUR_STEP = 1
+
+
+def schur_kernel(meta, yh, yl, own_ref, rh_ref, rl_ref, u_0, u_1, u_2, parent_ref, child_0, child_1, child_2, out_ref):
     step = pl.program_id(0)
     row, col = meta[32], meta[33]
     routes = []
     for n in ROUTED:
         routes.append(routed_from(meta, n))
 
-    for a in range(ROWS_STEP):
-        slot = step * ROWS_STEP + a
+    for a in range(SCHUR_STEP):
+        slot = step * SCHUR_STEP + a
         block_row = row + 8 * slot
         rows = slice(NB * a, NB * a + NB)
         for c in range(3):
@@ -420,19 +428,16 @@
                         put(h, jnp.zeros((NB, HB), F32))
 
                 lower = jnp.logical_and(in_lead, jnp.logical_not(upper))
-
-                @pl.when(jnp.logical_and(lower, block_col < CUT))
-                def _():
-                    block = head_ref[jnp.clip(place_head(block_col, block_row), 0, HEADS - 1)].T
-                    for h in range(2):
-                        put(h, block[:, HB * h : HB * h + HB])
-
-                @pl.when(jnp.logical_and(lower, block_col >= CUT))
-                def _():
-                    at = jnp.clip(place_tail(block_col - CUT, block_row - CUT), 0, TAILS - 1)
-                    block = tail_ref[at].T
-                    for h in range(2):
-                        put(h, block[:, HB * h : HB * h + HB])
+                for stage, u_ref in enumerate((u_0, u_1, u_2)):
+                    start, steps = STAGES[stage]
+                    inside = jnp.logical_and(block_col >= start, block_col < start + steps)
+
+                    @pl.when(jnp.logical_and(lower, inside))
+                    def _():
+                        n, count, _ = sizes(stage)
+                        block = u_ref[jnp.clip(place(n, block_col - start, block_row - start), 0, count - 1)].T
+                        for h in range(2):
+                            put(h, block[:, HB * h : HB * h + HB])
 
 
 def cost(microseconds):
@@ -492,14 +497,30 @@
             target = (3 * (p % 4) + 1 + 4 * ((p // 4 + flip) % 2)) % 8
             perm += [(p * 16 + q, target * 16 + (3 * q + 1) % 16) for q in range(1, 16)]
         got.append(lax.ppermute(picked[flip], ("prow", "pcol"), perm))
-    pieces, *got = lax.optimization_barrier((pieces, *got))
+    scratch = [
+        pltpu.VMEM((NB, NB), F32),
+        pltpu.VMEM((HB, HB), F32),
+        pltpu.VMEM((HB, HB), F32),
+        pltpu.VMEM((HB, HB), F32),
+    ]
+
+    def chain_shapes(stage):
+        _, count, rest = sizes(stage)
+        shapes = (shaped((count, NB, NB)), shaped((count, NB, NB), BF16), shaped((count, NB, NB), BF16))
+        return shapes + ((shaped((rest, NB, NB)),) if rest else ())
+
+    def chain_scratch(stage):
+        return [pltpu.VMEM((sizes(stage)[0] ** 2, NB, NB), F32)] + scratch
+
+    u_0, h_0, l_0, left_over = call(chain_first_kernel, chain_shapes(0), [SM, VM], chain_scratch(0), 18)(meta, lead_parts)
+    pieces, left_over, *got = lax.optimization_barrier((pieces, left_over, *got))
     slices = call(assemble_kernel, shaped((KB, 6, 32, LANES)), [SM, VM, VM, VM], [])(
         meta, mine[0:KB], rest[0:KB, 0:5], pieces
     )
 
     left_parts = lax.all_gather(slices, "pcol")
 
-    lead_parts, slices, *got = lax.optimization_barrier((lead_parts, slices, *got))
+    left_over, slices, *got = lax.optimization_barrier((left_over, slices, *got))
 
     residue = (3 * (row + 7)) % 4
     parity = ((row + 15 - 3 * residue) // 4) % 2
@@ -527,44 +548,23 @@
     pair = jnp.stack([jnp.where(low_side, pair_a, pair_b), jnp.where(low_side, pair_b, pair_a)])
     pairs = jnp.broadcast_to(pair[None], (8,) + pair.shape)
 
-    scratch = [
-        pltpu.VMEM((NB, NB), F32),
-        pltpu.VMEM((HB, HB), F32),
-        pltpu.VMEM((HB, HB), F32),
-        pltpu.VMEM((HB, HB), F32),
-    ]
-    head_u, head_h, head_l, left_over = call(
-        chain_head_kernel,
-        (
-            shaped((HEADS, NB, NB)),
-            shaped((HEADS, NB, NB), BF16),
-            shaped((HEADS, NB, NB), BF16),
-            shaped((TAILS, NB, NB)),
-        ),
-        [SM, VM],
-        [pltpu.VMEM((KB * KB, NB, NB), F32)] + scratch,
-        32,
-    )(meta, lead_parts)
+    u_1, h_1, l_1, left_over = call(
+        lambda *refs: chain_next_kernel(1, *refs), chain_shapes(1), [VM], chain_scratch(1), 28
+    )(left_over)
 
     left_over, pairs, down, up = lax.optimization_barrier((left_over, pairs, down, up))
     right_parts = lax.all_to_all(pairs, "prow", 0, 0, tiled=True).reshape(16, KB, 3, 32, LANES)
-    tail_u, tail_h, tail_l = call(
-        chain_tail_kernel,
-        (shaped((TAILS, NB, NB)), shaped((TAILS, NB, NB), BF16), shaped((TAILS, NB, NB), BF16)),
-        [VM],
-        [pltpu.VMEM((REST * REST, NB, NB), F32)] + scratch,
-        40,
-    )(left_over)
+    u_2, h_2, l_2 = call(lambda *refs: chain_next_kernel(2, *refs), chain_shapes(2), [VM], chain_scratch(2), 26)(left_over)
+    factors = (h_0, l_0, h_1, l_1, h_2, l_2)
 
     middle = jnp.concatenate([jnp.stack([chosen[0, 1], chosen[1, 1]]), down, up])
-    middle, tail_h = lax.optimization_barrier((middle, tail_h))
+    middle, *factors = lax.optimization_barrier((middle, *factors))
     below = lax.ppermute(middle, "pcol", [(q, (q + 1) % 16) for q in range(16)])
     above = lax.ppermute(middle, "pcol", [(q, (q + 15) % 16) for q in range(16)])
 
     rows = NB * ROWS_STEP
     steps = 6 // ROWS_STEP
-    whole_head = pl.BlockSpec((HEADS, NB, NB), lambda g: (0, 0, 0))
-    whole_tail = pl.BlockSpec((TAILS, NB, NB), lambda g: (0, 0, 0))
+    whole = [pl.BlockSpec((sizes(stage)[1], NB, NB), lambda g: (0, 0, 0)) for stage in range(3)]
     by_rows = pl.BlockSpec((rows, 1280), lambda g: (g, 0))
     own_rows = pl.BlockSpec((rows, NB), lambda g: (g, 0))
     yh, yl, own = pl.pallas_call(
@@ -574,34 +574,33 @@
         in_specs=[
             SM,
             pl.BlockSpec((16, KB, ROWS_STEP, 32, LANES), lambda g: (0, 0, g, 0, 0)),
-            whole_head,
-            whole_head,
-            whole_tail,
-            whole_tail,
+            *(spec for spec in whole for _ in range(2)),
         ],
         out_specs=(by_rows, by_rows, own_rows),
         scratch_shapes=[pltpu.VMEM((rows, 1280), F32)],
         compiler_params=pltpu.CompilerParams(vmem_limit_bytes=VMEM_LIMIT),
         cost_estimate=cost(20),
-    )(meta, left_parts, head_h, head_l, tail_h, tail_l)
+    )(meta, left_parts, *factors)
 
     right_parts, own = lax.optimization_barrier((right_parts, own))
     rh, rl = call(
         right_kernel,
         (shaped((768, 1280), BF16), shaped((768, 1280), BF16)),
-        [VM] * 5,
+        [VM] * 7,
         [pltpu.VMEM((768, 1280), F32)],
         12,
-    )(right_parts, head_h, head_l, tail_h, tail_l)
+    )(right_parts, *factors)
 
     whole_right = pl.BlockSpec((768, 1280), lambda g: (0, 0))
     whole_child = pl.BlockSpec((6, 512, LANES), lambda g: (0, 0, 0))
-    front_rows = pl.BlockSpec((1536 * ROWS_STEP, LANES), lambda g: (g, 0))
+    front_rows = pl.BlockSpec((1536 * SCHUR_STEP, LANES), lambda g: (g, 0))
+    y_rows = pl.BlockSpec((NB * SCHUR_STEP, 1280), lambda g: (g, 0))
+    own_block = pl.BlockSpec((NB * SCHUR_STEP, NB), lambda g: (g, 0))
     out = pl.pallas_call(
         schur_kernel,
-        grid=(steps,),
+        grid=(6 // SCHUR_STEP,),
         out_shape=shaped((9216, LANES)),
-        in_specs=[SM, by_rows, by_rows, own_rows, whole_right, whole_right, whole_head, whole_tail, front_rows]
+        in_specs=[SM, y_rows, y_rows, own_block, whole_right, whole_right, *whole, front_rows]
         + [whole_child] * 3,
         out_specs=front_rows,
         compiler_params=pltpu.CompilerParams(vmem_limit_bytes=VMEM_LIMIT),
@@ -613,8 +612,9 @@
         own,
         rh,
         rl,
-        head_u,
-        tail_u,
+        u_0,
+        u_1,
+        u_2,
         parent.reshape(9216, LANES),
         *(x.reshape(6, 512, LANES) for x in (above, middle, below)),
     )

time: 283 us -> 312 us (1.10)
  waiting for transfers between devices: 31.9 us -> 78.1 us
  blocking collectives: 53.6 us -> 26.5 us
  starting transfers between devices: 42.1 us -> 51.1 us
    all_gather x1, waiting for transfers between devices: 0.01 us -> 46.3 us  [per_device(): left_parts = lax.all_gather(slices, 'pcol')]
    all_to_all x1 -> x0, blocking collectives: 27.1 us -> none  [per_device(): rest = lax.all_to_all(rest, 'pcol', 0, 0, tiled=True)]
    all_to_all x0 -> x1, waiting for transfers between devices: none -> 21.9 us  [per_device(): rest = lax.all_to_all(rest, 'pcol', 0, 0, tiled=True)]
    all_to_all x1, waiting for transfers between devices: 13.2 us -> 0.01 us  [per_device(): pieces = lax.all_to_all(pieces, 'prow', 0, 0, tiled=True)]
    all_to_all x0 -> x1, starting transfers between devices: none -> 6.77 us  [per_device(): rest = lax.all_to_all(rest, 'pcol', 0, 0, tiled=True)]
    ppermute x1, waiting for transfers between devices: 4.5 us -> 0.01 us  [per_device(): lax.ppermute(middle, 'pcol', [(q, (q + 15) % 16) for q in range(16)])]
    ppermute x1, starting transfers between devices: 6.19 us -> 2.74 us  [per_device(): lax.ppermute(jnp.where(is_even, odd, even), ('prow', 'pcol'), perm_b)]
    ppermute x1, waiting for transfers between devices: 3.33 us -> 0.01 us  [per_device(): below = lax.ppermute(middle, 'pcol', [(q, (q + 1) % 16) for q in range(16)])]
  transfers between devices with their start and end apart: 15 -> 16, of which waited for: 6 -> 5; matrix products, arithmetic and copies ran while one was open for 4% -> 4% of each run, Pallas kernels for 36% -> 32%
where the time goes in v10:
time: 312 us; the launch traced here: 311 us
  Pallas kernels  124 us (40%)
  waiting for transfers between devices  78.1 us (25%)
  starting transfers between devices  51.1 us (16%)
  blocking collectives  26.5 us (8%)
  between operations  15.2 us (5%)
  local copies, waits for them, and re-layouts  11.9 us (4%)
  other arithmetic  4.41 us (1%)
    all_gather x1, waiting for transfers between devices, per_device(): left_parts = lax.all_gather(slices, 'pcol')  46.3 us
    pallas_call x1, Pallas kernels, per_device(): call(lambda *refs: chain_next_kernel(1, *refs), chain_shapes(1), [VM], ch...  27.3 us
    all_gather x1, blocking collectives, per_device(): chunk = lax.all_gather(chunk, 'pcol')  26.5 us
    pallas_call x1, Pallas kernels, per_device(): call(lambda *refs: chain_next_kernel(2, *refs), chain_shapes(2), [VM], ch...  22 us
    all_to_all x1, waiting for transfers between devices, per_device(): rest = lax.all_to_all(rest, 'pcol', 0, 0, tiled=True)  21.9 us
    pallas_call x1, Pallas kernels, per_device(): pl.pallas_call(schur_kernel, grid=(6 // SCHUR_STEP,), out_shape=shaped((9...  20.4 us
    pallas_call x1, Pallas kernels, per_device(): call(chain_first_kernel, chain_shapes(0), [SM, VM], chain_scratch(0), 18)  19.3 us
    pallas_call x1, Pallas kernels, per_device(): pl.pallas_call(left_kernel, grid=(steps,), out_shape=(shaped((1536, 1280)...  17.7 us
  transfers between devices with their start and end apart: 16, of which 5 were waited for; matrix products, arithmetic and copies ran while one was open for 4% of the time, Pallas kernels for 32%

profile of v10, /device:TPU:102, one launch (start us, length us, event | category | flops | bytes accessed | tf_op | source)
XLA Modules:
  0.0 310.7 jit_solution(5178088060790466104)
XLA Ops:
  6.5 1.1 slice.61
  7.6 1.1 slice.48
  8.7 0.8 pad_maximum_fusion.2
  9.6 6.9 %all-to-all-start = ((f32[16,2,32,128]{3,2,1,0:T(8,128)}), f32[16,2,32,128]{3,2,1,0:T(8,128)S(1)}, u32[]{:S(2)}, u32[]{:S(2)}) async-start(f32[16,2,32,128]{3,2,1,0:T(8,128)} %pad_maximum_fusion.2), calls=%async_computation | async-start | bytes 1048576 | tf_op jit(solution)/shard_map/all_to_all | solution.py:476
  16.5 0.0 all-gather.6.cloned.1.call-start
  16.6 0.1 reshape.24
  16.7 0.0 copy-done
  16.7 1.0 dynamic-slice_bitcast_fusion
  17.7 6.2 %all-to-all-done = f32[16,2,32,128]{3,2,1,0:T(8,128)S(1)} async-done(((f32[16,2,32,128]{3,2,1,0:T(8,128)}), f32[16,2,32,128]{3,2,1,0:T(8,128)S(1)}, u32[]{:S(2)}, u32[]{:S(2)}) %all-to-all-start) | async-done | bytes 524320 | tf_op jit(solution)/shard_map/all_to_all | solution.py:476
  24.0 3.2 %collective-permute-start.1 = (f32[1,32,128]{2,1,0:T(8,128)S(1)}, f32[1,32,128]{2,1,0:T(8,128)S(1)}, u32[]{:S(2)}, u32[]{:S(2)}) collective-permute-start(f32[1,32,128]{2,1,0:T(8,128)S(1)} %slice.56), channel_id=1, source_target_pairs={{0,112},{1,113},{2,114},{3,115},{4,116},{5,117},{6,118},{7,119},{8... | collective-permute-start | bytes 49160 | tf_op jit(solution)/shard_map/ppermute | solution.py:481
  27.2 2.4 collective-permute-start
  29.6 0.6 pad_add_fusion.meta
  30.2 0.0 collective-permute-done.1.got_b_ref
  30.2 1.1 collective-permute-done.got_a_ref
  31.3 0.0 copy-done.2
  31.3 0.6 copy-done.10
  32.0 1.6 shard_map.37
  33.6 26.5 %all-gather = f32[48,32,128]{2,1,0:T(8,128)} all-gather(f32[3,32,128]{2,1,0:T(8,128)} %shard_map.37), channel_id=2, replica_groups=mesh['prow'=8,'pcol'=16] {'pcol'}, dimensions={0}, use_global_device_ids=true | all-gather | bytes 835584 | tf_op jit(solution)/shard_map/all_gather | solution.py:483
  60.1 0.0 all-gather.6.cloned.1.call-update
  60.1 1.4 slice.64
  61.5 1.6 copy_bitcast_fusion
  63.1 6.8 %all-to-all-start.1 = ((f32[16,9,32,128]{3,2,1,0:T(8,128)}), f32[16,9,32,128]{3,2,1,0:T(8,128)S(1)}, u32[]{:S(2)}, u32[]{:S(2)}) async-start(f32[16,9,32,128]{3,2,1,0:T(8,128)} %copy_bitcast_fusion), calls=%async_computation.1 | async-start | bytes 4718592 | tf_op jit(solution)/shard_map/all_to_all | solution.py:488
  69.9 0.6 slice.51.first_ref
  70.5 21.9 %all-to-all-done.1 = f32[16,9,32,128]{3,2,1,0:T(8,128)S(1)} async-done(((f32[16,9,32,128]{3,2,1,0:T(8,128)}), f32[16,9,32,128]{3,2,1,0:T(8,128)S(1)}, u32[]{:S(2)}, u32[]{:S(2)}) %all-to-all-start.1) | async-done | bytes 2359328 | tf_op jit(solution)/shard_map/all_to_all | solution.py:488
  92.4 0.7 slice.66.parts_ref
  93.1 1.8 shard_map.38
  94.8 4.8 %all-to-all-start.2 = ((f32[8,2,32,128]{3,2,1,0:T(8,128)}), f32[8,2,32,128]{3,2,1,0:T(8,128)}, u32[]{:S(2)}, u32[]{:S(2)}) async-start(f32[8,2,32,128]{3,2,1,0:T(8,128)} %shard_map.38), calls=%async_computation.2 | async-start | bytes 524288 | tf_op jit(solution)/shard_map/all_to_all | solution.py:491
  99.6 0.0 all-gather.8.cloned.1.call-start
  99.7 2.8 collective-permute-start.2
  102.5 6.1 %collective-permute-start.3 = (f32[2,512,128]{2,1,0:T(8,128)}, f32[2,512,128]{2,1,0:T(8,128)S(1)}, u32[]{:S(2)}, u32[]{:S(2)}) collective-permute-start(f32[2,512,128]{2,1,0:T(8,128)} %get-tuple-element.56), channel_id=1, source_target_pairs={{1,84},{2,87},{3,90},{4,93},{5,80},{6,83},{7,86},{8,89},{9,92},{10... | collective-permute-start | bytes 1572872 | tf_op jit(solution)/shard_map/ppermute | solution.py:499
  108.6 0.8 slice.65.rest_ref
  109.4 19.3 %shard_map.39 = (f32[5,256,256]{2,1,0:T(8,128)}, bf16[5,256,256]{2,1,0:T(8,128)(2,1)}, bf16[5,256,256]{2,1,0:T(8,128)(2,1)}, f32[10,256,256]{2,1,0:T(8,128)}) custom-call(s32[34]{0:T(128)} %pad_add_fusion.meta, f32[8,16,3,32,128]{4,3,2,1,0:T(8,128)} %bitcast.52), custom_call_target="tpu_custom_call" | custom-call | flops 19800000512 | bytes 1048576 | tf_op jit(solution)/shard_map/pallas_call | solution.py:515
  128.8 0.0 all-to-all-done.2.got_ref
  128.8 0.0 collective-permute-done.2
  128.8 2.5 collective-permute-done.3
  131.2 2.3 shard_map.40
  133.5 0.0 all-gather.8.cloned.1.call-update
  133.6 0.7 fusion
  135.6 1.1 slice_select_fusion.1
  136.8 5.5 %collective-permute-start.4 = (f32[5,3,32,128]{3,2,1,0:T(8,128)S(1)}, f32[5,3,32,128]{3,2,1,0:T(8,128)S(1)}, u32[]{:S(2)}, u32[]{:S(2)}) collective-permute-start(f32[5,3,32,128]{3,2,1,0:T(8,128)S(1)} %get-tuple-element.103), channel_id=1, source_target_pairs={{0,0},{1,8},{2,16},{3,24},{4,32},{5,40},{6,48},{7,56},{8,64},{9,72... | collective-permute-start | bytes 737288 | tf_op jit(solution)/shard_map/ppermute | solution.py:545
  142.3 2.7 collective-permute-start.5
  145.0 0.1 constant_dynamic-slice_fusion.4
  145.2 0.0 collective-permute-start.6
  145.2 1.5 collective-permute-start.7
  146.7 27.3 %shard_map.41 = (f32[7,256,256]{2,1,0:T(8,128)}, bf16[7,256,256]{2,1,0:T(8,128)(2,1)}, bf16[7,256,256]{2,1,0:T(8,128)(2,1)}, f32[3,256,256]{2,1,0:T(8,128)}) custom-call(f32[10,256,256]{2,1,0:T(8,128)} %get-tuple-element.63.refs_0_), custom_call_target="tpu_custom_call" | custom-call | flops 30799998976 | bytes 1048576 | tf_op jit(solution)/shard_map/pallas_call | solution.py:551
  174.1 0.0 collective-permute-done.4
  174.1 0.0 collective-permute-done.5
  174.2 0.0 collective-permute-done.6
  174.2 0.0 collective-permute-done.7
  174.2 2.4 broadcast_in_dim.2
  176.6 4.6 %all-to-all-start.3 = ((f32[8,2,5,3,32,128]{5,4,3,2,1,0:T(8,128)}), f32[8,2,5,3,32,128]{5,4,3,2,1,0:T(8,128)}, u32[]{:S(2)}, u32[]{:S(2)}) async-start(f32[8,2,5,3,32,128]{5,4,3,2,1,0:T(8,128)} %broadcast_in_dim.2), calls=%async_computation.3 | async-start | bytes 7864320 | tf_op jit(solution)/shard_map/all_to_all | solution.py:556
  181.2 0.0 copy-start.5
  181.2 22.0 %shard_map.42 = (f32[3,256,256]{2,1,0:T(8,128)}, bf16[3,256,256]{2,1,0:T(8,128)(2,1)}, bf16[3,256,256]{2,1,0:T(8,128)(2,1)}) custom-call(f32[3,256,256]{2,1,0:T(8,128)} %get-tuple-element.72.refs_0_), custom_call_target="tpu_custom_call" | custom-call | flops 28600000512 | bytes 1048576 | tf_op jit(solution)/shard_map/pallas_call | solution.py:557
  203.2 0.1 pad_maximum_fusion.1.child_1
  203.3 3.7 %collective-permute-start.9 = (f32[6,512,128]{2,1,0:T(8,128)S(1)}, f32[6,512,128]{2,1,0:T(8,128)S(1)}, u32[]{:S(2)}, u32[]{:S(2)}) collective-permute-start(f32[6,512,128]{2,1,0:T(8,128)S(1)} %pad_maximum_fusion.1.child_1), channel_id=1, source_target_pairs={{0,1},{1,2},{2,3},{3,4},{4,5},{5,6},{6,7},{7,8},{8,9},{9,10},{10,1... | collective-permute-start | bytes 4718600 | tf_op jit(solution)/shard_map/ppermute | solution.py:562
  207.0 0.0 collective-permute-start.8
  207.0 46.3 %all-gather.8.cloned.1.call-done = f32[80,6,32,128]{3,2,1,0:T(8,128)} async-done(((f32[5,6,32,128]{3,2,1,0:T(8,128)}), f32[80,6,32,128]{3,2,1,0:T(8,128)}) %all-gather.8.cloned.1.call-update) | async-done | bytes 7864336 | tf_op jit(solution)/shard_map/all_gather | solution.py:521
  253.4 17.7 %shard_map.43 = (bf16[1536,1280]{1,0:T(8,128)(2,1)}, bf16[1536,1280]{1,0:T(8,128)(2,1)}, f32[1536,256]{1,0:T(8,128)}) custom-call(s32[34]{0:T(128)} %pad_add_fusion.meta, f32[16,5,6,32,128]{4,3,2,1,0:T(8,128)} %bitcast.51, bf16[5,256,256]{2,1,0:T(8,128)(2,1)} %get-tuple-element.75.refs_0_, bf16[5,256,256]{2,1,0:T(8,128)(2,1)} %get-tuple-element.76.refs_1_, ...), custom_call_target="tpu_custom_call" | custom-call | flops 22000001024 | bytes 1048576 | tf_op jit(solution)/shard_map/pallas_call | solution.py:570
  271.0 0.0 all-to-all-done.3
  271.0 11.2 %shard_map.44 = (bf16[768,1280]{1,0:T(8,128)(2,1)}, bf16[768,1280]{1,0:T(8,128)(2,1)}) custom-call(f32[16,5,3,32,128]{4,3,2,1,0:T(8,128)} %bitcast.20.parts_ref, bf16[5,256,256]{2,1,0:T(8,128)(2,1)} %get-tuple-element.75.refs_0_, bf16[5,256,256]{2,1,0:T(8,128)(2,1)} %get-tuple-element.76.refs_1_, bf16[7,256,256]{2,1,0:T(8,128)(2,1)} %get-tuple-element.77.refs_2_, ...), custom_call_target="tpu_custom_call" | custom-call | flops 13200000000 | bytes 1048576 | tf_op jit(solution)/shard_map/pallas_call | solution.py:586
  282.2 0.0 collective-permute-done.9.child_2
  282.2 0.0 collective-permute-done.8.child_0
  282.2 1.2 copy-done.9
  283.4 20.4 %shard_map.45 = f32[9216,128]{1,0:T(8,128)} custom-call(s32[34]{0:T(128)} %pad_add_fusion.meta, bf16[1536,1280]{1,0:T(8,128)(2,1)} %get-tuple-element.81.yh, bf16[1536,1280]{1,0:T(8,128)(2,1)} %get-tuple-element.82.yl, f32[1536,256]{1,0:T(8,128)} %get-tuple-element.85.own_ref, bf16[768,1280]{1,0:T(8,128)(2,1)} %get-tuple-element.87.rh_ref, ...), custom_call_target="tpu_custom_call" | custom-call | flops 19800000512 | bytes 1048576 | tf_op jit(solution)/shard_map/pallas_call | solution.py:599
  (31 shorter events, 0.2 us)
Async XLA Ops:
  6.5 10.1 %copy-start = (f32[4,1,256,1,1,256]{5,4,3,2,1,0:T(1,128)S(1)}, f32[4,1,256,1,1,256]{5,4,3,2,1,0:T(1,128)}, u32[]{:S(2)}) copy-start(f32[4,1,256,1,1,256]{5,4,3,2,1,0:T(1,128)} %param.4) | copy-start | bytes 3145732
  6.5 10.1 %copy-start.12 = (s32[2,16]{1,0:T(2,128)S(1)}, s32[2,16]{1,0:T(2,128)}, u32[]{:S(2)}) copy-start(s32[2,16]{1,0:T(2,128)} %param.5) | copy-start | bytes 388
  9.6 14.4 %all-to-all-start = ((f32[16,2,32,128]{3,2,1,0:T(8,128)}), f32[16,2,32,128]{3,2,1,0:T(8,128)S(1)}, u32[]{:S(2)}, u32[]{:S(2)}) async-start(f32[16,2,32,128]{3,2,1,0:T(8,128)} %pad_maximum_fusion.2), calls=%async_computation | async-start | bytes 1048576 | tf_op jit(solution)/shard_map/all_to_all | solution.py:476
  16.5 92.9 %all-gather.6.cloned.1.call-start = ((), (), s32[]{:S(2)}) async-start(), calls=%async_computation.4 | async-start | bytes 7077888 | tf_op jit(solution)/shard_map/all_gather | solution.py:484
  24.0 7.4 %copy-start.2 = (f32[7,32,128]{2,1,0:T(8,128)}, f32[7,32,128]{2,1,0:T(8,128)S(1)}, u32[]{:S(2)}) copy-start(f32[7,32,128]{2,1,0:T(8,128)S(1)} %pad_maximum_fusion.6.mine_ref) | copy-start | bytes 344068
  24.0 6.2 %collective-permute-start.1 = (f32[1,32,128]{2,1,0:T(8,128)S(1)}, f32[1,32,128]{2,1,0:T(8,128)S(1)}, u32[]{:S(2)}, u32[]{:S(2)}) collective-permute-start(f32[1,32,128]{2,1,0:T(8,128)S(1)} %slice.56), channel_id=1, source_target_pairs={{0,112},{1,113},{2,114},{3,115},{4,116},{5,117},{6,118},{7,119},{8... | collective-permute-start | bytes 49160 | tf_op jit(solution)/shard_map/ppermute | solution.py:481
  27.2 4.1 %collective-permute-start = (f32[3,32,128]{2,1,0:T(8,128)S(1)}, f32[3,32,128]{2,1,0:T(8,128)S(1)}, u32[]{:S(2)}, u32[]{:S(2)}) collective-permute-start(f32[3,32,128]{2,1,0:T(8,128)S(1)} %slice_select_fusion.2), channel_id=1, source_target_pairs={{0,96},{16,80},{1,97},{17,81},{2,98},{18,82},{3,99},{19,83},{4,100... | collective-permute-start | bytes 147464 | tf_op jit(solution)/shard_map/ppermute | solution.py:480
  30.2 1.1 copy-start.11
  31.3 0.6 copy-start.10
  63.1 6.8 %copy-start.3 = (f32[7,32,128]{2,1,0:T(8,128)S(1)}, f32[7,32,128]{2,1,0:T(8,128)}, u32[]{:S(2)}) copy-start(f32[7,32,128]{2,1,0:T(8,128)} %copy-done.2) | copy-start | bytes 344068
  63.1 29.3 %all-to-all-start.1 = ((f32[16,9,32,128]{3,2,1,0:T(8,128)}), f32[16,9,32,128]{3,2,1,0:T(8,128)S(1)}, u32[]{:S(2)}, u32[]{:S(2)}) async-start(f32[16,9,32,128]{3,2,1,0:T(8,128)} %copy_bitcast_fusion), calls=%async_computation.1 | async-start | bytes 4718592 | tf_op jit(solution)/shard_map/all_to_all | solution.py:488
  94.8 33.9 %all-to-all-start.2 = ((f32[8,2,32,128]{3,2,1,0:T(8,128)}), f32[8,2,32,128]{3,2,1,0:T(8,128)}, u32[]{:S(2)}, u32[]{:S(2)}) async-start(f32[8,2,32,128]{3,2,1,0:T(8,128)} %shard_map.38), calls=%async_computation.2 | async-start | bytes 524288 | tf_op jit(solution)/shard_map/all_to_all | solution.py:491
  99.6 153.7 %all-gather.8.cloned.1.call-start = ((), (), s32[]{:S(2)}) async-start(), calls=%async_computation.5 | async-start | bytes 8355840 | tf_op jit(solution)/shard_map/all_gather | solution.py:521
  99.7 29.1 %collective-permute-start.2 = (f32[2,512,128]{2,1,0:T(8,128)}, f32[2,512,128]{2,1,0:T(8,128)S(1)}, u32[]{:S(2)}, u32[]{:S(2)}) collective-permute-start(f32[2,512,128]{2,1,0:T(8,128)} %get-tuple-element.55), channel_id=1, source_target_pairs={{1,20},{2,23},{3,26},{4,29},{5,16},{6,19},{7,22},{8,25},{9,28},{10... | collective-permute-start | bytes 1572872 | tf_op jit(solution)/shard_map/ppermute | solution.py:499
  102.5 28.8 %collective-permute-start.3 = (f32[2,512,128]{2,1,0:T(8,128)}, f32[2,512,128]{2,1,0:T(8,128)S(1)}, u32[]{:S(2)}, u32[]{:S(2)}) collective-permute-start(f32[2,512,128]{2,1,0:T(8,128)} %get-tuple-element.56), channel_id=1, source_target_pairs={{1,84},{2,87},{3,90},{4,93},{5,80},{6,83},{7,86},{8,89},{9,92},{10... | collective-permute-start | bytes 1572872 | tf_op jit(solution)/shard_map/ppermute | solution.py:499
  131.2 2.4 copy-start.8
  136.8 37.3 %collective-permute-start.4 = (f32[5,3,32,128]{3,2,1,0:T(8,128)S(1)}, f32[5,3,32,128]{3,2,1,0:T(8,128)S(1)}, u32[]{:S(2)}, u32[]{:S(2)}) collective-permute-start(f32[5,3,32,128]{3,2,1,0:T(8,128)S(1)} %get-tuple-element.103), channel_id=1, source_target_pairs={{0,0},{1,8},{2,16},{3,24},{4,32},{5,40},{6,48},{7,56},{8,64},{9,72... | collective-permute-start | bytes 737288 | tf_op jit(solution)/shard_map/ppermute | solution.py:545
  142.3 31.8 %collective-permute-start.5 = (f32[5,3,32,128]{3,2,1,0:T(8,128)S(1)}, f32[5,3,32,128]{3,2,1,0:T(8,128)S(1)}, u32[]{:S(2)}, u32[]{:S(2)}) collective-permute-start(f32[5,3,32,128]{3,2,1,0:T(8,128)S(1)} %get-tuple-element.104), channel_id=1, source_target_pairs={{0,8},{1,0},{2,24},{3,16},{4,40},{5,32},{6,56},{7,48},{8,72},{9,64... | collective-permute-start | bytes 737288 | tf_op jit(solution)/shard_map/ppermute | solution.py:546
  145.2 29.0 %collective-permute-start.6 = (f32[2,512,128]{2,1,0:T(8,128)S(1)}, f32[2,512,128]{2,1,0:T(8,128)S(1)}, u32[]{:S(2)}, u32[]{:S(2)}) collective-permute-start(f32[2,512,128]{2,1,0:T(8,128)S(1)} %pad_maximum_fusion.3), channel_id=1, source_target_pairs={{0,112},{16,0},{32,16},{48,32},{64,48},{80,64},{96,80},{112,96},{1... | collective-permute-start | bytes 1572872 | tf_op jit(solution)/shard_map/ppermute | solution.py:536
  145.2 28.9 %collective-permute-start.7 = (f32[2,512,128]{2,1,0:T(8,128)S(1)}, f32[2,512,128]{2,1,0:T(8,128)S(1)}, u32[]{:S(2)}, u32[]{:S(2)}) collective-permute-start(f32[2,512,128]{2,1,0:T(8,128)S(1)} %pad_maximum_fusion.4), channel_id=1, source_target_pairs={{0,16},{16,32},{32,48},{48,64},{64,80},{80,96},{96,112},{112,0},{1... | collective-permute-start | bytes 1572872 | tf_op jit(solution)/shard_map/ppermute | solution.py:537
  174.2 2.5 copy-start.4
  174.2 2.4 copy-start.6
  176.6 94.4 %all-to-all-start.3 = ((f32[8,2,5,3,32,128]{5,4,3,2,1,0:T(8,128)}), f32[8,2,5,3,32,128]{5,4,3,2,1,0:T(8,128)}, u32[]{:S(2)}, u32[]{:S(2)}) async-start(f32[8,2,5,3,32,128]{5,4,3,2,1,0:T(8,128)} %broadcast_in_dim.2), calls=%async_computation.3 | async-start | bytes 7864320 | tf_op jit(solution)/shard_map/all_to_all | solution.py:556
  181.2 22.0 %copy-start.5 = (f32[2,512,128]{2,1,0:T(8,128)S(1)}, f32[2,512,128]{2,1,0:T(8,128)}, u32[]{:S(2)}) copy-start(f32[2,512,128]{2,1,0:T(8,128)} %copy-done.4) | copy-start | bytes 1572868
  181.2 22.0 %copy-start.7 = (f32[2,512,128]{2,1,0:T(8,128)S(1)}, f32[2,512,128]{2,1,0:T(8,128)}, u32[]{:S(2)}) copy-start(f32[2,512,128]{2,1,0:T(8,128)} %copy-done.6) | copy-start | bytes 1572868
  203.3 67.7 %copy-start.1 = (f32[6,512,128]{2,1,0:T(8,128)}, f32[6,512,128]{2,1,0:T(8,128)S(1)}, u32[]{:S(2)}) copy-start(f32[6,512,128]{2,1,0:T(8,128)S(1)} %pad_maximum_fusion.1.child_1) | copy-start | bytes 4718596
  203.3 78.9 %collective-permute-start.9 = (f32[6,512,128]{2,1,0:T(8,128)S(1)}, f32[6,512,128]{2,1,0:T(8,128)S(1)}, u32[]{:S(2)}, u32[]{:S(2)}) collective-permute-start(f32[6,512,128]{2,1,0:T(8,128)S(1)} %pad_maximum_fusion.1.child_1), channel_id=1, source_target_pairs={{0,1},{1,2},{2,3},{3,4},{4,5},{5,6},{6,7},{7,8},{8,9},{9,10},{10,1... | collective-permute-start | bytes 4718600 | tf_op jit(solution)/shard_map/ppermute | solution.py:562
  207.0 75.2 %collective-permute-start.8 = (f32[6,512,128]{2,1,0:T(8,128)S(1)}, f32[6,512,128]{2,1,0:T(8,128)}, u32[]{:S(2)}, u32[]{:S(2)}) collective-permute-start(f32[6,512,128]{2,1,0:T(8,128)S(1)} %pad_maximum_fusion.1.child_1), channel_id=1, source_target_pairs={{0,15},{1,0},{2,1},{3,2},{4,3},{5,4},{6,5},{7,6},{8,7},{9,8},{10,9... | collective-permute-start | bytes 4718600 | tf_op jit(solution)/shard_map/ppermute | solution.py:563
  282.2 1.2 copy-start.9
Sparse Core Ops, SparseCore 0:
  60.2 42.2 all-gather.5
  133.6 119.6 all-gather.7

commit v11 on v9

--- a/solution.py
+++ b/solution.py
@@ -304,27 +304,21 @@
 def solve_rows(raw_ref, yh_ref, yl_ref, factors):
     head_h, head_l, tail_h, tail_l = factors
 
-    def column(high, low, start, count):
-        return [ref[start : start + count].reshape(count * NB, NB) for ref in (high, low)]
+    def factor(m, k):
+        if m < CUT:
+            at = place_head(m, k)
+            return head_h[at], head_l[at]
+        at = place_tail(m - CUT, k - CUT)
+        return tail_h[at], tail_l[at]
 
     for k in range(KB):
         at = slice(NB * k, NB * k + NB)
         t = raw_ref[:, at]
-        if k > 0:
-            count = min(k, CUT)
-            before = slice(0, NB * count)
-            part = column(head_h, head_l, place_head(0, k), count)
-            t = t - dot3(yh_ref[:, before], yl_ref[:, before], *part, NN)
-        if k > CUT:
-            before = slice(NB * CUT, NB * k)
-            part = column(tail_h, tail_l, place_tail(0, k - CUT), k - CUT)
-            t = t - dot3(yh_ref[:, before], yl_ref[:, before], *part, NN)
+        for m in range(k):
+            am = slice(NB * m, NB * m + NB)
+            t = t - dot3(yh_ref[:, am], yl_ref[:, am], *factor(m, k), NN)
         high, low = split(t)
-        if k < CUT:
-            own = column(head_h, head_l, place_head(k, k), 1)
-        else:
-            own = column(tail_h, tail_l, place_tail(k - CUT, k - CUT), 1)
-        y = dot3(high, low, *own, NN)
+        y = dot3(high, low, *factor(k, k), NN)
         raw_ref[:, at] = y
         high, low = split(y)
         yh_ref[:, at] = high
@@ -363,6 +357,9 @@
             own_ref[...] = raw[:, NB * j : NB * j + NB]
 
 
+SCHUR_STEP = 1
+
+
 def schur_kernel(meta, yh, yl, own_ref, rh_ref, rl_ref, head_ref, tail_ref, parent_ref, child_0, child_1, child_2, out_ref):
     step = pl.program_id(0)
     row, col = meta[32], meta[33]
@@ -370,8 +367,8 @@
     for n in ROUTED:
         routes.append(routed_from(meta, n))
 
-    for a in range(ROWS_STEP):
-        slot = step * ROWS_STEP + a
+    for a in range(SCHUR_STEP):
+        slot = step * SCHUR_STEP + a
         block_row = row + 8 * slot
         rows = slice(NB * a, NB * a + NB)
         for c in range(3):
@@ -596,12 +593,14 @@
 
     whole_right = pl.BlockSpec((768, 1280), lambda g: (0, 0))
     whole_child = pl.BlockSpec((6, 512, LANES), lambda g: (0, 0, 0))
-    front_rows = pl.BlockSpec((1536 * ROWS_STEP, LANES), lambda g: (g, 0))
+    front_rows = pl.BlockSpec((1536 * SCHUR_STEP, LANES), lambda g: (g, 0))
+    y_rows = pl.BlockSpec((NB * SCHUR_STEP, 1280), lambda g: (g, 0))
+    own_block = pl.BlockSpec((NB * SCHUR_STEP, NB), lambda g: (g, 0))
     out = pl.pallas_call(
         schur_kernel,
-        grid=(steps,),
+        grid=(6 // SCHUR_STEP,),
         out_shape=shaped((9216, LANES)),
-        in_specs=[SM, by_rows, by_rows, own_rows, whole_right, whole_right, whole_head, whole_tail, front_rows]
+        in_specs=[SM, y_rows, y_rows, own_block, whole_right, whole_right, whole_head, whole_tail, front_rows]
         + [whole_child] * 3,
         out_specs=front_rows,
         compiler_params=pltpu.CompilerParams(vmem_limit_bytes=VMEM_LIMIT),

time: 283 us -> 282 us (level)
  Pallas kernels: 124 us -> 120 us
  transfers between devices with their start and end apart: 15 -> 15, of which waited for: 6 -> 6; matrix products, arithmetic and copies ran while one was open for 4% -> 4% of each run, Pallas kernels for 36% -> 35%
where the time goes in v11:
time: 282 us; the launch traced here: 279 us
  Pallas kernels  120 us (43%)
  blocking collectives  53.6 us (19%)
  starting transfers between devices  42.1 us (15%)
  waiting for transfers between devices  34.5 us (12%)
  between operations  15.1 us (5%)
  local copies, waits for them, and re-layouts  10.7 us (4%)
  other arithmetic  3 us (1%)
    pallas_call x1, Pallas kernels, per_device(): call(chain_tail_kernel, (shaped((TAILS, NB, NB)), shaped((TAILS, NB, NB),...  33.8 us
    pallas_call x1, Pallas kernels, per_device(): call(chain_head_kernel, (shaped((HEADS, NB, NB)), shaped((HEADS, NB, NB),...  31.8 us
    all_to_all x1, blocking collectives, per_device(): rest = lax.all_to_all(rest, 'pcol', 0, 0, tiled=True)  27.1 us
    all_gather x1, blocking collectives, per_device(): chunk = lax.all_gather(chunk, 'pcol')  26.5 us
    pallas_call x1, Pallas kernels, per_device(): pl.pallas_call(schur_kernel, grid=(6 // SCHUR_STEP,), out_shape=shaped((9...  20.5 us
    pallas_call x1, Pallas kernels, per_device(): pl.pallas_call(left_kernel, grid=(steps,), out_shape=(shaped((1536, 1280)...  17.6 us
    all_to_all x1, waiting for transfers between devices, per_device(): pieces = lax.all_to_all(pieces, 'prow', 0, 0, tiled=True)  13.2 us
    pallas_call x1, Pallas kernels, per_device(): call(right_kernel, (shaped((768, 1280), BF16), shaped((768, 1280), BF16))...  11.2 us
  transfers between devices with their start and end apart: 15, of which 6 were waited for; matrix products, arithmetic and copies ran while one was open for 4% of the time, Pallas kernels for 35%

profile of v11, /device:TPU:102, one launch (start us, length us, event | category | flops | bytes accessed | tf_op | source)
XLA Modules:
  0.0 279.4 jit_solution(12883473977278627392)
XLA Ops:
  6.5 1.1 slice.61
  7.6 1.1 slice.48
  8.7 0.8 pad_maximum_fusion.2
  9.6 6.9 %all-to-all-start = ((f32[16,2,32,128]{3,2,1,0:T(8,128)}), f32[16,2,32,128]{3,2,1,0:T(8,128)S(1)}, u32[]{:S(2)}, u32[]{:S(2)}) async-start(f32[16,2,32,128]{3,2,1,0:T(8,128)} %pad_maximum_fusion.2), calls=%async_computation | async-start | bytes 1048576 | tf_op jit(solution)/shard_map/all_to_all | solution.py:468
  16.5 0.0 all-gather.8.cloned.1.call-start
  16.6 0.0 copy-done.10
  16.6 0.1 reshape.24
  16.7 0.0 copy-done
  16.7 1.1 dynamic-slice_bitcast_fusion
  17.7 6.2 %all-to-all-done = f32[16,2,32,128]{3,2,1,0:T(8,128)S(1)} async-done(((f32[16,2,32,128]{3,2,1,0:T(8,128)}), f32[16,2,32,128]{3,2,1,0:T(8,128)S(1)}, u32[]{:S(2)}, u32[]{:S(2)}) %all-to-all-start) | async-done | bytes 524320 | tf_op jit(solution)/shard_map/all_to_all | solution.py:468
  24.0 3.2 %collective-permute-start.1 = (f32[1,32,128]{2,1,0:T(8,128)S(1)}, f32[1,32,128]{2,1,0:T(8,128)S(1)}, u32[]{:S(2)}, u32[]{:S(2)}) collective-permute-start(f32[1,32,128]{2,1,0:T(8,128)S(1)} %slice.56), channel_id=1, source_target_pairs={{0,112},{1,113},{2,114},{3,115},{4,116},{5,117},{6,118},{7,119},{8... | collective-permute-start | bytes 49160 | tf_op jit(solution)/shard_map/ppermute | solution.py:473
  27.2 2.4 collective-permute-start
  29.6 0.6 pad_add_fusion.meta
  30.2 0.0 collective-permute-done.1.got_b_ref
  30.2 1.1 collective-permute-done.got_a_ref
  31.3 0.0 copy-done.2
  31.3 0.6 copy-done.8
  32.0 1.6 shard_map.37
  33.6 26.5 %all-gather = f32[48,32,128]{2,1,0:T(8,128)} all-gather(f32[3,32,128]{2,1,0:T(8,128)} %shard_map.37), channel_id=2, replica_groups=mesh['prow'=8,'pcol'=16] {'pcol'}, dimensions={0}, use_global_device_ids=true | all-gather | bytes 835584 | tf_op jit(solution)/shard_map/all_gather | solution.py:475
  60.1 0.0 all-gather.8.cloned.1.call-update
  60.1 1.4 slice.64
  61.5 0.2 copy_bitcast_fusion
  61.7 27.1 %all_to_all.20 = f32[16,9,32,128]{3,2,1,0:T(8,128)S(1)} all-to-all(f32[16,9,32,128]{3,2,1,0:T(8,128)S(1)} %copy_bitcast_fusion), channel_id=1, replica_groups=mesh['prow'=8,'pcol'=16] {'pcol'}, dimensions={0} | all-to-all | bytes 4718592 | tf_op jit(solution)/shard_map/all_to_all | solution.py:480
  88.9 0.7 slice.66.parts_ref
  89.5 1.8 shard_map.38
  91.3 1.9 collective-permute-start.2
  93.2 6.2 %collective-permute-start.3 = (f32[2,512,128]{2,1,0:T(8,128)}, f32[2,512,128]{2,1,0:T(8,128)S(1)}, u32[]{:S(2)}, u32[]{:S(2)}) collective-permute-start(f32[2,512,128]{2,1,0:T(8,128)} %get-tuple-element.45), channel_id=1, source_target_pairs={{1,84},{2,87},{3,90},{4,93},{5,80},{6,83},{7,86},{8,89},{9,92},{10... | collective-permute-start | bytes 1572872 | tf_op jit(solution)/shard_map/ppermute | solution.py:491
  99.5 4.5 %all-to-all-start.2 = ((f32[8,2,32,128]{3,2,1,0:T(8,128)}), f32[8,2,32,128]{3,2,1,0:T(8,128)}, u32[]{:S(2)}, u32[]{:S(2)}) async-start(f32[8,2,32,128]{3,2,1,0:T(8,128)} %shard_map.38), calls=%async_computation.2 | async-start | bytes 524288 | tf_op jit(solution)/shard_map/all_to_all | solution.py:483
  104.0 0.0 all-gather.6.cloned.1.call-start
  104.1 0.6 slice.51.first_ref
  104.7 0.8 slice.65.rest_ref
  105.5 13.2 %all-to-all-done.2.got_ref = f32[8,2,32,128]{3,2,1,0:T(8,128)} async-done(((f32[8,2,32,128]{3,2,1,0:T(8,128)}), f32[8,2,32,128]{3,2,1,0:T(8,128)}, u32[]{:S(2)}, u32[]{:S(2)}) %all-to-all-start.2) | async-done | bytes 262176 | tf_op jit(solution)/shard_map/all_to_all | solution.py:483
  118.7 0.0 collective-permute-done.2
  118.7 3.5 %collective-permute-done.3 = f32[2,512,128]{2,1,0:T(8,128)S(1)} collective-permute-done((f32[2,512,128]{2,1,0:T(8,128)}, f32[2,512,128]{2,1,0:T(8,128)S(1)}, u32[]{:S(2)}, u32[]{:S(2)}) %collective-permute-start.3) | collective-permute-done | bytes 524320 | tf_op jit(solution)/shard_map/ppermute | solution.py:491
  122.2 2.3 shard_map.39
  124.5 0.0 all-gather.6.cloned.1.call-update
  124.6 0.0 copy-done.6
  124.6 0.6 fusion
  126.5 0.0 all-gather.8.cloned.1.call-done
  126.6 1.1 slice_select_fusion.1
  127.7 3.0 %collective-permute-start.4 = (f32[5,3,32,128]{3,2,1,0:T(8,128)S(1)}, f32[5,3,32,128]{3,2,1,0:T(8,128)S(1)}, u32[]{:S(2)}, u32[]{:S(2)}) collective-permute-start(f32[5,3,32,128]{3,2,1,0:T(8,128)S(1)} %get-tuple-element.83), channel_id=1, source_target_pairs={{0,0},{1,8},{2,16},{3,24},{4,32},{5,40},{6,48},{7,56},{8,64},{9,72... | collective-permute-start | bytes 737288 | tf_op jit(solution)/shard_map/ppermute | solution.py:521
  130.7 6.2 %collective-permute-start.5 = (f32[5,3,32,128]{3,2,1,0:T(8,128)S(1)}, f32[5,3,32,128]{3,2,1,0:T(8,128)S(1)}, u32[]{:S(2)}, u32[]{:S(2)}) collective-permute-start(f32[5,3,32,128]{3,2,1,0:T(8,128)S(1)} %get-tuple-element.84), channel_id=1, source_target_pairs={{0,8},{1,0},{2,24},{3,16},{4,40},{5,32},{6,56},{7,48},{8,72},{9,64... | collective-permute-start | bytes 737288 | tf_op jit(solution)/shard_map/ppermute | solution.py:522
  136.9 0.1 constant_dynamic-slice_fusion.4
  137.0 0.0 collective-permute-start.6
  137.1 0.5 collective-permute-start.7
  137.6 31.8 %shard_map.40 = (f32[9,256,256]{2,1,0:T(8,128)}, bf16[9,256,256]{2,1,0:T(8,128)(2,1)}, bf16[9,256,256]{2,1,0:T(8,128)(2,1)}, f32[6,256,256]{2,1,0:T(8,128)}) custom-call(s32[34]{0:T(128)} %pad_add_fusion.meta, f32[8,16,3,32,128]{4,3,2,1,0:T(8,128)} %bitcast.52), custom_call_target="tpu_custom_call" | custom-call | flops 35200000000 | bytes 1048576 | tf_op jit(solution)/shard_map/pallas_call | solution.py:533
  169.3 0.0 collective-permute-done.4
  169.4 0.0 collective-permute-done.5
  169.4 0.0 collective-permute-done.6
  169.5 0.0 collective-permute-done.7
  169.5 0.0 copy-start.4
  169.5 2.4 broadcast_in_dim.2
  171.9 5.0 %all-to-all-start.3 = ((f32[8,2,5,3,32,128]{5,4,3,2,1,0:T(8,128)}), f32[8,2,5,3,32,128]{5,4,3,2,1,0:T(8,128)}, u32[]{:S(2)}, u32[]{:S(2)}) async-start(f32[8,2,5,3,32,128]{5,4,3,2,1,0:T(8,128)} %broadcast_in_dim.2), calls=%async_computation.3 | async-start | bytes 7864320 | tf_op jit(solution)/shard_map/all_to_all | solution.py:547
  176.9 33.8 %shard_map.41 = (f32[6,256,256]{2,1,0:T(8,128)}, bf16[6,256,256]{2,1,0:T(8,128)(2,1)}, bf16[6,256,256]{2,1,0:T(8,128)(2,1)}) custom-call(f32[6,256,256]{2,1,0:T(8,128)} %get-tuple-element.58.rest_ref), custom_call_target="tpu_custom_call" | custom-call | flops 44000002048 | bytes 1048576 | tf_op jit(solution)/shard_map/pallas_call | solution.py:548
  210.7 0.1 pad_maximum_fusion.1.child_1
  210.8 1.0 collective-permute-start.9
  211.8 1.1 collective-permute-start.8
  212.9 17.6 %shard_map.42 = (bf16[1536,1280]{1,0:T(8,128)(2,1)}, bf16[1536,1280]{1,0:T(8,128)(2,1)}, f32[1536,256]{1,0:T(8,128)}) custom-call(s32[34]{0:T(128)} %pad_add_fusion.meta, f32[16,5,6,32,128]{4,3,2,1,0:T(8,128)} %bitcast.51, bf16[9,256,256]{2,1,0:T(8,128)(2,1)} %get-tuple-element.50.hh_ref, bf16[9,256,256]{2,1,0:T(8,128)(2,1)} %get-tuple-element.51.hl_ref, ...), custom_call_target="tpu_custom_call" | custom-call | flops 22000001024 | bytes 1048576 | tf_op jit(solution)/shard_map/pallas_call | solution.py:567
  230.5 0.0 all-to-all-done.3
  230.5 11.2 %shard_map.43 = (bf16[768,1280]{1,0:T(8,128)(2,1)}, bf16[768,1280]{1,0:T(8,128)(2,1)}) custom-call(f32[16,5,3,32,128]{4,3,2,1,0:T(8,128)} %bitcast.20.parts_ref, bf16[9,256,256]{2,1,0:T(8,128)(2,1)} %get-tuple-element.50.hh_ref, bf16[9,256,256]{2,1,0:T(8,128)(2,1)} %get-tuple-element.51.hl_ref, bf16[6,256,256]{2,1,0:T(8,128)(2,1)} %get-tuple-element.60.th_ref, ...), custom_call_target="tpu_custom_call" | custom-call | flops 13200000000 | bytes 1048576 | tf_op jit(solution)/shard_map/pallas_call | solution.py:586
  241.7 6.1 %collective-permute-done.9.child_2 = f32[6,512,128]{2,1,0:T(8,128)S(1)} collective-permute-done((f32[6,512,128]{2,1,0:T(8,128)S(1)}, f32[6,512,128]{2,1,0:T(8,128)S(1)}, u32[]{:S(2)}, u32[]{:S(2)}) %collective-permute-start.9) | collective-permute-done | bytes 1572896 | tf_op jit(solution)/shard_map/ppermute | solution.py:558
  247.8 4.3 %collective-permute-done.8.child_0 = f32[6,512,128]{2,1,0:T(8,128)} collective-permute-done((f32[6,512,128]{2,1,0:T(8,128)S(1)}, f32[6,512,128]{2,1,0:T(8,128)}, u32[]{:S(2)}, u32[]{:S(2)}) %collective-permute-start.8) | collective-permute-done | bytes 1572896 | tf_op jit(solution)/shard_map/ppermute | solution.py:559
  252.1 0.0 copy-done.7
  252.1 20.5 %shard_map.44 = f32[9216,128]{1,0:T(8,128)} custom-call(s32[34]{0:T(128)} %pad_add_fusion.meta, bf16[1536,1280]{1,0:T(8,128)(2,1)} %get-tuple-element.62.yh, bf16[1536,1280]{1,0:T(8,128)(2,1)} %get-tuple-element.63.yl, f32[1536,256]{1,0:T(8,128)} %get-tuple-element.66.own_ref, bf16[768,1280]{1,0:T(8,128)(2,1)} %get-tuple-element.68.rh_ref, ...), custom_call_target="tpu_custom_call" | custom-call | flops 19800000512 | bytes 1048576 | tf_op jit(solution)/shard_map/pallas_call | solution.py:599
  (25 shorter events, 0.2 us)
Async XLA Ops:
  6.5 10.1 %copy-start = (f32[4,1,256,1,1,256]{5,4,3,2,1,0:T(1,128)S(1)}, f32[4,1,256,1,1,256]{5,4,3,2,1,0:T(1,128)}, u32[]{:S(2)}) copy-start(f32[4,1,256,1,1,256]{5,4,3,2,1,0:T(1,128)} %param.4) | copy-start | bytes 3145732
  6.5 10.1 %copy-start.10 = (s32[2,16]{1,0:T(2,128)S(1)}, s32[2,16]{1,0:T(2,128)}, u32[]{:S(2)}) copy-start(s32[2,16]{1,0:T(2,128)} %param.5) | copy-start | bytes 388
  9.6 14.4 %all-to-all-start = ((f32[16,2,32,128]{3,2,1,0:T(8,128)}), f32[16,2,32,128]{3,2,1,0:T(8,128)S(1)}, u32[]{:S(2)}, u32[]{:S(2)}) async-start(f32[16,2,32,128]{3,2,1,0:T(8,128)} %pad_maximum_fusion.2), calls=%async_computation | async-start | bytes 1048576 | tf_op jit(solution)/shard_map/all_to_all | solution.py:468
  16.5 110.1 %all-gather.8.cloned.1.call-start = ((), (), s32[]{:S(2)}) async-start(), calls=%async_computation.5 | async-start | bytes 7077888 | tf_op jit(solution)/shard_map/all_gather | solution.py:476
  24.0 7.4 %copy-start.2 = (f32[7,32,128]{2,1,0:T(8,128)}, f32[7,32,128]{2,1,0:T(8,128)S(1)}, u32[]{:S(2)}) copy-start(f32[7,32,128]{2,1,0:T(8,128)S(1)} %pad_maximum_fusion.6.mine_ref) | copy-start | bytes 344068
  24.0 6.2 %collective-permute-start.1 = (f32[1,32,128]{2,1,0:T(8,128)S(1)}, f32[1,32,128]{2,1,0:T(8,128)S(1)}, u32[]{:S(2)}, u32[]{:S(2)}) collective-permute-start(f32[1,32,128]{2,1,0:T(8,128)S(1)} %slice.56), channel_id=1, source_target_pairs={{0,112},{1,113},{2,114},{3,115},{4,116},{5,117},{6,118},{7,119},{8... | collective-permute-start | bytes 49160 | tf_op jit(solution)/shard_map/ppermute | solution.py:473
  27.2 4.1 %collective-permute-start = (f32[3,32,128]{2,1,0:T(8,128)S(1)}, f32[3,32,128]{2,1,0:T(8,128)S(1)}, u32[]{:S(2)}, u32[]{:S(2)}) collective-permute-start(f32[3,32,128]{2,1,0:T(8,128)S(1)} %slice_select_fusion.2), channel_id=1, source_target_pairs={{0,96},{16,80},{1,97},{17,81},{2,98},{18,82},{3,99},{19,83},{4,100... | collective-permute-start | bytes 147464 | tf_op jit(solution)/shard_map/ppermute | solution.py:472
  30.2 1.1 copy-start.9
  31.3 0.6 copy-start.8
  89.5 14.5 %copy-start.3 = (f32[7,32,128]{2,1,0:T(8,128)S(1)}, f32[7,32,128]{2,1,0:T(8,128)}, u32[]{:S(2)}) copy-start(f32[7,32,128]{2,1,0:T(8,128)} %copy-done.2) | copy-start | bytes 344068
  91.3 27.4 %collective-permute-start.2 = (f32[2,512,128]{2,1,0:T(8,128)}, f32[2,512,128]{2,1,0:T(8,128)S(1)}, u32[]{:S(2)}, u32[]{:S(2)}) collective-permute-start(f32[2,512,128]{2,1,0:T(8,128)} %get-tuple-element.44), channel_id=1, source_target_pairs={{1,20},{2,23},{3,26},{4,29},{5,16},{6,19},{7,22},{8,25},{9,28},{10... | collective-permute-start | bytes 1572872 | tf_op jit(solution)/shard_map/ppermute | solution.py:491
  93.2 29.0 %collective-permute-start.3 = (f32[2,512,128]{2,1,0:T(8,128)}, f32[2,512,128]{2,1,0:T(8,128)S(1)}, u32[]{:S(2)}, u32[]{:S(2)}) collective-permute-start(f32[2,512,128]{2,1,0:T(8,128)} %get-tuple-element.45), channel_id=1, source_target_pairs={{1,84},{2,87},{3,90},{4,93},{5,80},{6,83},{7,86},{8,89},{9,92},{10... | collective-permute-start | bytes 1572872 | tf_op jit(solution)/shard_map/ppermute | solution.py:491
  99.5 19.2 %all-to-all-start.2 = ((f32[8,2,32,128]{3,2,1,0:T(8,128)}), f32[8,2,32,128]{3,2,1,0:T(8,128)}, u32[]{:S(2)}, u32[]{:S(2)}) async-start(f32[8,2,32,128]{3,2,1,0:T(8,128)} %shard_map.38), calls=%async_computation.2 | async-start | bytes 524288 | tf_op jit(solution)/shard_map/all_to_all | solution.py:483
  104.0 108.9 %all-gather.6.cloned.1.call-start = ((), (), s32[]{:S(2)}) async-start(), calls=%async_computation.4 | async-start | bytes 8355840 | tf_op jit(solution)/shard_map/all_gather | solution.py:497
  105.5 19.1 %copy-start.6 = (s32[34]{0:T(128)S(1)}, s32[34]{0:T(128)}, u32[]{:S(2)}) copy-start(s32[34]{0:T(128)} %pad_add_fusion.meta) | copy-start | bytes 412
  127.7 41.7 %collective-permute-start.4 = (f32[5,3,32,128]{3,2,1,0:T(8,128)S(1)}, f32[5,3,32,128]{3,2,1,0:T(8,128)S(1)}, u32[]{:S(2)}, u32[]{:S(2)}) collective-permute-start(f32[5,3,32,128]{3,2,1,0:T(8,128)S(1)} %get-tuple-element.83), channel_id=1, source_target_pairs={{0,0},{1,8},{2,16},{3,24},{4,32},{5,40},{6,48},{7,56},{8,64},{9,72... | collective-permute-start | bytes 737288 | tf_op jit(solution)/shard_map/ppermute | solution.py:521
  130.7 38.7 %collective-permute-start.5 = (f32[5,3,32,128]{3,2,1,0:T(8,128)S(1)}, f32[5,3,32,128]{3,2,1,0:T(8,128)S(1)}, u32[]{:S(2)}, u32[]{:S(2)}) collective-permute-start(f32[5,3,32,128]{3,2,1,0:T(8,128)S(1)} %get-tuple-element.84), channel_id=1, source_target_pairs={{0,8},{1,0},{2,24},{3,16},{4,40},{5,32},{6,56},{7,48},{8,72},{9,64... | collective-permute-start | bytes 737288 | tf_op jit(solution)/shard_map/ppermute | solution.py:522
  137.0 32.4 %collective-permute-start.6 = (f32[2,512,128]{2,1,0:T(8,128)S(1)}, f32[2,512,128]{2,1,0:T(8,128)S(1)}, u32[]{:S(2)}, u32[]{:S(2)}) collective-permute-start(f32[2,512,128]{2,1,0:T(8,128)S(1)} %pad_maximum_fusion.3), channel_id=1, source_target_pairs={{0,112},{16,0},{32,16},{48,32},{64,48},{80,64},{96,80},{112,96},{1... | collective-permute-start | bytes 1572872 | tf_op jit(solution)/shard_map/ppermute | solution.py:512
  137.1 32.4 %collective-permute-start.7 = (f32[2,512,128]{2,1,0:T(8,128)S(1)}, f32[2,512,128]{2,1,0:T(8,128)S(1)}, u32[]{:S(2)}, u32[]{:S(2)}) collective-permute-start(f32[2,512,128]{2,1,0:T(8,128)S(1)} %pad_maximum_fusion.4), channel_id=1, source_target_pairs={{0,16},{16,32},{32,48},{48,64},{64,80},{80,96},{96,112},{112,0},{1... | collective-permute-start | bytes 1572872 | tf_op jit(solution)/shard_map/ppermute | solution.py:513
  169.5 2.4 copy-start.4
  171.9 58.6 %all-to-all-start.3 = ((f32[8,2,5,3,32,128]{5,4,3,2,1,0:T(8,128)}), f32[8,2,5,3,32,128]{5,4,3,2,1,0:T(8,128)}, u32[]{:S(2)}, u32[]{:S(2)}) async-start(f32[8,2,5,3,32,128]{5,4,3,2,1,0:T(8,128)} %broadcast_in_dim.2), calls=%async_computation.3 | async-start | bytes 7864320 | tf_op jit(solution)/shard_map/all_to_all | solution.py:547
  176.9 33.8 %copy-start.5 = (f32[2,512,128]{2,1,0:T(8,128)S(1)}, f32[2,512,128]{2,1,0:T(8,128)}, u32[]{:S(2)}) copy-start(f32[2,512,128]{2,1,0:T(8,128)} %copy-done.4) | copy-start | bytes 1572868
  210.8 19.7 %copy-start.1 = (f32[6,512,128]{2,1,0:T(8,128)}, f32[6,512,128]{2,1,0:T(8,128)S(1)}, u32[]{:S(2)}) copy-start(f32[6,512,128]{2,1,0:T(8,128)S(1)} %pad_maximum_fusion.1.child_1) | copy-start | bytes 4718596
  210.8 37.0 %collective-permute-start.9 = (f32[6,512,128]{2,1,0:T(8,128)S(1)}, f32[6,512,128]{2,1,0:T(8,128)S(1)}, u32[]{:S(2)}, u32[]{:S(2)}) collective-permute-start(f32[6,512,128]{2,1,0:T(8,128)S(1)} %pad_maximum_fusion.1.child_1), channel_id=1, source_target_pairs={{0,1},{1,2},{2,3},{3,4},{4,5},{5,6},{6,7},{7,8},{8,9},{9,10},{10,1... | collective-permute-start | bytes 4718600 | tf_op jit(solution)/shard_map/ppermute | solution.py:558
  211.8 40.3 %collective-permute-start.8 = (f32[6,512,128]{2,1,0:T(8,128)S(1)}, f32[6,512,128]{2,1,0:T(8,128)}, u32[]{:S(2)}, u32[]{:S(2)}) collective-permute-start(f32[6,512,128]{2,1,0:T(8,128)S(1)} %pad_maximum_fusion.1.child_1), channel_id=1, source_target_pairs={{0,15},{1,0},{2,1},{3,2},{4,3},{5,4},{6,5},{7,6},{8,7},{9,8},{10,9... | collective-permute-start | bytes 4718600 | tf_op jit(solution)/shard_map/ppermute | solution.py:559
  247.8 4.3 %copy-start.7 = (f32[6,512,128]{2,1,0:T(8,128)}, f32[6,512,128]{2,1,0:T(8,128)S(1)}, u32[]{:S(2)}) copy-start(f32[6,512,128]{2,1,0:T(8,128)S(1)} %collective-permute-done.9.child_2) | copy-start | bytes 4718596
Sparse Core Ops, SparseCore 0:
  60.2 47.9 all-gather.7
  124.6 82.8 all-gather.5

commit v12 on v11

--- a/solution.py
+++ b/solution.py
@@ -476,11 +476,8 @@
     lead_parts = lax.all_gather(chunk, "prow")
 
     rest = jnp.concatenate([lead[1:], child], axis=0).transpose(1, 0, 2, 3)
-    rest, chunk = lax.optimization_barrier((rest, chunk))
+    rest, chunk, *picked = lax.optimization_barrier((rest, chunk, *picked))
     rest = lax.all_to_all(rest, "pcol", 0, 0, tiled=True)
-    pieces = call(pick_kernel, shaped((8, 2, 32, LANES)), [SM, VM], [])(meta, rest[0:2, 5:9])
-    pieces, *picked = lax.optimization_barrier((pieces, *picked))
-    pieces = lax.all_to_all(pieces, "prow", 0, 0, tiled=True)
 
     got = []
     for flip in range(2):
@@ -489,7 +486,10 @@
             target = (3 * (p % 4) + 1 + 4 * ((p // 4 + flip) % 2)) % 8
             perm += [(p * 16 + q, target * 16 + (3 * q + 1) % 16) for q in range(1, 16)]
         got.append(lax.ppermute(picked[flip], ("prow", "pcol"), perm))
-    pieces, *got = lax.optimization_barrier((pieces, *got))
+    rest, *got = lax.optimization_barrier((rest, *got))
+    pieces = call(pick_kernel, shaped((8, 2, 32, LANES)), [SM, VM], [])(meta, rest[0:2, 5:9])
+    pieces = lax.all_to_all(pieces, "prow", 0, 0, tiled=True)
+
     slices = call(assemble_kernel, shaped((KB, 6, 32, LANES)), [SM, VM, VM, VM], [])(
         meta, mine[0:KB], rest[0:KB, 0:5], pieces
     )

time: 282 us -> 295 us (1.046)
  blocking collectives: 53.6 us -> 26.5 us
  waiting for transfers between devices: 34.5 us -> 57.6 us
  starting transfers between devices: 42.1 us -> 56.7 us
    ppermute x2, waiting for transfers between devices: 3.55 us -> 33.3 us  [per_device(): got.append(lax.ppermute(picked[flip], ('prow', 'pcol'), perm))]
    all_to_all x1 -> x0, blocking collectives: 27.1 us -> none  [per_device(): rest = lax.all_to_all(rest, 'pcol', 0, 0, tiled=True)]
    all_to_all x1, starting transfers between devices: 4.55 us -> 11.9 us  [per_device(): pieces = lax.all_to_all(pieces, 'prow', 0, 0, tiled=True)]
    all_to_all x1, waiting for transfers between devices: 13.2 us -> 6.17 us  [per_device(): pieces = lax.all_to_all(pieces, 'prow', 0, 0, tiled=True)]
    all_to_all x0 -> x1, starting transfers between devices: none -> 6.64 us  [per_device(): rest = lax.all_to_all(rest, 'pcol', 0, 0, tiled=True)]
    ppermute x1, starting transfers between devices: 6.2 us -> 2.59 us  [per_device(): lax.ppermute(jnp.where(is_even, odd, even), ('prow', 'pcol'), perm_b)]
  transfers between devices with their start and end apart: 15 -> 16, of which waited for: 6 -> 7; matrix products, arithmetic and copies ran while one was open for 4% -> 4% of each run, Pallas kernels for 35% -> 34%
where the time goes in v12:
time: 295 us; the launch traced here: 291 us
  Pallas kernels  121 us (41%)
  waiting for transfers between devices  57.6 us (20%)
  starting transfers between devices  56.7 us (19%)
  blocking collectives  26.5 us (9%)
  between operations  15.1 us (5%)
  local copies, waits for them, and re-layouts  10.6 us (4%)
  other arithmetic  4.41 us (1%)
    pallas_call x1, Pallas kernels, per_device(): call(chain_tail_kernel, (shaped((TAILS, NB, NB)), shaped((TAILS, NB, NB),...  33.8 us
    ppermute x2, waiting for transfers between devices, per_device(): got.append(lax.ppermute(picked[flip], ('prow', 'pcol'), perm))  33.3 us
    pallas_call x1, Pallas kernels, per_device(): call(chain_head_kernel, (shaped((HEADS, NB, NB)), shaped((HEADS, NB, NB),...  31.8 us
    all_gather x1, blocking collectives, per_device(): chunk = lax.all_gather(chunk, 'pcol')  26.5 us
    pallas_call x1, Pallas kernels, per_device(): pl.pallas_call(schur_kernel, grid=(6 // SCHUR_STEP,), out_shape=shaped((9...  20.5 us
    pallas_call x1, Pallas kernels, per_device(): pl.pallas_call(left_kernel, grid=(steps,), out_shape=(shaped((1536, 1280)...  17.6 us
    all_to_all x1, starting transfers between devices, per_device(): pieces = lax.all_to_all(pieces, 'prow', 0, 0, tiled=True)  11.9 us
    pallas_call x1, Pallas kernels, per_device(): call(right_kernel, (shaped((768, 1280), BF16), shaped((768, 1280), BF16))...  11.2 us
  transfers between devices with their start and end apart: 16, of which 7 were waited for; matrix products, arithmetic and copies ran while one was open for 4% of the time, Pallas kernels for 34%

profile of v12, /device:TPU:102, one launch (start us, length us, event | category | flops | bytes accessed | tf_op | source)
XLA Modules:
  0.0 291.5 jit_solution(3828759784662129585)
XLA Ops:
  6.5 1.1 slice.61
  7.6 1.1 slice.48
  8.7 0.8 pad_maximum_fusion.2
  9.6 6.9 %all-to-all-start = ((f32[16,2,32,128]{3,2,1,0:T(8,128)}), f32[16,2,32,128]{3,2,1,0:T(8,128)S(1)}, u32[]{:S(2)}, u32[]{:S(2)}) async-start(f32[16,2,32,128]{3,2,1,0:T(8,128)} %pad_maximum_fusion.2), calls=%async_computation | async-start | bytes 1048576 | tf_op jit(solution)/shard_map/all_to_all | solution.py:468
  16.5 0.0 all-gather.8.cloned.1.call-start
  16.6 0.0 copy-done.12
  16.6 0.1 reshape.24
  16.7 0.0 copy-done
  16.7 1.1 dynamic-slice_bitcast_fusion
  17.8 6.2 %all-to-all-done = f32[16,2,32,128]{3,2,1,0:T(8,128)S(1)} async-done(((f32[16,2,32,128]{3,2,1,0:T(8,128)}), f32[16,2,32,128]{3,2,1,0:T(8,128)S(1)}, u32[]{:S(2)}, u32[]{:S(2)}) %all-to-all-start) | async-done | bytes 524320 | tf_op jit(solution)/shard_map/all_to_all | solution.py:468
  24.0 0.0 copy-start.2
  24.0 3.2 %collective-permute-start.1 = (f32[1,32,128]{2,1,0:T(8,128)S(1)}, f32[1,32,128]{2,1,0:T(8,128)S(1)}, u32[]{:S(2)}, u32[]{:S(2)}) collective-permute-start(f32[1,32,128]{2,1,0:T(8,128)S(1)} %slice.56), channel_id=1, source_target_pairs={{0,112},{1,113},{2,114},{3,115},{4,116},{5,117},{6,118},{7,119},{8... | collective-permute-start | bytes 49160 | tf_op jit(solution)/shard_map/ppermute | solution.py:473
  27.2 2.4 collective-permute-start
  29.6 0.6 pad_add_fusion.meta
  30.2 0.0 collective-permute-done.1.got_b_ref
  30.2 1.1 collective-permute-done.got_a_ref
  31.3 0.0 copy-done.2
  31.3 0.0 copy-done.11
  31.3 0.6 copy-done.10
  32.0 1.6 shard_map.37
  33.6 26.5 %all-gather = f32[48,32,128]{2,1,0:T(8,128)} all-gather(f32[3,32,128]{2,1,0:T(8,128)} %shard_map.37), channel_id=2, replica_groups=mesh['prow'=8,'pcol'=16] {'pcol'}, dimensions={0}, use_global_device_ids=true | all-gather | bytes 835584 | tf_op jit(solution)/shard_map/all_gather | solution.py:475
  60.1 0.0 all-gather.8.cloned.1.call-update
  60.1 1.4 slice.64
  61.5 1.6 copy_bitcast_fusion
  63.1 6.6 %all-to-all-start.1 = ((f32[16,9,32,128]{3,2,1,0:T(8,128)}), f32[16,9,32,128]{3,2,1,0:T(8,128)S(1)}, u32[]{:S(2)}, u32[]{:S(2)}) async-start(f32[16,9,32,128]{3,2,1,0:T(8,128)} %copy_bitcast_fusion), calls=%async_computation.1 | async-start | bytes 4718592 | tf_op jit(solution)/shard_map/all_to_all | solution.py:480
  69.8 1.9 collective-permute-start.2
  71.7 6.3 %collective-permute-start.3 = (f32[2,512,128]{2,1,0:T(8,128)}, f32[2,512,128]{2,1,0:T(8,128)S(1)}, u32[]{:S(2)}, u32[]{:S(2)}) collective-permute-start(f32[2,512,128]{2,1,0:T(8,128)} %get-tuple-element.43), channel_id=1, source_target_pairs={{1,84},{2,87},{3,90},{4,93},{5,80},{6,83},{7,86},{8,89},{9,92},{10... | collective-permute-start | bytes 1572872 | tf_op jit(solution)/shard_map/ppermute | solution.py:488
  78.0 27.7 %collective-permute-done.2 = f32[2,512,128]{2,1,0:T(8,128)S(1)} collective-permute-done((f32[2,512,128]{2,1,0:T(8,128)}, f32[2,512,128]{2,1,0:T(8,128)S(1)}, u32[]{:S(2)}, u32[]{:S(2)}) %collective-permute-start.2) | collective-permute-done | bytes 524320 | tf_op jit(solution)/shard_map/ppermute | solution.py:488
  105.7 5.6 %collective-permute-done.3 = f32[2,512,128]{2,1,0:T(8,128)S(1)} collective-permute-done((f32[2,512,128]{2,1,0:T(8,128)}, f32[2,512,128]{2,1,0:T(8,128)S(1)}, u32[]{:S(2)}, u32[]{:S(2)}) %collective-permute-start.3) | collective-permute-done | bytes 524320 | tf_op jit(solution)/shard_map/ppermute | solution.py:488
  111.3 0.0 all-to-all-done.1
  111.3 0.7 slice.58.parts_ref
  112.0 1.8 shard_map.38
  113.8 11.9 %all-to-all-start.2 = ((f32[8,2,32,128]{3,2,1,0:T(8,128)}), f32[8,2,32,128]{3,2,1,0:T(8,128)}, u32[]{:S(2)}, u32[]{:S(2)}) async-start(f32[8,2,32,128]{3,2,1,0:T(8,128)} %shard_map.38), calls=%async_computation.2 | async-start | bytes 524288 | tf_op jit(solution)/shard_map/all_to_all | solution.py:491
  125.6 0.0 all-gather.6.cloned.1.call-start
  125.7 0.6 slice.51.first_ref
  126.3 0.8 slice.57.rest_ref
  127.1 6.2 %all-to-all-done.2.got_ref = f32[8,2,32,128]{3,2,1,0:T(8,128)} async-done(((f32[8,2,32,128]{3,2,1,0:T(8,128)}), f32[8,2,32,128]{3,2,1,0:T(8,128)}, u32[]{:S(2)}, u32[]{:S(2)}) %all-to-all-start.2) | async-done | bytes 262176 | tf_op jit(solution)/shard_map/all_to_all | solution.py:491
  133.3 2.2 shard_map.39
  135.5 0.0 all-gather.6.cloned.1.call-update
  135.6 0.6 fusion
  137.5 0.0 all-gather.8.cloned.1.call-done
  137.5 1.1 slice_select_fusion.1
  138.6 4.8 %collective-permute-start.4 = (f32[5,3,32,128]{3,2,1,0:T(8,128)S(1)}, f32[5,3,32,128]{3,2,1,0:T(8,128)S(1)}, u32[]{:S(2)}, u32[]{:S(2)}) collective-permute-start(f32[5,3,32,128]{3,2,1,0:T(8,128)S(1)} %get-tuple-element.81), channel_id=1, source_target_pairs={{0,0},{1,8},{2,16},{3,24},{4,32},{5,40},{6,48},{7,56},{8,64},{9,72... | collective-permute-start | bytes 737288 | tf_op jit(solution)/shard_map/ppermute | solution.py:521
  143.5 2.6 collective-permute-start.5
  146.1 0.1 constant_dynamic-slice_fusion.4
  146.2 0.0 collective-permute-start.6
  146.3 2.1 collective-permute-start.7
  148.4 31.8 %shard_map.40 = (f32[9,256,256]{2,1,0:T(8,128)}, bf16[9,256,256]{2,1,0:T(8,128)(2,1)}, bf16[9,256,256]{2,1,0:T(8,128)(2,1)}, f32[6,256,256]{2,1,0:T(8,128)}) custom-call(s32[34]{0:T(128)} %pad_add_fusion.meta, f32[8,16,3,32,128]{4,3,2,1,0:T(8,128)} %bitcast.52), custom_call_target="tpu_custom_call" | custom-call | flops 35200000000 | bytes 1048576 | tf_op jit(solution)/shard_map/pallas_call | solution.py:533
  180.3 0.0 collective-permute-done.4
  180.3 0.0 collective-permute-done.5
  180.4 0.0 collective-permute-done.6
  180.4 0.0 collective-permute-done.7
  180.4 2.4 broadcast_in_dim.2
  182.8 4.7 %all-to-all-start.3 = ((f32[8,2,5,3,32,128]{5,4,3,2,1,0:T(8,128)}), f32[8,2,5,3,32,128]{5,4,3,2,1,0:T(8,128)}, u32[]{:S(2)}, u32[]{:S(2)}) async-start(f32[8,2,5,3,32,128]{5,4,3,2,1,0:T(8,128)} %broadcast_in_dim.2), calls=%async_computation.3 | async-start | bytes 7864320 | tf_op jit(solution)/shard_map/all_to_all | solution.py:547
  187.6 33.8 %shard_map.41 = (f32[6,256,256]{2,1,0:T(8,128)}, bf16[6,256,256]{2,1,0:T(8,128)(2,1)}, bf16[6,256,256]{2,1,0:T(8,128)(2,1)}) custom-call(f32[6,256,256]{2,1,0:T(8,128)} %get-tuple-element.56.rest_ref), custom_call_target="tpu_custom_call" | custom-call | flops 44000002048 | bytes 1048576 | tf_op jit(solution)/shard_map/pallas_call | solution.py:548
  221.4 0.1 pad_maximum_fusion.1.child_1
  221.5 3.0 %collective-permute-start.9 = (f32[6,512,128]{2,1,0:T(8,128)S(1)}, f32[6,512,128]{2,1,0:T(8,128)S(1)}, u32[]{:S(2)}, u32[]{:S(2)}) collective-permute-start(f32[6,512,128]{2,1,0:T(8,128)S(1)} %pad_maximum_fusion.1.child_1), channel_id=1, source_target_pairs={{0,1},{1,2},{2,3},{3,4},{4,5},{5,6},{6,7},{7,8},{8,9},{9,10},{10,1... | collective-permute-start | bytes 4718600 | tf_op jit(solution)/shard_map/ppermute | solution.py:558
  224.5 0.0 collective-permute-start.8
  224.5 17.6 %shard_map.42 = (bf16[1536,1280]{1,0:T(8,128)(2,1)}, bf16[1536,1280]{1,0:T(8,128)(2,1)}, f32[1536,256]{1,0:T(8,128)}) custom-call(s32[34]{0:T(128)} %pad_add_fusion.meta, f32[16,5,6,32,128]{4,3,2,1,0:T(8,128)} %bitcast.51, bf16[9,256,256]{2,1,0:T(8,128)(2,1)} %get-tuple-element.48.hh_ref, bf16[9,256,256]{2,1,0:T(8,128)(2,1)} %get-tuple-element.49.hl_ref, ...), custom_call_target="tpu_custom_call" | custom-call | flops 22000001024 | bytes 1048576 | tf_op jit(solution)/shard_map/pallas_call | solution.py:567
  242.1 0.0 all-to-all-done.3
  242.1 11.2 %shard_map.43 = (bf16[768,1280]{1,0:T(8,128)(2,1)}, bf16[768,1280]{1,0:T(8,128)(2,1)}) custom-call(f32[16,5,3,32,128]{4,3,2,1,0:T(8,128)} %bitcast.20.parts_ref, bf16[9,256,256]{2,1,0:T(8,128)(2,1)} %get-tuple-element.48.hh_ref, bf16[9,256,256]{2,1,0:T(8,128)(2,1)} %get-tuple-element.49.hl_ref, bf16[6,256,256]{2,1,0:T(8,128)(2,1)} %get-tuple-element.58.th_ref, ...), custom_call_target="tpu_custom_call" | custom-call | flops 13200000000 | bytes 1048576 | tf_op jit(solution)/shard_map/pallas_call | solution.py:586
  253.3 5.2 %collective-permute-done.9.child_2 = f32[6,512,128]{2,1,0:T(8,128)S(1)} collective-permute-done((f32[6,512,128]{2,1,0:T(8,128)S(1)}, f32[6,512,128]{2,1,0:T(8,128)S(1)}, u32[]{:S(2)}, u32[]{:S(2)}) %collective-permute-start.9) | collective-permute-done | bytes 1572896 | tf_op jit(solution)/shard_map/ppermute | solution.py:558
  258.5 5.6 %collective-permute-done.8.child_0 = f32[6,512,128]{2,1,0:T(8,128)} collective-permute-done((f32[6,512,128]{2,1,0:T(8,128)S(1)}, f32[6,512,128]{2,1,0:T(8,128)}, u32[]{:S(2)}, u32[]{:S(2)}) %collective-permute-start.8) | collective-permute-done | bytes 1572896 | tf_op jit(solution)/shard_map/ppermute | solution.py:559
  264.1 20.5 %shard_map.44 = f32[9216,128]{1,0:T(8,128)} custom-call(s32[34]{0:T(128)} %pad_add_fusion.meta, bf16[1536,1280]{1,0:T(8,128)(2,1)} %get-tuple-element.60.yh, bf16[1536,1280]{1,0:T(8,128)(2,1)} %get-tuple-element.61.yl, f32[1536,256]{1,0:T(8,128)} %get-tuple-element.64.own_ref, bf16[768,1280]{1,0:T(8,128)(2,1)} %get-tuple-element.66.rh_ref, ...), custom_call_target="tpu_custom_call" | custom-call | flops 19800000512 | bytes 1048576 | tf_op jit(solution)/shard_map/pallas_call | solution.py:599
  (30 shorter events, 0.2 us)
Async XLA Ops:
  6.5 10.1 %copy-start = (f32[4,1,256,1,1,256]{5,4,3,2,1,0:T(1,128)S(1)}, f32[4,1,256,1,1,256]{5,4,3,2,1,0:T(1,128)}, u32[]{:S(2)}) copy-start(f32[4,1,256,1,1,256]{5,4,3,2,1,0:T(1,128)} %param.4) | copy-start | bytes 3145732
  6.5 10.1 %copy-start.12 = (s32[2,16]{1,0:T(2,128)S(1)}, s32[2,16]{1,0:T(2,128)}, u32[]{:S(2)}) copy-start(s32[2,16]{1,0:T(2,128)} %param.5) | copy-start | bytes 388
  9.6 14.4 %all-to-all-start = ((f32[16,2,32,128]{3,2,1,0:T(8,128)}), f32[16,2,32,128]{3,2,1,0:T(8,128)S(1)}, u32[]{:S(2)}, u32[]{:S(2)}) async-start(f32[16,2,32,128]{3,2,1,0:T(8,128)} %pad_maximum_fusion.2), calls=%async_computation | async-start | bytes 1048576 | tf_op jit(solution)/shard_map/all_to_all | solution.py:468
  16.5 121.0 %all-gather.8.cloned.1.call-start = ((), (), s32[]{:S(2)}) async-start(), calls=%async_computation.5 | async-start | bytes 7077888 | tf_op jit(solution)/shard_map/all_gather | solution.py:476
  24.0 7.4 %copy-start.2 = (f32[7,32,128]{2,1,0:T(8,128)}, f32[7,32,128]{2,1,0:T(8,128)S(1)}, u32[]{:S(2)}) copy-start(f32[7,32,128]{2,1,0:T(8,128)S(1)} %pad_maximum_fusion.6.mine_ref) | copy-start | bytes 344068
  24.0 6.2 %collective-permute-start.1 = (f32[1,32,128]{2,1,0:T(8,128)S(1)}, f32[1,32,128]{2,1,0:T(8,128)S(1)}, u32[]{:S(2)}, u32[]{:S(2)}) collective-permute-start(f32[1,32,128]{2,1,0:T(8,128)S(1)} %slice.56), channel_id=1, source_target_pairs={{0,112},{1,113},{2,114},{3,115},{4,116},{5,117},{6,118},{7,119},{8... | collective-permute-start | bytes 49160 | tf_op jit(solution)/shard_map/ppermute | solution.py:473
  27.2 4.1 %collective-permute-start = (f32[3,32,128]{2,1,0:T(8,128)S(1)}, f32[3,32,128]{2,1,0:T(8,128)S(1)}, u32[]{:S(2)}, u32[]{:S(2)}) collective-permute-start(f32[3,32,128]{2,1,0:T(8,128)S(1)} %slice_select_fusion.2), channel_id=1, source_target_pairs={{0,96},{16,80},{1,97},{17,81},{2,98},{18,82},{3,99},{19,83},{4,100... | collective-permute-start | bytes 147464 | tf_op jit(solution)/shard_map/ppermute | solution.py:472
  30.2 1.1 copy-start.11
  31.3 0.6 copy-start.10
  63.1 48.2 %all-to-all-start.1 = ((f32[16,9,32,128]{3,2,1,0:T(8,128)}), f32[16,9,32,128]{3,2,1,0:T(8,128)S(1)}, u32[]{:S(2)}, u32[]{:S(2)}) async-start(f32[16,9,32,128]{3,2,1,0:T(8,128)} %copy_bitcast_fusion), calls=%async_computation.1 | async-start | bytes 4718592 | tf_op jit(solution)/shard_map/all_to_all | solution.py:480
  69.8 35.9 %collective-permute-start.2 = (f32[2,512,128]{2,1,0:T(8,128)}, f32[2,512,128]{2,1,0:T(8,128)S(1)}, u32[]{:S(2)}, u32[]{:S(2)}) collective-permute-start(f32[2,512,128]{2,1,0:T(8,128)} %get-tuple-element.42), channel_id=1, source_target_pairs={{1,20},{2,23},{3,26},{4,29},{5,16},{6,19},{7,22},{8,25},{9,28},{10... | collective-permute-start | bytes 1572872 | tf_op jit(solution)/shard_map/ppermute | solution.py:488
  71.7 39.6 %collective-permute-start.3 = (f32[2,512,128]{2,1,0:T(8,128)}, f32[2,512,128]{2,1,0:T(8,128)S(1)}, u32[]{:S(2)}, u32[]{:S(2)}) collective-permute-start(f32[2,512,128]{2,1,0:T(8,128)} %get-tuple-element.43), channel_id=1, source_target_pairs={{1,84},{2,87},{3,90},{4,93},{5,80},{6,83},{7,86},{8,89},{9,92},{10... | collective-permute-start | bytes 1572872 | tf_op jit(solution)/shard_map/ppermute | solution.py:488
  112.0 13.7 %copy-start.3 = (f32[7,32,128]{2,1,0:T(8,128)S(1)}, f32[7,32,128]{2,1,0:T(8,128)}, u32[]{:S(2)}) copy-start(f32[7,32,128]{2,1,0:T(8,128)} %copy-done.2) | copy-start | bytes 344068
  113.8 19.5 %all-to-all-start.2 = ((f32[8,2,32,128]{3,2,1,0:T(8,128)}), f32[8,2,32,128]{3,2,1,0:T(8,128)}, u32[]{:S(2)}, u32[]{:S(2)}) async-start(f32[8,2,32,128]{3,2,1,0:T(8,128)} %shard_map.38), calls=%async_computation.2 | async-start | bytes 524288 | tf_op jit(solution)/shard_map/all_to_all | solution.py:491
  125.6 98.9 %all-gather.6.cloned.1.call-start = ((), (), s32[]{:S(2)}) async-start(), calls=%async_computation.4 | async-start | bytes 8355840 | tf_op jit(solution)/shard_map/all_gather | solution.py:497
  127.1 8.5 %copy-start.8 = (s32[34]{0:T(128)S(1)}, s32[34]{0:T(128)}, u32[]{:S(2)}) copy-start(s32[34]{0:T(128)} %pad_add_fusion.meta) | copy-start | bytes 412
  138.6 41.6 %collective-permute-start.4 = (f32[5,3,32,128]{3,2,1,0:T(8,128)S(1)}, f32[5,3,32,128]{3,2,1,0:T(8,128)S(1)}, u32[]{:S(2)}, u32[]{:S(2)}) collective-permute-start(f32[5,3,32,128]{3,2,1,0:T(8,128)S(1)} %get-tuple-element.81), channel_id=1, source_target_pairs={{0,0},{1,8},{2,16},{3,24},{4,32},{5,40},{6,48},{7,56},{8,64},{9,72... | collective-permute-start | bytes 737288 | tf_op jit(solution)/shard_map/ppermute | solution.py:521
  143.5 36.8 %collective-permute-start.5 = (f32[5,3,32,128]{3,2,1,0:T(8,128)S(1)}, f32[5,3,32,128]{3,2,1,0:T(8,128)S(1)}, u32[]{:S(2)}, u32[]{:S(2)}) collective-permute-start(f32[5,3,32,128]{3,2,1,0:T(8,128)S(1)} %get-tuple-element.82), channel_id=1, source_target_pairs={{0,8},{1,0},{2,24},{3,16},{4,40},{5,32},{6,56},{7,48},{8,72},{9,64... | collective-permute-start | bytes 737288 | tf_op jit(solution)/shard_map/ppermute | solution.py:522
  146.2 34.1 %collective-permute-start.6 = (f32[2,512,128]{2,1,0:T(8,128)S(1)}, f32[2,512,128]{2,1,0:T(8,128)S(1)}, u32[]{:S(2)}, u32[]{:S(2)}) collective-permute-start(f32[2,512,128]{2,1,0:T(8,128)S(1)} %pad_maximum_fusion.3), channel_id=1, source_target_pairs={{0,112},{16,0},{32,16},{48,32},{64,48},{80,64},{96,80},{112,96},{1... | collective-permute-start | bytes 1572872 | tf_op jit(solution)/shard_map/ppermute | solution.py:512
  146.3 34.1 %collective-permute-start.7 = (f32[2,512,128]{2,1,0:T(8,128)S(1)}, f32[2,512,128]{2,1,0:T(8,128)S(1)}, u32[]{:S(2)}, u32[]{:S(2)}) collective-permute-start(f32[2,512,128]{2,1,0:T(8,128)S(1)} %pad_maximum_fusion.4), channel_id=1, source_target_pairs={{0,16},{16,32},{32,48},{48,64},{64,80},{80,96},{96,112},{112,0},{1... | collective-permute-start | bytes 1572872 | tf_op jit(solution)/shard_map/ppermute | solution.py:513
  180.4 2.5 copy-start.4
  180.4 2.4 copy-start.6
  182.8 59.3 %all-to-all-start.3 = ((f32[8,2,5,3,32,128]{5,4,3,2,1,0:T(8,128)}), f32[8,2,5,3,32,128]{5,4,3,2,1,0:T(8,128)}, u32[]{:S(2)}, u32[]{:S(2)}) async-start(f32[8,2,5,3,32,128]{5,4,3,2,1,0:T(8,128)} %broadcast_in_dim.2), calls=%async_computation.3 | async-start | bytes 7864320 | tf_op jit(solution)/shard_map/all_to_all | solution.py:547
  187.6 33.8 %copy-start.5 = (f32[2,512,128]{2,1,0:T(8,128)S(1)}, f32[2,512,128]{2,1,0:T(8,128)}, u32[]{:S(2)}) copy-start(f32[2,512,128]{2,1,0:T(8,128)} %copy-done.4) | copy-start | bytes 1572868
  187.6 33.8 %copy-start.7 = (f32[2,512,128]{2,1,0:T(8,128)S(1)}, f32[2,512,128]{2,1,0:T(8,128)}, u32[]{:S(2)}) copy-start(f32[2,512,128]{2,1,0:T(8,128)} %copy-done.6) | copy-start | bytes 1572868
  221.5 20.6 %copy-start.1 = (f32[6,512,128]{2,1,0:T(8,128)}, f32[6,512,128]{2,1,0:T(8,128)S(1)}, u32[]{:S(2)}) copy-start(f32[6,512,128]{2,1,0:T(8,128)S(1)} %pad_maximum_fusion.1.child_1) | copy-start | bytes 4718596
  221.5 37.0 %collective-permute-start.9 = (f32[6,512,128]{2,1,0:T(8,128)S(1)}, f32[6,512,128]{2,1,0:T(8,128)S(1)}, u32[]{:S(2)}, u32[]{:S(2)}) collective-permute-start(f32[6,512,128]{2,1,0:T(8,128)S(1)} %pad_maximum_fusion.1.child_1), channel_id=1, source_target_pairs={{0,1},{1,2},{2,3},{3,4},{4,5},{5,6},{6,7},{7,8},{8,9},{9,10},{10,1... | collective-permute-start | bytes 4718600 | tf_op jit(solution)/shard_map/ppermute | solution.py:558
  224.5 39.6 %collective-permute-start.8 = (f32[6,512,128]{2,1,0:T(8,128)S(1)}, f32[6,512,128]{2,1,0:T(8,128)}, u32[]{:S(2)}, u32[]{:S(2)}) collective-permute-start(f32[6,512,128]{2,1,0:T(8,128)S(1)} %pad_maximum_fusion.1.child_1), channel_id=1, source_target_pairs={{0,15},{1,0},{2,1},{3,2},{4,3},{5,4},{6,5},{7,6},{8,7},{9,8},{10,9... | collective-permute-start | bytes 4718600 | tf_op jit(solution)/shard_map/ppermute | solution.py:559
  258.5 5.6 %copy-start.9 = (f32[6,512,128]{2,1,0:T(8,128)}, f32[6,512,128]{2,1,0:T(8,128)S(1)}, u32[]{:S(2)}) copy-start(f32[6,512,128]{2,1,0:T(8,128)S(1)} %collective-permute-done.9.child_2) | copy-start | bytes 4718596
Sparse Core Ops, SparseCore 0:
  60.2 52.5 all-gather.7
  135.7 83.2 all-gather.5

commit v13 on v11

--- a/solution.py
+++ b/solution.py
@@ -360,7 +360,7 @@
 SCHUR_STEP = 1
 
 
-def schur_kernel(meta, yh, yl, own_ref, rh_ref, rl_ref, head_ref, tail_ref, parent_ref, child_0, child_1, child_2, out_ref):
+def schur_kernel(meta, yh, yl, own_ref, rh_ref, rl_ref, head_ref, tail_ref, parent_ref, child_0, more_0, child_1, child_2, more_2, out_ref):
     step = pl.program_id(0)
     row, col = meta[32], meta[33]
     routes = []
@@ -388,13 +388,14 @@
                 for n, (child, there, to) in enumerate(routes):
                     here = jnp.logical_and(there, to == slot)
                     here = jnp.logical_and(here, meta[child * 16 + source] == block_col)
-                    for d, child_ref in enumerate((child_0, child_1, child_2)):
+                    for d, child_ref in enumerate(((child_0, more_0), (child_1,), (child_2, more_2))):
 
                         @pl.when(jnp.logical_and(here, turn == d))
                         def _():
+                            per = 6 // len(child_ref)
                             for h in range(2):
                                 at = pl.ds(1536 * a + 2 * c + h, NB, stride=6)
-                                out_ref[at, :] = out_ref[at, :] + child_ref[n, pl.ds(h, NB, stride=2), :]
+                                out_ref[at, :] = out_ref[at, :] + child_ref[n // per][n % per, pl.ds(h, NB, stride=2), :]
 
             @pl.when(jnp.logical_and(block_row < KB, block_col >= KB))
             def _():
@@ -555,8 +556,9 @@
 
     middle = jnp.concatenate([jnp.stack([chosen[0, 1], chosen[1, 1]]), down, up])
     middle, tail_h = lax.optimization_barrier((middle, tail_h))
-    below = lax.ppermute(middle, "pcol", [(q, (q + 1) % 16) for q in range(16)])
-    above = lax.ppermute(middle, "pcol", [(q, (q + 15) % 16) for q in range(16)])
+    halves = (middle[0:3], middle[3:6])
+    below = [lax.ppermute(half, "pcol", [(q, (q + 1) % 16) for q in range(16)]) for half in halves]
+    above = [lax.ppermute(half, "pcol", [(q, (q + 15) % 16) for q in range(16)]) for half in halves]
 
     rows = NB * ROWS_STEP
     steps = 6 // ROWS_STEP
@@ -593,6 +595,7 @@
 
     whole_right = pl.BlockSpec((768, 1280), lambda g: (0, 0))
     whole_child = pl.BlockSpec((6, 512, LANES), lambda g: (0, 0, 0))
+    half_child = pl.BlockSpec((3, 512, LANES), lambda g: (0, 0, 0))
     front_rows = pl.BlockSpec((1536 * SCHUR_STEP, LANES), lambda g: (g, 0))
     y_rows = pl.BlockSpec((NB * SCHUR_STEP, 1280), lambda g: (g, 0))
     own_block = pl.BlockSpec((NB * SCHUR_STEP, NB), lambda g: (g, 0))
@@ -601,7 +604,7 @@
         grid=(6 // SCHUR_STEP,),
         out_shape=shaped((9216, LANES)),
         in_specs=[SM, y_rows, y_rows, own_block, whole_right, whole_right, whole_head, whole_tail, front_rows]
-        + [whole_child] * 3,
+        + [half_child, half_child, whole_child, half_child, half_child],
         out_specs=front_rows,
         compiler_params=pltpu.CompilerParams(vmem_limit_bytes=VMEM_LIMIT),
         cost_estimate=cost(18),
@@ -615,7 +618,9 @@
         head_u,
         tail_u,
         parent.reshape(9216, LANES),
-        *(x.reshape(6, 512, LANES) for x in (above, middle, below)),
+        *above,
+        middle,
+        *below,
     )
     return out.reshape(6, 1, NB, 3, 1, NB)
 

time: 282 us -> 282 us (level)
  waiting for transfers between devices: 34.5 us -> 30.1 us
  starting transfers between devices: 42.1 us -> 46.4 us
    ppermute x2 -> x4, waiting for transfers between devices: 10.4 us -> 6.03 us  [the longest x2 4.07 us: per_device(): lax.ppermute(half, 'pcol', [(q, (q + 15) % 16) for q in range(16)])]
    ppermute x2 -> x4, starting transfers between devices: 2.09 us -> 6.33 us  [the longest x2 5.22 us: per_device(): lax.ppermute(half, 'pcol', [(q, (q + 1) % 16) for q in range(16)])]
  transfers between devices with their start and end apart: 15 -> 17, of which waited for: 6 -> 6; matrix products, arithmetic and copies ran while one was open for 4% -> 4% of each run, Pallas kernels for 35% -> 35%
where the time goes in v13:
time: 282 us; the launch traced here: 280 us
  Pallas kernels  121 us (43%)
  blocking collectives  53.6 us (19%)
  starting transfers between devices  46.4 us (16%)
  waiting for transfers between devices  30.1 us (11%)
  between operations  15.1 us (5%)
  local copies, waits for them, and re-layouts  10.7 us (4%)
  other arithmetic  3.08 us (1%)
    pallas_call x1, Pallas kernels, per_device(): call(chain_tail_kernel, (shaped((TAILS, NB, NB)), shaped((TAILS, NB, NB),...  33.8 us
    pallas_call x1, Pallas kernels, per_device(): call(chain_head_kernel, (shaped((HEADS, NB, NB)), shaped((HEADS, NB, NB),...  31.8 us
    all_to_all x1, blocking collectives, per_device(): rest = lax.all_to_all(rest, 'pcol', 0, 0, tiled=True)  27.2 us
    all_gather x1, blocking collectives, per_device(): chunk = lax.all_gather(chunk, 'pcol')  26.4 us
    pallas_call x1, Pallas kernels, per_device(): pl.pallas_call(schur_kernel, grid=(6 // SCHUR_STEP,), out_shape=shaped((9...  20.5 us
    pallas_call x1, Pallas kernels, per_device(): pl.pallas_call(left_kernel, grid=(steps,), out_shape=(shaped((1536, 1280)...  17.6 us
    all_to_all x1, waiting for transfers between devices, per_device(): pieces = lax.all_to_all(pieces, 'prow', 0, 0, tiled=True)  13.2 us
    pallas_call x1, Pallas kernels, per_device(): call(right_kernel, (shaped((768, 1280), BF16), shaped((768, 1280), BF16))...  11.2 us
  transfers between devices with their start and end apart: 17, of which 6 were waited for; matrix products, arithmetic and copies ran while one was open for 4% of the time, Pallas kernels for 35%

profile of v13, /device:TPU:102, one launch (start us, length us, event | category | flops | bytes accessed | tf_op | source)
XLA Modules:
  0.0 279.6 jit_solution(3079702801202693473)
XLA Ops:
  6.5 1.1 slice.69
  7.6 1.1 slice.54
  8.7 0.8 pad_maximum_fusion.2
  9.6 6.9 %all-to-all-start = ((f32[16,2,32,128]{3,2,1,0:T(8,128)}), f32[16,2,32,128]{3,2,1,0:T(8,128)S(1)}, u32[]{:S(2)}, u32[]{:S(2)}) async-start(f32[16,2,32,128]{3,2,1,0:T(8,128)} %pad_maximum_fusion.2), calls=%async_computation | async-start | bytes 1048576 | tf_op jit(solution)/shard_map/all_to_all | solution.py:469
  16.5 0.0 all-gather.8.cloned.1.call-start
  16.6 0.1 reshape.24
  16.7 1.1 dynamic-slice_bitcast_fusion
  17.7 6.2 %all-to-all-done = f32[16,2,32,128]{3,2,1,0:T(8,128)S(1)} async-done(((f32[16,2,32,128]{3,2,1,0:T(8,128)}), f32[16,2,32,128]{3,2,1,0:T(8,128)S(1)}, u32[]{:S(2)}, u32[]{:S(2)}) %all-to-all-start) | async-done | bytes 524320 | tf_op jit(solution)/shard_map/all_to_all | solution.py:469
  24.0 0.0 copy-start.2
  24.0 3.2 %collective-permute-start.1 = (f32[1,32,128]{2,1,0:T(8,128)S(1)}, f32[1,32,128]{2,1,0:T(8,128)S(1)}, u32[]{:S(2)}, u32[]{:S(2)}) collective-permute-start(f32[1,32,128]{2,1,0:T(8,128)S(1)} %slice.62), channel_id=1, source_target_pairs={{0,112},{1,113},{2,114},{3,115},{4,116},{5,117},{6,118},{7,119},{8... | collective-permute-start | bytes 49160 | tf_op jit(solution)/shard_map/ppermute | solution.py:474
  27.2 2.4 collective-permute-start
  29.6 0.7 pad_add_fusion.meta
  30.3 0.0 collective-permute-done.1.got_b_ref
  30.3 1.1 collective-permute-done.got_a_ref
  31.3 0.6 copy-done.7
  32.0 1.6 shard_map.37
  33.6 26.4 %all-gather = f32[48,32,128]{2,1,0:T(8,128)} all-gather(f32[3,32,128]{2,1,0:T(8,128)} %shard_map.37), channel_id=2, replica_groups=mesh['prow'=8,'pcol'=16] {'pcol'}, dimensions={0}, use_global_device_ids=true | all-gather | bytes 835584 | tf_op jit(solution)/shard_map/all_gather | solution.py:476
  60.0 0.0 all-gather.8.cloned.1.call-update
  60.0 1.4 slice.72
  61.4 0.2 copy_bitcast_fusion
  61.7 27.2 %all_to_all.20 = f32[16,9,32,128]{3,2,1,0:T(8,128)S(1)} all-to-all(f32[16,9,32,128]{3,2,1,0:T(8,128)S(1)} %copy_bitcast_fusion), channel_id=1, replica_groups=mesh['prow'=8,'pcol'=16] {'pcol'}, dimensions={0} | all-to-all | bytes 4718592 | tf_op jit(solution)/shard_map/all_to_all | solution.py:481
  88.8 0.7 slice.74.parts_ref
  89.5 1.8 shard_map.38
  91.3 1.9 collective-permute-start.2
  93.2 6.2 %collective-permute-start.3 = (f32[2,512,128]{2,1,0:T(8,128)}, f32[2,512,128]{2,1,0:T(8,128)S(1)}, u32[]{:S(2)}, u32[]{:S(2)}) collective-permute-start(f32[2,512,128]{2,1,0:T(8,128)} %get-tuple-element.45), channel_id=1, source_target_pairs={{1,84},{2,87},{3,90},{4,93},{5,80},{6,83},{7,86},{8,89},{9,92},{10... | collective-permute-start | bytes 1572872 | tf_op jit(solution)/shard_map/ppermute | solution.py:492
  99.4 4.6 %all-to-all-start.2 = ((f32[8,2,32,128]{3,2,1,0:T(8,128)}), f32[8,2,32,128]{3,2,1,0:T(8,128)}, u32[]{:S(2)}, u32[]{:S(2)}) async-start(f32[8,2,32,128]{3,2,1,0:T(8,128)} %shard_map.38), calls=%async_computation.2 | async-start | bytes 524288 | tf_op jit(solution)/shard_map/all_to_all | solution.py:484
  104.0 0.0 all-gather.6.cloned.1.call-start
  104.0 0.6 slice.57.first_ref
  104.7 0.8 slice.73.rest_ref
  105.5 13.2 %all-to-all-done.2.got_ref = f32[8,2,32,128]{3,2,1,0:T(8,128)} async-done(((f32[8,2,32,128]{3,2,1,0:T(8,128)}), f32[8,2,32,128]{3,2,1,0:T(8,128)}, u32[]{:S(2)}, u32[]{:S(2)}) %all-to-all-start.2) | async-done | bytes 262176 | tf_op jit(solution)/shard_map/all_to_all | solution.py:484
  118.7 0.0 collective-permute-done.2
  118.7 3.6 %collective-permute-done.3 = f32[2,512,128]{2,1,0:T(8,128)S(1)} collective-permute-done((f32[2,512,128]{2,1,0:T(8,128)}, f32[2,512,128]{2,1,0:T(8,128)S(1)}, u32[]{:S(2)}, u32[]{:S(2)}) %collective-permute-start.3) | collective-permute-done | bytes 524320 | tf_op jit(solution)/shard_map/ppermute | solution.py:492
  122.2 2.3 shard_map.39
  124.5 0.0 all-gather.6.cloned.1.call-update
  124.6 0.6 fusion.1
  126.5 0.0 all-gather.8.cloned.1.call-done
  126.6 1.1 slice_select_fusion.1
  127.7 3.0 %collective-permute-start.4 = (f32[5,3,32,128]{3,2,1,0:T(8,128)S(1)}, f32[5,3,32,128]{3,2,1,0:T(8,128)S(1)}, u32[]{:S(2)}, u32[]{:S(2)}) collective-permute-start(f32[5,3,32,128]{3,2,1,0:T(8,128)S(1)} %get-tuple-element.85), channel_id=1, source_target_pairs={{0,0},{1,8},{2,16},{3,24},{4,32},{5,40},{6,48},{7,56},{8,64},{9,72... | collective-permute-start | bytes 737288 | tf_op jit(solution)/shard_map/ppermute | solution.py:522
  130.7 6.2 %collective-permute-start.5 = (f32[5,3,32,128]{3,2,1,0:T(8,128)S(1)}, f32[5,3,32,128]{3,2,1,0:T(8,128)S(1)}, u32[]{:S(2)}, u32[]{:S(2)}) collective-permute-start(f32[5,3,32,128]{3,2,1,0:T(8,128)S(1)} %get-tuple-element.86), channel_id=1, source_target_pairs={{0,8},{1,0},{2,24},{3,16},{4,40},{5,32},{6,56},{7,48},{8,72},{9,64... | collective-permute-start | bytes 737288 | tf_op jit(solution)/shard_map/ppermute | solution.py:523
  136.9 0.1 constant_dynamic-slice_fusion.4
  137.0 0.0 collective-permute-start.6
  137.1 0.5 collective-permute-start.7
  137.6 31.8 %shard_map.40 = (f32[9,256,256]{2,1,0:T(8,128)}, bf16[9,256,256]{2,1,0:T(8,128)(2,1)}, bf16[9,256,256]{2,1,0:T(8,128)(2,1)}, f32[6,256,256]{2,1,0:T(8,128)}) custom-call(s32[34]{0:T(128)} %pad_add_fusion.meta, f32[8,16,3,32,128]{4,3,2,1,0:T(8,128)} %bitcast.52), custom_call_target="tpu_custom_call" | custom-call | flops 35200000000 | bytes 1048576 | tf_op jit(solution)/shard_map/pallas_call | solution.py:534
  169.3 0.0 collective-permute-done.4
  169.3 0.0 collective-permute-done.5
  169.4 0.0 collective-permute-done.6
  169.4 0.0 collective-permute-done.7
  169.5 2.4 broadcast_in_dim.2
  171.9 5.1 %all-to-all-start.3 = ((f32[8,2,5,3,32,128]{5,4,3,2,1,0:T(8,128)}), f32[8,2,5,3,32,128]{5,4,3,2,1,0:T(8,128)}, u32[]{:S(2)}, u32[]{:S(2)}) async-start(f32[8,2,5,3,32,128]{5,4,3,2,1,0:T(8,128)} %broadcast_in_dim.2), calls=%async_computation.3 | async-start | bytes 7864320 | tf_op jit(solution)/shard_map/all_to_all | solution.py:548
  177.0 33.8 %shard_map.41 = (f32[6,256,256]{2,1,0:T(8,128)}, bf16[6,256,256]{2,1,0:T(8,128)(2,1)}, bf16[6,256,256]{2,1,0:T(8,128)(2,1)}) custom-call(f32[6,256,256]{2,1,0:T(8,128)} %get-tuple-element.58.rest_ref), custom_call_target="tpu_custom_call" | custom-call | flops 44000002048 | bytes 1048576 | tf_op jit(solution)/shard_map/pallas_call | solution.py:549
  210.8 0.1 pad_maximum_fusion.1.child_1
  210.9 0.1 fusion
  211.0 1.0 collective-permute-start.11
  212.0 1.1 collective-permute-start.9
  213.1 4.2 %collective-permute-start.10 = (f32[3,512,128]{2,1,0:T(8,128)S(1)}, f32[3,512,128]{2,1,0:T(8,128)}, u32[]{:S(2)}, u32[]{:S(2)}) collective-permute-start(f32[3,512,128]{2,1,0:T(8,128)S(1)} %get-tuple-element.74), channel_id=1, source_target_pairs={{0,1},{1,2},{2,3},{3,4},{4,5},{5,6},{6,7},{7,8},{8,9},{9,10},{10,1... | collective-permute-start | bytes 2359304 | tf_op jit(solution)/shard_map/ppermute | solution.py:560
  217.4 0.0 collective-permute-start.8
  217.4 17.6 %shard_map.42 = (bf16[1536,1280]{1,0:T(8,128)(2,1)}, bf16[1536,1280]{1,0:T(8,128)(2,1)}, f32[1536,256]{1,0:T(8,128)}) custom-call(s32[34]{0:T(128)} %pad_add_fusion.meta, f32[16,5,6,32,128]{4,3,2,1,0:T(8,128)} %bitcast.51, bf16[9,256,256]{2,1,0:T(8,128)(2,1)} %get-tuple-element.50.hh_ref, bf16[9,256,256]{2,1,0:T(8,128)(2,1)} %get-tuple-element.51.hl_ref, ...), custom_call_target="tpu_custom_call" | custom-call | flops 22000001024 | bytes 1048576 | tf_op jit(solution)/shard_map/pallas_call | solution.py:569
  235.0 0.0 all-to-all-done.3
  235.0 11.2 %shard_map.43 = (bf16[768,1280]{1,0:T(8,128)(2,1)}, bf16[768,1280]{1,0:T(8,128)(2,1)}) custom-call(f32[16,5,3,32,128]{4,3,2,1,0:T(8,128)} %bitcast.20.parts_ref, bf16[9,256,256]{2,1,0:T(8,128)(2,1)} %get-tuple-element.50.hh_ref, bf16[9,256,256]{2,1,0:T(8,128)(2,1)} %get-tuple-element.51.hl_ref, bf16[6,256,256]{2,1,0:T(8,128)(2,1)} %get-tuple-element.60.th_ref, ...), custom_call_target="tpu_custom_call" | custom-call | flops 13200000000 | bytes 1048576 | tf_op jit(solution)/shard_map/pallas_call | solution.py:588
  246.2 0.0 collective-permute-done.11.more_2
  246.2 0.0 collective-permute-done.9.more_0
  246.2 2.0 collective-permute-done.10.child_2
  248.2 4.1 %collective-permute-done.8.child_0 = f32[3,512,128]{2,1,0:T(8,128)} collective-permute-done((f32[3,512,128]{2,1,0:T(8,128)S(1)}, f32[3,512,128]{2,1,0:T(8,128)}, u32[]{:S(2)}, u32[]{:S(2)}) %collective-permute-start.8) | collective-permute-done | bytes 786464 | tf_op jit(solution)/shard_map/ppermute | solution.py:561
  252.3 20.5 %shard_map.44 = f32[9216,128]{1,0:T(8,128)} custom-call(s32[34]{0:T(128)} %pad_add_fusion.meta, bf16[1536,1280]{1,0:T(8,128)(2,1)} %get-tuple-element.62.yh, bf16[1536,1280]{1,0:T(8,128)(2,1)} %get-tuple-element.63.yl, f32[1536,256]{1,0:T(8,128)} %get-tuple-element.66.own_ref, bf16[768,1280]{1,0:T(8,128)(2,1)} %get-tuple-element.68.rh_ref, ...), custom_call_target="tpu_custom_call" | custom-call | flops 19800000512 | bytes 1048576 | tf_op jit(solution)/shard_map/pallas_call | solution.py:602
  (28 shorter events, 0.2 us)
Async XLA Ops:
  6.5 10.1 %copy-start.1 = (f32[4,1,256,1,1,256]{5,4,3,2,1,0:T(1,128)S(1)}, f32[4,1,256,1,1,256]{5,4,3,2,1,0:T(1,128)}, u32[]{:S(2)}) copy-start(f32[4,1,256,1,1,256]{5,4,3,2,1,0:T(1,128)} %param.4) | copy-start | bytes 3145732
  6.5 10.1 %copy-start.9 = (s32[2,16]{1,0:T(2,128)S(1)}, s32[2,16]{1,0:T(2,128)}, u32[]{:S(2)}) copy-start(s32[2,16]{1,0:T(2,128)} %param.5) | copy-start | bytes 388
  9.6 14.4 %all-to-all-start = ((f32[16,2,32,128]{3,2,1,0:T(8,128)}), f32[16,2,32,128]{3,2,1,0:T(8,128)S(1)}, u32[]{:S(2)}, u32[]{:S(2)}) async-start(f32[16,2,32,128]{3,2,1,0:T(8,128)} %pad_maximum_fusion.2), calls=%async_computation | async-start | bytes 1048576 | tf_op jit(solution)/shard_map/all_to_all | solution.py:469
  16.5 110.1 %all-gather.8.cloned.1.call-start = ((), (), s32[]{:S(2)}) async-start(), calls=%async_computation.5 | async-start | bytes 7077888 | tf_op jit(solution)/shard_map/all_gather | solution.py:477
  24.0 7.4 %copy-start.2 = (f32[7,32,128]{2,1,0:T(8,128)}, f32[7,32,128]{2,1,0:T(8,128)S(1)}, u32[]{:S(2)}) copy-start(f32[7,32,128]{2,1,0:T(8,128)S(1)} %pad_maximum_fusion.6.mine_ref) | copy-start | bytes 344068
  24.0 6.3 %collective-permute-start.1 = (f32[1,32,128]{2,1,0:T(8,128)S(1)}, f32[1,32,128]{2,1,0:T(8,128)S(1)}, u32[]{:S(2)}, u32[]{:S(2)}) collective-permute-start(f32[1,32,128]{2,1,0:T(8,128)S(1)} %slice.62), channel_id=1, source_target_pairs={{0,112},{1,113},{2,114},{3,115},{4,116},{5,117},{6,118},{7,119},{8... | collective-permute-start | bytes 49160 | tf_op jit(solution)/shard_map/ppermute | solution.py:474
  27.2 4.1 %collective-permute-start = (f32[3,32,128]{2,1,0:T(8,128)S(1)}, f32[3,32,128]{2,1,0:T(8,128)S(1)}, u32[]{:S(2)}, u32[]{:S(2)}) collective-permute-start(f32[3,32,128]{2,1,0:T(8,128)S(1)} %slice_select_fusion.2), channel_id=1, source_target_pairs={{0,96},{16,80},{1,97},{17,81},{2,98},{18,82},{3,99},{19,83},{4,100... | collective-permute-start | bytes 147464 | tf_op jit(solution)/shard_map/ppermute | solution.py:473
  30.3 1.1 copy-start.8
  31.3 0.6 copy-start.7
  89.5 14.6 %copy-start.3 = (f32[7,32,128]{2,1,0:T(8,128)S(1)}, f32[7,32,128]{2,1,0:T(8,128)}, u32[]{:S(2)}) copy-start(f32[7,32,128]{2,1,0:T(8,128)} %copy-done.2) | copy-start | bytes 344068
  91.3 27.4 %collective-permute-start.2 = (f32[2,512,128]{2,1,0:T(8,128)}, f32[2,512,128]{2,1,0:T(8,128)S(1)}, u32[]{:S(2)}, u32[]{:S(2)}) collective-permute-start(f32[2,512,128]{2,1,0:T(8,128)} %get-tuple-element.44), channel_id=1, source_target_pairs={{1,20},{2,23},{3,26},{4,29},{5,16},{6,19},{7,22},{8,25},{9,28},{10... | collective-permute-start | bytes 1572872 | tf_op jit(solution)/shard_map/ppermute | solution.py:492
  93.2 29.1 %collective-permute-start.3 = (f32[2,512,128]{2,1,0:T(8,128)}, f32[2,512,128]{2,1,0:T(8,128)S(1)}, u32[]{:S(2)}, u32[]{:S(2)}) collective-permute-start(f32[2,512,128]{2,1,0:T(8,128)} %get-tuple-element.45), channel_id=1, source_target_pairs={{1,84},{2,87},{3,90},{4,93},{5,80},{6,83},{7,86},{8,89},{9,92},{10... | collective-permute-start | bytes 1572872 | tf_op jit(solution)/shard_map/ppermute | solution.py:492
  99.4 19.2 %all-to-all-start.2 = ((f32[8,2,32,128]{3,2,1,0:T(8,128)}), f32[8,2,32,128]{3,2,1,0:T(8,128)}, u32[]{:S(2)}, u32[]{:S(2)}) async-start(f32[8,2,32,128]{3,2,1,0:T(8,128)} %shard_map.38), calls=%async_computation.2 | async-start | bytes 524288 | tf_op jit(solution)/shard_map/all_to_all | solution.py:484
  104.0 113.4 %all-gather.6.cloned.1.call-start = ((), (), s32[]{:S(2)}) async-start(), calls=%async_computation.4 | async-start | bytes 8355840 | tf_op jit(solution)/shard_map/all_gather | solution.py:498
  105.5 19.2 %copy-start.6 = (s32[34]{0:T(128)S(1)}, s32[34]{0:T(128)}, u32[]{:S(2)}) copy-start(s32[34]{0:T(128)} %pad_add_fusion.meta) | copy-start | bytes 412
  127.7 41.7 %collective-permute-start.4 = (f32[5,3,32,128]{3,2,1,0:T(8,128)S(1)}, f32[5,3,32,128]{3,2,1,0:T(8,128)S(1)}, u32[]{:S(2)}, u32[]{:S(2)}) collective-permute-start(f32[5,3,32,128]{3,2,1,0:T(8,128)S(1)} %get-tuple-element.85), channel_id=1, source_target_pairs={{0,0},{1,8},{2,16},{3,24},{4,32},{5,40},{6,48},{7,56},{8,64},{9,72... | collective-permute-start | bytes 737288 | tf_op jit(solution)/shard_map/ppermute | solution.py:522
  130.7 38.7 %collective-permute-start.5 = (f32[5,3,32,128]{3,2,1,0:T(8,128)S(1)}, f32[5,3,32,128]{3,2,1,0:T(8,128)S(1)}, u32[]{:S(2)}, u32[]{:S(2)}) collective-permute-start(f32[5,3,32,128]{3,2,1,0:T(8,128)S(1)} %get-tuple-element.86), channel_id=1, source_target_pairs={{0,8},{1,0},{2,24},{3,16},{4,40},{5,32},{6,56},{7,48},{8,72},{9,64... | collective-permute-start | bytes 737288 | tf_op jit(solution)/shard_map/ppermute | solution.py:523
  137.0 32.4 %collective-permute-start.6 = (f32[2,512,128]{2,1,0:T(8,128)S(1)}, f32[2,512,128]{2,1,0:T(8,128)S(1)}, u32[]{:S(2)}, u32[]{:S(2)}) collective-permute-start(f32[2,512,128]{2,1,0:T(8,128)S(1)} %pad_maximum_fusion.3), channel_id=1, source_target_pairs={{0,112},{16,0},{32,16},{48,32},{64,48},{80,64},{96,80},{112,96},{1... | collective-permute-start | bytes 1572872 | tf_op jit(solution)/shard_map/ppermute | solution.py:513
  137.1 32.4 %collective-permute-start.7 = (f32[2,512,128]{2,1,0:T(8,128)S(1)}, f32[2,512,128]{2,1,0:T(8,128)S(1)}, u32[]{:S(2)}, u32[]{:S(2)}) collective-permute-start(f32[2,512,128]{2,1,0:T(8,128)S(1)} %pad_maximum_fusion.4), channel_id=1, source_target_pairs={{0,16},{16,32},{32,48},{48,64},{64,80},{80,96},{96,112},{112,0},{1... | collective-permute-start | bytes 1572872 | tf_op jit(solution)/shard_map/ppermute | solution.py:514
  169.5 2.4 copy-start.4
  171.9 63.1 %all-to-all-start.3 = ((f32[8,2,5,3,32,128]{5,4,3,2,1,0:T(8,128)}), f32[8,2,5,3,32,128]{5,4,3,2,1,0:T(8,128)}, u32[]{:S(2)}, u32[]{:S(2)}) async-start(f32[8,2,5,3,32,128]{5,4,3,2,1,0:T(8,128)} %broadcast_in_dim.2), calls=%async_computation.3 | async-start | bytes 7864320 | tf_op jit(solution)/shard_map/all_to_all | solution.py:548
  177.0 33.8 %copy-start.5 = (f32[2,512,128]{2,1,0:T(8,128)S(1)}, f32[2,512,128]{2,1,0:T(8,128)}, u32[]{:S(2)}) copy-start(f32[2,512,128]{2,1,0:T(8,128)} %copy-done.4) | copy-start | bytes 1572868
  210.9 24.1 %copy-start = (f32[6,512,128]{2,1,0:T(8,128)}, f32[6,512,128]{2,1,0:T(8,128)S(1)}, u32[]{:S(2)}) copy-start(f32[6,512,128]{2,1,0:T(8,128)S(1)} %pad_maximum_fusion.1.child_1) | copy-start | bytes 4718596
  211.0 35.2 %collective-permute-start.11 = (f32[3,512,128]{2,1,0:T(8,128)S(1)}, f32[3,512,128]{2,1,0:T(8,128)}, u32[]{:S(2)}, u32[]{:S(2)}) collective-permute-start(f32[3,512,128]{2,1,0:T(8,128)S(1)} %get-tuple-element.73), channel_id=1, source_target_pairs={{0,1},{1,2},{2,3},{3,4},{4,5},{5,6},{6,7},{7,8},{8,9},{9,10},{10,1... | collective-permute-start | bytes 2359304 | tf_op jit(solution)/shard_map/ppermute | solution.py:560
  212.0 34.2 %collective-permute-start.9 = (f32[3,512,128]{2,1,0:T(8,128)S(1)}, f32[3,512,128]{2,1,0:T(8,128)}, u32[]{:S(2)}, u32[]{:S(2)}) collective-permute-start(f32[3,512,128]{2,1,0:T(8,128)S(1)} %get-tuple-element.73), channel_id=1, source_target_pairs={{0,15},{1,0},{2,1},{3,2},{4,3},{5,4},{6,5},{7,6},{8,7},{9,8},{10,9... | collective-permute-start | bytes 2359304 | tf_op jit(solution)/shard_map/ppermute | solution.py:561
  213.1 35.1 %collective-permute-start.10 = (f32[3,512,128]{2,1,0:T(8,128)S(1)}, f32[3,512,128]{2,1,0:T(8,128)}, u32[]{:S(2)}, u32[]{:S(2)}) collective-permute-start(f32[3,512,128]{2,1,0:T(8,128)S(1)} %get-tuple-element.74), channel_id=1, source_target_pairs={{0,1},{1,2},{2,3},{3,4},{4,5},{5,6},{6,7},{7,8},{8,9},{9,10},{10,1... | collective-permute-start | bytes 2359304 | tf_op jit(solution)/shard_map/ppermute | solution.py:560
  217.4 34.9 %collective-permute-start.8 = (f32[3,512,128]{2,1,0:T(8,128)S(1)}, f32[3,512,128]{2,1,0:T(8,128)}, u32[]{:S(2)}, u32[]{:S(2)}) collective-permute-start(f32[3,512,128]{2,1,0:T(8,128)S(1)} %get-tuple-element.74), channel_id=1, source_target_pairs={{0,15},{1,0},{2,1},{3,2},{4,3},{5,4},{6,5},{7,6},{8,7},{9,8},{10,9... | collective-permute-start | bytes 2359304 | tf_op jit(solution)/shard_map/ppermute | solution.py:561
Sparse Core Ops, SparseCore 0:
  60.2 47.8 all-gather.7
  124.6 83.0 all-gather.5
